TPU v7x, 32 devices: a whole 2x2x4 slice. The times are simulated.
32 devices in a mesh: grid: 8 (over z, core), pencil: 4 (over y, x).
Axes of the slice: x: 2, y: 2, z: 4, core: 2. Of those that a mesh axis runs over, the one named last changes fastest.
Arguments:
- field: bfloat16 [8, 512, 256, 128], P('grid', 'pencil'), may hold values from -6 to 6
- levels: int32 [8, 3], P('grid'), may hold values from 7 to 9, as said below
- coefficients: int32 [8], P('grid'), may hold values from -2 to 2
- failed: int32 [8], P('grid'), may hold values 0 or 1
- owner_map: int32 [64], replicated, may hold values from -1 to 47, as said below
- velocity: float32 [3], replicated, may hold values from -1 to 1
- diffusivity: float32 [3], replicated, may hold values from 0.5 to 4
Outputs:
- combined: float32 [48, 2, 128, 4096], P('grid', None, 'pencil')
Inputs may be any that keep to these rules, and one draw needn't show every extreme that they name: `levels`: each row is (9, 8, 7) or (8, 9, 7); each occurs in 4 rows. `owner_map`: blocks held by no grid map to -1; every other block maps to a distinct row, and every row is named once. Owner o holds rows o * 6 to o * 6 + 5: 2 blocks held by grids of both level vectors and 2 held only by grids of each one, so every grid holds exactly 4 of each owner's blocks.
All inputs are finite; a program needn't handle non-finite values. No bound on the sum of `failed` on one device may be relied on, other than what follows from the above.
Results may differ from a plain program's by a relative error of at most 0.0056.
Values may be sent and summed in bfloat16 or wider, within the bound.
No kernel may reach another device: no remote copies, remote signals or barrier semaphores. Data moves between devices by JAX's collectives and lax.ppermute only.
A program may use at most 320 MiB of HBM per device.

v0:
```python
import math

import jax
import jax.numpy as jnp
from jax import lax
from jax.sharding import PartitionSpec as P


def signed_modes(positions, length):
    return jnp.where(positions < length // 2, positions, positions - length).astype(jnp.float32)


def dft_tables(length):
    positions = jnp.arange(length, dtype=jnp.int32)
    product = positions[:, None] * positions[None, :] % length
    angles = product.astype(jnp.float32) * (2.0 * math.pi / length)
    return jnp.stack([jnp.cos(angles), -jnp.sin(angles)]).astype(jnp.bfloat16)


def complex_table(length):
    tables = dft_tables(length)
    return jnp.stack([jnp.stack([tables[0], -tables[1]]), jnp.stack([tables[1], tables[0]])])


def apply_factor(
    spectrum,
    z_modes,
    long_modes,
    mid_modes,
    swapped,
    velocity,
    diffusivity,
    long_len,
    mid_len,
    z_len,
):
    nu_long = jnp.where(swapped, diffusivity[1], diffusivity[0])
    nu_mid = jnp.where(swapped, diffusivity[0], diffusivity[1])
    speed_long = jnp.where(swapped, velocity[1], velocity[0])
    speed_mid = jnp.where(swapped, velocity[0], velocity[1])
    z_grid = z_modes[:, None, None]
    long_grid = long_modes[None, :, None]
    mid_grid = mid_modes[None, None, :]
    exponent = (
        diffusivity[2] * z_grid * z_grid
        + nu_long * long_grid * long_grid
        + nu_mid * mid_grid * mid_grid
    ) * (-4.0 / (long_len * long_len))
    phases = (velocity[2] * z_grid + speed_long * long_grid + speed_mid * mid_grid) * (
        -2.0 * math.pi / mid_len
    )
    magnitude = jnp.exp(exponent) * (1.0 / math.sqrt(long_len * mid_len * z_len))
    factor_re = magnitude * jnp.cos(phases)
    factor_im = magnitude * jnp.sin(phases)
    real_part = spectrum[0] * factor_re - spectrum[1] * factor_im
    imag_part = spectrum[0] * factor_im + spectrum[1] * factor_re
    return jnp.stack([real_part, imag_part])


def block_rows(swapped, owner_map, per_long, per_mid):
    along_long = jnp.arange(per_long, dtype=jnp.int32)[:, None] * jnp.ones((1, per_mid), jnp.int32)
    mid_raw = jnp.arange(per_mid, dtype=jnp.int32)
    mid_global = jnp.where(mid_raw < per_mid // 2, mid_raw, mid_raw + per_long - per_mid)
    along_mid = jnp.ones((per_long, 1), jnp.int32) * mid_global[None, :]
    block_x = jnp.where(swapped, along_mid, along_long)
    block_y = jnp.where(swapped, along_long, along_mid)
    return owner_map[(block_x * per_long + block_y).reshape(-1)]


def turn_inner(grouped):
    return grouped.transpose(0, 1, 2, 3, 5, 4)


def keep_inner(grouped):
    return grouped


def body(field, levels, coefficients, failed, owner_map, velocity, diffusivity):
    samples = field[0]
    local_long, mid_len, z_len = samples.shape
    pencils = lax.axis_size("pencil")
    grid_count = lax.axis_size("grid")
    long_len = local_long * pencils
    z_local = z_len // pencils
    block_len = mid_len // 4
    per_long = long_len // block_len
    per_mid = mid_len // block_len
    swapped = levels[0, 0] < levels[0, 1]
    along_z = jnp.einsum(
        "abc,pck->pabk", samples, dft_tables(z_len), preferred_element_type=jnp.float32
    ).astype(jnp.bfloat16)
    along_mid = jnp.einsum(
        "qabc,pqbd->padc", along_z, complex_table(mid_len), preferred_element_type=jnp.float32
    ).astype(jnp.bfloat16)
    table_long = complex_table(long_len)
    spectrum = jnp.einsum(
        "qabc,pqae->pceb",
        lax.all_to_all(along_mid, "pencil", split_axis=3, concat_axis=1, tiled=True),
        table_long,
        preferred_element_type=jnp.float32,
    )
    z_start = lax.axis_index("pencil") * z_local
    z_modes = signed_modes(z_start + jnp.arange(z_local, dtype=jnp.int32), z_len)
    long_modes = signed_modes(jnp.arange(long_len, dtype=jnp.int32), long_len)
    mid_modes = signed_modes(jnp.arange(mid_len, dtype=jnp.int32), mid_len)
    shifted = apply_factor(
        spectrum,
        z_modes,
        long_modes,
        mid_modes,
        swapped,
        velocity,
        diffusivity,
        long_len,
        mid_len,
        z_len,
    )
    grouped = shifted.reshape(2, z_local, per_long, block_len, per_mid, block_len).transpose(
        2, 4, 0, 1, 3, 5
    )
    turned = lax.cond(swapped, turn_inner, keep_inner, grouped)
    held_count = per_long * per_mid
    blocks = turned.reshape(held_count, 2, z_local, block_len * block_len)
    row_ids = block_rows(swapped, owner_map, per_long, per_mid)
    weight = (coefficients[0] * (1 - failed[0])).astype(jnp.float32)
    weighted = blocks * weight
    slot_count = (2 * held_count - per_mid * per_mid) // grid_count
    capacity = held_count // grid_count
    owners = row_ids // slot_count
    slot_ids = row_ids % slot_count
    positions_all = jnp.arange(held_count, dtype=jnp.int32)
    earlier = (owners[:, None] == owners[None, :]) & (
        positions_all[None, :] < positions_all[:, None]
    )
    rank_in = jnp.sum(earlier.astype(jnp.int32), axis=1)
    target = owners * capacity + rank_in
    outgoing = (
        jnp.zeros_like(weighted)
        .at[target]
        .set(weighted)
        .reshape(grid_count, capacity, 2, z_local, block_len * block_len)
    )
    labels = (
        jnp.zeros((held_count,), jnp.float32)
        .at[target]
        .set(slot_ids.astype(jnp.float32))
        .reshape(grid_count, capacity)
    )
    incoming, got_labels = (
        lax.all_to_all(outgoing, "grid", split_axis=0, concat_axis=0, tiled=True),
        lax.all_to_all(labels, "grid", split_axis=0, concat_axis=0, tiled=True),
    )
    selector = (
        got_labels.reshape(1, -1)
        == jnp.arange(slot_count, dtype=jnp.int32).astype(jnp.float32)[:, None]
    ).astype(jnp.float32)
    combined = jnp.dot(
        selector, incoming.reshape(grid_count * capacity, -1), precision=lax.Precision.HIGHEST
    ).reshape(slot_count, 2, z_local, block_len * block_len)
    return combined


def solution(mesh):
    placed = (P("grid", "pencil", None, None), P("grid", None), P("grid"), P("grid"), P(), P(), P())
    return jax.shard_map(
        body, mesh=mesh, in_specs=placed, out_specs=P("grid", None, "pencil", None), check_vma=False
    )
```

profile of v0, /device:TPU:0, one launch (start us, length us, event | category | flops | bytes accessed | tf_op | source)
XLA Modules:
  0.0 1526.3 jit_solution(4649278032232605509)
XLA Ops:
  0.0 0.0 copy-start
  0.0 1.1 negate_convert_fusion.1
  1.1 1.0 fusion.38
  2.1 0.3 negate_convert_fusion.2
  2.4 17.5 %fusion.6 = bf16[2,128,256,128]{3,2,1,0:T(8,128)(2,1)} fusion(bf16[1,128,256,128]{3,2,1,0:T(8,128)(2,1)} %param.9, bf16[1,2,256,256]{2,3,1,0:T(8,128)(2,1)S(1)} %get-tuple-element.19, bf16[1,2,256,256]{2,3,1,0:T(8,128)(2,1)S(1)} %get-tuple-element.18, bf16[1,128,128]{1,2,0:T(8,128)(2,1)S(1)} %get-tuple-element.31, ...), kind=kOutput, calls=%fused_computation.17 | convolution fusion | flops 10755375104 | bytes 25755648 | tf_op jit(solution)/shard_map/qabc,pqbd->padc/dot_general | solution.py:92
  19.9 22.9 %copy.30 = bf16[2,128,256,128]{2,1,0,3:T(8,128)(2,1)} copy(bf16[2,128,256,128]{3,2,1,0:T(8,128)(2,1)} %fusion.6) | data formatting | bytes 33554432 | tf_op jit(solution)/shard_map/convert_element_type | solution.py:94
  42.8 7.1 all-to-all-start.1
  50.0 0.0 copy-done.4
  50.0 0.6 fusion.61
  51.9 0.7 fusion.60
  55.2 0.0 copy-done.3
  55.2 0.7 fusion.59
  59.7 0.1 add.266
  59.9 0.7 gather_fusion
  60.6 0.2 convert_reduce_fusion
  60.8 0.7 scatter_custom_fusion
  61.5 0.7 all_to_all.22
  62.1 1.3 multiply_multiply_fusion.2
  63.5 4.0 fusion.27
  67.6 4.3 negate_convert_fusion
  71.9 0.2 maximum_bitcast_fusion.2
  72.1 0.1 broadcast_add_fusion
  72.2 0.1 broadcast_add_fusion.1
  72.3 161.4 %all-to-all-done.1 = bf16[2,128,256,128]{2,1,0,3:T(8,128)(2,1)} async-done(((bf16[2,128,256,128]{2,1,0,3:T(8,128)(2,1)}), bf16[2,128,256,128]{2,1,0,3:T(8,128)(2,1)}, u32[]{:S(2)}, u32[]{:S(2)}) %all-to-all-start.1) | async-done | bytes 16777248 | tf_op jit(solution)/shard_map/all_to_all | solution.py:98
  233.7 5.3 all-to-all-start
  239.0 14.0 copy.32
  253.0 27.1 %convolution_bitcast_fusion = f32[2,32,512,256]{3,2,1,0:T(8,128)} fusion(bf16[2,512,256,32,1]{2,1,0,3,4:T(8,128)(2,1)} %bitcast.111, bf16[1,2,512,512]{2,3,1,0:T(8,128)(2,1)S(1)} %get-tuple-element.17, bf16[1,2,512,512]{2,3,1,0:T(8,128)(2,1)S(1)} %get-tuple-element.16), kind=kOutput, calls=%fused_computation.6 | convolution fusion | flops 17184063488 | bytes 52428800 | tf_op jit(solution)/shard_map/qabc,pqae->pceb/dot_general | solution.py:96
  280.1 77.1 %multiply_add_fusion = (f32[1,32,512,256]{3,2,1,0:T(8,128)}, f32[1,32,512,256]{3,2,1,0:T(8,128)}) fusion(f32[2,32,512,256]{3,2,1,0:T(8,128)} %convolution_bitcast_fusion, f32[256]{0:T(256)S(1)} %get-tuple-element.38, f32[32,512]{1,0:T(8,128)S(1)} %broadcast_add_fusion, f32[256]{0:T(256)S(1)} %get-tuple-element.37, f32[32,512]{1,0:T(8,128)S(1)} %broadcast_add_fusion.1), kind=kLoop, calls=%fused_computation.9 | loop fusion | flops 54525952 | bytes 67241984 | tf_op jit(solution)/shard_map/add | solution.py:56
  357.2 28.4 %stack.67 = f32[1,32,8,64,4,64]{5,4,3,2,1,0:T(4,128)} reshape(f32[1,32,512,256]{3,2,1,0:T(8,128)} %get-tuple-element.15) | data formatting | bytes 33554432 | tf_op jit(solution)/shard_map/stack | solution.py:57
  385.6 23.0 %constant_dynamic-update-slice_fusion.1 = f32[2,32,8,64,4,64]{5,4,3,2,1,0:T(4,128)} fusion(f32[1,32,8,64,4,64]{5,4,3,2,1,0:T(4,128)} %stack.67), kind=kLoop, calls=%fused_computation.75 | loop fusion | bytes 50331648
  408.6 28.4 %stack.68 = f32[1,32,8,64,4,64]{5,4,3,2,1,0:T(4,128)} reshape(f32[1,32,512,256]{3,2,1,0:T(8,128)} %get-tuple-element.14) | data formatting | bytes 33554432 | tf_op jit(solution)/shard_map/stack | solution.py:57
  437.0 23.0 %constant_dynamic-update-slice_fusion = f32[2,32,8,64,4,64]{5,4,3,2,1,0:T(4,128)} fusion(f32[2,32,8,64,4,64]{5,4,3,2,1,0:T(4,128)} %constant_dynamic-update-slice_fusion.1, f32[1,32,8,64,4,64]{5,4,3,2,1,0:T(4,128)} %stack.68), kind=kLoop, calls=%fused_computation.74 | loop fusion | bytes 67108864 | tf_op jit(solution)/shard_map/stack | solution.py:57
  460.0 99.0 %conditional.1 = (f32[32,2,32,4096]{3,2,1,0:T(8,128)}) conditional(s32[]{:T(128)} %convert_element_type.135, f32[8,4,2,32,64,64]{5,1,4,0,3,2:T(4,128)} %bitcast.42, f32[2,32,8,64,4,64]{5,4,3,2,1,0:T(4,128)} %constant_dynamic-update-slice_fusion), branch_computations={%region_2.3_spmd, %region_3.4_spmd} | conditional | bytes 134217728 | solution.py:121
  460.2 44.0 %copy.33 = f32[8,4,2,32,64,64]{5,4,3,2,1,0:T(8,128)} copy(f32[8,4,2,32,64,64]{5,1,4,0,3,2:T(4,128)} %param) | data formatting | bytes 67108864 | tf_op jit(solution)/shard_map/transpose
  504.2 54.8 %reshape.527 = f32[32,2,32,4096]{3,2,1,0:T(8,128)} reshape(f32[8,4,2,32,64,64]{5,4,3,2,1,0:T(8,128)} %copy.33) | data formatting | bytes 67108864 | tf_op jit(solution)/shard_map/reshape | solution.py:123
  559.0 22.8 %broadcast_multiply_fusion = f32[32,2,32,4096]{3,2,1,0:T(8,128)} fusion(f32[32,2,32,4096]{3,2,1,0:T(8,128)} %get-tuple-element.39, f32[]{:T(128)} %bitcast.43), kind=kLoop, calls=%fused_computation.8 | loop fusion | flops 8388608 | bytes 67108864 | tf_op jit(solution)/shard_map/mul | solution.py:126
  581.8 11.2 broadcast_in_dim.5
  593.0 59.8 %scatter_fusion = f32[32,2,32,4096]{3,2,1,0:T(8,128)} fusion(f32[32,2,32,4096]{3,2,1,0:T(8,128)} %broadcast_in_dim.5, s32[32]{0:T(128)S(1)} %copy-done.6, f32[32,2,32,4096]{3,2,1,0:T(8,128)} %broadcast_multiply_fusion), kind=kCustom, calls=%fused_computation.2 | custom fusion | bytes 100663424 | tf_op jit(solution)/shard_map/scatter | solution.py:140
  652.9 0.0 all-to-all-done
  652.9 36.5 %all-to-all-start.2 = ((f32[8,4,2,32,4096]{4,3,2,1,0:T(8,128)}), f32[8,4,2,32,4096]{4,3,2,1,0:T(8,128)}, u32[]{:S(2)}, u32[]{:S(2)}) async-start(f32[8,4,2,32,4096]{4,3,2,1,0:T(8,128)} %bitcast.108), calls=%async_computation.2 | async-start | bytes 67108864 | tf_op jit(solution)/shard_map/all_to_all | solution.py:150
  689.3 0.5 broadcast.697
  689.9 1.3 reduce.3
  691.2 0.1 eq.39
  691.3 720.5 %all-to-all-done.2 = f32[8,4,2,32,4096]{4,3,2,1,0:T(8,128)} async-done(((f32[8,4,2,32,4096]{4,3,2,1,0:T(8,128)}), f32[8,4,2,32,4096]{4,3,2,1,0:T(8,128)}, u32[]{:S(2)}, u32[]{:S(2)}) %all-to-all-start.2) | async-done | bytes 33554464 | tf_op jit(solution)/shard_map/all_to_all | solution.py:150
  1411.8 32.4 %reshape.532 = f32[32,262144]{1,0:T(8,128)} reshape(f32[8,4,2,32,4096]{4,3,2,1,0:T(8,128)} %all-to-all-done.2) | data formatting | bytes 67108864 | tf_op jit(solution)/shard_map/reshape | solution.py:158
  1444.1 31.8 %copy.45 = f32[4,8,64,4096]{3,2,1,0:T(8,128)} copy(f32[4,8,64,4096]{3,1,2,0:T(8,128)} %bitcast.110) | data formatting | bytes 67108864
  1475.9 40.5 %fusion = f32[6,2,32,4096]{3,0,2,1:T(8,128)} fusion(f32[2,32,4096,32]{2,1,0,3:T(8,128)} %bitcast.109, f32[32]{0:T(128)S(1)} %eq.39, f32[6]{0:T(128)S(1)} %iota_convert_fusion), kind=kOutput, calls=%fused_computation.4 | convolution fusion | flops 603979968 | bytes 39846040 | tf_op jit(solution)/shard_map/dot_general | solution.py:157
  1516.4 9.7 copy.35
  (22 shorter events, 0.2 us)
Async XLA Ops:
  0.0 59.8 %copy-start = (s32[64]{0:T(128)S(1)}, s32[64]{0:T(128)}, u32[]{:S(2)}) copy-start(s32[64]{0:T(128)} %param.13) | copy-start | bytes 772
  42.8 7.2 copy-start.4
  42.8 9.0 copy-start.2
  42.8 12.4 copy-start.3
  42.8 190.9 %all-to-all-start.1 = ((bf16[2,128,256,128]{2,1,0,3:T(8,128)(2,1)}), bf16[2,128,256,128]{2,1,0,3:T(8,128)(2,1)}, u32[]{:S(2)}, u32[]{:S(2)}) async-start(bf16[2,128,256,128]{2,1,0,3:T(8,128)(2,1)} %copy.30), calls=%async_computation.1 | async-start | bytes 33554432 | tf_op jit(solution)/shard_map/all_to_all | solution.py:98
  60.8 11.1 copy-start.5
  233.7 419.2 %all-to-all-start = ((f32[8,1,4]{2,1,0:T(1,128)}), f32[8,1,4]{2,1,0:T(1,128)}, u32[]{:S(2)}, u32[]{:S(2)}) async-start(f32[8,1,4]{2,1,0:T(1,128)} %bitcast.7), calls=%async_computation | async-start | bytes 8192 | tf_op jit(solution)/shard_map/all_to_all | solution.py:151
  581.8 11.2 copy-start.6
  652.9 758.9 %all-to-all-start.2 = ((f32[8,4,2,32,4096]{4,3,2,1,0:T(8,128)}), f32[8,4,2,32,4096]{4,3,2,1,0:T(8,128)}, u32[]{:S(2)}, u32[]{:S(2)}) async-start(f32[8,4,2,32,4096]{4,3,2,1,0:T(8,128)} %bitcast.108), calls=%async_computation.2 | async-start | bytes 67108864 | tf_op jit(solution)/shard_map/all_to_all | solution.py:150
  1475.9 50.2 %copy-start.1 = (s32[64]{0:T(128)S(1)}, s32[64]{0:T(128)}, u32[]{:S(2)}) copy-start(s32[64]{0:T(128)} %param.13) | copy-start | bytes 772
where the time goes:
time: 1540 us; the launch traced here: 1530 us
  waiting for transfers between devices  882 us (57%)
  local copies, waits for them, and re-layouts  388 us (25%)
  other arithmetic  114 us (7%)
  matrix products  85 us (6%)
  starting transfers between devices  48.9 us (3%)
    all_to_all x1, waiting for transfers between devices, body(): lax.all_to_all(outgoing, 'grid', split_axis=0, concat_axis=0, tiled=True)  720 us
    all_to_all x1, waiting for transfers between devices, body(): lax.all_to_all(along_mid, 'pencil', split_axis=3, concat_axis=1, tiled=True)  161 us
    another operation x3, local copies, waits for them, and re-layouts, apply_factor(): return jnp.stack([real_part, imag_part])  79.8 us
    add x1, other arithmetic, apply_factor(): imag_part = spectrum[0] * factor_im + spectrum[1] * factor_re  77.1 us
    scatter x1, local copies, waits for them, and re-layouts, body(): outgoing = jnp.zeros_like(weighted).at[target].set(weighted).reshape(grid...  59.8 us
    reshape x1, local copies, waits for them, and re-layouts, body(): blocks = turned.reshape(held_count, 2, z_local, block_len * block_len)  54.8 us
    unnamed x16, local copies, waits for them, and re-layouts  54.8 us
    transpose x1, local copies, waits for them, and re-layouts  44 us
  transfers between devices with their start and end apart: 3, of which 2 were waited for; matrix products, arithmetic and copies ran while one was open for 28% of the time, Pallas kernels for 0%

commit v1 on v0

--- a/solution.py
+++ b/solution.py
@@ -1,9 +1,16 @@
+import functools
 import math
 
 import jax
 import jax.numpy as jnp
+import numpy as np
 from jax import lax
+from jax.experimental import pallas as pl
+from jax.experimental.pallas import tpu as pltpu
 from jax.sharding import PartitionSpec as P
+
+CHUNKS = 2
+VMEM_LIMIT = 56 * 1024 * 1024
 
 
 def signed_modes(positions, length):
@@ -75,7 +82,7 @@
     return grouped
 
 
-def body(field, levels, coefficients, failed, owner_map, velocity, diffusivity):
+def wide_body(field, levels, coefficients, failed, owner_map, velocity, diffusivity):
     samples = field[0]
     local_long, mid_len, z_len = samples.shape
     pencils = lax.axis_size("pencil")
@@ -160,8 +167,386 @@
     return combined
 
 
+def host_tables(length):
+    positions = np.arange(length)
+    angles = (positions[:, None] * positions[None, :] % length) * (2.0 * math.pi / length)
+    return np.cos(angles), -np.sin(angles)
+
+
+def z_table(chunk, chunks, grid_count, pencils, z_len):
+    groups = pencils // 2
+    per_device = z_len // (grid_count * pencils)
+    slots = per_device // chunks
+    cos, sin = host_tables(z_len)
+    table = np.zeros((grid_count, 2, chunks, groups, slots, chunks, z_len))
+    for device in range(grid_count):
+        for group in range(groups):
+            for slot in range(slots):
+                index = chunk * slots + slot
+                mode = group * (z_len // pencils) + device * per_device + index
+                parts = [cos[:, mode], sin[:, mode]]
+                if mode == 0:
+                    parts[1] = cos[:, z_len // 2]
+                for half in range(chunks):
+                    table[device, 0, half, group, slot, half] = parts[0]
+                    table[device, 1, half, group, slot, half] = parts[1]
+    return jnp.asarray(table.reshape(-1, chunks * z_len), jnp.bfloat16)
+
+
+def mid_table(mid_len, block_len):
+    cos, sin = host_tables(mid_len)
+    order = np.arange(mid_len).reshape(mid_len // block_len, block_len // 2, 2).transpose(2, 0, 1).reshape(-1)
+    plain = np.concatenate([cos, sin], axis=1)
+    turned = np.concatenate([cos[:, order], sin[:, order]], axis=1)
+    return jnp.asarray(np.stack([plain, turned]), jnp.bfloat16)
+
+
+def long_tables(long_len, block_len, pencils):
+    cos, sin = host_tables(long_len)
+    order = np.arange(long_len).reshape(long_len // block_len, block_len // 2, 2).transpose(2, 0, 1).reshape(-1)
+    real = np.stack([cos, -sin]).reshape(2, long_len, pencils, -1).transpose(1, 2, 0, 3).reshape(long_len, -1)
+    imag = np.stack([sin, cos]).reshape(2, long_len, pencils, -1).transpose(1, 2, 0, 3).reshape(long_len, -1)
+    first = np.concatenate([real[order], imag[order]], axis=0)
+    second = np.concatenate([real, imag], axis=0).T
+    return jnp.asarray(first, jnp.bfloat16), jnp.asarray(second, jnp.bfloat16)
+
+
+def z_kernel(table_ref, field_ref, out_ref):
+    halves, rows, mid_len, z_len = field_ref.shape
+    lines = [field_ref[half].reshape(rows * mid_len, z_len) for half in range(halves)]
+    joined = jnp.concatenate(lines, axis=1)
+    out_ref[...] = lax.dot_general(
+        table_ref[...], joined, (((1,), (1,)), ((), ())), preferred_element_type=jnp.float32
+    ).astype(jnp.bfloat16)
+
+
+def transform_z(samples, table, chunks):
+    local_long, mid_len, z_len = samples.shape
+    columns = table.shape[0]
+    rows = 8
+    split = samples.reshape(chunks, local_long // chunks, mid_len, z_len)
+    return pl.pallas_call(
+        z_kernel,
+        grid=(local_long // chunks // rows,),
+        in_specs=[
+            pl.BlockSpec(table.shape, lambda i: (0, 0)),
+            pl.BlockSpec((chunks, rows, mid_len, z_len), lambda i: (0, i, 0, 0)),
+        ],
+        out_specs=pl.BlockSpec((columns, rows * mid_len), lambda i: (0, i)),
+        out_shape=jax.ShapeDtypeStruct((columns, local_long // chunks * mid_len), jnp.bfloat16),
+        compiler_params=pltpu.CompilerParams(vmem_limit_bytes=VMEM_LIMIT),
+        cost_estimate=pl.CostEstimate(
+            flops=2 * columns * samples.size, bytes_accessed=4 * samples.size, transcendentals=0
+        ),
+        name="transform_z",
+    )(table, split)
+
+
+def mid_kernel(first_chunk, rows, weights_ref, place_ref, table_ref, *refs):
+    sources, out_ref = refs[:-1], refs[-1]
+    columns = sources[0].shape[0]
+    mid_len = table_ref.shape[1]
+    half = columns // 2
+    pencils, classes, slots, _, halves = out_ref.shape[:5]
+    groups = pencils // 2
+    lead = place_ref[0] == 0
+    row_ids = lax.broadcasted_iota(jnp.int32, (rows, half, mid_len), 1)
+    special = lead & (row_ids % (groups * slots) == 0)
+    for kind in range(classes):
+        total = None
+        for number, source in enumerate(sources):
+            term = source[...].astype(jnp.float32) * weights_ref[kind, number]
+            total = term if total is None else total + term
+        total = total.astype(jnp.bfloat16)
+        lines = jnp.concatenate([total[:, a * mid_len : (a + 1) * mid_len] for a in range(rows)], axis=0)
+        product = jnp.dot(lines, table_ref[kind], preferred_element_type=jnp.float32)
+        product = product.reshape(rows, columns, 2 * mid_len)
+        re_cos, re_sin = product[:, :half, :mid_len], product[:, :half, mid_len:]
+        im_cos, im_sin = product[:, half:, :mid_len], product[:, half:, mid_len:]
+        plus = [re_cos - im_sin, re_sin + im_cos]
+        minus = [re_cos + im_sin, re_sin - im_cos]
+        if first_chunk:
+            plus = [jnp.where(special, re_cos, plus[0]), jnp.where(special, re_sin, plus[1])]
+            minus = [jnp.where(special, im_cos, minus[0]), jnp.where(special, im_sin, minus[1])]
+        for part in range(2):
+            up = jnp.transpose(plus[part], (1, 0, 2))
+            down = jnp.transpose(minus[part], (1, 0, 2))
+            for piece in range(halves):
+                for group in range(groups):
+                    for slot in range(slots):
+                        at = (piece * groups + group) * slots + slot
+                        out_ref[group, kind, slot, part, piece] = up[at].astype(jnp.bfloat16)
+                        value = down[at]
+                        if first_chunk and slot == 0:
+                            other = (piece * groups + (group + 1) % groups) * slots
+                            value = jnp.where(lead, down[other], value)
+                        out_ref[pencils - 1 - group, kind, slot, part, piece] = value.astype(jnp.bfloat16)
+
+
+def transform_mid(sources, weights, place, table, first_chunk, chunks, pencils, slots):
+    columns, length = sources[0].shape
+    classes, mid_len, _ = table.shape
+    lines = length // mid_len
+    rows = 16
+    shape = (pencils, classes, slots, 2, chunks, lines, mid_len)
+    return pl.pallas_call(
+        functools.partial(mid_kernel, first_chunk, rows),
+        grid=(lines // rows,),
+        in_specs=[
+            pl.BlockSpec(memory_space=pltpu.SMEM),
+            pl.BlockSpec(memory_space=pltpu.SMEM),
+            pl.BlockSpec(table.shape, lambda i: (0, 0, 0)),
+        ]
+        + [pl.BlockSpec((columns, rows * mid_len), lambda i: (0, i))] * len(sources),
+        out_specs=pl.BlockSpec(shape[:5] + (rows, mid_len), lambda i: (0, 0, 0, 0, 0, i, 0)),
+        out_shape=jax.ShapeDtypeStruct(shape, jnp.bfloat16),
+        compiler_params=pltpu.CompilerParams(vmem_limit_bytes=VMEM_LIMIT),
+        cost_estimate=pl.CostEstimate(
+            flops=8 * columns * length * mid_len,
+            bytes_accessed=2 * len(sources) * columns * length + 2 * math.prod(shape),
+            transcendentals=0,
+        ),
+        name="transform_mid",
+    )(weights, place, table, *sources)
+
+
+def long_kernel(rows_ref, place_ref, z_ref, first_ref, second_ref, plane_ref, *refs):
+    sources, out_ref, gathered = refs[:-2], refs[-2], refs[-1]
+    pencils = len(sources)
+    classes, _, _, local_long, mid_len = sources[0].shape
+    depth = 2 * pencils * local_long
+    long_len = pencils * local_long
+    pairs = out_ref.shape[3]
+    per_long = long_len // (2 * pairs)
+    per_mid = mid_len // (2 * pairs)
+    edge = per_mid // 2
+    slot = pl.program_id(0)
+    for number, source in enumerate(sources):
+        for kind in range(classes):
+            gathered[kind, place_ref[1] ^ number] = source[kind, 0]
+    first = jnp.dot(first_ref[...], gathered[0].reshape(depth, mid_len), preferred_element_type=jnp.float32)
+    second = lax.dot_general(
+        gathered[1].reshape(depth, mid_len),
+        second_ref[...],
+        (((0,), (0,)), ((), ())),
+        preferred_element_type=jnp.float32,
+    )
+    z_re, z_im = z_ref[0, slot], z_ref[1, slot]
+    low = lax.broadcasted_iota(jnp.int32, (pairs, 4 * pairs), 1) < 2 * pairs
+    span = 4 * pairs
+    for across in range(per_long):
+        held = across < edge or across >= per_long - edge
+        narrow = across if across < edge else across - (per_long - per_mid)
+        for couple in range(per_long // 2):
+            near = couple < edge // 2 or couple >= (per_long - edge) // 2
+            thin = couple if couple < edge // 2 else couple - (per_long - per_mid) // 2
+            if not held and not near:
+                continue
+            tiles = []
+            for parity in range(2):
+                parts = []
+                for part in range(2):
+                    value = None
+                    if near:
+                        top = ((part * 2 + parity) * per_long + across) * pairs
+                        value = first[top : top + pairs, thin * span : (thin + 1) * span]
+                    if held:
+                        top = (parity * per_mid + narrow) * pairs
+                        left = part * long_len + couple * span
+                        term = second[top : top + pairs, left : left + span]
+                        value = term if value is None else value + term
+                    parts.append(value)
+                top = across * pairs
+                plane_re = plane_ref[0, parity, top : top + pairs, couple * span : (couple + 1) * span]
+                plane_im = plane_ref[1, parity, top : top + pairs, couple * span : (couple + 1) * span]
+                factor_re = plane_re * z_re - plane_im * z_im
+                factor_im = plane_re * z_im + plane_im * z_re
+                tiles.append(
+                    [
+                        parts[0] * factor_re - parts[1] * factor_im,
+                        parts[0] * factor_im + parts[1] * factor_re,
+                    ]
+                )
+            for part in range(2):
+                even, odd = tiles[0][part], tiles[1][part]
+                block = across * per_long + 2 * couple
+                left = jnp.where(low, even, pltpu.roll(odd, 2 * pairs, 1))
+                right = jnp.where(low, pltpu.roll(even, 2 * pairs, 1), odd)
+                out_ref[rows_ref[block], 0, part] = left.astype(jnp.bfloat16)
+                out_ref[rows_ref[block + 1], 0, part] = right.astype(jnp.bfloat16)
+
+
+def transform_long(sources, row_ids, place, z_factor, first, second, plane, row_count, pairs):
+    classes, slots, _, local_long, mid_len = sources[0].shape
+    pencils = len(sources)
+    depth = 2 * pencils * local_long
+    shape = (row_count, slots, 2, pairs, 4 * pairs)
+    return pl.pallas_call(
+        long_kernel,
+        grid=(slots,),
+        in_specs=[
+            pl.BlockSpec(memory_space=pltpu.SMEM),
+            pl.BlockSpec(memory_space=pltpu.SMEM),
+            pl.BlockSpec(memory_space=pltpu.SMEM),
+            pl.BlockSpec(first.shape, lambda i: (0, 0)),
+            pl.BlockSpec(second.shape, lambda i: (0, 0)),
+            pl.BlockSpec(plane.shape, lambda i: (0, 0, 0, 0)),
+        ]
+        + [pl.BlockSpec((classes, 1, 2, local_long, mid_len), lambda i: (0, i, 0, 0, 0))] * pencils,
+        out_specs=pl.BlockSpec((row_count, 1, 2, pairs, 4 * pairs), lambda i: (0, i, 0, 0, 0)),
+        out_shape=jax.ShapeDtypeStruct(shape, jnp.bfloat16),
+        scratch_shapes=[pltpu.VMEM((classes, pencils, 2, local_long, mid_len), jnp.bfloat16)],
+        compiler_params=pltpu.CompilerParams(vmem_limit_bytes=VMEM_LIMIT),
+        cost_estimate=pl.CostEstimate(
+            flops=2 * classes * slots * depth * depth * mid_len,
+            bytes_accessed=2 * pencils * sources[0].size + 2 * math.prod(shape) + 4 * depth * depth,
+            transcendentals=0,
+        ),
+        name="transform_long",
+    )(row_ids, place, z_factor, first, second, plane, *sources)
+
+
+def rows_kernel(grid_count, place_ref, *refs):
+    sources, out_ref, gathered = refs[:-2], refs[-2], refs[-1]
+    chunks = len(sources) // grid_count
+    slots, _, pairs, span = sources[0].shape[1:]
+    z_local = out_ref.shape[2]
+    for chunk in range(chunks):
+        for number in range(grid_count):
+            for slot in range(slots):
+                spot = (place_ref[0] ^ number) * (chunks * slots) + chunk * slots + slot
+                gathered[spot] = sources[chunk * grid_count + number][0, slot, 0]
+
+    def write(order):
+        for top in range(0, z_local, 8):
+            taken = jnp.stack([gathered[order(top + k)].astype(jnp.float32) for k in range(8)])
+            turned = jnp.transpose(taken, (1, 0, 2))
+            for pair in range(pairs):
+                out_ref[0, 0, top : top + 8, pair * span : (pair + 1) * span] = turned[pair]
+
+    @pl.when(place_ref[1] == 0)
+    def _():
+        write(lambda z: z)
+
+    @pl.when(place_ref[1] != 0)
+    def _():
+        write(lambda z: (z_local - z) % z_local)
+
+
+def lay_rows(sources, place, grid_count, z_local):
+    rows, slots, _, pairs, span = sources[0].shape
+    return pl.pallas_call(
+        functools.partial(rows_kernel, grid_count),
+        grid=(rows, 2),
+        in_specs=[pl.BlockSpec(memory_space=pltpu.SMEM)]
+        + [pl.BlockSpec((1, slots, 1, pairs, span), lambda i, j: (i, 0, j, 0, 0))] * len(sources),
+        out_specs=pl.BlockSpec((1, 1, z_local, pairs * span), lambda i, j: (i, j, 0, 0)),
+        out_shape=jax.ShapeDtypeStruct((rows, 2, z_local, pairs * span), jnp.float32),
+        scratch_shapes=[pltpu.VMEM((z_local, pairs, span), jnp.bfloat16)],
+        compiler_params=pltpu.CompilerParams(vmem_limit_bytes=VMEM_LIMIT),
+        cost_estimate=pl.CostEstimate(
+            flops=0, bytes_accessed=6 * len(sources) * sources[0].size, transcendentals=0
+        ),
+        name="lay_rows",
+    )(place, *sources)
+
+
+def exchange(parts, axis):
+    count = parts.shape[0]
+    me = lax.axis_index(axis)
+    got = []
+    for step in range(count):
+        sent = lax.dynamic_index_in_dim(parts, me ^ step, keepdims=False)
+        if step:
+            sent = lax.ppermute(sent, axis, [(d, d ^ step) for d in range(count)])
+        got.append(sent)
+    return got
+
+
+def mode_factor(modes, diffusion, speed, long_len, mid_len):
+    magnitude = jnp.exp(diffusion * modes * modes * (-4.0 / (long_len * long_len)))
+    phase = speed * modes * (-2.0 * math.pi / mid_len)
+    return magnitude * jnp.cos(phase), magnitude * jnp.sin(phase)
+
+
+def body(field, levels, coefficients, failed, owner_map, velocity, diffusivity):
+    samples = field[0]
+    local_long, mid_len, z_len = samples.shape
+    pencils = lax.axis_size("pencil")
+    grid_count = lax.axis_size("grid")
+    long_len = local_long * pencils
+    z_local = z_len // pencils
+    block_len = mid_len // 4
+    per_long = long_len // block_len
+    per_mid = mid_len // block_len
+    row_count = 2 * per_long * per_mid - per_mid * per_mid
+    per_device = z_len // (grid_count * pencils)
+    slots = per_device // CHUNKS
+    me = lax.axis_index("grid")
+    pencil = lax.axis_index("pencil")
+
+    weight = (coefficients[0] * (1 - failed[0])).astype(jnp.float32)
+    swapped = levels[0, 0] < levels[0, 1]
+    mine = jnp.stack([jnp.where(swapped, 0.0, weight), jnp.where(swapped, weight, 0.0)])
+    weights = lax.all_gather(mine, "grid", axis=1)
+    near = jnp.take(weights, me ^ jnp.arange(grid_count, dtype=jnp.int32), axis=1)
+
+    positions = jnp.arange(long_len, dtype=jnp.int32)
+    modes = signed_modes(positions, long_len)
+    x_re, x_im = mode_factor(modes, diffusivity[0], velocity[0], long_len, mid_len)
+    y_re, y_im = mode_factor(modes, diffusivity[1], velocity[1], long_len, mid_len)
+    by_parity = [v.reshape(long_len // 2, 2).T[:, :, None] for v in (x_re, x_im)]
+    plane = jnp.stack(
+        [by_parity[0] * y_re - by_parity[1] * y_im, by_parity[0] * y_im + by_parity[1] * y_re]
+    )
+    place_in = me * per_device + jnp.arange(per_device, dtype=jnp.int32)
+    back = pencil >= pencils // 2
+    z_index = pencil * z_local + jnp.where(back, (z_local - place_in) % z_local, place_in)
+    z_re, z_im = mode_factor(
+        signed_modes(z_index, z_len), diffusivity[2], velocity[2], long_len, mid_len
+    )
+    z_factor = jnp.stack([z_re, z_im]) * (1.0 / math.sqrt(long_len * mid_len * z_len))
+
+    place = jnp.stack([me, pencil]).astype(jnp.int32)
+    side = jnp.stack([me, back.astype(jnp.int32)]).astype(jnp.int32)
+    mid = mid_table(mid_len, block_len)
+    first, second = long_tables(long_len, block_len, pencils)
+
+    arrived = []
+    for chunk in range(CHUNKS):
+        along_z = transform_z(samples, z_table(chunk, CHUNKS, grid_count, pencils, z_len), CHUNKS)
+        parts = along_z.reshape(grid_count, -1, along_z.shape[1])
+        sources = exchange(parts, "grid")
+        along_mid = transform_mid(sources, near, place, mid, chunk == 0, CHUNKS, pencils, slots)
+        along_mid = along_mid.reshape(along_mid.shape[:4] + (local_long, mid_len))
+        lines = exchange(along_mid, "pencil")
+        rows = transform_long(
+            lines,
+            owner_map,
+            place,
+            z_factor[:, chunk * slots : (chunk + 1) * slots],
+            first,
+            second,
+            plane,
+            row_count,
+            block_len // 2,
+        )
+        arrived += exchange(rows.reshape((grid_count, -1) + rows.shape[1:]), "grid")
+    return lay_rows(arrived, side, grid_count, z_local)
+
+
 def solution(mesh):
     placed = (P("grid", "pencil", None, None), P("grid", None), P("grid"), P("grid"), P(), P(), P())
-    return jax.shard_map(
-        body, mesh=mesh, in_specs=placed, out_specs=P("grid", None, "pencil", None), check_vma=False
-    )
+    devices = mesh.shape["grid"] * mesh.shape["pencil"]
+
+    def run(field, *rest):
+        few = field.shape[3] % (devices * CHUNKS) == 0 and mesh.shape["pencil"] % 2 == 0
+        return jax.shard_map(
+            body if few else wide_body,
+            mesh=mesh,
+            in_specs=placed,
+            out_specs=P("grid", None, "pencil", None),
+            check_vma=False,
+        )(field, *rest)
+
+    return run

time: 1540 us -> 319 us (0.21)
  waiting for transfers between devices: 882 us -> 111 us
  local copies, waits for them, and re-layouts: 388 us -> 23.6 us
  other arithmetic: 114 us -> 7.46 us
  matrix products: 85 us -> 0 us
  Pallas kernels: 0 us -> 54 us
  starting transfers between devices: 48.9 us -> 99.6 us
  blocking collectives: 0 us -> 18.4 us
    all_to_all x3 -> x0, waiting for transfers between devices: 882 us -> none  [the longest x1 720 us: body(): lax.all_to_all(outgoing, 'grid', split_axis=0, concat_axis=0, tiled=True)]
    ppermute x0 -> x34, waiting for transfers between devices: none -> 111 us  [exchange(): sent = lax.ppermute(sent, axis, [(d, d ^ step) for d in range(count)])]
    ppermute x0 -> x34, starting transfers between devices: none -> 99.6 us  [exchange(): sent = lax.ppermute(sent, axis, [(d, d ^ step) for d in range(count)])]
    reshape x2 -> x0, local copies, waits for them, and re-layouts: 87.2 us -> none  [the longest x1 54.8 us: body(): blocks = turned.reshape(held_count, 2, z_local, block_len * block_len)]
    dot_general x3 -> x0, matrix products: 85 us -> none  [the longest x1 40.5 us: body(): jnp.dot(selector, incoming.reshape(grid_count * capacity, -1), precision=...]
    another operation x3 -> x0, local copies, waits for them, and re-layouts: 79.8 us -> none  [apply_factor(): return jnp.stack([real_part, imag_part])]
    add x4 -> x0, other arithmetic: 77.3 us -> none  [the longest x1 77.1 us: apply_factor(): imag_part = spectrum[0] * factor_im + spectrum[1] * factor_re]
    scatter x2 -> x0, local copies, waits for them, and re-layouts: 60.5 us -> none  [the longest x1 59.8 us: body(): outgoing = jnp.zeros_like(weighted).at[target].set(weighted).reshape(grid...]
  transfers between devices with their start and end apart: 3 -> 34, of which waited for: 2 -> 11; matrix products, arithmetic and copies ran while one was open for 28% -> 8% of each run, Pallas kernels for 0% -> 11%
where the time goes in v1:
time: 319 us; the launch traced here: 317 us
  waiting for transfers between devices  111 us (35%)
  starting transfers between devices  99.6 us (31%)
  Pallas kernels  54 us (17%)
  local copies, waits for them, and re-layouts  23.6 us (7%)
  blocking collectives  18.4 us (6%)
  other arithmetic  7.46 us (2%)
    ppermute x34, waiting for transfers between devices, exchange(): sent = lax.ppermute(sent, axis, [(d, d ^ step) for d in range(count)])  111 us
    ppermute x34, starting transfers between devices, exchange(): sent = lax.ppermute(sent, axis, [(d, d ^ step) for d in range(count)])  99.6 us
    squeeze x6, local copies, waits for them, and re-layouts, exchange(): sent = lax.dynamic_index_in_dim(parts, me ^ step, keepdims=False)  18.5 us
    all_gather x1, blocking collectives, body(): weights = lax.all_gather(mine, 'grid', axis=1)  18.4 us
    pallas_call x2, Pallas kernels, transform_z(): pl.pallas_call(z_kernel, grid=(local_long // chunks // rows,), in_specs=[...  18 us
    pallas_call x2, Pallas kernels, transform_long(): pl.pallas_call(long_kernel, grid=(slots,), in_specs=[pl.BlockSpec(memory_...  14.8 us
    pallas_call x2, Pallas kernels, transform_mid(): pl.pallas_call(functools.partial(mid_kernel, first_chunk, rows), grid=(li...  12.2 us
    pallas_call x1, Pallas kernels, lay_rows(): pl.pallas_call(functools.partial(rows_kernel, grid_count), grid=(rows, 2)...  8.94 us
  transfers between devices with their start and end apart: 34, of which 11 were waited for; matrix products, arithmetic and copies ran while one was open for 8% of the time, Pallas kernels for 11%

profile of v1, /device:TPU:0, one launch (start us, length us, event | category | flops | bytes accessed | tf_op | source)
XLA Modules:
  0.0 317.2 jit_solution(6185058317792899638)
XLA Ops:
  0.0 9.0 %transform_z.2 = bf16[128,16384]{1,0:T(8,128)(2,1)} custom-call(bf16[128,256]{1,0:T(8,128)(2,1)} %constant.180.clone.table_ref, bf16[2,64,256,128]{3,2,1,0:T(8,128)(2,1)} %bitcast.109), custom_call_target="tpu_custom_call" | custom-call | flops 1073741824 | bytes 16777216 | tf_op jit(solution)/shard_map/transform_z/pallas_call | solution.py:228
  9.0 4.1 %dynamic-slice_bitcast_fusion.16 = (bf16[16,16384]{1,0:T(8,128)(2,1)}, bf16[16,16384]{1,0:T(8,128)(2,1)}, bf16[16,16384]{1,0:T(8,128)(2,1)S(1)}, bf16[16,16384]{...) fusion(bf16[8,16,16384]{2,1,0:T(8,128)(2,1)} %bitcast.111, ...), kind=kLoop, calls=%fused_computation.20 | loop fusion | bytes 8388640 | tf_op jit(solution)/shard_map/jit(dynamic_index_in_dim)/squeeze | solution.py:459
  13.1 4.5 %collective-permute-start.6 = (bf16[16,16384]{1,0:T(8,128)(2,1)}, bf16[16,16384]{1,0:T(8,128)(2,1)S(1)}, u32[]{:S(2)}, u32[]{:S(2)}) collective-permute-start(bf16[16,16384]{1,0:T(8,128)(2,1)} %get-tuple-element.13), channel_id=1, source_target_pairs={{0,28},{4,24},{8,20},{12,16},{16,12},{20,8},{24,4},{28,0},{1,29},{... | collective-permute-start | bytes 1572872 | tf_op jit(solution)/shard_map/ppermute | solution.py:461
  18.6 2.2 collective-permute-start.3
  26.2 9.0 %transform_z.3 = bf16[128,16384]{1,0:T(8,128)(2,1)} custom-call(bf16[128,256]{1,0:T(8,128)(2,1)} %constant.181.clone.table_ref, bf16[2,64,256,128]{3,2,1,0:T(8,128)(2,1)} %bitcast.110), custom_call_target="tpu_custom_call" | custom-call | flops 1073741824 | bytes 16777216 | tf_op jit(solution)/shard_map/transform_z/pallas_call | solution.py:228
  35.2 4.2 %dynamic-slice_bitcast_fusion.4 = (bf16[16,16384]{1,0:T(8,128)(2,1)}, bf16[16,16384]{1,0:T(8,128)(2,1)}, bf16[16,16384]{1,0:T(8,128)(2,1)}, bf16[16,16384]{1,0:T...) fusion(bf16[8,16,16384]{2,1,0:T(8,128)(2,1)} %bitcast.112, ...), kind=kLoop, calls=%fused_computation.8 | loop fusion | bytes 8388640 | tf_op jit(solution)/shard_map/jit(dynamic_index_in_dim)/squeeze | solution.py:459
  39.4 1.2 sine_multiply_fusion.2
  40.7 1.3 sine_multiply_fusion.1
  42.1 33.3 %collective-permute-start.1 = (bf16[16,16384]{1,0:T(8,128)(2,1)}, bf16[16,16384]{1,0:T(8,128)(2,1)}, u32[]{:S(2)}, u32[]{:S(2)}) collective-permute-start(bf16[16,16384]{1,0:T(8,128)(2,1)} %get-tuple-element.18), channel_id=1, source_target_pairs={{0,8},{4,12},{8,0},{12,4},{16,24},{20,28},{24,16},{28,20},{1,9},{5... | collective-permute-start | bytes 1572872 | tf_op jit(solution)/shard_map/ppermute | solution.py:461
  75.5 21.9 %collective-permute-done.4.refs_5_ = bf16[16,16384]{1,0:T(8,128)(2,1)S(1)} collective-permute-done((bf16[16,16384]{1,0:T(8,128)(2,1)S(1)}, bf16[16,16384]{1,0:T(8,128)(2,1)S(1)}, u32[]{:S(2)}, u32[]{:S(2)}) %collective-permute-start.4) | collective-permute-done | bytes 524320 | tf_op jit(solution)/shard_map/ppermute | solution.py:461
  97.4 2.2 collective-permute-start.23
  99.6 20.4 %collective-permute-done.3.refs_4_ = bf16[16,16384]{1,0:T(8,128)(2,1)S(1)} collective-permute-done((bf16[16,16384]{1,0:T(8,128)(2,1)}, bf16[16,16384]{1,0:T(8,128)(2,1)S(1)}, u32[]{:S(2)}, u32[]{:S(2)}) %collective-permute-start.3) | collective-permute-done | bytes 524320 | tf_op jit(solution)/shard_map/ppermute | solution.py:461
  120.1 2.4 collective-permute-start.22
  122.5 18.4 %all-gather = f32[8,1,2]{2,1,0:T(1,128)S(1)} all-gather(f32[1,1,2]{2,1,0:T(1,128)S(1)} %maximum_bitcast_fusion), channel_id=1, replica_groups=mesh['grid'=8,'pencil'=4] {'grid'}, dimensions={0}, use_global_device_ids=true | all-gather | bytes 72 | tf_op jit(solution)/shard_map/all_gather | solution.py:491
  141.5 1.2 sine_multiply_fusion
  142.8 17.2 %collective-permute-start.21 = (bf16[16,16384]{1,0:T(8,128)(2,1)}, bf16[16,16384]{1,0:T(8,128)(2,1)S(1)}, u32[]{:S(2)}, u32[]{:S(2)}) collective-permute-start(bf16[16,16384]{1,0:T(8,128)(2,1)} %get-tuple-element.7), channel_id=1, source_target_pairs={{0,20},{4,16},{8,28},{12,24},{16,4},{20,0},{24,12},{28,8},{1,21},{... | collective-permute-start | bytes 1572872 | tf_op jit(solution)/shard_map/ppermute | solution.py:461
  161.3 1.3 collective-permute-start.19
  162.7 6.2 %transform_mid.2 = bf16[4,2,2,2,2,64,256]{6,5,4,3,2,1,0:T(8,128)(2,1)} custom-call(f32[2,8]{1,0:T(2,128)} %select_bitcast_fusion.weights_ref, s32[2]{0:T(128)} %pad_add_fusion.1.place_ref, bf16[2,256,512]{2,1,0:T(8,128)(2,1)} %constant.177.clone.table_ref, bf16[16,16384]{1,0:T(8,128)(2,1)} %get-tuple-element.20.refs_0_, ...), custom_call_target="tpu_custom_call" | custom-call | flops 536870912 | bytes 6291456 | tf_op jit(solution)/shard_map/transform_mid/pallas_call | solution.py:292
  169.4 2.5 dynamic-slice_bitcast_fusion.12
  172.0 23.0 %collective-permute-done.21.refs_5_ = bf16[16,16384]{1,0:T(8,128)(2,1)S(1)} collective-permute-done((bf16[16,16384]{1,0:T(8,128)(2,1)}, bf16[16,16384]{1,0:T(8,128)(2,1)S(1)}, u32[]{:S(2)}, u32[]{:S(2)}) %collective-permute-start.21) | collective-permute-done | bytes 524320 | tf_op jit(solution)/shard_map/ppermute | solution.py:461
  195.0 2.4 collective-permute-start.9
  197.7 8.8 %collective-permute-done.20.refs_4_ = bf16[16,16384]{1,0:T(8,128)(2,1)S(1)} collective-permute-done((bf16[16,16384]{1,0:T(8,128)(2,1)}, bf16[16,16384]{1,0:T(8,128)(2,1)S(1)}, u32[]{:S(2)}, u32[]{:S(2)}) %collective-permute-start.20) | collective-permute-done | bytes 524320 | tf_op jit(solution)/shard_map/ppermute | solution.py:461
  206.5 1.5 collective-permute-start.8
  208.0 1.5 collective-permute-start.7
  210.6 6.0 %transform_mid.3 = bf16[4,2,2,2,2,64,256]{6,5,4,3,2,1,0:T(8,128)(2,1)} custom-call(f32[2,8]{1,0:T(2,128)} %select_bitcast_fusion.weights_ref, s32[2]{0:T(128)} %pad_add_fusion.1.place_ref, bf16[2,256,512]{2,1,0:T(8,128)(2,1)} %constant.177.clone.table_ref, bf16[16,16384]{1,0:T(8,128)(2,1)} %get-tuple-element.12.refs_0_, bf16[16,16384]{1,0:T(8,128)(2,1)} %copy-done.10, ...), custom_call_target="tpu_custom_call" | custom-call | flops 536870912 | bytes 6291456 | tf_op jit(solution)/shard_map/transform_mid/pallas_call | solution.py:292
  216.6 2.5 dynamic-slice_bitcast_fusion
  219.1 1.2 collective-permute-start.26
  221.1 1.5 collective-permute-start.24
  223.3 1.5 pad_maximum_fusion.plane_ref
  225.8 7.4 %transform_long.2 = bf16[48,2,2,32,128]{4,3,2,1,0:T(8,128)(2,1)} custom-call(s32[64]{0:T(128)} %rows_ref.3, s32[2]{0:T(128)} %pad_add_fusion.1.place_ref, f32[2,2]{1,0:T(2,128)} %get-tuple-element.48.z_ref, bf16[1024,1024]{1,0:T(8,128)(2,1)} %constant.178.clone.first_ref, bf16[1024,1024]{1,0:T(8,128)(2,1)} %constant.179.clone.second_ref, ...), custom_call_target="tpu_custom_call" | custom-call | flops 2147483648 | bytes 7864320 | tf_op jit(solution)/shard_map/transform_long/pallas_call | solution.py:384
  233.2 2.6 dynamic-slice_bitcast_fusion.32
  235.8 2.4 collective-permute-start.16
  238.2 1.3 collective-permute-start.15
  239.5 4.8 %collective-permute-done.25.refs_2_ = bf16[2,2,2,128,256]{4,3,2,1,0:T(8,128)(2,1)S(1)} collective-permute-done((bf16[2,2,2,128,256]{4,3,2,1,0:T(8,128)(2,1)S(1)}, bf16[2,2,2,128,256]{4,3,2,1,0:T(8,128)(2,1)S(1)}, u32[]{:S(2)}, u32[]{:S(2)}) %collective-permute-start.25) | collective-permute-done | bytes 524320 | tf_op jit(solution)/shard_map/ppermute | solution.py:461
  244.3 2.6 collective-permute-start.13
  246.9 1.7 collective-permute-start.12
  248.6 7.4 %transform_long.3 = bf16[48,2,2,32,128]{4,3,2,1,0:T(8,128)(2,1)} custom-call(s32[64]{0:T(128)} %rows_ref.3, s32[2]{0:T(128)} %pad_add_fusion.1.place_ref, f32[2,2]{1,0:T(2,128)} %get-tuple-element.47.z_ref, bf16[1024,1024]{1,0:T(8,128)(2,1)} %constant.178.clone.first_ref, bf16[1024,1024]{1,0:T(8,128)(2,1)} %constant.179.clone.second_ref, ...), custom_call_target="tpu_custom_call" | custom-call | flops 2147483648 | bytes 7864320 | tf_op jit(solution)/shard_map/transform_long/pallas_call | solution.py:384
  256.0 2.5 dynamic-slice_bitcast_fusion.24
  258.6 2.1 collective-permute-start.11
  260.7 8.0 %collective-permute-done.14.refs_5_ = bf16[6,2,2,32,128]{4,3,2,1,0:T(8,128)(2,1)S(1)} collective-permute-done((bf16[6,2,2,32,128]{4,3,2,1,0:T(8,128)(2,1)S(1)}, bf16[6,2,2,32,128]{4,3,2,1,0:T(8,128)(2,1)S(1)}, u32[]{:S(2)}, u32[]{:S(2)}) %collective-permute-start.14) | collective-permute-done | bytes 196640 | tf_op jit(solution)/shard_map/ppermute | solution.py:461
  269.5 3.4 %collective-permute-done.13.refs_4_ = bf16[6,2,2,32,128]{4,3,2,1,0:T(8,128)(2,1)S(1)} collective-permute-done((bf16[6,2,2,32,128]{4,3,2,1,0:T(8,128)(2,1)S(1)}, bf16[6,2,2,32,128]{4,3,2,1,0:T(8,128)(2,1)S(1)}, u32[]{:S(2)}, u32[]{:S(2)}) %collective-permute-start.13) | collective-permute-done | bytes 196640 | tf_op jit(solution)/shard_map/ppermute | solution.py:461
  272.9 1.2 collective-permute-start.32
  274.1 7.7 %collective-permute-done.11.refs_2_ = bf16[6,2,2,32,128]{4,3,2,1,0:T(8,128)(2,1)S(1)} collective-permute-done((bf16[6,2,2,32,128]{4,3,2,1,0:T(8,128)(2,1)S(1)}, bf16[6,2,2,32,128]{4,3,2,1,0:T(8,128)(2,1)S(1)}, u32[]{:S(2)}, u32[]{:S(2)}) %collective-permute-start.11) | collective-permute-done | bytes 196640 | tf_op jit(solution)/shard_map/ppermute | solution.py:461
  281.9 12.5 %collective-permute-start.28 = (bf16[6,2,2,32,128]{4,3,2,1,0:T(8,128)(2,1)S(1)}, bf16[6,2,2,32,128]{4,3,2,1,0:T(8,128)(2,1)}, u32[]{:S(2)}, u32[]{:S(2)}) collective-permute-start(bf16[6,2,2,32,128]{4,3,2,1,0:T(8,128)(2,1)S(1)} %get-tuple-element.34), channel_id=1, source_target_pairs={{0,8},{4,12},{8,0},{12,4},{16,24},{20,28},{24,16},{28,20},{1,9},{5... | collective-permute-start | bytes 589832 | tf_op jit(solution)/shard_map/ppermute | solution.py:461
  295.0 7.4 %collective-permute-done.31.refs_13_ = bf16[6,2,2,32,128]{4,3,2,1,0:T(8,128)(2,1)S(1)} collective-permute-done((bf16[6,2,2,32,128]{4,3,2,1,0:T(8,128)(2,1)S(1)}, bf16[6,2,2,32,128]{4,3,2,1,0:T(8,128)(2,1)S(1)}, u32[]{:S(2)}, u32[]{:S(2)}) %collective-permute-start.31) | collective-permute-done | bytes 196640 | tf_op jit(solution)/shard_map/ppermute | solution.py:461
  302.4 4.3 %collective-permute-done.30.refs_12_ = bf16[6,2,2,32,128]{4,3,2,1,0:T(8,128)(2,1)S(1)} collective-permute-done((bf16[6,2,2,32,128]{4,3,2,1,0:T(8,128)(2,1)S(1)}, bf16[6,2,2,32,128]{4,3,2,1,0:T(8,128)(2,1)S(1)}, u32[]{:S(2)}, u32[]{:S(2)}) %collective-permute-start.30) | collective-permute-done | bytes 196640 | tf_op jit(solution)/shard_map/ppermute | solution.py:461
  306.6 1.5 collective-permute-done.28.refs_10_
  308.3 8.9 %lay_rows.1 = f32[6,2,32,4096]{3,2,1,0:T(8,128)} custom-call(s32[2]{0:T(128)} %pad_add_fusion.place_ref, bf16[6,2,2,32,128]{4,3,2,1,0:T(8,128)(2,1)} %get-tuple-element.44.refs_0_, bf16[6,2,2,32,128]{4,3,2,1,0:T(8,128)(2,1)} %copy-done.23, bf16[6,2,2,32,128]{4,3,2,1,0:T(8,128)(2,1)} %copy-done.22, bf16[6,2,2,32,128]{4,3,2,1,0:T(8,128)(2,1)} %copy-done.21, ...), custom_call_target="tpu_custom_call" | custom-call | bytes 9437184 | tf_op jit(solution)/shard_map/lay_rows/pallas_call | solution.py:438
  (117 shorter events, 11.8 us)
Async XLA Ops:
  9.0 16.6 %copy-start.30 = (f32[3]{0:T(128)S(1)}, f32[3]{0:T(128)}, u32[]{:S(2)}) copy-start(f32[3]{0:T(128)} %param.18) | copy-start | bytes 40
  13.1 28.9 %collective-permute-start.6 = (bf16[16,16384]{1,0:T(8,128)(2,1)}, bf16[16,16384]{1,0:T(8,128)(2,1)S(1)}, u32[]{:S(2)}, u32[]{:S(2)}) collective-permute-start(bf16[16,16384]{1,0:T(8,128)(2,1)} %get-tuple-element.13), channel_id=1, source_target_pairs={{0,28},{4,24},{8,20},{12,16},{16,12},{20,8},{24,4},{28,0},{1,29},{... | collective-permute-start | bytes 1572872 | tf_op jit(solution)/shard_map/ppermute | solution.py:461
  17.6 57.8 %collective-permute-start.5 = (bf16[16,16384]{1,0:T(8,128)(2,1)}, bf16[16,16384]{1,0:T(8,128)(2,1)S(1)}, u32[]{:S(2)}, u32[]{:S(2)}) collective-permute-start(bf16[16,16384]{1,0:T(8,128)(2,1)} %get-tuple-element.14), channel_id=1, source_target_pairs={{0,24},{4,28},{8,16},{12,20},{16,8},{20,12},{24,0},{28,4},{1,25},{... | collective-permute-start | bytes 1572872 | tf_op jit(solution)/shard_map/ppermute | solution.py:461
  18.2 79.2 %collective-permute-start.4 = (bf16[16,16384]{1,0:T(8,128)(2,1)S(1)}, bf16[16,16384]{1,0:T(8,128)(2,1)S(1)}, u32[]{:S(2)}, u32[]{:S(2)}) collective-permute-start(bf16[16,16384]{1,0:T(8,128)(2,1)S(1)} %get-tuple-element.15), channel_id=1, source_target_pairs={{0,20},{4,16},{8,28},{12,24},{16,4},{20,0},{24,12},{28,8},{1,21},{... | collective-permute-start | bytes 1572872 | tf_op jit(solution)/shard_map/ppermute | solution.py:461
  18.6 101.4 %collective-permute-start.3 = (bf16[16,16384]{1,0:T(8,128)(2,1)}, bf16[16,16384]{1,0:T(8,128)(2,1)S(1)}, u32[]{:S(2)}, u32[]{:S(2)}) collective-permute-start(bf16[16,16384]{1,0:T(8,128)(2,1)} %get-tuple-element.16), channel_id=1, source_target_pairs={{0,16},{4,20},{8,24},{12,28},{16,0},{20,4},{24,8},{28,12},{1,17},{... | collective-permute-start | bytes 1572872 | tf_op jit(solution)/shard_map/ppermute | solution.py:461
  20.8 122.0 %collective-permute-start.2 = (bf16[16,16384]{1,0:T(8,128)(2,1)}, bf16[16,16384]{1,0:T(8,128)(2,1)S(1)}, u32[]{:S(2)}, u32[]{:S(2)}) collective-permute-start(bf16[16,16384]{1,0:T(8,128)(2,1)} %get-tuple-element.17), channel_id=1, source_target_pairs={{0,12},{4,8},{8,4},{12,0},{16,28},{20,24},{24,20},{28,16},{1,13},{... | collective-permute-start | bytes 1572872 | tf_op jit(solution)/shard_map/ppermute | solution.py:461
  42.1 120.6 %copy-start = (bf16[16,16384]{1,0:T(8,128)(2,1)}, bf16[16,16384]{1,0:T(8,128)(2,1)S(1)}, u32[]{:S(2)}) copy-start(bf16[16,16384]{1,0:T(8,128)(2,1)S(1)} %collective-permute-done.6.refs_7_) | copy-start | bytes 1572868
  42.1 119.1 %collective-permute-start.1 = (bf16[16,16384]{1,0:T(8,128)(2,1)}, bf16[16,16384]{1,0:T(8,128)(2,1)}, u32[]{:S(2)}, u32[]{:S(2)}) collective-permute-start(bf16[16,16384]{1,0:T(8,128)(2,1)} %get-tuple-element.18), channel_id=1, source_target_pairs={{0,8},{4,12},{8,0},{12,4},{16,24},{20,28},{24,16},{28,20},{1,9},{5... | collective-permute-start | bytes 1572872 | tf_op jit(solution)/shard_map/ppermute | solution.py:461
  75.4 87.2 %copy-start.1 = (bf16[16,16384]{1,0:T(8,128)(2,1)}, bf16[16,16384]{1,0:T(8,128)(2,1)S(1)}, u32[]{:S(2)}) copy-start(bf16[16,16384]{1,0:T(8,128)(2,1)S(1)} %collective-permute-done.5.refs_6_) | copy-start | bytes 1572868
  75.4 85.9 %collective-permute-start = (bf16[16,16384]{1,0:T(8,128)(2,1)}, bf16[16,16384]{1,0:T(8,128)(2,1)}, u32[]{:S(2)}, u32[]{:S(2)}) collective-permute-start(bf16[16,16384]{1,0:T(8,128)(2,1)} %get-tuple-element.19), channel_id=1, source_target_pairs={{0,4},{4,0},{8,12},{12,8},{16,20},{20,16},{24,28},{28,24},{1,5},{5... | collective-permute-start | bytes 1572872 | tf_op jit(solution)/shard_map/ppermute | solution.py:461
  97.4 65.2 %copy-start.2 = (bf16[16,16384]{1,0:T(8,128)(2,1)}, bf16[16,16384]{1,0:T(8,128)(2,1)S(1)}, u32[]{:S(2)}) copy-start(bf16[16,16384]{1,0:T(8,128)(2,1)S(1)} %collective-permute-done.4.refs_5_) | copy-start | bytes 1572868
  97.4 71.4 %collective-permute-start.23 = (bf16[16,16384]{1,0:T(8,128)(2,1)}, bf16[16,16384]{1,0:T(8,128)(2,1)S(1)}, u32[]{:S(2)}, u32[]{:S(2)}) collective-permute-start(bf16[16,16384]{1,0:T(8,128)(2,1)} %get-tuple-element.5), channel_id=1, source_target_pairs={{0,28},{4,24},{8,20},{12,16},{16,12},{20,8},{24,4},{28,0},{1,29},{... | collective-permute-start | bytes 1572872 | tf_op jit(solution)/shard_map/ppermute | solution.py:461
  120.1 42.6 %copy-start.3 = (bf16[16,16384]{1,0:T(8,128)(2,1)}, bf16[16,16384]{1,0:T(8,128)(2,1)S(1)}, u32[]{:S(2)}) copy-start(bf16[16,16384]{1,0:T(8,128)(2,1)S(1)} %collective-permute-done.3.refs_4_) | copy-start | bytes 1572868
  120.1 49.3 %collective-permute-start.22 = (bf16[16,16384]{1,0:T(8,128)(2,1)}, bf16[16,16384]{1,0:T(8,128)(2,1)}, u32[]{:S(2)}, u32[]{:S(2)}) collective-permute-start(bf16[16,16384]{1,0:T(8,128)(2,1)} %get-tuple-element.6), channel_id=1, source_target_pairs={{0,24},{4,28},{8,16},{12,20},{16,8},{20,12},{24,0},{28,4},{1,25},{... | collective-permute-start | bytes 1572872 | tf_op jit(solution)/shard_map/ppermute | solution.py:461
  142.8 19.9 %copy-start.4 = (bf16[16,16384]{1,0:T(8,128)(2,1)}, bf16[16,16384]{1,0:T(8,128)(2,1)S(1)}, u32[]{:S(2)}) copy-start(bf16[16,16384]{1,0:T(8,128)(2,1)S(1)} %collective-permute-done.2.refs_3_) | copy-start | bytes 1572868
  142.8 52.2 %collective-permute-start.21 = (bf16[16,16384]{1,0:T(8,128)(2,1)}, bf16[16,16384]{1,0:T(8,128)(2,1)S(1)}, u32[]{:S(2)}, u32[]{:S(2)}) collective-permute-start(bf16[16,16384]{1,0:T(8,128)(2,1)} %get-tuple-element.7), channel_id=1, source_target_pairs={{0,20},{4,16},{8,28},{12,24},{16,4},{20,0},{24,12},{28,8},{1,21},{... | collective-permute-start | bytes 1572872 | tf_op jit(solution)/shard_map/ppermute | solution.py:461
  161.2 45.3 %collective-permute-start.20 = (bf16[16,16384]{1,0:T(8,128)(2,1)}, bf16[16,16384]{1,0:T(8,128)(2,1)S(1)}, u32[]{:S(2)}, u32[]{:S(2)}) collective-permute-start(bf16[16,16384]{1,0:T(8,128)(2,1)} %get-tuple-element.8), channel_id=1, source_target_pairs={{0,16},{4,20},{8,24},{12,28},{16,0},{20,4},{24,8},{28,12},{1,17},{... | collective-permute-start | bytes 1572872 | tf_op jit(solution)/shard_map/ppermute | solution.py:461
  161.3 46.7 %collective-permute-start.19 = (bf16[16,16384]{1,0:T(8,128)(2,1)}, bf16[16,16384]{1,0:T(8,128)(2,1)S(1)}, u32[]{:S(2)}, u32[]{:S(2)}) collective-permute-start(bf16[16,16384]{1,0:T(8,128)(2,1)} %get-tuple-element.9), channel_id=1, source_target_pairs={{0,12},{4,8},{8,4},{12,0},{16,28},{20,24},{24,20},{28,16},{1,13},{... | collective-permute-start | bytes 1572872 | tf_op jit(solution)/shard_map/ppermute | solution.py:461
  168.8 40.7 %collective-permute-start.18 = (bf16[16,16384]{1,0:T(8,128)(2,1)}, bf16[16,16384]{1,0:T(8,128)(2,1)S(1)}, u32[]{:S(2)}, u32[]{:S(2)}) collective-permute-start(bf16[16,16384]{1,0:T(8,128)(2,1)} %get-tuple-element.10), channel_id=1, source_target_pairs={{0,8},{4,12},{8,0},{12,4},{16,24},{20,28},{24,16},{28,20},{1,9},{5... | collective-permute-start | bytes 1572872 | tf_op jit(solution)/shard_map/ppermute | solution.py:461
  169.4 40.2 %collective-permute-start.17 = (bf16[16,16384]{1,0:T(8,128)(2,1)}, bf16[16,16384]{1,0:T(8,128)(2,1)S(1)}, u32[]{:S(2)}, u32[]{:S(2)}) collective-permute-start(bf16[16,16384]{1,0:T(8,128)(2,1)} %get-tuple-element.11), channel_id=1, source_target_pairs={{0,4},{4,0},{8,12},{12,8},{16,20},{20,16},{24,28},{28,24},{1,5},{5... | collective-permute-start | bytes 1572872 | tf_op jit(solution)/shard_map/ppermute | solution.py:461
  195.0 26.1 %collective-permute-start.9 = (bf16[2,2,2,128,256]{4,3,2,1,0:T(8,128)(2,1)S(1)}, bf16[2,2,2,128,256]{4,3,2,1,0:T(8,128)(2,1)S(1)}, u32[]{:S(2)}, u32[]{:S(2)}) collective-permute-start(bf16[2,2,2,128,256]{4,3,2,1,0:T(8,128)(2,1)S(1)} %get-tuple-element.25), channel_id=1, source_target_pairs={{0,3},{1,2},{2,1},{3,0},{4,7},{5,6},{6,5},{7,4},{8,11},{9,10},{10,... | collective-permute-start | bytes 1572872 | tf_op jit(solution)/shard_map/ppermute | solution.py:461
  206.5 18.2 %collective-permute-start.8 = (bf16[2,2,2,128,256]{4,3,2,1,0:T(8,128)(2,1)S(1)}, bf16[2,2,2,128,256]{4,3,2,1,0:T(8,128)(2,1)S(1)}, u32[]{:S(2)}, u32[]{:S(2)}) collective-permute-start(bf16[2,2,2,128,256]{4,3,2,1,0:T(8,128)(2,1)S(1)} %get-tuple-element.26), channel_id=1, source_target_pairs={{0,2},{1,3},{2,0},{3,1},{4,6},{5,7},{6,4},{7,5},{8,10},{9,11},{10,... | collective-permute-start | bytes 1572872 | tf_op jit(solution)/shard_map/ppermute | solution.py:461
  208.0 16.7 %collective-permute-start.7 = (bf16[2,2,2,128,256]{4,3,2,1,0:T(8,128)(2,1)S(1)}, bf16[2,2,2,128,256]{4,3,2,1,0:T(8,128)(2,1)S(1)}, u32[]{:S(2)}, u32[]{:S(2)}) collective-permute-start(bf16[2,2,2,128,256]{4,3,2,1,0:T(8,128)(2,1)S(1)} %get-tuple-element.27), channel_id=1, source_target_pairs={{0,1},{1,0},{2,3},{3,2},{4,5},{5,4},{6,7},{7,6},{8,9},{9,8},{10,11... | collective-permute-start | bytes 1572872 | tf_op jit(solution)/shard_map/ppermute | solution.py:461
  219.1 20.3 %collective-permute-start.26 = (bf16[2,2,2,128,256]{4,3,2,1,0:T(8,128)(2,1)S(1)}, bf16[2,2,2,128,256]{4,3,2,1,0:T(8,128)(2,1)S(1)}, u32[]{:S(2)}, u32[]{:S(2)}) collective-permute-start(bf16[2,2,2,128,256]{4,3,2,1,0:T(8,128)(2,1)S(1)} %get-tuple-element.21), channel_id=1, source_target_pairs={{0,3},{1,2},{2,1},{3,0},{4,7},{5,6},{6,5},{7,4},{8,11},{9,10},{10,... | collective-permute-start | bytes 1572872 | tf_op jit(solution)/shard_map/ppermute | solution.py:461
  220.4 23.9 %collective-permute-start.25 = (bf16[2,2,2,128,256]{4,3,2,1,0:T(8,128)(2,1)S(1)}, bf16[2,2,2,128,256]{4,3,2,1,0:T(8,128)(2,1)S(1)}, u32[]{:S(2)}, u32[]{:S(2)}) collective-permute-start(bf16[2,2,2,128,256]{4,3,2,1,0:T(8,128)(2,1)S(1)} %get-tuple-element.22), channel_id=1, source_target_pairs={{0,2},{1,3},{2,0},{3,1},{4,6},{5,7},{6,4},{7,5},{8,10},{9,11},{10,... | collective-permute-start | bytes 1572872 | tf_op jit(solution)/shard_map/ppermute | solution.py:461
  221.1 25.8 %collective-permute-start.24 = (bf16[2,2,2,128,256]{4,3,2,1,0:T(8,128)(2,1)S(1)}, bf16[2,2,2,128,256]{4,3,2,1,0:T(8,128)(2,1)S(1)}, u32[]{:S(2)}, u32[]{:S(2)}) collective-permute-start(bf16[2,2,2,128,256]{4,3,2,1,0:T(8,128)(2,1)S(1)} %get-tuple-element.23), channel_id=1, source_target_pairs={{0,1},{1,0},{2,3},{3,2},{4,5},{5,4},{6,7},{7,6},{8,9},{9,8},{10,11... | collective-permute-start | bytes 1572872 | tf_op jit(solution)/shard_map/ppermute | solution.py:461
  235.8 22.8 %collective-permute-start.16 = (bf16[6,2,2,32,128]{4,3,2,1,0:T(8,128)(2,1)S(1)}, bf16[6,2,2,32,128]{4,3,2,1,0:T(8,128)(2,1)S(1)}, u32[]{:S(2)}, u32[]{:S(2)}) collective-permute-start(bf16[6,2,2,32,128]{4,3,2,1,0:T(8,128)(2,1)S(1)} %get-tuple-element.37), channel_id=1, source_target_pairs={{0,28},{4,24},{8,20},{12,16},{16,12},{20,8},{24,4},{28,0},{1,29},{... | collective-permute-start | bytes 589832 | tf_op jit(solution)/shard_map/ppermute | solution.py:461
  238.2 22.5 %collective-permute-start.15 = (bf16[6,2,2,32,128]{4,3,2,1,0:T(8,128)(2,1)S(1)}, bf16[6,2,2,32,128]{4,3,2,1,0:T(8,128)(2,1)S(1)}, u32[]{:S(2)}, u32[]{:S(2)}) collective-permute-start(bf16[6,2,2,32,128]{4,3,2,1,0:T(8,128)(2,1)S(1)} %get-tuple-element.38), channel_id=1, source_target_pairs={{0,24},{4,28},{8,16},{12,20},{16,8},{20,12},{24,0},{28,4},{1,25},{... | collective-permute-start | bytes 589832 | tf_op jit(solution)/shard_map/ppermute | solution.py:461
  239.5 29.1 %collective-permute-start.14 = (bf16[6,2,2,32,128]{4,3,2,1,0:T(8,128)(2,1)S(1)}, bf16[6,2,2,32,128]{4,3,2,1,0:T(8,128)(2,1)S(1)}, u32[]{:S(2)}, u32[]{:S(2)}) collective-permute-start(bf16[6,2,2,32,128]{4,3,2,1,0:T(8,128)(2,1)S(1)} %get-tuple-element.39), channel_id=1, source_target_pairs={{0,20},{4,16},{8,28},{12,24},{16,4},{20,0},{24,12},{28,8},{1,21},{... | collective-permute-start | bytes 589832 | tf_op jit(solution)/shard_map/ppermute | solution.py:461
  244.3 28.6 %collective-permute-start.13 = (bf16[6,2,2,32,128]{4,3,2,1,0:T(8,128)(2,1)S(1)}, bf16[6,2,2,32,128]{4,3,2,1,0:T(8,128)(2,1)S(1)}, u32[]{:S(2)}, u32[]{:S(2)}) collective-permute-start(bf16[6,2,2,32,128]{4,3,2,1,0:T(8,128)(2,1)S(1)} %get-tuple-element.40), channel_id=1, source_target_pairs={{0,16},{4,20},{8,24},{12,28},{16,0},{20,4},{24,8},{28,12},{1,17},{... | collective-permute-start | bytes 589832 | tf_op jit(solution)/shard_map/ppermute | solution.py:461
  246.9 27.1 %collective-permute-start.12 = (bf16[6,2,2,32,128]{4,3,2,1,0:T(8,128)(2,1)S(1)}, bf16[6,2,2,32,128]{4,3,2,1,0:T(8,128)(2,1)S(1)}, u32[]{:S(2)}, u32[]{:S(2)}) collective-permute-start(bf16[6,2,2,32,128]{4,3,2,1,0:T(8,128)(2,1)S(1)} %get-tuple-element.41), channel_id=1, source_target_pairs={{0,12},{4,8},{8,4},{12,0},{16,28},{20,24},{24,20},{28,16},{1,13},{... | collective-permute-start | bytes 589832 | tf_op jit(solution)/shard_map/ppermute | solution.py:461
  258.6 49.6 %copy-start.17 = (bf16[6,2,2,32,128]{4,3,2,1,0:T(8,128)(2,1)}, bf16[6,2,2,32,128]{4,3,2,1,0:T(8,128)(2,1)S(1)}, u32[]{:S(2)}) copy-start(bf16[6,2,2,32,128]{4,3,2,1,0:T(8,128)(2,1)S(1)} %collective-permute-done.16.refs_7_) | copy-start | bytes 589828
  258.6 23.2 %collective-permute-start.11 = (bf16[6,2,2,32,128]{4,3,2,1,0:T(8,128)(2,1)S(1)}, bf16[6,2,2,32,128]{4,3,2,1,0:T(8,128)(2,1)S(1)}, u32[]{:S(2)}, u32[]{:S(2)}) collective-permute-start(bf16[6,2,2,32,128]{4,3,2,1,0:T(8,128)(2,1)S(1)} %get-tuple-element.42), channel_id=1, source_target_pairs={{0,8},{4,12},{8,0},{12,4},{16,24},{20,28},{24,16},{28,20},{1,9},{5... | collective-permute-start | bytes 589832 | tf_op jit(solution)/shard_map/ppermute | solution.py:461
  260.6 47.5 %copy-start.18 = (bf16[6,2,2,32,128]{4,3,2,1,0:T(8,128)(2,1)}, bf16[6,2,2,32,128]{4,3,2,1,0:T(8,128)(2,1)S(1)}, u32[]{:S(2)}) copy-start(bf16[6,2,2,32,128]{4,3,2,1,0:T(8,128)(2,1)S(1)} %collective-permute-done.15.refs_6_) | copy-start | bytes 589828
  260.6 21.1 %collective-permute-start.10 = (bf16[6,2,2,32,128]{4,3,2,1,0:T(8,128)(2,1)S(1)}, bf16[6,2,2,32,128]{4,3,2,1,0:T(8,128)(2,1)S(1)}, u32[]{:S(2)}, u32[]{:S(2)}) collective-permute-start(bf16[6,2,2,32,128]{4,3,2,1,0:T(8,128)(2,1)S(1)} %get-tuple-element.43), channel_id=1, source_target_pairs={{0,4},{4,0},{8,12},{12,8},{16,20},{20,16},{24,28},{28,24},{1,5},{5... | collective-permute-start | bytes 589832 | tf_op jit(solution)/shard_map/ppermute | solution.py:461
  268.6 39.6 %copy-start.19 = (bf16[6,2,2,32,128]{4,3,2,1,0:T(8,128)(2,1)}, bf16[6,2,2,32,128]{4,3,2,1,0:T(8,128)(2,1)S(1)}, u32[]{:S(2)}) copy-start(bf16[6,2,2,32,128]{4,3,2,1,0:T(8,128)(2,1)S(1)} %collective-permute-done.14.refs_5_) | copy-start | bytes 589828
  268.6 13.2 %collective-permute-start.33 = (bf16[6,2,2,32,128]{4,3,2,1,0:T(8,128)(2,1)S(1)}, bf16[6,2,2,32,128]{4,3,2,1,0:T(8,128)(2,1)S(1)}, u32[]{:S(2)}, u32[]{:S(2)}) collective-permute-start(bf16[6,2,2,32,128]{4,3,2,1,0:T(8,128)(2,1)S(1)} %get-tuple-element.29), channel_id=1, source_target_pairs={{0,28},{4,24},{8,20},{12,16},{16,12},{20,8},{24,4},{28,0},{1,29},{... | collective-permute-start | bytes 589832 | tf_op jit(solution)/shard_map/ppermute | solution.py:461
  272.9 35.3 %copy-start.20 = (bf16[6,2,2,32,128]{4,3,2,1,0:T(8,128)(2,1)}, bf16[6,2,2,32,128]{4,3,2,1,0:T(8,128)(2,1)S(1)}, u32[]{:S(2)}) copy-start(bf16[6,2,2,32,128]{4,3,2,1,0:T(8,128)(2,1)S(1)} %collective-permute-done.13.refs_4_) | copy-start | bytes 589828
  272.9 21.5 %collective-permute-start.32 = (bf16[6,2,2,32,128]{4,3,2,1,0:T(8,128)(2,1)S(1)}, bf16[6,2,2,32,128]{4,3,2,1,0:T(8,128)(2,1)S(1)}, u32[]{:S(2)}, u32[]{:S(2)}) collective-permute-start(bf16[6,2,2,32,128]{4,3,2,1,0:T(8,128)(2,1)S(1)} %get-tuple-element.30), channel_id=1, source_target_pairs={{0,24},{4,28},{8,16},{12,20},{16,8},{20,12},{24,0},{28,4},{1,25},{... | collective-permute-start | bytes 589832 | tf_op jit(solution)/shard_map/ppermute | solution.py:461
  274.0 34.2 %copy-start.21 = (bf16[6,2,2,32,128]{4,3,2,1,0:T(8,128)(2,1)}, bf16[6,2,2,32,128]{4,3,2,1,0:T(8,128)(2,1)S(1)}, u32[]{:S(2)}) copy-start(bf16[6,2,2,32,128]{4,3,2,1,0:T(8,128)(2,1)S(1)} %collective-permute-done.12.refs_3_) | copy-start | bytes 589828
  274.0 28.3 %collective-permute-start.31 = (bf16[6,2,2,32,128]{4,3,2,1,0:T(8,128)(2,1)S(1)}, bf16[6,2,2,32,128]{4,3,2,1,0:T(8,128)(2,1)S(1)}, u32[]{:S(2)}, u32[]{:S(2)}) collective-permute-start(bf16[6,2,2,32,128]{4,3,2,1,0:T(8,128)(2,1)S(1)} %get-tuple-element.31), channel_id=1, source_target_pairs={{0,20},{4,16},{8,28},{12,24},{16,4},{20,0},{24,12},{28,8},{1,21},{... | collective-permute-start | bytes 589832 | tf_op jit(solution)/shard_map/ppermute | solution.py:461
  281.8 26.5 %copy-start.22 = (bf16[6,2,2,32,128]{4,3,2,1,0:T(8,128)(2,1)}, bf16[6,2,2,32,128]{4,3,2,1,0:T(8,128)(2,1)S(1)}, u32[]{:S(2)}) copy-start(bf16[6,2,2,32,128]{4,3,2,1,0:T(8,128)(2,1)S(1)} %collective-permute-done.11.refs_2_) | copy-start | bytes 589828
  281.8 24.9 %collective-permute-start.30 = (bf16[6,2,2,32,128]{4,3,2,1,0:T(8,128)(2,1)S(1)}, bf16[6,2,2,32,128]{4,3,2,1,0:T(8,128)(2,1)S(1)}, u32[]{:S(2)}, u32[]{:S(2)}) collective-permute-start(bf16[6,2,2,32,128]{4,3,2,1,0:T(8,128)(2,1)S(1)} %get-tuple-element.32), channel_id=1, source_target_pairs={{0,16},{4,20},{8,24},{12,28},{16,0},{20,4},{24,8},{28,12},{1,17},{... | collective-permute-start | bytes 589832 | tf_op jit(solution)/shard_map/ppermute | solution.py:461
  281.8 26.5 %copy-start.23 = (bf16[6,2,2,32,128]{4,3,2,1,0:T(8,128)(2,1)}, bf16[6,2,2,32,128]{4,3,2,1,0:T(8,128)(2,1)S(1)}, u32[]{:S(2)}) copy-start(bf16[6,2,2,32,128]{4,3,2,1,0:T(8,128)(2,1)S(1)} %collective-permute-done.10.refs_1_) | copy-start | bytes 589828
  281.8 24.9 %collective-permute-start.29 = (bf16[6,2,2,32,128]{4,3,2,1,0:T(8,128)(2,1)S(1)}, bf16[6,2,2,32,128]{4,3,2,1,0:T(8,128)(2,1)S(1)}, u32[]{:S(2)}, u32[]{:S(2)}) collective-permute-start(bf16[6,2,2,32,128]{4,3,2,1,0:T(8,128)(2,1)S(1)} %get-tuple-element.33), channel_id=1, source_target_pairs={{0,12},{4,8},{8,4},{12,0},{16,28},{20,24},{24,20},{28,16},{1,13},{... | collective-permute-start | bytes 589832 | tf_op jit(solution)/shard_map/ppermute | solution.py:461
  281.9 26.4 %copy-start.24 = (bf16[6,2,2,32,128]{4,3,2,1,0:T(8,128)(2,1)}, bf16[6,2,2,32,128]{4,3,2,1,0:T(8,128)(2,1)S(1)}, u32[]{:S(2)}) copy-start(bf16[6,2,2,32,128]{4,3,2,1,0:T(8,128)(2,1)S(1)} %collective-permute-done.33.refs_15_) | copy-start | bytes 589828
  281.9 26.3 %collective-permute-start.28 = (bf16[6,2,2,32,128]{4,3,2,1,0:T(8,128)(2,1)S(1)}, bf16[6,2,2,32,128]{4,3,2,1,0:T(8,128)(2,1)}, u32[]{:S(2)}, u32[]{:S(2)}) collective-permute-start(bf16[6,2,2,32,128]{4,3,2,1,0:T(8,128)(2,1)S(1)} %get-tuple-element.34), channel_id=1, source_target_pairs={{0,8},{4,12},{8,0},{12,4},{16,24},{20,28},{24,16},{28,20},{1,9},{5... | collective-permute-start | bytes 589832 | tf_op jit(solution)/shard_map/ppermute | solution.py:461
  294.4 13.8 %collective-permute-start.27 = (bf16[6,2,2,32,128]{4,3,2,1,0:T(8,128)(2,1)S(1)}, bf16[6,2,2,32,128]{4,3,2,1,0:T(8,128)(2,1)}, u32[]{:S(2)}, u32[]{:S(2)}) collective-permute-start(bf16[6,2,2,32,128]{4,3,2,1,0:T(8,128)(2,1)S(1)} %get-tuple-element.35), channel_id=1, source_target_pairs={{0,4},{4,0},{8,12},{12,8},{16,20},{20,16},{24,28},{28,24},{1,5},{5... | collective-permute-start | bytes 589832 | tf_op jit(solution)/shard_map/ppermute | solution.py:461
  (18 other events, 97.8 us)

commit v2 on v1

--- a/solution.py
+++ b/solution.py
@@ -211,54 +211,142 @@
     return jnp.asarray(first, jnp.bfloat16), jnp.asarray(second, jnp.bfloat16)
 
 
-def z_kernel(table_ref, field_ref, out_ref):
+def z_kernel(weight_ref, table_ref, field_ref, *out_refs):
     halves, rows, mid_len, z_len = field_ref.shape
-    lines = [field_ref[half].reshape(rows * mid_len, z_len) for half in range(halves)]
-    joined = jnp.concatenate(lines, axis=1)
-    out_ref[...] = lax.dot_general(
-        table_ref[...], joined, (((1,), (1,)), ((), ())), preferred_element_type=jnp.float32
-    ).astype(jnp.bfloat16)
-
-
-def transform_z(samples, table, chunks):
+    tiles, _, columns, lanes = out_refs[0].shape
+    last = pl.num_programs(0) - 1
+
+    @pl.when(pl.program_id(0) < last)
+    def _():
+        lines = [field_ref[half].reshape(rows * mid_len, z_len) for half in range(halves)]
+        joined = jnp.concatenate(lines, axis=1)
+        found = lax.dot_general(
+            table_ref[...], joined, (((1,), (1,)), ((), ())), preferred_element_type=jnp.float32
+        ).astype(jnp.bfloat16)
+        for unit, out_ref in enumerate(out_refs):
+            for tile in range(tiles):
+                for row in range(rows):
+                    left = row * mid_len + tile * lanes
+                    out_ref[tile, row] = found[unit * columns : (unit + 1) * columns, left : left + lanes]
+
+    @pl.when(pl.program_id(0) == last)
+    def _():
+        for out_ref in out_refs:
+            for tile in range(tiles):
+                out_ref[tile, 0] = jnp.full((columns, lanes), weight_ref[tile], jnp.float32).astype(jnp.bfloat16)
+
+
+def transform_z(samples, table, weight, chunks, units):
     local_long, mid_len, z_len = samples.shape
-    columns = table.shape[0]
+    columns = table.shape[0] // units
     rows = 8
-    split = samples.reshape(chunks, local_long // chunks, mid_len, z_len)
+    lines = local_long // chunks
+    steps = lines // rows
+    tiles = weight.shape[0]
+    lanes = mid_len // tiles
+    split = samples.reshape(chunks, lines, mid_len, z_len)
     return pl.pallas_call(
         z_kernel,
-        grid=(local_long // chunks // rows,),
+        grid=(steps + 1,),
         in_specs=[
+            pl.BlockSpec(memory_space=pltpu.SMEM),
             pl.BlockSpec(table.shape, lambda i: (0, 0)),
-            pl.BlockSpec((chunks, rows, mid_len, z_len), lambda i: (0, i, 0, 0)),
+            pl.BlockSpec((chunks, rows, mid_len, z_len), lambda i: (0, jnp.minimum(i, steps - 1), 0, 0)),
         ],
-        out_specs=pl.BlockSpec((columns, rows * mid_len), lambda i: (0, i)),
-        out_shape=jax.ShapeDtypeStruct((columns, local_long // chunks * mid_len), jnp.bfloat16),
+        out_specs=[pl.BlockSpec((tiles, rows, columns, lanes), lambda i: (0, i, 0, 0))] * units,
+        out_shape=[jax.ShapeDtypeStruct((tiles, lines + 1, columns, lanes), jnp.bfloat16)] * units,
         compiler_params=pltpu.CompilerParams(vmem_limit_bytes=VMEM_LIMIT),
         cost_estimate=pl.CostEstimate(
-            flops=2 * columns * samples.size, bytes_accessed=4 * samples.size, transcendentals=0
+            flops=2 * units * columns * samples.size, bytes_accessed=4 * samples.size, transcendentals=0
         ),
         name="transform_z",
-    )(table, split)
-
-
-def mid_kernel(first_chunk, rows, weights_ref, place_ref, table_ref, *refs):
-    sources, out_ref = refs[:-1], refs[-1]
-    columns = sources[0].shape[0]
-    mid_len = table_ref.shape[1]
+    )(weight, table, split)
+
+
+def unit_specs(shape, rows):
+    tiles, lines, columns, lanes = shape
+    return [
+        pl.BlockSpec((tiles, rows, columns, lanes), lambda i: (0, i, 0, 0)),
+        pl.BlockSpec((tiles, 1, columns, lanes), lambda i: (0, lines - 1, 0, 0)),
+    ]
+
+
+def weighted_sum(sources, weights, kind):
+    total = None
+    for source, weight in zip(sources, weights):
+        term = source * weight[kind]
+        total = term if total is None else total + term
+    return total
+
+
+def relay_kernel(place_ref, *refs):
+    out_refs = refs[-2:]
+    passing = [refs[-4], refs[-3]]
+    sources, weights = refs[:-4:2], refs[1:-4:2]
+    rows = out_refs[0].shape[1]
+    last = pl.num_programs(0) - 1
+    outer = place_ref[2] != 0
+
+    @pl.when(outer)
+    def _():
+        for out_ref, source in zip(out_refs, passing):
+            out_ref[...] = source[...]
+
+    @pl.when(jnp.logical_not(outer))
+    def _():
+        values = [source[...].astype(jnp.float32) for source in sources]
+        scales = [weight[...].astype(jnp.float32) for weight in weights]
+        for kind, out_ref in enumerate(out_refs):
+            out_ref[...] = weighted_sum(values, scales, kind).astype(jnp.bfloat16)
+
+    @pl.when(jnp.logical_not(outer) & (pl.program_id(0) == last))
+    def _():
+        for kind, out_ref in enumerate(out_refs):
+            for tile in range(out_ref.shape[0]):
+                out_ref[tile, rows - 1] = jnp.full(out_ref.shape[2:], float(tile == kind), jnp.bfloat16)
+
+
+def relay(sources, passing, place):
+    shape = sources[0].shape
+    rows = 13 if shape[1] % 13 == 0 else 1
+    specs = unit_specs(shape, rows)
+    return pl.pallas_call(
+        relay_kernel,
+        grid=(shape[1] // rows,),
+        in_specs=[pl.BlockSpec(memory_space=pltpu.SMEM)] + specs * len(sources) + specs[:1] * 2,
+        out_specs=specs[:1] * 2,
+        out_shape=[jax.ShapeDtypeStruct(shape, jnp.bfloat16)] * 2,
+        compiler_params=pltpu.CompilerParams(vmem_limit_bytes=VMEM_LIMIT),
+        cost_estimate=pl.CostEstimate(
+            flops=0, bytes_accessed=2 * (len(sources) + 4) * math.prod(shape), transcendentals=0
+        ),
+        name="relay",
+    )(place, *[ref for source in sources for ref in (source, source)], *passing)
+
+
+def mid_kernel(first_chunk, place_ref, table_ref, *refs):
+    pencils = 4
+    refs, out_refs, gathered = refs[: -pencils - 1], refs[-pencils - 1 : -1], refs[-1]
+    tiles, rows, columns, lanes = refs[0].shape
+    mid_len = tiles * lanes
     half = columns // 2
-    pencils, classes, slots, _, halves = out_ref.shape[:5]
+    classes, slots, _, halves = out_refs[0].shape[:4]
     groups = pencils // 2
     lead = place_ref[0] == 0
+    outer = place_ref[2] != 0
     row_ids = lax.broadcasted_iota(jnp.int32, (rows, half, mid_len), 1)
     special = lead & (row_ids % (groups * slots) == 0)
+    sources = [ref[...] for ref in refs[0::2]]
+    weights = [ref[...] for ref in refs[1::2]]
+    for kept in (sources, weights):
+        for spare in (-1, -2):
+            kept[spare - 2] = jnp.where(outer, kept[spare], kept[spare - 2])
+        del kept[-2:]
+    sources = [source.astype(jnp.float32) for source in sources]
+    weights = [weight.astype(jnp.float32) for weight in weights]
     for kind in range(classes):
-        total = None
-        for number, source in enumerate(sources):
-            term = source[...].astype(jnp.float32) * weights_ref[kind, number]
-            total = term if total is None else total + term
-        total = total.astype(jnp.bfloat16)
-        lines = jnp.concatenate([total[:, a * mid_len : (a + 1) * mid_len] for a in range(rows)], axis=0)
+        total = weighted_sum(sources, weights, kind).astype(jnp.bfloat16)
+        lines = jnp.concatenate([total[tile].reshape(rows * columns, lanes) for tile in range(tiles)], axis=1)
         product = jnp.dot(lines, table_ref[kind], preferred_element_type=jnp.float32)
         product = product.reshape(rows, columns, 2 * mid_len)
         re_cos, re_sin = product[:, :half, :mid_len], product[:, :half, mid_len:]
@@ -275,48 +363,48 @@
                 for group in range(groups):
                     for slot in range(slots):
                         at = (piece * groups + group) * slots + slot
-                        out_ref[group, kind, slot, part, piece] = up[at].astype(jnp.bfloat16)
+                        gathered[group, kind, slot, part, piece] = up[at].astype(jnp.bfloat16)
                         value = down[at]
                         if first_chunk and slot == 0:
                             other = (piece * groups + (group + 1) % groups) * slots
                             value = jnp.where(lead, down[other], value)
-                        out_ref[pencils - 1 - group, kind, slot, part, piece] = value.astype(jnp.bfloat16)
-
-
-def transform_mid(sources, weights, place, table, first_chunk, chunks, pencils, slots):
-    columns, length = sources[0].shape
+                        gathered[pencils - 1 - group, kind, slot, part, piece] = value.astype(jnp.bfloat16)
+    for step, out_ref in enumerate(out_refs):
+        out_ref[...] = gathered[place_ref[1] ^ step]
+
+
+def transform_mid(sources, place, table, first_chunk, chunks, pencils, slots):
+    tiles, lines, columns, lanes = sources[0].shape
+    lines -= 1
     classes, mid_len, _ = table.shape
-    lines = length // mid_len
     rows = 16
-    shape = (pencils, classes, slots, 2, chunks, lines, mid_len)
+    shape = (classes, slots, 2, chunks, lines, mid_len)
+    block = shape[:4] + (rows, mid_len)
+    size = sources[0].size
     return pl.pallas_call(
-        functools.partial(mid_kernel, first_chunk, rows),
+        functools.partial(mid_kernel, first_chunk),
         grid=(lines // rows,),
-        in_specs=[
-            pl.BlockSpec(memory_space=pltpu.SMEM),
-            pl.BlockSpec(memory_space=pltpu.SMEM),
-            pl.BlockSpec(table.shape, lambda i: (0, 0, 0)),
-        ]
-        + [pl.BlockSpec((columns, rows * mid_len), lambda i: (0, i))] * len(sources),
-        out_specs=pl.BlockSpec(shape[:5] + (rows, mid_len), lambda i: (0, 0, 0, 0, 0, i, 0)),
-        out_shape=jax.ShapeDtypeStruct(shape, jnp.bfloat16),
+        in_specs=[pl.BlockSpec(memory_space=pltpu.SMEM), pl.BlockSpec(table.shape, lambda i: (0, 0, 0))]
+        + unit_specs(sources[0].shape, rows) * len(sources),
+        out_specs=[pl.BlockSpec(block, lambda i: (0, 0, 0, 0, i, 0))] * pencils,
+        out_shape=[jax.ShapeDtypeStruct(shape, jnp.bfloat16)] * pencils,
+        scratch_shapes=[pltpu.VMEM((pencils,) + block, jnp.bfloat16)],
         compiler_params=pltpu.CompilerParams(vmem_limit_bytes=VMEM_LIMIT),
         cost_estimate=pl.CostEstimate(
-            flops=8 * columns * length * mid_len,
-            bytes_accessed=2 * len(sources) * columns * length + 2 * math.prod(shape),
+            flops=8 * size * mid_len,
+            bytes_accessed=2 * len(sources) * size + 2 * pencils * math.prod(shape),
             transcendentals=0,
         ),
         name="transform_mid",
-    )(weights, place, table, *sources)
-
-
-def long_kernel(rows_ref, place_ref, z_ref, first_ref, second_ref, plane_ref, *refs):
-    sources, out_ref, gathered = refs[:-2], refs[-2], refs[-1]
-    pencils = len(sources)
+    )(place, table, *[ref for source in sources for ref in (source, source)])
+
+
+def long_kernel(pencils, rows_ref, place_ref, z_ref, first_ref, second_ref, plane_ref, *refs):
+    sources, out_refs, gathered, laid = refs[:pencils], refs[pencils:-2], refs[-2], refs[-1]
     classes, _, _, local_long, mid_len = sources[0].shape
     depth = 2 * pencils * local_long
     long_len = pencils * local_long
-    pairs = out_ref.shape[3]
+    owned, _, _, pairs, _ = out_refs[0].shape
     per_long = long_len // (2 * pairs)
     per_mid = mid_len // (2 * pairs)
     edge = per_mid // 2
@@ -372,17 +460,22 @@
                 block = across * per_long + 2 * couple
                 left = jnp.where(low, even, pltpu.roll(odd, 2 * pairs, 1))
                 right = jnp.where(low, pltpu.roll(even, 2 * pairs, 1), odd)
-                out_ref[rows_ref[block], 0, part] = left.astype(jnp.bfloat16)
-                out_ref[rows_ref[block + 1], 0, part] = right.astype(jnp.bfloat16)
-
-
-def transform_long(sources, row_ids, place, z_factor, first, second, plane, row_count, pairs):
+                laid[rows_ref[block], part] = left.astype(jnp.bfloat16)
+                laid[rows_ref[block + 1], part] = right.astype(jnp.bfloat16)
+    for step, out_ref in enumerate(out_refs):
+        top = (place_ref[0] ^ step) * owned
+        for row in range(owned):
+            out_ref[row, 0] = laid[top + row]
+
+
+def transform_long(sources, row_ids, place, z_factor, first, second, plane, row_count, grid_count, pairs):
     classes, slots, _, local_long, mid_len = sources[0].shape
     pencils = len(sources)
     depth = 2 * pencils * local_long
-    shape = (row_count, slots, 2, pairs, 4 * pairs)
+    owned = row_count // grid_count
+    shape = (owned, slots, 2, pairs, 4 * pairs)
     return pl.pallas_call(
-        long_kernel,
+        functools.partial(long_kernel, pencils),
         grid=(slots,),
         in_specs=[
             pl.BlockSpec(memory_space=pltpu.SMEM),
@@ -393,13 +486,16 @@
             pl.BlockSpec(plane.shape, lambda i: (0, 0, 0, 0)),
         ]
         + [pl.BlockSpec((classes, 1, 2, local_long, mid_len), lambda i: (0, i, 0, 0, 0))] * pencils,
-        out_specs=pl.BlockSpec((row_count, 1, 2, pairs, 4 * pairs), lambda i: (0, i, 0, 0, 0)),
-        out_shape=jax.ShapeDtypeStruct(shape, jnp.bfloat16),
-        scratch_shapes=[pltpu.VMEM((classes, pencils, 2, local_long, mid_len), jnp.bfloat16)],
+        out_specs=[pl.BlockSpec((owned, 1, 2, pairs, 4 * pairs), lambda i: (0, i, 0, 0, 0))] * grid_count,
+        out_shape=[jax.ShapeDtypeStruct(shape, jnp.bfloat16)] * grid_count,
+        scratch_shapes=[
+            pltpu.VMEM((classes, pencils, 2, local_long, mid_len), jnp.bfloat16),
+            pltpu.VMEM((row_count, 2, pairs, 4 * pairs), jnp.bfloat16),
+        ],
         compiler_params=pltpu.CompilerParams(vmem_limit_bytes=VMEM_LIMIT),
         cost_estimate=pl.CostEstimate(
             flops=2 * classes * slots * depth * depth * mid_len,
-            bytes_accessed=2 * pencils * sources[0].size + 2 * math.prod(shape) + 4 * depth * depth,
+            bytes_accessed=2 * pencils * sources[0].size + 2 * grid_count * math.prod(shape) + 4 * depth * depth,
             transcendentals=0,
         ),
         name="transform_long",
@@ -452,15 +548,61 @@
 
 
 def exchange(parts, axis):
-    count = parts.shape[0]
-    me = lax.axis_index(axis)
-    got = []
-    for step in range(count):
-        sent = lax.dynamic_index_in_dim(parts, me ^ step, keepdims=False)
-        if step:
-            sent = lax.ppermute(sent, axis, [(d, d ^ step) for d in range(count)])
-        got.append(sent)
-    return got
+    count = len(parts)
+    got = {0: parts[0]}
+    for step in reversed(range(1, count)):
+        got[step] = lax.ppermute(parts[step], axis, [(d, d ^ step) for d in range(count)])
+    return [got[step] for step in range(count)]
+
+
+FAR = (3, 0, 3, 0)
+NEXT = (1, 2, 1, 2)
+THIRD = (2, 3, 0, 1)
+PAIR_SAME = [(d, d ^ 2) for d in range(8)]
+PAIR_CROSS = [(d, d ^ 3) for d in range(8)]
+INNER_SAME = [(2, 4), (4, 2), (3, 5), (5, 3)]
+INNER_CROSS = [(2, 5), (5, 2), (3, 4), (4, 3)]
+INNER_CORES = [(d, d ^ 1) for d in range(2, 6)]
+CORES = [(d, d ^ 1) for d in range(8)]
+ENTER_SAME = [(0, 2), (1, 3), (6, 4), (7, 5)]
+ENTER_CROSS = [(0, 3), (1, 2), (6, 5), (7, 4)]
+JUMP_SAME = [(d, d ^ 4) for d in range(8)]
+JUMP_MIXED = [(0, 5), (1, 4), (6, 3), (7, 2), (2, 6), (3, 7), (4, 0), (5, 1)]
+
+
+def unit_order(me):
+    chips = jnp.stack(
+        [jnp.array(chip, jnp.int32)[me // 2] for chip in (FAR, NEXT, THIRD, (0, 1, 2, 3))]
+    )
+    core = me % 2
+    return jnp.stack([2 * chips + core, 2 * chips + 1 - core], axis=1).reshape(-1)
+
+
+def gather_grids(units, place):
+    far_same, far_cross, next_same, next_cross, third_same, third_cross, own, other = units
+    pair_same = lax.ppermute(far_same, "grid", PAIR_SAME)
+    pair_cross = lax.ppermute(far_cross, "grid", PAIR_CROSS)
+    inner_core = lax.ppermute(third_cross, "grid", INNER_CORES)
+    inner_same = lax.ppermute(next_same, "grid", INNER_SAME)
+    inner_cross = lax.ppermute(next_cross, "grid", INNER_CROSS)
+    core = lax.ppermute(other, "grid", CORES)
+    sums = relay([third_same, inner_core, pair_same, pair_cross], [third_same, third_cross], place)
+    enter_same = lax.ppermute(next_same, "grid", ENTER_SAME)
+    enter_cross = lax.ppermute(next_cross, "grid", ENTER_CROSS)
+    jump_same = lax.ppermute(sums[0], "grid", JUMP_SAME)
+    jump_mixed = lax.ppermute(sums[1], "grid", JUMP_MIXED)
+    return [
+        own,
+        core,
+        enter_same,
+        enter_cross,
+        jump_same,
+        jump_mixed,
+        inner_same,
+        inner_cross,
+        pair_same,
+        pair_cross,
+    ]
 
 
 def mode_factor(modes, diffusion, speed, long_len, mid_len):
@@ -488,9 +630,6 @@
     weight = (coefficients[0] * (1 - failed[0])).astype(jnp.float32)
     swapped = levels[0, 0] < levels[0, 1]
     mine = jnp.stack([jnp.where(swapped, 0.0, weight), jnp.where(swapped, weight, 0.0)])
-    weights = lax.all_gather(mine, "grid", axis=1)
-    near = jnp.take(weights, me ^ jnp.arange(grid_count, dtype=jnp.int32), axis=1)
-
     positions = jnp.arange(long_len, dtype=jnp.int32)
     modes = signed_modes(positions, long_len)
     x_re, x_im = mode_factor(modes, diffusivity[0], velocity[0], long_len, mid_len)
@@ -507,18 +646,21 @@
     )
     z_factor = jnp.stack([z_re, z_im]) * (1.0 / math.sqrt(long_len * mid_len * z_len))
 
-    place = jnp.stack([me, pencil]).astype(jnp.int32)
+    outer = (me < 2) | (me >= grid_count - 2)
+    place = jnp.stack([me, pencil, outer.astype(jnp.int32)]).astype(jnp.int32)
     side = jnp.stack([me, back.astype(jnp.int32)]).astype(jnp.int32)
     mid = mid_table(mid_len, block_len)
     first, second = long_tables(long_len, block_len, pencils)
+    order = unit_order(me)
 
     arrived = []
     for chunk in range(CHUNKS):
-        along_z = transform_z(samples, z_table(chunk, CHUNKS, grid_count, pencils, z_len), CHUNKS)
-        parts = along_z.reshape(grid_count, -1, along_z.shape[1])
-        sources = exchange(parts, "grid")
-        along_mid = transform_mid(sources, near, place, mid, chunk == 0, CHUNKS, pencils, slots)
-        along_mid = along_mid.reshape(along_mid.shape[:4] + (local_long, mid_len))
+        table = z_table(chunk, CHUNKS, grid_count, pencils, z_len)
+        table = table.reshape(grid_count, -1, table.shape[1])[order].reshape(table.shape)
+        units = transform_z(samples, table, mine, CHUNKS, grid_count)
+        sources = gather_grids(units, place)
+        along_mid = transform_mid(sources, place, mid, chunk == 0, CHUNKS, pencils, slots)
+        along_mid = [v.reshape(v.shape[:3] + (local_long, mid_len)) for v in along_mid]
         lines = exchange(along_mid, "pencil")
         rows = transform_long(
             lines,
@@ -529,9 +671,10 @@
             second,
             plane,
             row_count,
+            grid_count,
             block_len // 2,
         )
-        arrived += exchange(rows.reshape((grid_count, -1) + rows.shape[1:]), "grid")
+        arrived += exchange(rows, "grid")
     return lay_rows(arrived, side, grid_count, z_local)
 
 
@@ -540,7 +683,7 @@
     devices = mesh.shape["grid"] * mesh.shape["pencil"]
 
     def run(field, *rest):
-        few = field.shape[3] % (devices * CHUNKS) == 0 and mesh.shape["pencil"] % 2 == 0
+        few = mesh.shape["grid"] == 8 and mesh.shape["pencil"] == 4 and field.shape[3] % (devices * CHUNKS) == 0
         return jax.shard_map(
             body if few else wide_body,
             mesh=mesh,

time: 319 us -> 302 us (0.947)
  the two profiles are of different devices: /device:TPU:0 before, /device:TPU:21 now
where the time goes in v2:
time: 302 us; the launch traced here: 300 us
  waiting for transfers between devices  131 us (43%)
  starting transfers between devices  78.4 us (26%)
  Pallas kernels  65.9 us (22%)
  local copies, waits for them, and re-layouts  12.6 us (4%)
  other arithmetic  9.25 us (3%)
  between operations  3.19 us (1%)
    ppermute x20, waiting for transfers between devices, exchange(): lax.ppermute(parts[step], axis, [(d, d ^ step) for d in range(count)])  52 us
    ppermute x20, starting transfers between devices, exchange(): lax.ppermute(parts[step], axis, [(d, d ^ step) for d in range(count)])  30.7 us
    ppermute x2, waiting for transfers between devices, gather_grids(): inner_cross = lax.ppermute(next_cross, 'grid', INNER_CROSS)  26.4 us
    pallas_call x2, Pallas kernels, transform_z(): pl.pallas_call(z_kernel, grid=(steps + 1,), in_specs=[pl.BlockSpec(memory...  18.5 us
    ppermute x2, waiting for transfers between devices, gather_grids(): jump_mixed = lax.ppermute(sums[1], 'grid', JUMP_MIXED)  17.6 us
    ppermute x2, waiting for transfers between devices, gather_grids(): pair_cross = lax.ppermute(far_cross, 'grid', PAIR_CROSS)  16.9 us
    pallas_call x2, Pallas kernels, transform_long(): pl.pallas_call(functools.partial(long_kernel, pencils), grid=(slots,), in...  15.3 us
    ppermute x2, starting transfers between devices, gather_grids(): core = lax.ppermute(other, 'grid', CORES)  14.2 us
  transfers between devices with their start and end apart: 40, of which 15 were waited for; matrix products, arithmetic and copies ran while one was open for 3% of the time, Pallas kernels for 16%

profile of v2, /device:TPU:21, one launch (start us, length us, event | category | flops | bytes accessed | tf_op | source)
XLA Modules:
  0.0 300.4 jit_solution(14640631297910017645)
XLA Ops:
  1.3 1.3 fusion.12
  7.6 1.9 broadcast_add_fusion
  10.2 2.0 gather_fusion
  12.2 9.2 %transform_z.2 = (bf16[2,65,16,128]{3,2,1,0:T(8,128)(2,1)}, bf16[2,65,16,128]{3,2,1,0:T(8,128)(2,1)}, bf16[2,65,16,128]{3,2,1,0:T(8,128)(2,1)}, bf16[2,65,16,128...) custom-call(f32[2]{0:T(128)} %pad_maximum_fusion.1.weight_ref, ...), custom_call_target="tpu_custom_call" | custom-call | flops 1073741824 | bytes 16777216 | tf_op jit(solution)/shard_map/transform_z/pallas_call | solution.py:248
  22.1 1.3 collective-permute-start.4
  23.8 2.1 collective-permute-start.8
  27.2 2.4 collective-permute-start.3
  29.6 6.4 %collective-permute-done.4.refs_4_.refs_5_.refs_16_.refs_17_ = bf16[2,65,16,128]{3,2,1,0:T(8,128)(2,1)S(1)} collective-permute-done((bf16[2,65,16,128]{3,2,1,0:T(8,128)(2,1)}, bf16[2,65,16,128]{3,2,1,0:T(8,128)(2,1)S(1)}, u32[]{:S(2)}, u32[]{:S(2)}) %collective-permute-start.4) | collective-permute-done | bytes 532512 | tf_op jit(solution)/shard_map/ppermute | solution.py:583
  36.0 3.3 %collective-permute-start.9 = (bf16[2,65,16,128]{3,2,1,0:T(8,128)(2,1)}, bf16[2,65,16,128]{3,2,1,0:T(8,128)(2,1)}, u32[]{:S(2)}, u32[]{:S(2)}) collective-permute-start(bf16[2,65,16,128]{3,2,1,0:T(8,128)(2,1)} %get-tuple-element.52), channel_id=1, source_target_pairs={{8,20},{20,8},{12,16},{16,12},{9,21},{21,9},{13,17},{17,13},{10,22... | collective-permute-start | bytes 1597448 | tf_op jit(solution)/shard_map/ppermute | solution.py:587
  39.3 9.2 %collective-permute-done.5.refs_6_.refs_7_.refs_18_.refs_19_ = bf16[2,65,16,128]{3,2,1,0:T(8,128)(2,1)S(1)} collective-permute-done((bf16[2,65,16,128]{3,2,1,0:T(8,128)(2,1)}, bf16[2,65,16,128]{3,2,1,0:T(8,128)(2,1)S(1)}, u32[]{:S(2)}, u32[]{:S(2)}) %collective-permute-start.5) | collective-permute-done | bytes 532512 | tf_op jit(solution)/shard_map/ppermute | solution.py:584
  50.9 9.3 %transform_z.3 = (bf16[2,65,16,128]{3,2,1,0:T(8,128)(2,1)}, bf16[2,65,16,128]{3,2,1,0:T(8,128)(2,1)}, bf16[2,65,16,128]{3,2,1,0:T(8,128)(2,1)}, bf16[2,65,16,128...) custom-call(f32[2]{0:T(128)} %pad_maximum_fusion.1.weight_ref, ...), custom_call_target="tpu_custom_call" | custom-call | flops 1073741824 | bytes 16777216 | tf_op jit(solution)/shard_map/transform_z/pallas_call | solution.py:248
  60.2 2.2 collective-permute-start.24
  64.4 2.2 collective-permute-start.23
  67.3 5.1 %relay.2 = (bf16[2,65,16,128]{3,2,1,0:T(8,128)(2,1)}, bf16[2,65,16,128]{3,2,1,0:T(8,128)(2,1)}) custom-call(s32[3]{0:T(128)} %pad_add_fusion.2.place_ref, bf16[2,65,16,128]{3,2,1,0:T(8,128)(2,1)} %get-tuple-element.53.refs_0_.refs_1_.refs_8_, bf16[2,65,16,128]{3,2,1,0:T(8,128)(2,1)} %get-tuple-element.53.refs_0_.refs_1_.refs_8_, ...), custom_call_target="tpu_custom_call" | custom-call | bytes 4259840 | tf_op jit(solution)/shard_map/relay/pallas_call | solution.py:313
  72.7 2.1 collective-permute-start.7
  74.9 6.8 %collective-permute-done.24.refs_4_.refs_5_.refs_16_.refs_17_ = bf16[2,65,16,128]{3,2,1,0:T(8,128)(2,1)S(1)} collective-permute-done((bf16[2,65,16,128]{3,2,1,0:T(8,128)(2,1)}, bf16[2,65,16,128]{3,2,1,0:T(8,128)(2,1)S(1)}, u32[]{:S(2)}, u32[]{:S(2)}) %collective-permute-start.24) | collective-permute-done | bytes 532512 | tf_op jit(solution)/shard_map/ppermute | solution.py:583
  81.7 13.5 %collective-permute-start.20 = (bf16[2,65,16,128]{3,2,1,0:T(8,128)(2,1)S(1)}, bf16[2,65,16,128]{3,2,1,0:T(8,128)(2,1)S(1)}, u32[]{:S(2)}, u32[]{:S(2)}) collective-permute-start(bf16[2,65,16,128]{3,2,1,0:T(8,128)(2,1)S(1)} %copy-done.37), channel_id=1, source_target_pairs={{0,4},{4,0},{8,12},{12,8},{16,20},{20,16},{24,28},{28,24},{1,5},{5... | collective-permute-start | bytes 1597448 | tf_op jit(solution)/shard_map/ppermute | solution.py:588
  95.2 7.7 %collective-permute-done.25.refs_6_.refs_7_.refs_18_.refs_19_ = bf16[2,65,16,128]{3,2,1,0:T(8,128)(2,1)S(1)} collective-permute-done((bf16[2,65,16,128]{3,2,1,0:T(8,128)(2,1)}, bf16[2,65,16,128]{3,2,1,0:T(8,128)(2,1)S(1)}, u32[]{:S(2)}, u32[]{:S(2)}) %collective-permute-start.25) | collective-permute-done | bytes 532512 | tf_op jit(solution)/shard_map/ppermute | solution.py:584
  102.9 2.8 collective-permute-start.28
  108.2 4.7 %collective-permute-start.29 = (bf16[2,65,16,128]{3,2,1,0:T(8,128)(2,1)S(1)}, bf16[2,65,16,128]{3,2,1,0:T(8,128)(2,1)S(1)}, u32[]{:S(2)}, u32[]{:S(2)}) collective-permute-start(bf16[2,65,16,128]{3,2,1,0:T(8,128)(2,1)S(1)} %copy-done.35), channel_id=1, source_target_pairs={{8,20},{20,8},{12,16},{16,12},{9,21},{21,9},{13,17},{17,13},{10,22... | collective-permute-start | bytes 1597448 | tf_op jit(solution)/shard_map/ppermute | solution.py:587
  112.9 6.2 %collective-permute-done.7.refs_10_.refs_11_ = bf16[2,65,16,128]{3,2,1,0:T(8,128)(2,1)S(1)} collective-permute-done((bf16[2,65,16,128]{3,2,1,0:T(8,128)(2,1)}, bf16[2,65,16,128]{3,2,1,0:T(8,128)(2,1)S(1)}, u32[]{:S(2)}, u32[]{:S(2)}) %collective-permute-start.7) | collective-permute-done | bytes 532512 | tf_op jit(solution)/shard_map/ppermute | solution.py:593
  120.4 1.3 sine_multiply_fusion.1
  123.0 5.0 %relay.3 = (bf16[2,65,16,128]{3,2,1,0:T(8,128)(2,1)}, bf16[2,65,16,128]{3,2,1,0:T(8,128)(2,1)}) custom-call(s32[3]{0:T(128)} %pad_add_fusion.2.place_ref, bf16[2,65,16,128]{3,2,1,0:T(8,128)(2,1)} %get-tuple-element.75.refs_0_.refs_1_.refs_8_, bf16[2,65,16,128]{3,2,1,0:T(8,128)(2,1)} %get-tuple-element.75.refs_0_.refs_1_.refs_8_, ...), custom_call_target="tpu_custom_call" | custom-call | bytes 4259840 | tf_op jit(solution)/shard_map/relay/pallas_call | solution.py:313
  128.0 6.6 %transform_mid.2 = (bf16[2,2,2,2,64,256]{5,4,3,2,1,0:T(8,128)(2,1)}, bf16[2,2,2,2,64,256]{5,4,3,2,1,0:T(8,128)(2,1)}, bf16[2,2,2,2,64,256]{5,4,3,2,1,0:T(8,128)(2,1)}, bf16[2,2,2,2,64,256]{5,4,3,2,1,0:T(8,128)(2,1)}) custom-call(s32[3]{0:T(128)} %pad_add_fusion.2.place_ref, bf16[2,256,512]{2,1,0:T(8,128)(2,1)} %constant.111.clone.table_ref, ...), custom_call_target="tpu_custom_call" | custom-call | flops 545259520 | bytes 7421952 | tf_op jit(solution)/shard_map/transform_mid/pallas_call | solution.py:384
  134.6 3.2 %collective-permute-start.26 = (bf16[2,65,16,128]{3,2,1,0:T(8,128)(2,1)}, bf16[2,65,16,128]{3,2,1,0:T(8,128)(2,1)S(1)}, u32[]{:S(2)}, u32[]{:S(2)}) collective-permute-start(bf16[2,65,16,128]{3,2,1,0:T(8,128)(2,1)} %get-tuple-element.79), channel_id=1, source_target_pairs={{0,16},{4,20},{8,24},{12,28},{16,0},{20,4},{24,8},{28,12},{1,17},{... | collective-permute-start | bytes 1597448 | tf_op jit(solution)/shard_map/ppermute | solution.py:592
  139.6 26.4 %collective-permute-done.29.refs_14_.refs_15_ = bf16[2,65,16,128]{3,2,1,0:T(8,128)(2,1)S(1)} collective-permute-done((bf16[2,65,16,128]{3,2,1,0:T(8,128)(2,1)S(1)}, bf16[2,65,16,128]{3,2,1,0:T(8,128)(2,1)S(1)}, u32[]{:S(2)}, u32[]{:S(2)}) %collective-permute-start.29) | collective-permute-done | bytes 532512 | tf_op jit(solution)/shard_map/ppermute | solution.py:587
  166.3 2.2 collective-permute-start.12
  168.4 1.5 pad_maximum_fusion.plane_ref
  171.2 5.0 %collective-permute-done.26.refs_8_.refs_9_ = bf16[2,65,16,128]{3,2,1,0:T(8,128)(2,1)S(1)} collective-permute-done((bf16[2,65,16,128]{3,2,1,0:T(8,128)(2,1)}, bf16[2,65,16,128]{3,2,1,0:T(8,128)(2,1)S(1)}, u32[]{:S(2)}, u32[]{:S(2)}) %collective-permute-start.26) | collective-permute-done | bytes 532512 | tf_op jit(solution)/shard_map/ppermute | solution.py:592
  176.2 11.4 %collective-permute-done.27.refs_10_.refs_11_ = bf16[2,65,16,128]{3,2,1,0:T(8,128)(2,1)S(1)} collective-permute-done((bf16[2,65,16,128]{3,2,1,0:T(8,128)(2,1)}, bf16[2,65,16,128]{3,2,1,0:T(8,128)(2,1)S(1)}, u32[]{:S(2)}, u32[]{:S(2)}) %collective-permute-start.27) | collective-permute-done | bytes 532512 | tf_op jit(solution)/shard_map/ppermute | solution.py:593
  188.4 6.5 %transform_mid.3 = (bf16[2,2,2,2,64,256]{5,4,3,2,1,0:T(8,128)(2,1)}, bf16[2,2,2,2,64,256]{5,4,3,2,1,0:T(8,128)(2,1)}, bf16[2,2,2,2,64,256]{5,4,3,2,1,0:T(8,128)(2,1)}, bf16[2,2,2,2,64,256]{5,4,3,2,1,0:T(8,128)(2,1)}) custom-call(s32[3]{0:T(128)} %pad_add_fusion.2.place_ref, bf16[2,256,512]{2,1,0:T(8,128)(2,1)} %constant.111.clone.table_ref, ...), custom_call_target="tpu_custom_call" | custom-call | flops 545259520 | bytes 7421952 | tf_op jit(solution)/shard_map/transform_mid/pallas_call | solution.py:384
  198.2 7.6 %transform_long.2 = (bf16[6,2,2,32,128]{4,3,2,1,0:T(8,128)(2,1)}, bf16[6,2,2,32,128]{4,3,2,1,0:T(8,128)(2,1)}, bf16[6,2,2,32,128]{4,3,2,1,0:T(8,128)(2,1)}, bf16...) custom-call(s32[64]{0:T(128)} %rows_ref.3, ...), custom_call_target="tpu_custom_call" | custom-call | flops 2147483648 | bytes 7864320 | tf_op jit(solution)/shard_map/transform_long/pallas_call | solution.py:477
  205.8 1.4 collective-permute-start.13
  207.3 2.3 collective-permute-start.14
  209.7 3.0 collective-permute-start.15
  212.9 6.4 %collective-permute-done.32.refs_3_ = bf16[2,2,2,128,256]{4,3,2,1,0:T(8,128)(2,1)S(1)} collective-permute-done((bf16[2,2,2,128,256]{4,3,2,1,0:T(8,128)(2,1)}, bf16[2,2,2,128,256]{4,3,2,1,0:T(8,128)(2,1)S(1)}, u32[]{:S(2)}, u32[]{:S(2)}) %collective-permute-start.32) | collective-permute-done | bytes 524320 | tf_op jit(solution)/shard_map/ppermute | solution.py:554
  219.3 5.6 %collective-permute-start.17 = (bf16[6,2,2,32,128]{4,3,2,1,0:T(8,128)(2,1)}, bf16[6,2,2,32,128]{4,3,2,1,0:T(8,128)(2,1)S(1)}, u32[]{:S(2)}, u32[]{:S(2)}) collective-permute-start(bf16[6,2,2,32,128]{4,3,2,1,0:T(8,128)(2,1)} %get-tuple-element.68), channel_id=1, source_target_pairs={{0,20},{4,16},{8,28},{12,24},{16,4},{20,0},{24,12},{28,8},{1,21},{... | collective-permute-start | bytes 589832 | tf_op jit(solution)/shard_map/ppermute | solution.py:554
  224.9 7.7 %transform_long.3 = (bf16[6,2,2,32,128]{4,3,2,1,0:T(8,128)(2,1)}, bf16[6,2,2,32,128]{4,3,2,1,0:T(8,128)(2,1)}, bf16[6,2,2,32,128]{4,3,2,1,0:T(8,128)(2,1)}, bf16...) custom-call(s32[64]{0:T(128)} %rows_ref.3, ...), custom_call_target="tpu_custom_call" | custom-call | flops 2147483648 | bytes 7864320 | tf_op jit(solution)/shard_map/transform_long/pallas_call | solution.py:477
  233.4 2.0 collective-permute-start.19
  235.5 3.1 %collective-permute-start.34 = (bf16[6,2,2,32,128]{4,3,2,1,0:T(8,128)(2,1)}, bf16[6,2,2,32,128]{4,3,2,1,0:T(8,128)(2,1)S(1)}, u32[]{:S(2)}, u32[]{:S(2)}) collective-permute-start(bf16[6,2,2,32,128]{4,3,2,1,0:T(8,128)(2,1)} %get-tuple-element.87), channel_id=1, source_target_pairs={{0,8},{4,12},{8,0},{12,4},{16,24},{20,28},{24,16},{28,20},{1,9},{5... | collective-permute-start | bytes 589832 | tf_op jit(solution)/shard_map/ppermute | solution.py:554
  238.5 5.9 %collective-permute-done.17.refs_5_ = bf16[6,2,2,32,128]{4,3,2,1,0:T(8,128)(2,1)S(1)} collective-permute-done((bf16[6,2,2,32,128]{4,3,2,1,0:T(8,128)(2,1)}, bf16[6,2,2,32,128]{4,3,2,1,0:T(8,128)(2,1)S(1)}, u32[]{:S(2)}, u32[]{:S(2)}) %collective-permute-start.17) | collective-permute-done | bytes 196640 | tf_op jit(solution)/shard_map/ppermute | solution.py:554
  244.4 4.8 %collective-permute-start.35 = (bf16[6,2,2,32,128]{4,3,2,1,0:T(8,128)(2,1)}, bf16[6,2,2,32,128]{4,3,2,1,0:T(8,128)(2,1)S(1)}, u32[]{:S(2)}, u32[]{:S(2)}) collective-permute-start(bf16[6,2,2,32,128]{4,3,2,1,0:T(8,128)(2,1)} %get-tuple-element.88), channel_id=1, source_target_pairs={{0,12},{4,8},{8,4},{12,0},{16,28},{20,24},{24,20},{28,16},{1,13},{... | collective-permute-start | bytes 589832 | tf_op jit(solution)/shard_map/ppermute | solution.py:554
  249.2 2.7 collective-permute-done.18.refs_6_
  251.9 10.3 %collective-permute-done.19.refs_7_ = bf16[6,2,2,32,128]{4,3,2,1,0:T(8,128)(2,1)S(1)} collective-permute-done((bf16[6,2,2,32,128]{4,3,2,1,0:T(8,128)(2,1)S(1)}, bf16[6,2,2,32,128]{4,3,2,1,0:T(8,128)(2,1)S(1)}, u32[]{:S(2)}, u32[]{:S(2)}) %collective-permute-start.19) | collective-permute-done | bytes 196640 | tf_op jit(solution)/shard_map/ppermute | solution.py:554
  264.1 15.9 %collective-permute-done.37.refs_13_ = bf16[6,2,2,32,128]{4,3,2,1,0:T(8,128)(2,1)S(1)} collective-permute-done((bf16[6,2,2,32,128]{4,3,2,1,0:T(8,128)(2,1)}, bf16[6,2,2,32,128]{4,3,2,1,0:T(8,128)(2,1)S(1)}, u32[]{:S(2)}, u32[]{:S(2)}) %collective-permute-start.37) | collective-permute-done | bytes 196640 | tf_op jit(solution)/shard_map/ppermute | solution.py:554
  280.0 5.8 %collective-permute-done.38.refs_14_ = bf16[6,2,2,32,128]{4,3,2,1,0:T(8,128)(2,1)S(1)} collective-permute-done((bf16[6,2,2,32,128]{4,3,2,1,0:T(8,128)(2,1)}, bf16[6,2,2,32,128]{4,3,2,1,0:T(8,128)(2,1)S(1)}, u32[]{:S(2)}, u32[]{:S(2)}) %collective-permute-start.38) | collective-permute-done | bytes 196640 | tf_op jit(solution)/shard_map/ppermute | solution.py:554
  285.9 4.8 %collective-permute-done.39.refs_15_ = bf16[6,2,2,32,128]{4,3,2,1,0:T(8,128)(2,1)S(1)} collective-permute-done((bf16[6,2,2,32,128]{4,3,2,1,0:T(8,128)(2,1)}, bf16[6,2,2,32,128]{4,3,2,1,0:T(8,128)(2,1)S(1)}, u32[]{:S(2)}, u32[]{:S(2)}) %collective-permute-start.39) | collective-permute-done | bytes 196640 | tf_op jit(solution)/shard_map/ppermute | solution.py:554
  291.3 8.9 %lay_rows.1 = f32[6,2,32,4096]{3,2,1,0:T(8,128)} custom-call(s32[2]{0:T(128)} %pad_add_fusion.1.place_ref, bf16[6,2,2,32,128]{4,3,2,1,0:T(8,128)(2,1)} %get-tuple-element.63.refs_0_, bf16[6,2,2,32,128]{4,3,2,1,0:T(8,128)(2,1)} %copy-done.18, bf16[6,2,2,32,128]{4,3,2,1,0:T(8,128)(2,1)} %copy-done.19, bf16[6,2,2,32,128]{4,3,2,1,0:T(8,128)(2,1)} %copy-done.20, ...), custom_call_target="tpu_custom_call" | custom-call | bytes 9437184 | tf_op jit(solution)/shard_map/lay_rows/pallas_call | solution.py:534
  (146 shorter events, 28.2 us)
Async XLA Ops:
  21.4 5.8 %collective-permute-start = (bf16[2,65,16,128]{3,2,1,0:T(8,128)(2,1)}, bf16[2,65,16,128]{3,2,1,0:T(8,128)(2,1)S(1)}, u32[]{:S(2)}, u32[]{:S(2)}) collective-permute-start(bf16[2,65,16,128]{3,2,1,0:T(8,128)(2,1)} %get-tuple-element.50), channel_id=1, source_target_pairs={{0,4},{4,0},{8,12},{12,8},{16,20},{20,16},{24,28},{28,24},{1,5},{5... | collective-permute-start | bytes 1597448 | tf_op jit(solution)/shard_map/ppermute | solution.py:588
  22.1 13.9 %collective-permute-start.4 = (bf16[2,65,16,128]{3,2,1,0:T(8,128)(2,1)}, bf16[2,65,16,128]{3,2,1,0:T(8,128)(2,1)S(1)}, u32[]{:S(2)}, u32[]{:S(2)}) collective-permute-start(bf16[2,65,16,128]{3,2,1,0:T(8,128)(2,1)} %get-tuple-element.55), channel_id=1, source_target_pairs={{0,8},{4,12},{8,0},{12,4},{16,24},{20,28},{24,16},{28,20},{1,9},{5... | collective-permute-start | bytes 1597448 | tf_op jit(solution)/shard_map/ppermute | solution.py:583
  23.4 25.0 %collective-permute-start.5 = (bf16[2,65,16,128]{3,2,1,0:T(8,128)(2,1)}, bf16[2,65,16,128]{3,2,1,0:T(8,128)(2,1)S(1)}, u32[]{:S(2)}, u32[]{:S(2)}) collective-permute-start(bf16[2,65,16,128]{3,2,1,0:T(8,128)(2,1)} %get-tuple-element.56), channel_id=1, source_target_pairs={{0,12},{4,8},{8,4},{12,0},{16,28},{20,24},{24,20},{28,16},{1,13},{... | collective-permute-start | bytes 1597448 | tf_op jit(solution)/shard_map/ppermute | solution.py:584
  23.8 36.4 %collective-permute-start.8 = (bf16[2,65,16,128]{3,2,1,0:T(8,128)(2,1)}, bf16[2,65,16,128]{3,2,1,0:T(8,128)(2,1)S(1)}, u32[]{:S(2)}, u32[]{:S(2)}) collective-permute-start(bf16[2,65,16,128]{3,2,1,0:T(8,128)(2,1)} %get-tuple-element.51), channel_id=1, source_target_pairs={{8,16},{16,8},{12,20},{20,12},{9,17},{17,9},{13,21},{21,13},{10,18... | collective-permute-start | bytes 1597448 | tf_op jit(solution)/shard_map/ppermute | solution.py:586
  25.9 36.5 %collective-permute-start.1 = (bf16[2,65,16,128]{3,2,1,0:T(8,128)(2,1)}, bf16[2,65,16,128]{3,2,1,0:T(8,128)(2,1)S(1)}, u32[]{:S(2)}, u32[]{:S(2)}) collective-permute-start(bf16[2,65,16,128]{3,2,1,0:T(8,128)(2,1)} %get-tuple-element.51), channel_id=1, source_target_pairs={{0,8},{4,12},{24,16},{28,20},{1,9},{5,13},{25,17},{29,21},{2,10},{... | collective-permute-start | bytes 1597448 | tf_op jit(solution)/shard_map/ppermute | solution.py:590
  27.2 37.1 %collective-permute-start.3 = (bf16[2,65,16,128]{3,2,1,0:T(8,128)(2,1)}, bf16[2,65,16,128]{3,2,1,0:T(8,128)(2,1)}, u32[]{:S(2)}, u32[]{:S(2)}) collective-permute-start(bf16[2,65,16,128]{3,2,1,0:T(8,128)(2,1)} %get-tuple-element.54.refs_9_), channel_id=1, source_target_pairs={{8,12},{12,8},{16,20},{20,16},{9,13},{13,9},{17,21},{21,17},{10,14... | collective-permute-start | bytes 1597448 | tf_op jit(solution)/shard_map/ppermute | solution.py:585
  36.0 36.4 %collective-permute-start.9 = (bf16[2,65,16,128]{3,2,1,0:T(8,128)(2,1)}, bf16[2,65,16,128]{3,2,1,0:T(8,128)(2,1)}, u32[]{:S(2)}, u32[]{:S(2)}) collective-permute-start(bf16[2,65,16,128]{3,2,1,0:T(8,128)(2,1)} %get-tuple-element.52), channel_id=1, source_target_pairs={{8,20},{20,8},{12,16},{16,12},{9,21},{21,9},{13,17},{17,13},{10,22... | collective-permute-start | bytes 1597448 | tf_op jit(solution)/shard_map/ppermute | solution.py:587
  48.4 24.3 %collective-permute-start.2 = (bf16[2,65,16,128]{3,2,1,0:T(8,128)(2,1)}, bf16[2,65,16,128]{3,2,1,0:T(8,128)(2,1)}, u32[]{:S(2)}, u32[]{:S(2)}) collective-permute-start(bf16[2,65,16,128]{3,2,1,0:T(8,128)(2,1)} %get-tuple-element.52), channel_id=1, source_target_pairs={{0,12},{4,8},{24,20},{28,16},{1,13},{5,9},{25,21},{29,17},{2,14},{... | collective-permute-start | bytes 1597448 | tf_op jit(solution)/shard_map/ppermute | solution.py:591
  60.2 21.4 %collective-permute-start.24 = (bf16[2,65,16,128]{3,2,1,0:T(8,128)(2,1)}, bf16[2,65,16,128]{3,2,1,0:T(8,128)(2,1)S(1)}, u32[]{:S(2)}, u32[]{:S(2)}) collective-permute-start(bf16[2,65,16,128]{3,2,1,0:T(8,128)(2,1)} %get-tuple-element.77), channel_id=1, source_target_pairs={{0,8},{4,12},{8,0},{12,4},{16,24},{20,28},{24,16},{28,20},{1,9},{5... | collective-permute-start | bytes 1597448 | tf_op jit(solution)/shard_map/ppermute | solution.py:583
  63.3 39.6 %collective-permute-start.25 = (bf16[2,65,16,128]{3,2,1,0:T(8,128)(2,1)}, bf16[2,65,16,128]{3,2,1,0:T(8,128)(2,1)S(1)}, u32[]{:S(2)}, u32[]{:S(2)}) collective-permute-start(bf16[2,65,16,128]{3,2,1,0:T(8,128)(2,1)} %get-tuple-element.78), channel_id=1, source_target_pairs={{0,12},{4,8},{8,4},{12,0},{16,28},{20,24},{24,20},{28,16},{1,13},{... | collective-permute-start | bytes 1597448 | tf_op jit(solution)/shard_map/ppermute | solution.py:584
  64.4 41.3 %collective-permute-start.23 = (bf16[2,65,16,128]{3,2,1,0:T(8,128)(2,1)}, bf16[2,65,16,128]{3,2,1,0:T(8,128)(2,1)}, u32[]{:S(2)}, u32[]{:S(2)}) collective-permute-start(bf16[2,65,16,128]{3,2,1,0:T(8,128)(2,1)} %get-tuple-element.76.refs_9_), channel_id=1, source_target_pairs={{8,12},{12,8},{16,20},{20,16},{9,13},{13,9},{17,21},{21,17},{10,14... | collective-permute-start | bytes 1597448 | tf_op jit(solution)/shard_map/ppermute | solution.py:585
  67.3 40.4 %copy-start.34 = (f32[3]{0:T(128)S(1)}, f32[3]{0:T(128)}, u32[]{:S(2)}) copy-start(f32[3]{0:T(128)} %param.22) | copy-start | bytes 40
  67.3 40.9 %copy-start.35 = (bf16[2,65,16,128]{3,2,1,0:T(8,128)(2,1)S(1)}, bf16[2,65,16,128]{3,2,1,0:T(8,128)(2,1)}, u32[]{:S(2)}) copy-start(bf16[2,65,16,128]{3,2,1,0:T(8,128)(2,1)} %get-tuple-element.74) | copy-start | bytes 1597444
  72.4 35.8 %collective-permute-start.6 = (bf16[2,65,16,128]{3,2,1,0:T(8,128)(2,1)}, bf16[2,65,16,128]{3,2,1,0:T(8,128)(2,1)S(1)}, u32[]{:S(2)}, u32[]{:S(2)}) collective-permute-start(bf16[2,65,16,128]{3,2,1,0:T(8,128)(2,1)} %get-tuple-element.57), channel_id=1, source_target_pairs={{0,16},{4,20},{8,24},{12,28},{16,0},{20,4},{24,8},{28,12},{1,17},{... | collective-permute-start | bytes 1597448 | tf_op jit(solution)/shard_map/ppermute | solution.py:592
  72.7 46.4 %collective-permute-start.7 = (bf16[2,65,16,128]{3,2,1,0:T(8,128)(2,1)}, bf16[2,65,16,128]{3,2,1,0:T(8,128)(2,1)S(1)}, u32[]{:S(2)}, u32[]{:S(2)}) collective-permute-start(bf16[2,65,16,128]{3,2,1,0:T(8,128)(2,1)} %get-tuple-element.58), channel_id=1, source_target_pairs={{0,20},{4,16},{24,12},{28,8},{8,24},{12,28},{16,0},{20,4},{1,21},{... | collective-permute-start | bytes 1597448 | tf_op jit(solution)/shard_map/ppermute | solution.py:593
  81.7 41.3 %copy-start = (bf16[2,65,16,128]{3,2,1,0:T(8,128)(2,1)}, bf16[2,65,16,128]{3,2,1,0:T(8,128)(2,1)S(1)}, u32[]{:S(2)}) copy-start(bf16[2,65,16,128]{3,2,1,0:T(8,128)(2,1)S(1)} %collective-permute-done.24.refs_4_.refs_5_.refs_16_.refs_17_) | copy-start | bytes 1597444
  81.7 52.9 %collective-permute-start.20 = (bf16[2,65,16,128]{3,2,1,0:T(8,128)(2,1)S(1)}, bf16[2,65,16,128]{3,2,1,0:T(8,128)(2,1)S(1)}, u32[]{:S(2)}, u32[]{:S(2)}) collective-permute-start(bf16[2,65,16,128]{3,2,1,0:T(8,128)(2,1)S(1)} %copy-done.37), channel_id=1, source_target_pairs={{0,4},{4,0},{8,12},{12,8},{16,20},{20,16},{24,28},{28,24},{1,5},{5... | collective-permute-start | bytes 1597448 | tf_op jit(solution)/shard_map/ppermute | solution.py:588
  102.9 35.0 %collective-permute-start.28 = (bf16[2,65,16,128]{3,2,1,0:T(8,128)(2,1)S(1)}, bf16[2,65,16,128]{3,2,1,0:T(8,128)(2,1)S(1)}, u32[]{:S(2)}, u32[]{:S(2)}) collective-permute-start(bf16[2,65,16,128]{3,2,1,0:T(8,128)(2,1)S(1)} %copy-done.36), channel_id=1, source_target_pairs={{8,16},{16,8},{12,20},{20,12},{9,17},{17,9},{13,21},{21,13},{10,18... | collective-permute-start | bytes 1597448 | tf_op jit(solution)/shard_map/ppermute | solution.py:586
  105.7 32.5 %collective-permute-start.21 = (bf16[2,65,16,128]{3,2,1,0:T(8,128)(2,1)S(1)}, bf16[2,65,16,128]{3,2,1,0:T(8,128)(2,1)S(1)}, u32[]{:S(2)}, u32[]{:S(2)}) collective-permute-start(bf16[2,65,16,128]{3,2,1,0:T(8,128)(2,1)S(1)} %copy-done.36), channel_id=1, source_target_pairs={{0,8},{4,12},{24,16},{28,20},{1,9},{5,13},{25,17},{29,21},{2,10},{... | collective-permute-start | bytes 1597448 | tf_op jit(solution)/shard_map/ppermute | solution.py:590
  108.2 57.8 %collective-permute-start.29 = (bf16[2,65,16,128]{3,2,1,0:T(8,128)(2,1)S(1)}, bf16[2,65,16,128]{3,2,1,0:T(8,128)(2,1)S(1)}, u32[]{:S(2)}, u32[]{:S(2)}) collective-permute-start(bf16[2,65,16,128]{3,2,1,0:T(8,128)(2,1)S(1)} %copy-done.35), channel_id=1, source_target_pairs={{8,20},{20,8},{12,16},{16,12},{9,21},{21,9},{13,17},{17,13},{10,22... | collective-permute-start | bytes 1597448 | tf_op jit(solution)/shard_map/ppermute | solution.py:587
  119.1 47.2 %collective-permute-start.22 = (bf16[2,65,16,128]{3,2,1,0:T(8,128)(2,1)S(1)}, bf16[2,65,16,128]{3,2,1,0:T(8,128)(2,1)}, u32[]{:S(2)}, u32[]{:S(2)}) collective-permute-start(bf16[2,65,16,128]{3,2,1,0:T(8,128)(2,1)S(1)} %copy-done.35), channel_id=1, source_target_pairs={{0,12},{4,8},{24,20},{28,16},{1,13},{5,9},{25,21},{29,17},{2,14},{... | collective-permute-start | bytes 1597448 | tf_op jit(solution)/shard_map/ppermute | solution.py:591
  134.6 41.5 %collective-permute-start.26 = (bf16[2,65,16,128]{3,2,1,0:T(8,128)(2,1)}, bf16[2,65,16,128]{3,2,1,0:T(8,128)(2,1)S(1)}, u32[]{:S(2)}, u32[]{:S(2)}) collective-permute-start(bf16[2,65,16,128]{3,2,1,0:T(8,128)(2,1)} %get-tuple-element.79), channel_id=1, source_target_pairs={{0,16},{4,20},{8,24},{12,28},{16,0},{20,4},{24,8},{28,12},{1,17},{... | collective-permute-start | bytes 1597448 | tf_op jit(solution)/shard_map/ppermute | solution.py:592
  137.9 49.7 %collective-permute-start.27 = (bf16[2,65,16,128]{3,2,1,0:T(8,128)(2,1)}, bf16[2,65,16,128]{3,2,1,0:T(8,128)(2,1)S(1)}, u32[]{:S(2)}, u32[]{:S(2)}) collective-permute-start(bf16[2,65,16,128]{3,2,1,0:T(8,128)(2,1)} %get-tuple-element.80), channel_id=1, source_target_pairs={{0,20},{4,16},{24,12},{28,8},{8,24},{12,28},{16,0},{20,4},{1,21},{... | collective-permute-start | bytes 1597448 | tf_op jit(solution)/shard_map/ppermute | solution.py:593
  138.1 58.2 %collective-permute-start.10 = (bf16[2,2,2,128,256]{4,3,2,1,0:T(8,128)(2,1)}, bf16[2,2,2,128,256]{4,3,2,1,0:T(8,128)(2,1)}, u32[]{:S(2)}, u32[]{:S(2)}) collective-permute-start(bf16[2,2,2,128,256]{4,3,2,1,0:T(8,128)(2,1)} %bitcast.37), channel_id=1, source_target_pairs={{0,1},{1,0},{2,3},{3,2},{4,5},{5,4},{6,7},{7,6},{8,9},{9,8},{10,11... | collective-permute-start | bytes 1572872 | tf_op jit(solution)/shard_map/ppermute | solution.py:554
  166.0 32.2 %collective-permute-start.11 = (bf16[2,2,2,128,256]{4,3,2,1,0:T(8,128)(2,1)}, bf16[2,2,2,128,256]{4,3,2,1,0:T(8,128)(2,1)}, u32[]{:S(2)}, u32[]{:S(2)}) collective-permute-start(bf16[2,2,2,128,256]{4,3,2,1,0:T(8,128)(2,1)} %bitcast.23), channel_id=1, source_target_pairs={{0,2},{1,3},{2,0},{3,1},{4,6},{5,7},{6,4},{7,5},{8,10},{9,11},{10,... | collective-permute-start | bytes 1572872 | tf_op jit(solution)/shard_map/ppermute | solution.py:554
  166.3 32.0 %collective-permute-start.12 = (bf16[2,2,2,128,256]{4,3,2,1,0:T(8,128)(2,1)}, bf16[2,2,2,128,256]{4,3,2,1,0:T(8,128)(2,1)}, u32[]{:S(2)}, u32[]{:S(2)}) collective-permute-start(bf16[2,2,2,128,256]{4,3,2,1,0:T(8,128)(2,1)} %bitcast.24), channel_id=1, source_target_pairs={{0,3},{1,2},{2,1},{3,0},{4,7},{5,6},{6,5},{7,4},{8,11},{9,10},{10,... | collective-permute-start | bytes 1572872 | tf_op jit(solution)/shard_map/ppermute | solution.py:554
  194.8 14.8 %collective-permute-start.30 = (bf16[2,2,2,128,256]{4,3,2,1,0:T(8,128)(2,1)}, bf16[2,2,2,128,256]{4,3,2,1,0:T(8,128)(2,1)S(1)}, u32[]{:S(2)}, u32[]{:S(2)}) collective-permute-start(bf16[2,2,2,128,256]{4,3,2,1,0:T(8,128)(2,1)} %bitcast.40), channel_id=1, source_target_pairs={{0,1},{1,0},{2,3},{3,2},{4,5},{5,4},{6,7},{7,6},{8,9},{9,8},{10,11... | collective-permute-start | bytes 1572872 | tf_op jit(solution)/shard_map/ppermute | solution.py:554
  196.1 16.5 %collective-permute-start.31 = (bf16[2,2,2,128,256]{4,3,2,1,0:T(8,128)(2,1)}, bf16[2,2,2,128,256]{4,3,2,1,0:T(8,128)(2,1)S(1)}, u32[]{:S(2)}, u32[]{:S(2)}) collective-permute-start(bf16[2,2,2,128,256]{4,3,2,1,0:T(8,128)(2,1)} %bitcast.39), channel_id=1, source_target_pairs={{0,2},{1,3},{2,0},{3,1},{4,6},{5,7},{6,4},{7,5},{8,10},{9,11},{10,... | collective-permute-start | bytes 1572872 | tf_op jit(solution)/shard_map/ppermute | solution.py:554
  196.3 22.9 %collective-permute-start.32 = (bf16[2,2,2,128,256]{4,3,2,1,0:T(8,128)(2,1)}, bf16[2,2,2,128,256]{4,3,2,1,0:T(8,128)(2,1)S(1)}, u32[]{:S(2)}, u32[]{:S(2)}) collective-permute-start(bf16[2,2,2,128,256]{4,3,2,1,0:T(8,128)(2,1)} %bitcast.38), channel_id=1, source_target_pairs={{0,3},{1,2},{2,1},{3,0},{4,7},{5,6},{6,5},{7,4},{8,11},{9,10},{10,... | collective-permute-start | bytes 1572872 | tf_op jit(solution)/shard_map/ppermute | solution.py:554
  205.8 26.8 %collective-permute-start.13 = (bf16[6,2,2,32,128]{4,3,2,1,0:T(8,128)(2,1)}, bf16[6,2,2,32,128]{4,3,2,1,0:T(8,128)(2,1)S(1)}, u32[]{:S(2)}, u32[]{:S(2)}) collective-permute-start(bf16[6,2,2,32,128]{4,3,2,1,0:T(8,128)(2,1)} %get-tuple-element.64), channel_id=1, source_target_pairs={{0,4},{4,0},{8,12},{12,8},{16,20},{20,16},{24,28},{28,24},{1,5},{5... | collective-permute-start | bytes 589832 | tf_op jit(solution)/shard_map/ppermute | solution.py:554
  207.3 26.1 %collective-permute-start.14 = (bf16[6,2,2,32,128]{4,3,2,1,0:T(8,128)(2,1)}, bf16[6,2,2,32,128]{4,3,2,1,0:T(8,128)(2,1)S(1)}, u32[]{:S(2)}, u32[]{:S(2)}) collective-permute-start(bf16[6,2,2,32,128]{4,3,2,1,0:T(8,128)(2,1)} %get-tuple-element.65), channel_id=1, source_target_pairs={{0,8},{4,12},{8,0},{12,4},{16,24},{20,28},{24,16},{28,20},{1,9},{5... | collective-permute-start | bytes 589832 | tf_op jit(solution)/shard_map/ppermute | solution.py:554
  209.7 25.8 %collective-permute-start.15 = (bf16[6,2,2,32,128]{4,3,2,1,0:T(8,128)(2,1)}, bf16[6,2,2,32,128]{4,3,2,1,0:T(8,128)(2,1)S(1)}, u32[]{:S(2)}, u32[]{:S(2)}) collective-permute-start(bf16[6,2,2,32,128]{4,3,2,1,0:T(8,128)(2,1)} %get-tuple-element.66), channel_id=1, source_target_pairs={{0,12},{4,8},{8,4},{12,0},{16,28},{20,24},{24,20},{28,16},{1,13},{... | collective-permute-start | bytes 589832 | tf_op jit(solution)/shard_map/ppermute | solution.py:554
  212.7 22.8 %collective-permute-start.16 = (bf16[6,2,2,32,128]{4,3,2,1,0:T(8,128)(2,1)}, bf16[6,2,2,32,128]{4,3,2,1,0:T(8,128)(2,1)S(1)}, u32[]{:S(2)}, u32[]{:S(2)}) collective-permute-start(bf16[6,2,2,32,128]{4,3,2,1,0:T(8,128)(2,1)} %get-tuple-element.67), channel_id=1, source_target_pairs={{0,16},{4,20},{8,24},{12,28},{16,0},{20,4},{24,8},{28,12},{1,17},{... | collective-permute-start | bytes 589832 | tf_op jit(solution)/shard_map/ppermute | solution.py:554
  219.3 25.1 %collective-permute-start.17 = (bf16[6,2,2,32,128]{4,3,2,1,0:T(8,128)(2,1)}, bf16[6,2,2,32,128]{4,3,2,1,0:T(8,128)(2,1)S(1)}, u32[]{:S(2)}, u32[]{:S(2)}) collective-permute-start(bf16[6,2,2,32,128]{4,3,2,1,0:T(8,128)(2,1)} %get-tuple-element.68), channel_id=1, source_target_pairs={{0,20},{4,16},{8,28},{12,24},{16,4},{20,0},{24,12},{28,8},{1,21},{... | collective-permute-start | bytes 589832 | tf_op jit(solution)/shard_map/ppermute | solution.py:554
  232.6 58.0 %copy-start.18 = (bf16[6,2,2,32,128]{4,3,2,1,0:T(8,128)(2,1)}, bf16[6,2,2,32,128]{4,3,2,1,0:T(8,128)(2,1)S(1)}, u32[]{:S(2)}) copy-start(bf16[6,2,2,32,128]{4,3,2,1,0:T(8,128)(2,1)S(1)} %collective-permute-done.13.refs_1_) | copy-start | bytes 589828
  232.6 19.3 %collective-permute-start.18 = (bf16[6,2,2,32,128]{4,3,2,1,0:T(8,128)(2,1)S(1)}, bf16[6,2,2,32,128]{4,3,2,1,0:T(8,128)(2,1)S(1)}, u32[]{:S(2)}, u32[]{:S(2)}) collective-permute-start(bf16[6,2,2,32,128]{4,3,2,1,0:T(8,128)(2,1)S(1)} %copy-done.39), channel_id=1, source_target_pairs={{0,24},{4,28},{8,16},{12,20},{16,8},{20,12},{24,0},{28,4},{1,25},{... | collective-permute-start | bytes 589832 | tf_op jit(solution)/shard_map/ppermute | solution.py:554
  233.4 57.2 %copy-start.19 = (bf16[6,2,2,32,128]{4,3,2,1,0:T(8,128)(2,1)}, bf16[6,2,2,32,128]{4,3,2,1,0:T(8,128)(2,1)S(1)}, u32[]{:S(2)}) copy-start(bf16[6,2,2,32,128]{4,3,2,1,0:T(8,128)(2,1)S(1)} %collective-permute-done.14.refs_2_) | copy-start | bytes 589828
  233.4 28.8 %collective-permute-start.19 = (bf16[6,2,2,32,128]{4,3,2,1,0:T(8,128)(2,1)S(1)}, bf16[6,2,2,32,128]{4,3,2,1,0:T(8,128)(2,1)S(1)}, u32[]{:S(2)}, u32[]{:S(2)}) collective-permute-start(bf16[6,2,2,32,128]{4,3,2,1,0:T(8,128)(2,1)S(1)} %copy-done.38), channel_id=1, source_target_pairs={{0,28},{4,24},{8,20},{12,16},{16,12},{20,8},{24,4},{28,0},{1,29},{... | collective-permute-start | bytes 589832 | tf_op jit(solution)/shard_map/ppermute | solution.py:554
  235.4 55.2 %copy-start.20 = (bf16[6,2,2,32,128]{4,3,2,1,0:T(8,128)(2,1)}, bf16[6,2,2,32,128]{4,3,2,1,0:T(8,128)(2,1)S(1)}, u32[]{:S(2)}) copy-start(bf16[6,2,2,32,128]{4,3,2,1,0:T(8,128)(2,1)S(1)} %collective-permute-done.15.refs_3_) | copy-start | bytes 589828
  235.4 26.8 %collective-permute-start.33 = (bf16[6,2,2,32,128]{4,3,2,1,0:T(8,128)(2,1)}, bf16[6,2,2,32,128]{4,3,2,1,0:T(8,128)(2,1)S(1)}, u32[]{:S(2)}, u32[]{:S(2)}) collective-permute-start(bf16[6,2,2,32,128]{4,3,2,1,0:T(8,128)(2,1)} %get-tuple-element.86), channel_id=1, source_target_pairs={{0,4},{4,0},{8,12},{12,8},{16,20},{20,16},{24,28},{28,24},{1,5},{5... | collective-permute-start | bytes 589832 | tf_op jit(solution)/shard_map/ppermute | solution.py:554
  235.4 55.2 %copy-start.21 = (bf16[6,2,2,32,128]{4,3,2,1,0:T(8,128)(2,1)}, bf16[6,2,2,32,128]{4,3,2,1,0:T(8,128)(2,1)S(1)}, u32[]{:S(2)}) copy-start(bf16[6,2,2,32,128]{4,3,2,1,0:T(8,128)(2,1)S(1)} %collective-permute-done.16.refs_4_) | copy-start | bytes 589828
  235.5 27.9 %collective-permute-start.34 = (bf16[6,2,2,32,128]{4,3,2,1,0:T(8,128)(2,1)}, bf16[6,2,2,32,128]{4,3,2,1,0:T(8,128)(2,1)S(1)}, u32[]{:S(2)}, u32[]{:S(2)}) collective-permute-start(bf16[6,2,2,32,128]{4,3,2,1,0:T(8,128)(2,1)} %get-tuple-element.87), channel_id=1, source_target_pairs={{0,8},{4,12},{8,0},{12,4},{16,24},{20,28},{24,16},{28,20},{1,9},{5... | collective-permute-start | bytes 589832 | tf_op jit(solution)/shard_map/ppermute | solution.py:554
  244.4 46.2 %copy-start.22 = (bf16[6,2,2,32,128]{4,3,2,1,0:T(8,128)(2,1)}, bf16[6,2,2,32,128]{4,3,2,1,0:T(8,128)(2,1)S(1)}, u32[]{:S(2)}) copy-start(bf16[6,2,2,32,128]{4,3,2,1,0:T(8,128)(2,1)S(1)} %collective-permute-done.17.refs_5_) | copy-start | bytes 589828
  244.4 19.6 %collective-permute-start.35 = (bf16[6,2,2,32,128]{4,3,2,1,0:T(8,128)(2,1)}, bf16[6,2,2,32,128]{4,3,2,1,0:T(8,128)(2,1)S(1)}, u32[]{:S(2)}, u32[]{:S(2)}) collective-permute-start(bf16[6,2,2,32,128]{4,3,2,1,0:T(8,128)(2,1)} %get-tuple-element.88), channel_id=1, source_target_pairs={{0,12},{4,8},{8,4},{12,0},{16,28},{20,24},{24,20},{28,16},{1,13},{... | collective-permute-start | bytes 589832 | tf_op jit(solution)/shard_map/ppermute | solution.py:554
  251.9 12.1 %collective-permute-start.36 = (bf16[6,2,2,32,128]{4,3,2,1,0:T(8,128)(2,1)}, bf16[6,2,2,32,128]{4,3,2,1,0:T(8,128)(2,1)S(1)}, u32[]{:S(2)}, u32[]{:S(2)}) collective-permute-start(bf16[6,2,2,32,128]{4,3,2,1,0:T(8,128)(2,1)} %get-tuple-element.89), channel_id=1, source_target_pairs={{0,16},{4,20},{8,24},{12,28},{16,0},{20,4},{24,8},{28,12},{1,17},{... | collective-permute-start | bytes 589832 | tf_op jit(solution)/shard_map/ppermute | solution.py:554
  262.3 17.7 %collective-permute-start.37 = (bf16[6,2,2,32,128]{4,3,2,1,0:T(8,128)(2,1)}, bf16[6,2,2,32,128]{4,3,2,1,0:T(8,128)(2,1)S(1)}, u32[]{:S(2)}, u32[]{:S(2)}) collective-permute-start(bf16[6,2,2,32,128]{4,3,2,1,0:T(8,128)(2,1)} %get-tuple-element.90), channel_id=1, source_target_pairs={{0,20},{4,16},{8,28},{12,24},{16,4},{20,0},{24,12},{28,8},{1,21},{... | collective-permute-start | bytes 589832 | tf_op jit(solution)/shard_map/ppermute | solution.py:554
  262.3 23.6 %collective-permute-start.38 = (bf16[6,2,2,32,128]{4,3,2,1,0:T(8,128)(2,1)}, bf16[6,2,2,32,128]{4,3,2,1,0:T(8,128)(2,1)S(1)}, u32[]{:S(2)}, u32[]{:S(2)}) collective-permute-start(bf16[6,2,2,32,128]{4,3,2,1,0:T(8,128)(2,1)} %get-tuple-element.91), channel_id=1, source_target_pairs={{0,24},{4,28},{8,16},{12,20},{16,8},{20,12},{24,0},{28,4},{1,25},{... | collective-permute-start | bytes 589832 | tf_op jit(solution)/shard_map/ppermute | solution.py:554
  263.4 27.3 %collective-permute-start.39 = (bf16[6,2,2,32,128]{4,3,2,1,0:T(8,128)(2,1)}, bf16[6,2,2,32,128]{4,3,2,1,0:T(8,128)(2,1)S(1)}, u32[]{:S(2)}, u32[]{:S(2)}) collective-permute-start(bf16[6,2,2,32,128]{4,3,2,1,0:T(8,128)(2,1)} %get-tuple-element.92), channel_id=1, source_target_pairs={{0,28},{4,24},{8,20},{12,16},{16,12},{20,8},{24,4},{28,0},{1,29},{... | collective-permute-start | bytes 589832 | tf_op jit(solution)/shard_map/ppermute | solution.py:554
  (32 other events, 615.3 us)

commit v3 on v2

--- a/solution.py
+++ b/solution.py
@@ -10,6 +10,7 @@
 from jax.sharding import PartitionSpec as P
 
 CHUNKS = 2
+MID_COST = 40
 VMEM_LIMIT = 56 * 1024 * 1024
 
 
@@ -211,17 +212,24 @@
     return jnp.asarray(first, jnp.bfloat16), jnp.asarray(second, jnp.bfloat16)
 
 
-def z_kernel(weight_ref, table_ref, field_ref, *out_refs):
+def z_kernel(levels_ref, coefficient_ref, failed_ref, table_ref, field_ref, *out_refs):
     halves, rows, mid_len, z_len = field_ref.shape
     tiles, _, columns, lanes = out_refs[0].shape
     last = pl.num_programs(0) - 1
+    me = lax.axis_index("grid")
+    chip, core = me // 2, me % 2
+    odd = chip % 2
+    units = []
+    for aim in (3 - 3 * odd, 1 + odd, (chip + 2) % 4, chip):
+        units += [2 * aim + core, 2 * aim + 1 - core]
 
     @pl.when(pl.program_id(0) < last)
     def _():
         lines = [field_ref[half].reshape(rows * mid_len, z_len) for half in range(halves)]
         joined = jnp.concatenate(lines, axis=1)
+        table = [table_ref[chunk, unit] for chunk in range(halves) for unit in units]
         found = lax.dot_general(
-            table_ref[...], joined, (((1,), (1,)), ((), ())), preferred_element_type=jnp.float32
+            jnp.concatenate(table, axis=0), joined, (((1,), (1,)), ((), ())), preferred_element_type=jnp.float32
         ).astype(jnp.bfloat16)
         for unit, out_ref in enumerate(out_refs):
             for tile in range(tiles):
@@ -231,26 +239,33 @@
 
     @pl.when(pl.program_id(0) == last)
     def _():
-        for out_ref in out_refs:
-            for tile in range(tiles):
-                out_ref[tile, 0] = jnp.full((columns, lanes), weight_ref[tile], jnp.float32).astype(jnp.bfloat16)
-
-
-def transform_z(samples, table, weight, chunks, units):
+        weight = (coefficient_ref[0] * (1 - failed_ref[0])).astype(jnp.float32)
+        swapped = levels_ref[0, 0] < levels_ref[0, 1]
+        for tile in range(tiles):
+            value = jnp.where(swapped == (tile == 1), weight, 0.0)
+            value = jnp.full((columns, lanes), value, jnp.float32).astype(jnp.bfloat16)
+            for out_ref in out_refs:
+                out_ref[tile, 0] = value
+
+
+def transform_z(samples, levels, coefficients, failed, table):
     local_long, mid_len, z_len = samples.shape
-    columns = table.shape[0] // units
+    chunks, units, columns, _ = table.shape
     rows = 8
     lines = local_long // chunks
     steps = lines // rows
-    tiles = weight.shape[0]
+    tiles = 2
     lanes = mid_len // tiles
+    units *= chunks
     split = samples.reshape(chunks, lines, mid_len, z_len)
     return pl.pallas_call(
         z_kernel,
         grid=(steps + 1,),
         in_specs=[
             pl.BlockSpec(memory_space=pltpu.SMEM),
-            pl.BlockSpec(table.shape, lambda i: (0, 0)),
+            pl.BlockSpec(memory_space=pltpu.SMEM),
+            pl.BlockSpec(memory_space=pltpu.SMEM),
+            pl.BlockSpec(table.shape, lambda i: (0, 0, 0, 0)),
             pl.BlockSpec((chunks, rows, mid_len, z_len), lambda i: (0, jnp.minimum(i, steps - 1), 0, 0)),
         ],
         out_specs=[pl.BlockSpec((tiles, rows, columns, lanes), lambda i: (0, i, 0, 0))] * units,
@@ -260,7 +275,12 @@
             flops=2 * units * columns * samples.size, bytes_accessed=4 * samples.size, transcendentals=0
         ),
         name="transform_z",
-    )(weight, table, split)
+    )(levels, coefficients, failed, table, split)
+
+
+def is_outer():
+    me = lax.axis_index("grid")
+    return (me < 2) | (me >= 6)
 
 
 def unit_specs(shape, rows):
@@ -279,13 +299,13 @@
     return total
 
 
-def relay_kernel(place_ref, *refs):
+def relay_kernel(*refs):
     out_refs = refs[-2:]
     passing = [refs[-4], refs[-3]]
     sources, weights = refs[:-4:2], refs[1:-4:2]
     rows = out_refs[0].shape[1]
     last = pl.num_programs(0) - 1
-    outer = place_ref[2] != 0
+    outer = is_outer()
 
     @pl.when(outer)
     def _():
@@ -306,14 +326,14 @@
                 out_ref[tile, rows - 1] = jnp.full(out_ref.shape[2:], float(tile == kind), jnp.bfloat16)
 
 
-def relay(sources, passing, place):
+def relay(sources, passing):
     shape = sources[0].shape
     rows = 13 if shape[1] % 13 == 0 else 1
     specs = unit_specs(shape, rows)
     return pl.pallas_call(
         relay_kernel,
         grid=(shape[1] // rows,),
-        in_specs=[pl.BlockSpec(memory_space=pltpu.SMEM)] + specs * len(sources) + specs[:1] * 2,
+        in_specs=specs * len(sources) + specs[:1] * 2,
         out_specs=specs[:1] * 2,
         out_shape=[jax.ShapeDtypeStruct(shape, jnp.bfloat16)] * 2,
         compiler_params=pltpu.CompilerParams(vmem_limit_bytes=VMEM_LIMIT),
@@ -321,19 +341,21 @@
             flops=0, bytes_accessed=2 * (len(sources) + 4) * math.prod(shape), transcendentals=0
         ),
         name="relay",
-    )(place, *[ref for source in sources for ref in (source, source)], *passing)
-
-
-def mid_kernel(first_chunk, place_ref, table_ref, *refs):
-    pencils = 4
-    refs, out_refs, gathered = refs[: -pencils - 1], refs[-pencils - 1 : -1], refs[-1]
+    )(*[ref for source in sources for ref in (source, source)], *passing)
+
+
+def mid_kernel(first_chunk, apart, table_ref, *refs):
+    out_refs = []
+    if apart:
+        refs, out_refs = refs[: -apart - 1] + refs[-1:], refs[-apart - 1 : -1]
+    refs, out_ref = refs[:-1], refs[-1]
     tiles, rows, columns, lanes = refs[0].shape
     mid_len = tiles * lanes
     half = columns // 2
-    classes, slots, _, halves = out_refs[0].shape[:4]
+    pencils, classes, slots, _, halves = out_ref.shape[:5]
     groups = pencils // 2
-    lead = place_ref[0] == 0
-    outer = place_ref[2] != 0
+    lead = lax.axis_index("grid") == 0
+    outer = is_outer()
     row_ids = lax.broadcasted_iota(jnp.int32, (rows, half, mid_len), 1)
     special = lead & (row_ids % (groups * slots) == 0)
     sources = [ref[...] for ref in refs[0::2]]
@@ -363,58 +385,70 @@
                 for group in range(groups):
                     for slot in range(slots):
                         at = (piece * groups + group) * slots + slot
-                        gathered[group, kind, slot, part, piece] = up[at].astype(jnp.bfloat16)
+                        out_ref[group, kind, slot, part, piece] = up[at].astype(jnp.bfloat16)
                         value = down[at]
                         if first_chunk and slot == 0:
                             other = (piece * groups + (group + 1) % groups) * slots
                             value = jnp.where(lead, down[other], value)
-                        gathered[pencils - 1 - group, kind, slot, part, piece] = value.astype(jnp.bfloat16)
-    for step, out_ref in enumerate(out_refs):
-        out_ref[...] = gathered[place_ref[1] ^ step]
-
-
-def transform_mid(sources, place, table, first_chunk, chunks, pencils, slots):
+                        out_ref[pencils - 1 - group, kind, slot, part, piece] = value.astype(jnp.bfloat16)
+    for step, apart_ref in enumerate(out_refs):
+        apart_ref[...] = out_ref[lax.axis_index("pencil") ^ step]
+
+
+def transform_mid(sources, table, first_chunk, apart, chunks, pencils, slots):
     tiles, lines, columns, lanes = sources[0].shape
     lines -= 1
     classes, mid_len, _ = table.shape
     rows = 16
-    shape = (classes, slots, 2, chunks, lines, mid_len)
-    block = shape[:4] + (rows, mid_len)
+    shape = (pencils, classes, slots, 2, chunks, lines, mid_len)
+    block = shape[:5] + (rows, mid_len)
+    if apart:
+        layout = dict(
+            out_specs=[pl.BlockSpec(block[1:], lambda i: (0, 0, 0, 0, i, 0))] * pencils,
+            out_shape=[jax.ShapeDtypeStruct(shape[1:], jnp.bfloat16)] * pencils,
+            scratch_shapes=[pltpu.VMEM(block, jnp.bfloat16)],
+        )
+    else:
+        layout = dict(
+            out_specs=pl.BlockSpec(block, lambda i: (0, 0, 0, 0, 0, i, 0)),
+            out_shape=jax.ShapeDtypeStruct(shape, jnp.bfloat16),
+        )
     size = sources[0].size
     return pl.pallas_call(
-        functools.partial(mid_kernel, first_chunk),
+        functools.partial(mid_kernel, first_chunk, pencils if apart else 0),
         grid=(lines // rows,),
-        in_specs=[pl.BlockSpec(memory_space=pltpu.SMEM), pl.BlockSpec(table.shape, lambda i: (0, 0, 0))]
+        in_specs=[pl.BlockSpec(table.shape, lambda i: (0, 0, 0))]
         + unit_specs(sources[0].shape, rows) * len(sources),
-        out_specs=[pl.BlockSpec(block, lambda i: (0, 0, 0, 0, i, 0))] * pencils,
-        out_shape=[jax.ShapeDtypeStruct(shape, jnp.bfloat16)] * pencils,
-        scratch_shapes=[pltpu.VMEM((pencils,) + block, jnp.bfloat16)],
         compiler_params=pltpu.CompilerParams(vmem_limit_bytes=VMEM_LIMIT),
         cost_estimate=pl.CostEstimate(
-            flops=8 * size * mid_len,
-            bytes_accessed=2 * len(sources) * size + 2 * pencils * math.prod(shape),
+            flops=MID_COST * 8 * size * mid_len,
+            bytes_accessed=2 * len(sources) * size + 2 * math.prod(shape),
             transcendentals=0,
         ),
         name="transform_mid",
-    )(place, table, *[ref for source in sources for ref in (source, source)])
-
-
-def long_kernel(pencils, rows_ref, place_ref, z_ref, first_ref, second_ref, plane_ref, *refs):
-    sources, out_refs, gathered, laid = refs[:pencils], refs[pencils:-2], refs[-2], refs[-1]
-    classes, _, _, local_long, mid_len = sources[0].shape
+        **layout,
+    )(table, *[ref for source in sources for ref in (source, source)])
+
+
+def long_kernel(rows_ref, z_ref, first_ref, second_ref, plane_ref, *refs):
+    if len(refs) == 2:
+        source_ref, out_ref = refs
+    else:
+        sources, out_ref, source_ref = refs[:-2], refs[-2], refs[-1]
+        for step, source in enumerate(sources):
+            source_ref[lax.axis_index("pencil") ^ step] = source[...]
+    pencils, classes, _, _, local_long, mid_len = source_ref.shape
     depth = 2 * pencils * local_long
     long_len = pencils * local_long
-    owned, _, _, pairs, _ = out_refs[0].shape
+    pairs = out_ref.shape[3]
     per_long = long_len // (2 * pairs)
     per_mid = mid_len // (2 * pairs)
     edge = per_mid // 2
     slot = pl.program_id(0)
-    for number, source in enumerate(sources):
-        for kind in range(classes):
-            gathered[kind, place_ref[1] ^ number] = source[kind, 0]
-    first = jnp.dot(first_ref[...], gathered[0].reshape(depth, mid_len), preferred_element_type=jnp.float32)
+    lines = [source_ref[:, kind, 0].reshape(depth, mid_len) for kind in range(classes)]
+    first = jnp.dot(first_ref[...], lines[0], preferred_element_type=jnp.float32)
     second = lax.dot_general(
-        gathered[1].reshape(depth, mid_len),
+        lines[1],
         second_ref[...],
         (((0,), (0,)), ((), ())),
         preferred_element_type=jnp.float32,
@@ -460,104 +494,91 @@
                 block = across * per_long + 2 * couple
                 left = jnp.where(low, even, pltpu.roll(odd, 2 * pairs, 1))
                 right = jnp.where(low, pltpu.roll(even, 2 * pairs, 1), odd)
-                laid[rows_ref[block], part] = left.astype(jnp.bfloat16)
-                laid[rows_ref[block + 1], part] = right.astype(jnp.bfloat16)
-    for step, out_ref in enumerate(out_refs):
-        top = (place_ref[0] ^ step) * owned
-        for row in range(owned):
-            out_ref[row, 0] = laid[top + row]
-
-
-def transform_long(sources, row_ids, place, z_factor, first, second, plane, row_count, grid_count, pairs):
-    classes, slots, _, local_long, mid_len = sources[0].shape
-    pencils = len(sources)
+                out_ref[rows_ref[block], 0, part] = left.astype(jnp.bfloat16)
+                out_ref[rows_ref[block + 1], 0, part] = right.astype(jnp.bfloat16)
+
+
+def transform_long(sources, row_ids, z_factor, first, second, plane, row_count, pairs):
+    if len(sources) == 1:
+        pencils, classes, slots, _, local_long, mid_len = sources[0].shape
+    else:
+        pencils = len(sources)
+        classes, slots, _, local_long, mid_len = sources[0].shape
+    block = (pencils, classes, 1, 2, local_long, mid_len)
+    if len(sources) == 1:
+        specs = [pl.BlockSpec(block, lambda i: (0, 0, i, 0, 0, 0))]
+        scratch = []
+    else:
+        specs = [pl.BlockSpec(block[1:], lambda i: (0, i, 0, 0, 0))] * pencils
+        scratch = [pltpu.VMEM(block, jnp.bfloat16)]
     depth = 2 * pencils * local_long
-    owned = row_count // grid_count
-    shape = (owned, slots, 2, pairs, 4 * pairs)
+    shape = (row_count, slots, 2, pairs, 4 * pairs)
     return pl.pallas_call(
-        functools.partial(long_kernel, pencils),
+        long_kernel,
         grid=(slots,),
         in_specs=[
-            pl.BlockSpec(memory_space=pltpu.SMEM),
             pl.BlockSpec(memory_space=pltpu.SMEM),
             pl.BlockSpec(memory_space=pltpu.SMEM),
             pl.BlockSpec(first.shape, lambda i: (0, 0)),
             pl.BlockSpec(second.shape, lambda i: (0, 0)),
             pl.BlockSpec(plane.shape, lambda i: (0, 0, 0, 0)),
         ]
-        + [pl.BlockSpec((classes, 1, 2, local_long, mid_len), lambda i: (0, i, 0, 0, 0))] * pencils,
-        out_specs=[pl.BlockSpec((owned, 1, 2, pairs, 4 * pairs), lambda i: (0, i, 0, 0, 0))] * grid_count,
-        out_shape=[jax.ShapeDtypeStruct(shape, jnp.bfloat16)] * grid_count,
-        scratch_shapes=[
-            pltpu.VMEM((classes, pencils, 2, local_long, mid_len), jnp.bfloat16),
-            pltpu.VMEM((row_count, 2, pairs, 4 * pairs), jnp.bfloat16),
-        ],
+        + specs,
+        scratch_shapes=scratch,
+        out_specs=pl.BlockSpec((row_count, 1, 2, pairs, 4 * pairs), lambda i: (0, i, 0, 0, 0)),
+        out_shape=jax.ShapeDtypeStruct(shape, jnp.bfloat16),
         compiler_params=pltpu.CompilerParams(vmem_limit_bytes=VMEM_LIMIT),
         cost_estimate=pl.CostEstimate(
             flops=2 * classes * slots * depth * depth * mid_len,
-            bytes_accessed=2 * pencils * sources[0].size + 2 * grid_count * math.prod(shape) + 4 * depth * depth,
+            bytes_accessed=4 * slots * math.prod(block) + 2 * math.prod(shape) + 4 * depth * depth,
             transcendentals=0,
         ),
         name="transform_long",
-    )(row_ids, place, z_factor, first, second, plane, *sources)
-
-
-def rows_kernel(grid_count, place_ref, *refs):
-    sources, out_ref, gathered = refs[:-2], refs[-2], refs[-1]
-    chunks = len(sources) // grid_count
-    slots, _, pairs, span = sources[0].shape[1:]
+    )(row_ids, z_factor, first, second, plane, *sources)
+
+
+def rows_kernel(*refs):
+    sources, out_ref = refs[:-1], refs[-1]
+    back = lax.axis_index("pencil") >= 2
+    _, _, slots, _, pairs, span = sources[0].shape
     z_local = out_ref.shape[2]
-    for chunk in range(chunks):
-        for number in range(grid_count):
-            for slot in range(slots):
-                spot = (place_ref[0] ^ number) * (chunks * slots) + chunk * slots + slot
-                gathered[spot] = sources[chunk * grid_count + number][0, slot, 0]
 
     def write(order):
         for top in range(0, z_local, 8):
-            taken = jnp.stack([gathered[order(top + k)].astype(jnp.float32) for k in range(8)])
-            turned = jnp.transpose(taken, (1, 0, 2))
+            taken = []
+            for z in range(top, top + 8):
+                chunk, slot = divmod(order(z) % (len(sources) * slots), slots)
+                device = order(z) // (len(sources) * slots)
+                taken.append(sources[chunk][device, 0, slot, 0].astype(jnp.float32))
+            turned = jnp.transpose(jnp.stack(taken), (1, 0, 2))
             for pair in range(pairs):
                 out_ref[0, 0, top : top + 8, pair * span : (pair + 1) * span] = turned[pair]
 
-    @pl.when(place_ref[1] == 0)
+    @pl.when(jnp.logical_not(back))
     def _():
         write(lambda z: z)
 
-    @pl.when(place_ref[1] != 0)
+    @pl.when(back)
     def _():
         write(lambda z: (z_local - z) % z_local)
 
 
-def lay_rows(sources, place, grid_count, z_local):
-    rows, slots, _, pairs, span = sources[0].shape
+def lay_rows(sources, z_local):
+    grid_count, rows, slots, _, pairs, span = sources[0].shape
     return pl.pallas_call(
-        functools.partial(rows_kernel, grid_count),
+        rows_kernel,
         grid=(rows, 2),
-        in_specs=[pl.BlockSpec(memory_space=pltpu.SMEM)]
-        + [pl.BlockSpec((1, slots, 1, pairs, span), lambda i, j: (i, 0, j, 0, 0))] * len(sources),
+        in_specs=[pl.BlockSpec((grid_count, 1, slots, 1, pairs, span), lambda i, j: (0, i, 0, j, 0, 0))] * len(sources),
         out_specs=pl.BlockSpec((1, 1, z_local, pairs * span), lambda i, j: (i, j, 0, 0)),
         out_shape=jax.ShapeDtypeStruct((rows, 2, z_local, pairs * span), jnp.float32),
-        scratch_shapes=[pltpu.VMEM((z_local, pairs, span), jnp.bfloat16)],
         compiler_params=pltpu.CompilerParams(vmem_limit_bytes=VMEM_LIMIT),
         cost_estimate=pl.CostEstimate(
             flops=0, bytes_accessed=6 * len(sources) * sources[0].size, transcendentals=0
         ),
         name="lay_rows",
-    )(place, *sources)
-
-
-def exchange(parts, axis):
-    count = len(parts)
-    got = {0: parts[0]}
-    for step in reversed(range(1, count)):
-        got[step] = lax.ppermute(parts[step], axis, [(d, d ^ step) for d in range(count)])
-    return [got[step] for step in range(count)]
-
-
-FAR = (3, 0, 3, 0)
-NEXT = (1, 2, 1, 2)
-THIRD = (2, 3, 0, 1)
+    )(*sources)
+
+
 PAIR_SAME = [(d, d ^ 2) for d in range(8)]
 PAIR_CROSS = [(d, d ^ 3) for d in range(8)]
 INNER_SAME = [(2, 4), (4, 2), (3, 5), (5, 3)]
@@ -570,39 +591,47 @@
 JUMP_MIXED = [(0, 5), (1, 4), (6, 3), (7, 2), (2, 6), (3, 7), (4, 0), (5, 1)]
 
 
-def unit_order(me):
-    chips = jnp.stack(
-        [jnp.array(chip, jnp.int32)[me // 2] for chip in (FAR, NEXT, THIRD, (0, 1, 2, 3))]
-    )
-    core = me % 2
-    return jnp.stack([2 * chips + core, 2 * chips + 1 - core], axis=1).reshape(-1)
-
-
-def gather_grids(units, place):
-    far_same, far_cross, next_same, next_cross, third_same, third_cross, own, other = units
-    pair_same = lax.ppermute(far_same, "grid", PAIR_SAME)
-    pair_cross = lax.ppermute(far_cross, "grid", PAIR_CROSS)
-    inner_core = lax.ppermute(third_cross, "grid", INNER_CORES)
-    inner_same = lax.ppermute(next_same, "grid", INNER_SAME)
-    inner_cross = lax.ppermute(next_cross, "grid", INNER_CROSS)
-    core = lax.ppermute(other, "grid", CORES)
-    sums = relay([third_same, inner_core, pair_same, pair_cross], [third_same, third_cross], place)
-    enter_same = lax.ppermute(next_same, "grid", ENTER_SAME)
-    enter_cross = lax.ppermute(next_cross, "grid", ENTER_CROSS)
-    jump_same = lax.ppermute(sums[0], "grid", JUMP_SAME)
-    jump_mixed = lax.ppermute(sums[1], "grid", JUMP_MIXED)
-    return [
-        own,
-        core,
-        enter_same,
-        enter_cross,
-        jump_same,
-        jump_mixed,
-        inner_same,
-        inner_cross,
-        pair_same,
-        pair_cross,
+def after(values, earlier):
+    return lax.optimization_barrier((list(values), list(earlier)))[0]
+
+
+def send(value, pairs):
+    return lax.ppermute(value, "grid", pairs)
+
+
+def exchange(parts, axis):
+    count = len(parts)
+    got = {0: parts[0]}
+    for step in reversed(range(1, count)):
+        got[step] = lax.ppermute(parts[step], axis, [(d, d ^ step) for d in range(count)])
+    return [got[step] for step in range(count)]
+
+
+def gather_grids(chunks):
+    early = []
+    for units in chunks:
+        first = [units[0], units[1], units[5], units[2], units[3]]
+        if early:
+            first = [after([value], [twin])[0] for value, twin in zip(first, early[-1])]
+        plans = (PAIR_SAME, PAIR_CROSS, INNER_CORES, INNER_SAME, INNER_CROSS)
+        early.append([send(value, pairs) for value, pairs in zip(first, plans)])
+    sums = []
+    for units, got in zip(chunks, early):
+        third = after(units[4:6], got[3:] if sums else [])
+        sums.append(relay([third[0], got[2], got[0], got[1]], third))
+    late = []
+    for units, passed in zip(chunks, sums):
+        second = [passed[0], passed[1], units[2], units[3]]
+        twins = late[-1] if late else [None, None] + early[-1][:2]
+        second = [value if twin is None else after([value], [twin])[0] for value, twin in zip(second, twins)]
+        plans = (JUMP_SAME, JUMP_MIXED, ENTER_SAME, ENTER_CROSS)
+        late.append([send(value, pairs) for value, pairs in zip(second, plans)])
+    cores = [send(units[7], CORES) for units in chunks]
+    found = [
+        [units[6], core] + second + first[3:5] + first[0:2]
+        for units, core, second, first in zip(chunks, cores, late, early)
     ]
+    return found, sums, late
 
 
 def mode_factor(modes, diffusion, speed, long_len, mid_len):
@@ -627,9 +656,6 @@
     me = lax.axis_index("grid")
     pencil = lax.axis_index("pencil")
 
-    weight = (coefficients[0] * (1 - failed[0])).astype(jnp.float32)
-    swapped = levels[0, 0] < levels[0, 1]
-    mine = jnp.stack([jnp.where(swapped, 0.0, weight), jnp.where(swapped, weight, 0.0)])
     positions = jnp.arange(long_len, dtype=jnp.int32)
     modes = signed_modes(positions, long_len)
     x_re, x_im = mode_factor(modes, diffusivity[0], velocity[0], long_len, mid_len)
@@ -646,36 +672,44 @@
     )
     z_factor = jnp.stack([z_re, z_im]) * (1.0 / math.sqrt(long_len * mid_len * z_len))
 
-    outer = (me < 2) | (me >= grid_count - 2)
-    place = jnp.stack([me, pencil, outer.astype(jnp.int32)]).astype(jnp.int32)
-    side = jnp.stack([me, back.astype(jnp.int32)]).astype(jnp.int32)
     mid = mid_table(mid_len, block_len)
     first, second = long_tables(long_len, block_len, pencils)
-    order = unit_order(me)
-
+    tables = [z_table(chunk, CHUNKS, grid_count, pencils, z_len) for chunk in range(CHUNKS)]
+    tables = jnp.stack([v.reshape(grid_count, -1, v.shape[1]) for v in tables])
+    units = transform_z(samples, levels, coefficients, failed, tables)
+    units = [list(units[chunk * grid_count : (chunk + 1) * grid_count]) for chunk in range(CHUNKS)]
+
+    units[0][4], plane, z_factor = lax.optimization_barrier((units[0][4], plane, z_factor))
+    found, sums, late = gather_grids(units)
     arrived = []
-    for chunk in range(CHUNKS):
-        table = z_table(chunk, CHUNKS, grid_count, pencils, z_len)
-        table = table.reshape(grid_count, -1, table.shape[1])[order].reshape(table.shape)
-        units = transform_z(samples, table, mine, CHUNKS, grid_count)
-        sources = gather_grids(units, place)
-        along_mid = transform_mid(sources, place, mid, chunk == 0, CHUNKS, pencils, slots)
-        along_mid = [v.reshape(v.shape[:3] + (local_long, mid_len)) for v in along_mid]
-        lines = exchange(along_mid, "pencil")
+    rows = None
+    for chunk, sources in enumerate(found):
+        if chunk + 1 < CHUNKS:
+            sources = after(sources, sums[chunk + 1])
+        if rows is not None:
+            sources = after(sources, [rows])
+        apart = chunk == CHUNKS - 1
+        along_mid = transform_mid(sources, mid, chunk == 0, apart, CHUNKS, pencils, slots)
+        if apart:
+            along_mid = [v.reshape(v.shape[:3] + (local_long, mid_len)) for v in along_mid]
+            lines = exchange(along_mid, "pencil")
+        else:
+            along_mid = along_mid.reshape(along_mid.shape[:4] + (local_long, mid_len))
+            lines = [lax.all_to_all(along_mid, "pencil", split_axis=0, concat_axis=0, tiled=True)]
         rows = transform_long(
             lines,
             owner_map,
-            place,
             z_factor[:, chunk * slots : (chunk + 1) * slots],
             first,
             second,
             plane,
             row_count,
-            grid_count,
             block_len // 2,
         )
-        arrived += exchange(rows, "grid")
-    return lay_rows(arrived, side, grid_count, z_local)
+        rows = rows.reshape((grid_count, -1) + rows.shape[1:])
+        sent = after([rows], late[-1])[0]
+        arrived.append(lax.all_to_all(sent, "grid", split_axis=0, concat_axis=0, tiled=True))
+    return lay_rows(arrived, z_local)
 
 
 def solution(mesh):

time: 302 us -> 277 us (0.917)
  the two profiles are of different devices: /device:TPU:21 before, /device:TPU:0 now
where the time goes in v3:
time: 277 us; the launch traced here: 276 us
  waiting for transfers between devices  97.6 us (35%)
  starting transfers between devices  66.6 us (24%)
  Pallas kernels  55.9 us (20%)
  blocking collectives  42.7 us (15%)
  other arithmetic  5.64 us (2%)
  local copies, waits for them, and re-layouts  5.4 us (2%)
    ppermute x20, waiting for transfers between devices, send(): return lax.ppermute(value, 'grid', pairs)  57.5 us
    ppermute x20, starting transfers between devices, send(): return lax.ppermute(value, 'grid', pairs)  55.6 us
    all_to_all x1, blocking collectives, body(): lax.all_to_all(sent, 'grid', split_axis=0, concat_axis=0, tiled=True)  42.7 us
    ppermute x3, waiting for transfers between devices, exchange(): lax.ppermute(parts[step], axis, [(d, d ^ step) for d in range(count)])  23.7 us
    all_to_all x1, waiting for transfers between devices, body(): lax.all_to_all(along_mid, 'pencil', split_axis=0, concat_axis=0, tiled=True)  16.4 us
    pallas_call x2, Pallas kernels, transform_long(): pl.pallas_call(long_kernel, grid=(slots,), in_specs=[pl.BlockSpec(memory_...  14.7 us
    pallas_call x2, Pallas kernels, transform_mid(): pl.pallas_call(functools.partial(mid_kernel, first_chunk, pencils if apar...  13 us
    pallas_call x1, Pallas kernels, transform_z(): pl.pallas_call(z_kernel, grid=(steps + 1,), in_specs=[pl.BlockSpec(memory...  10.3 us
  transfers between devices with their start and end apart: 25, of which 11 were waited for; matrix products, arithmetic and copies ran while one was open for 3% of the time, Pallas kernels for 11%

profile of v3, /device:TPU:0, one launch (start us, length us, event | category | flops | bytes accessed | tf_op | source)
XLA Modules:
  0.0 275.6 jit_solution(8659523801526010608)
XLA Ops:
  1.3 10.3 %transform_z.1 = (bf16[2,65,16,128]{3,2,1,0:T(8,128)(2,1)}, bf16[2,65,16,128]{3,2,1,0:T(8,128)(2,1)}, bf16[2,65,16,128]{3,2,1,0:T(8,128)(2,1)}, bf16[2,65,16,128...) custom-call(s32[1,3]{1,0:T(1,128)} %levels_ref.1, ...), custom_call_target="tpu_custom_call" | custom-call | flops 2147483648 | bytes 16777216 | tf_op jit(solution)/shard_map/transform_z/pallas_call | solution.py:261
  11.6 3.1 %collective-permute-start.2 = (bf16[2,65,16,128]{3,2,1,0:T(8,128)(2,1)}, bf16[2,65,16,128]{3,2,1,0:T(8,128)(2,1)S(1)}, u32[]{:S(2)}, u32[]{:S(2)}) collective-permute-start(bf16[2,65,16,128]{3,2,1,0:T(8,128)(2,1)} %get-tuple-element.77), channel_id=1, source_target_pairs={{0,8},{4,12},{8,0},{12,4},{16,24},{20,28},{24,16},{28,20},{1,9},{5... | collective-permute-start | bytes 1597448 | tf_op jit(solution)/shard_map/ppermute | solution.py:599
  14.7 0.7 collective-permute-start.1
  15.4 0.7 collective-permute-start.10
  16.1 0.7 collective-permute-start.11
  16.8 0.6 fusion.12
  18.0 1.3 sine_multiply_fusion.2
  19.3 1.4 sine_multiply_fusion.1
  20.7 1.2 sine_multiply_fusion
  21.9 6.0 %collective-permute-done.2.refs_4_.refs_5_.refs_16_.refs_17_ = bf16[2,65,16,128]{3,2,1,0:T(8,128)(2,1)S(1)} collective-permute-done((bf16[2,65,16,128]{3,2,1,0:T(8,128)(2,1)}, bf16[2,65,16,128]{3,2,1,0:T(8,128)(2,1)S(1)}, u32[]{:S(2)}, u32[]{:S(2)}) %collective-permute-start.2) | collective-permute-done | bytes 532512 | tf_op jit(solution)/shard_map/ppermute | solution.py:599
  27.8 2.1 collective-permute-start.6
  29.9 9.0 %collective-permute-done.3.refs_6_.refs_7_.refs_18_.refs_19_ = bf16[2,65,16,128]{3,2,1,0:T(8,128)(2,1)S(1)} collective-permute-done((bf16[2,65,16,128]{3,2,1,0:T(8,128)(2,1)}, bf16[2,65,16,128]{3,2,1,0:T(8,128)(2,1)S(1)}, u32[]{:S(2)}, u32[]{:S(2)}) %collective-permute-start.3) | collective-permute-done | bytes 532512 | tf_op jit(solution)/shard_map/ppermute | solution.py:599
  38.9 2.1 collective-permute-start.8
  41.0 0.7 collective-permute-start.14
  41.7 0.7 collective-permute-start.12
  42.4 0.7 collective-permute-start.13
  43.5 1.5 pad_maximum_fusion.plane_ref
  45.0 4.5 %relay.2 = (bf16[2,65,16,128]{3,2,1,0:T(8,128)(2,1)}, bf16[2,65,16,128]{3,2,1,0:T(8,128)(2,1)}) custom-call(bf16[2,65,16,128]{3,2,1,0:T(8,128)(2,1)} %get-tuple-element.76.refs_0_.refs_1_.refs_8_, bf16[2,65,16,128]{3,2,1,0:T(8,128)(2,1)} %get-tuple-element.76.refs_0_.refs_1_.refs_8_, bf16[2,65,16,128]{3,2,1,0:T(8,128)(2,1)} %copy-done.6, ...), custom_call_target="tpu_custom_call" | custom-call | bytes 4259840 | tf_op jit(solution)/shard_map/relay/pallas_call | solution.py:333
  49.6 1.1 collective-permute-done.6.refs_4_.refs_5_.refs_16_.refs_17_
  50.6 9.9 %collective-permute-done.8.refs_6_.refs_7_.refs_18_.refs_19_ = bf16[2,65,16,128]{3,2,1,0:T(8,128)(2,1)S(1)} collective-permute-done((bf16[2,65,16,128]{3,2,1,0:T(8,128)(2,1)}, bf16[2,65,16,128]{3,2,1,0:T(8,128)(2,1)S(1)}, u32[]{:S(2)}, u32[]{:S(2)}) %collective-permute-start.8) | collective-permute-done | bytes 532512 | tf_op jit(solution)/shard_map/ppermute | solution.py:599
  60.6 2.6 collective-permute-start.4
  63.8 2.9 %collective-permute-start.7 = (bf16[2,65,16,128]{3,2,1,0:T(8,128)(2,1)S(1)}, bf16[2,65,16,128]{3,2,1,0:T(8,128)(2,1)S(1)}, u32[]{:S(2)}, u32[]{:S(2)}) collective-permute-start(bf16[2,65,16,128]{3,2,1,0:T(8,128)(2,1)S(1)} %copy-done.16), channel_id=1, source_target_pairs={{0,8},{4,12},{24,16},{28,20},{1,9},{5,13},{25,17},{29,21},{2,10},{... | collective-permute-start | bytes 1597448 | tf_op jit(solution)/shard_map/ppermute | solution.py:599
  66.7 30.0 %collective-permute-start.9 = (bf16[2,65,16,128]{3,2,1,0:T(8,128)(2,1)S(1)}, bf16[2,65,16,128]{3,2,1,0:T(8,128)(2,1)S(1)}, u32[]{:S(2)}, u32[]{:S(2)}) collective-permute-start(bf16[2,65,16,128]{3,2,1,0:T(8,128)(2,1)S(1)} %copy-done.15), channel_id=1, source_target_pairs={{0,12},{4,8},{24,20},{28,16},{1,13},{5,9},{25,21},{29,17},{2,14},{... | collective-permute-start | bytes 1597448 | tf_op jit(solution)/shard_map/ppermute | solution.py:599
  96.8 4.3 %relay.3 = (bf16[2,65,16,128]{3,2,1,0:T(8,128)(2,1)}, bf16[2,65,16,128]{3,2,1,0:T(8,128)(2,1)}) custom-call(bf16[2,65,16,128]{3,2,1,0:T(8,128)(2,1)} %get-tuple-element.96.refs_0_.refs_1_.refs_8_, bf16[2,65,16,128]{3,2,1,0:T(8,128)(2,1)} %get-tuple-element.96.refs_0_.refs_1_.refs_8_, bf16[2,65,16,128]{3,2,1,0:T(8,128)(2,1)} %copy-done.7, ...), custom_call_target="tpu_custom_call" | custom-call | bytes 4259840 | tf_op jit(solution)/shard_map/relay/pallas_call | solution.py:333
  101.2 4.8 %collective-permute-done.4.refs_4_.refs_5_ = bf16[2,65,16,128]{3,2,1,0:T(8,128)(2,1)S(1)} collective-permute-done((bf16[2,65,16,128]{3,2,1,0:T(8,128)(2,1)}, bf16[2,65,16,128]{3,2,1,0:T(8,128)(2,1)S(1)}, u32[]{:S(2)}, u32[]{:S(2)}) %collective-permute-start.4) | collective-permute-done | bytes 532512 | tf_op jit(solution)/shard_map/ppermute | solution.py:599
  105.9 11.2 %collective-permute-done.5.refs_6_.refs_7_ = bf16[2,65,16,128]{3,2,1,0:T(8,128)(2,1)S(1)} collective-permute-done((bf16[2,65,16,128]{3,2,1,0:T(8,128)(2,1)}, bf16[2,65,16,128]{3,2,1,0:T(8,128)(2,1)S(1)}, u32[]{:S(2)}, u32[]{:S(2)}) %collective-permute-start.5) | collective-permute-done | bytes 532512 | tf_op jit(solution)/shard_map/ppermute | solution.py:599
  117.2 0.8 copy-done.24
  118.4 6.5 %transform_mid.2 = bf16[4,2,2,2,2,64,256]{6,5,4,3,2,1,0:T(8,128)(2,1)} custom-call(bf16[2,256,512]{2,1,0:T(8,128)(2,1)} %constant.63.clone.table_ref, bf16[2,65,16,128]{3,2,1,0:T(8,128)(2,1)} %get-tuple-element.101.refs_0_.refs_1_, bf16[2,65,16,128]{3,2,1,0:T(8,128)(2,1)} %get-tuple-element.101.refs_0_.refs_1_, bf16[2,65,16,128]{3,2,1,0:T(8,128)(2,1)} %copy-done.22, ...), custom_call_target="tpu_custom_call" | custom-call | flops 21810380800 | bytes 7421952 | tf_op jit(solution)/shard_map/transform_mid/pallas_call | solution.py:417
  124.8 3.9 %all-to-all-start = ((bf16[4,2,2,2,128,256]{5,4,3,2,1,0:T(8,128)(2,1)}), bf16[4,2,2,2,128,256]{5,4,3,2,1,0:T(8,128)(2,1)S(1)}, u32[]{:S(2)}, u32[]{:S(2)}) async-start(bf16[4,2,2,2,128,256]{5,4,3,2,1,0:T(8,128)(2,1)} %bitcast.17), calls=%async_computation | async-start | bytes 4194304 | tf_op jit(solution)/shard_map/all_to_all | solution.py:698
  128.7 2.9 %collective-permute-start.15 = (bf16[2,65,16,128]{3,2,1,0:T(8,128)(2,1)}, bf16[2,65,16,128]{3,2,1,0:T(8,128)(2,1)}, u32[]{:S(2)}, u32[]{:S(2)}) collective-permute-start(bf16[2,65,16,128]{3,2,1,0:T(8,128)(2,1)} %get-tuple-element.111), channel_id=1, source_target_pairs={{0,16},{4,20},{8,24},{12,28},{16,0},{20,4},{24,8},{28,12},{1,17},{... | collective-permute-start | bytes 1597448 | tf_op jit(solution)/shard_map/ppermute | solution.py:599
  131.6 3.0 %collective-permute-start.17 = (bf16[2,65,16,128]{3,2,1,0:T(8,128)(2,1)}, bf16[2,65,16,128]{3,2,1,0:T(8,128)(2,1)}, u32[]{:S(2)}, u32[]{:S(2)}) collective-permute-start(bf16[2,65,16,128]{3,2,1,0:T(8,128)(2,1)} %get-tuple-element.113), channel_id=1, source_target_pairs={{0,8},{4,12},{24,16},{28,20},{1,9},{5,13},{25,17},{29,21},{2,10},{... | collective-permute-start | bytes 1597448 | tf_op jit(solution)/shard_map/ppermute | solution.py:599
  134.7 2.1 collective-permute-start.18
  136.8 0.6 fusion.10
  137.4 16.4 %all-to-all-done.refs_0_ = bf16[4,2,2,2,128,256]{5,4,3,2,1,0:T(8,128)(2,1)S(1)} async-done(((bf16[4,2,2,2,128,256]{5,4,3,2,1,0:T(8,128)(2,1)}), bf16[4,2,2,2,128,256]{5,4,3,2,1,0:T(8,128)(2,1)S(1)}, u32[]{:S(2)}, u32[]{:S(2)}) %all-to-all-start) | async-done | bytes 2097184 | tf_op jit(solution)/shard_map/all_to_all | solution.py:698
  153.8 1.3 copy-done
  155.1 7.3 %transform_long.2 = bf16[48,2,2,32,128]{4,3,2,1,0:T(8,128)(2,1)} custom-call(s32[64]{0:T(128)} %rows_ref.3, f32[2,2]{1,0:T(2,128)} %get-tuple-element.136.z_ref, bf16[1024,1024]{1,0:T(8,128)(2,1)} %constant.64.clone.first_ref, bf16[1024,1024]{1,0:T(8,128)(2,1)} %constant.65.clone.second_ref, f32[2,2,256,512]{3,2,1,0:T(8,128)} %pad_maximum_fusion.plane_ref, ...), custom_call_target="tpu_custom_call" | custom-call | flops 2147483648 | bytes 9961472 | tf_op jit(solution)/shard_map/transform_long/pallas_call | solution.py:516
  162.4 4.2 %collective-permute-done.16.refs_6_.refs_7_ = bf16[2,65,16,128]{3,2,1,0:T(8,128)(2,1)} collective-permute-done((bf16[2,65,16,128]{3,2,1,0:T(8,128)(2,1)}, bf16[2,65,16,128]{3,2,1,0:T(8,128)(2,1)}, u32[]{:S(2)}, u32[]{:S(2)}) %collective-permute-start.16) | collective-permute-done | bytes 532512 | tf_op jit(solution)/shard_map/ppermute | solution.py:599
  166.6 11.3 %collective-permute-done.15.refs_4_.refs_5_ = bf16[2,65,16,128]{3,2,1,0:T(8,128)(2,1)} collective-permute-done((bf16[2,65,16,128]{3,2,1,0:T(8,128)(2,1)}, bf16[2,65,16,128]{3,2,1,0:T(8,128)(2,1)}, u32[]{:S(2)}, u32[]{:S(2)}) %collective-permute-start.15) | collective-permute-done | bytes 532512 | tf_op jit(solution)/shard_map/ppermute | solution.py:599
  177.9 3.6 %all-to-all-start.1 = ((bf16[8,6,2,2,32,128]{5,4,3,2,1,0:T(8,128)(2,1)}), bf16[8,6,2,2,32,128]{5,4,3,2,1,0:T(8,128)(2,1)S(1)}, u32[]{:S(2)}, u32[]{:S(2)}) async-start(bf16[8,6,2,2,32,128]{5,4,3,2,1,0:T(8,128)(2,1)} %bitcast.15), calls=%async_computation.1 | async-start | bytes 3145728 | tf_op jit(solution)/shard_map/all_to_all | solution.py:711
  181.5 6.5 %transform_mid.3 = (bf16[2,2,2,2,64,256]{5,4,3,2,1,0:T(8,128)(2,1)}, bf16[2,2,2,2,64,256]{5,4,3,2,1,0:T(8,128)(2,1)}, bf16[2,2,2,2,64,256]{5,4,3,2,1,0:T(8,128)(2,1)}, bf16[2,2,2,2,64,256]{5,4,3,2,1,0:T(8,128)(2,1)}) custom-call(bf16[2,256,512]{2,1,0:T(8,128)(2,1)} %constant.63.clone.table_ref, bf16[2,65,16,128]{3,2,1,0:T(8,128)(2,1)} %get-tuple-element.118.refs_0_.refs_1_, ...), custom_call_target="tpu_custom_call" | custom-call | flops 21810380800 | bytes 7421952 | tf_op jit(solution)/shard_map/transform_mid/pallas_call | solution.py:417
  188.0 1.9 collective-permute-start.20
  189.9 1.5 collective-permute-start.21
  191.6 11.4 %collective-permute-done.20.refs_1_ = bf16[2,2,2,128,256]{4,3,2,1,0:T(8,128)(2,1)S(1)} collective-permute-done((bf16[2,2,2,128,256]{4,3,2,1,0:T(8,128)(2,1)}, bf16[2,2,2,128,256]{4,3,2,1,0:T(8,128)(2,1)S(1)}, u32[]{:S(2)}, u32[]{:S(2)}) %collective-permute-start.20) | collective-permute-done | bytes 524320 | tf_op jit(solution)/shard_map/ppermute | solution.py:606
  203.1 12.2 %collective-permute-done.21.refs_2_ = bf16[2,2,2,128,256]{4,3,2,1,0:T(8,128)(2,1)S(1)} collective-permute-done((bf16[2,2,2,128,256]{4,3,2,1,0:T(8,128)(2,1)}, bf16[2,2,2,128,256]{4,3,2,1,0:T(8,128)(2,1)S(1)}, u32[]{:S(2)}, u32[]{:S(2)}) %collective-permute-start.21) | collective-permute-done | bytes 524320 | tf_op jit(solution)/shard_map/ppermute | solution.py:606
  215.3 0.8 copy-done.9
  216.3 7.4 %transform_long.3 = bf16[48,2,2,32,128]{4,3,2,1,0:T(8,128)(2,1)} custom-call(s32[64]{0:T(128)} %rows_ref.3, f32[2,2]{1,0:T(2,128)} %get-tuple-element.135.z_ref, bf16[1024,1024]{1,0:T(8,128)(2,1)} %constant.64.clone.first_ref, bf16[1024,1024]{1,0:T(8,128)(2,1)} %constant.65.clone.second_ref, f32[2,2,256,512]{3,2,1,0:T(8,128)} %pad_maximum_fusion.plane_ref, ...), custom_call_target="tpu_custom_call" | custom-call | flops 2147483648 | bytes 9961472 | tf_op jit(solution)/shard_map/transform_long/pallas_call | solution.py:516
  223.7 42.7 %all_to_all.15.refs_1_ = bf16[8,6,2,2,32,128]{5,4,3,2,1,0:T(8,128)(2,1)} all-to-all(bf16[8,6,2,2,32,128]{5,4,3,2,1,0:T(8,128)(2,1)} %bitcast.16), channel_id=1, replica_groups=mesh['grid'=8,'pencil'=4] {'grid'}, dimensions={0} | all-to-all | bytes 3145728 | tf_op jit(solution)/shard_map/all_to_all | solution.py:711
  266.4 9.2 %lay_rows.1 = f32[6,2,32,4096]{3,2,1,0:T(8,128)} custom-call(bf16[8,6,2,2,32,128]{5,4,3,2,1,0:T(8,128)(2,1)} %copy-done.1, bf16[8,6,2,2,32,128]{5,4,3,2,1,0:T(8,128)(2,1)} %all_to_all.15.refs_1_), custom_call_target="tpu_custom_call" | custom-call | bytes 9437184 | tf_op jit(solution)/shard_map/lay_rows/pallas_call | solution.py:568
  (74 shorter events, 2.4 us)
Async XLA Ops:
  1.3 15.5 %copy-start.11 = (f32[3]{0:T(128)S(1)}, f32[3]{0:T(128)}, u32[]{:S(2)}) copy-start(f32[3]{0:T(128)} %param.17) | copy-start | bytes 40
  1.3 16.1 %copy-start.12 = (f32[3]{0:T(128)S(1)}, f32[3]{0:T(128)}, u32[]{:S(2)}) copy-start(f32[3]{0:T(128)} %param.18) | copy-start | bytes 40
  11.6 16.2 %collective-permute-start.2 = (bf16[2,65,16,128]{3,2,1,0:T(8,128)(2,1)}, bf16[2,65,16,128]{3,2,1,0:T(8,128)(2,1)S(1)}, u32[]{:S(2)}, u32[]{:S(2)}) collective-permute-start(bf16[2,65,16,128]{3,2,1,0:T(8,128)(2,1)} %get-tuple-element.77), channel_id=1, source_target_pairs={{0,8},{4,12},{8,0},{12,4},{16,24},{20,28},{24,16},{28,20},{1,9},{5... | collective-permute-start | bytes 1597448 | tf_op jit(solution)/shard_map/ppermute | solution.py:599
  14.7 24.2 %collective-permute-start.3 = (bf16[2,65,16,128]{3,2,1,0:T(8,128)(2,1)}, bf16[2,65,16,128]{3,2,1,0:T(8,128)(2,1)S(1)}, u32[]{:S(2)}, u32[]{:S(2)}) collective-permute-start(bf16[2,65,16,128]{3,2,1,0:T(8,128)(2,1)} %get-tuple-element.78), channel_id=1, source_target_pairs={{0,12},{4,8},{8,4},{12,0},{16,28},{20,24},{24,20},{28,16},{1,13},{... | collective-permute-start | bytes 1597448 | tf_op jit(solution)/shard_map/ppermute | solution.py:599
  14.7 26.3 %collective-permute-start.1 = (bf16[2,65,16,128]{3,2,1,0:T(8,128)(2,1)}, bf16[2,65,16,128]{3,2,1,0:T(8,128)(2,1)S(1)}, u32[]{:S(2)}, u32[]{:S(2)}) collective-permute-start(bf16[2,65,16,128]{3,2,1,0:T(8,128)(2,1)} %get-tuple-element.79.refs_9_), channel_id=1, source_target_pairs={{8,12},{12,8},{16,20},{20,16},{9,13},{13,9},{17,21},{21,17},{10,14... | collective-permute-start | bytes 1597448 | tf_op jit(solution)/shard_map/ppermute | solution.py:599
  15.4 26.3 %collective-permute-start.10 = (bf16[2,65,16,128]{3,2,1,0:T(8,128)(2,1)}, bf16[2,65,16,128]{3,2,1,0:T(8,128)(2,1)S(1)}, u32[]{:S(2)}, u32[]{:S(2)}) collective-permute-start(bf16[2,65,16,128]{3,2,1,0:T(8,128)(2,1)} %get-tuple-element.85), channel_id=1, source_target_pairs={{8,16},{16,8},{12,20},{20,12},{9,17},{17,9},{13,21},{21,13},{10,18... | collective-permute-start | bytes 1597448 | tf_op jit(solution)/shard_map/ppermute | solution.py:599
  16.1 26.4 %collective-permute-start.11 = (bf16[2,65,16,128]{3,2,1,0:T(8,128)(2,1)}, bf16[2,65,16,128]{3,2,1,0:T(8,128)(2,1)S(1)}, u32[]{:S(2)}, u32[]{:S(2)}) collective-permute-start(bf16[2,65,16,128]{3,2,1,0:T(8,128)(2,1)} %get-tuple-element.89), channel_id=1, source_target_pairs={{8,20},{20,8},{12,16},{16,12},{9,21},{21,9},{13,17},{17,13},{10,22... | collective-permute-start | bytes 1597448 | tf_op jit(solution)/shard_map/ppermute | solution.py:599
  27.8 17.2 %copy-start.3 = (bf16[2,65,16,128]{3,2,1,0:T(8,128)(2,1)}, bf16[2,65,16,128]{3,2,1,0:T(8,128)(2,1)S(1)}, u32[]{:S(2)}) copy-start(bf16[2,65,16,128]{3,2,1,0:T(8,128)(2,1)S(1)} %collective-permute-done.2.refs_4_.refs_5_.refs_16_.refs_17_) | copy-start | bytes 1597444
  27.8 22.8 %collective-permute-start.6 = (bf16[2,65,16,128]{3,2,1,0:T(8,128)(2,1)}, bf16[2,65,16,128]{3,2,1,0:T(8,128)(2,1)S(1)}, u32[]{:S(2)}, u32[]{:S(2)}) collective-permute-start(bf16[2,65,16,128]{3,2,1,0:T(8,128)(2,1)} %get-tuple-element.84), channel_id=1, source_target_pairs={{0,8},{4,12},{8,0},{12,4},{16,24},{20,28},{24,16},{28,20},{1,9},{5... | collective-permute-start | bytes 1597448 | tf_op jit(solution)/shard_map/ppermute | solution.py:599
  38.9 6.1 %copy-start.5 = (bf16[2,65,16,128]{3,2,1,0:T(8,128)(2,1)}, bf16[2,65,16,128]{3,2,1,0:T(8,128)(2,1)S(1)}, u32[]{:S(2)}) copy-start(bf16[2,65,16,128]{3,2,1,0:T(8,128)(2,1)S(1)} %collective-permute-done.3.refs_6_.refs_7_.refs_18_.refs_19_) | copy-start | bytes 1597444
  38.9 21.7 %collective-permute-start.8 = (bf16[2,65,16,128]{3,2,1,0:T(8,128)(2,1)}, bf16[2,65,16,128]{3,2,1,0:T(8,128)(2,1)S(1)}, u32[]{:S(2)}, u32[]{:S(2)}) collective-permute-start(bf16[2,65,16,128]{3,2,1,0:T(8,128)(2,1)} %get-tuple-element.88), channel_id=1, source_target_pairs={{0,12},{4,8},{8,4},{12,0},{16,28},{20,24},{24,20},{28,16},{1,13},{... | collective-permute-start | bytes 1597448 | tf_op jit(solution)/shard_map/ppermute | solution.py:599
  41.0 4.0 %copy-start.6 = (bf16[2,65,16,128]{3,2,1,0:T(8,128)(2,1)}, bf16[2,65,16,128]{3,2,1,0:T(8,128)(2,1)S(1)}, u32[]{:S(2)}) copy-start(bf16[2,65,16,128]{3,2,1,0:T(8,128)(2,1)S(1)} %collective-permute-done.1.refs_2_.refs_3_) | copy-start | bytes 1597444
  41.0 22.2 %collective-permute-start.14 = (bf16[2,65,16,128]{3,2,1,0:T(8,128)(2,1)}, bf16[2,65,16,128]{3,2,1,0:T(8,128)(2,1)S(1)}, u32[]{:S(2)}, u32[]{:S(2)}) collective-permute-start(bf16[2,65,16,128]{3,2,1,0:T(8,128)(2,1)} %get-tuple-element.98.refs_9_), channel_id=1, source_target_pairs={{8,12},{12,8},{16,20},{20,16},{9,13},{13,9},{17,21},{21,17},{10,14... | collective-permute-start | bytes 1597448 | tf_op jit(solution)/shard_map/ppermute | solution.py:599
  41.7 3.3 %copy-start.18 = (bf16[2,65,16,128]{3,2,1,0:T(8,128)(2,1)}, bf16[2,65,16,128]{3,2,1,0:T(8,128)(2,1)S(1)}, u32[]{:S(2)}) copy-start(bf16[2,65,16,128]{3,2,1,0:T(8,128)(2,1)S(1)} %collective-permute-done.10.refs_12_.refs_13_) | copy-start | bytes 1597444
  41.7 22.0 %collective-permute-start.12 = (bf16[2,65,16,128]{3,2,1,0:T(8,128)(2,1)}, bf16[2,65,16,128]{3,2,1,0:T(8,128)(2,1)S(1)}, u32[]{:S(2)}, u32[]{:S(2)}) collective-permute-start(bf16[2,65,16,128]{3,2,1,0:T(8,128)(2,1)} %get-tuple-element.113), channel_id=1, source_target_pairs={{8,16},{16,8},{12,20},{20,12},{9,17},{17,9},{13,21},{21,13},{10,18... | collective-permute-start | bytes 1597448 | tf_op jit(solution)/shard_map/ppermute | solution.py:599
  42.4 2.5 copy-start.19
  42.4 24.2 %collective-permute-start.13 = (bf16[2,65,16,128]{3,2,1,0:T(8,128)(2,1)}, bf16[2,65,16,128]{3,2,1,0:T(8,128)(2,1)S(1)}, u32[]{:S(2)}, u32[]{:S(2)}) collective-permute-start(bf16[2,65,16,128]{3,2,1,0:T(8,128)(2,1)} %get-tuple-element.114), channel_id=1, source_target_pairs={{8,20},{20,8},{12,16},{16,12},{9,21},{21,9},{13,17},{17,13},{10,22... | collective-permute-start | bytes 1597448 | tf_op jit(solution)/shard_map/ppermute | solution.py:599
  45.0 5.7 %copy-start.17 = (bf16[2,65,16,128]{3,2,1,0:T(8,128)(2,1)S(1)}, bf16[2,65,16,128]{3,2,1,0:T(8,128)(2,1)}, u32[]{:S(2)}) copy-start(bf16[2,65,16,128]{3,2,1,0:T(8,128)(2,1)} %get-tuple-element.73) | copy-start | bytes 1597444
  45.0 18.8 %copy-start.16 = (bf16[2,65,16,128]{3,2,1,0:T(8,128)(2,1)S(1)}, bf16[2,65,16,128]{3,2,1,0:T(8,128)(2,1)}, u32[]{:S(2)}) copy-start(bf16[2,65,16,128]{3,2,1,0:T(8,128)(2,1)} %get-tuple-element.85) | copy-start | bytes 1597444
  45.0 21.7 %copy-start.15 = (bf16[2,65,16,128]{3,2,1,0:T(8,128)(2,1)S(1)}, bf16[2,65,16,128]{3,2,1,0:T(8,128)(2,1)}, u32[]{:S(2)}) copy-start(bf16[2,65,16,128]{3,2,1,0:T(8,128)(2,1)} %get-tuple-element.89) | copy-start | bytes 1597444
  50.6 46.1 %copy-start.2 = (bf16[2,65,16,128]{3,2,1,0:T(8,128)(2,1)}, bf16[2,65,16,128]{3,2,1,0:T(8,128)(2,1)S(1)}, u32[]{:S(2)}) copy-start(bf16[2,65,16,128]{3,2,1,0:T(8,128)(2,1)S(1)} %collective-permute-done.6.refs_4_.refs_5_.refs_16_.refs_17_) | copy-start | bytes 1597444
  50.6 50.5 %collective-permute-start = (bf16[2,65,16,128]{3,2,1,0:T(8,128)(2,1)S(1)}, bf16[2,65,16,128]{3,2,1,0:T(8,128)(2,1)S(1)}, u32[]{:S(2)}, u32[]{:S(2)}) collective-permute-start(bf16[2,65,16,128]{3,2,1,0:T(8,128)(2,1)S(1)} %copy-done.17), channel_id=1, source_target_pairs={{0,4},{4,0},{8,12},{12,8},{16,20},{20,16},{24,28},{28,24},{1,5},{5... | collective-permute-start | bytes 1597448 | tf_op jit(solution)/shard_map/ppermute | solution.py:599
  60.6 36.2 %copy-start.4 = (bf16[2,65,16,128]{3,2,1,0:T(8,128)(2,1)}, bf16[2,65,16,128]{3,2,1,0:T(8,128)(2,1)S(1)}, u32[]{:S(2)}) copy-start(bf16[2,65,16,128]{3,2,1,0:T(8,128)(2,1)S(1)} %collective-permute-done.8.refs_6_.refs_7_.refs_18_.refs_19_) | copy-start | bytes 1597444
  60.6 45.4 %collective-permute-start.4 = (bf16[2,65,16,128]{3,2,1,0:T(8,128)(2,1)}, bf16[2,65,16,128]{3,2,1,0:T(8,128)(2,1)S(1)}, u32[]{:S(2)}, u32[]{:S(2)}) collective-permute-start(bf16[2,65,16,128]{3,2,1,0:T(8,128)(2,1)} %get-tuple-element.80), channel_id=1, source_target_pairs={{0,16},{4,20},{8,24},{12,28},{16,0},{20,4},{24,8},{28,12},{1,17},{... | collective-permute-start | bytes 1597448 | tf_op jit(solution)/shard_map/ppermute | solution.py:599
  63.2 33.6 %copy-start.7 = (bf16[2,65,16,128]{3,2,1,0:T(8,128)(2,1)}, bf16[2,65,16,128]{3,2,1,0:T(8,128)(2,1)S(1)}, u32[]{:S(2)}) copy-start(bf16[2,65,16,128]{3,2,1,0:T(8,128)(2,1)S(1)} %collective-permute-done.14.refs_2_.refs_3_) | copy-start | bytes 1597444
  63.2 54.0 %collective-permute-start.5 = (bf16[2,65,16,128]{3,2,1,0:T(8,128)(2,1)}, bf16[2,65,16,128]{3,2,1,0:T(8,128)(2,1)S(1)}, u32[]{:S(2)}, u32[]{:S(2)}) collective-permute-start(bf16[2,65,16,128]{3,2,1,0:T(8,128)(2,1)} %get-tuple-element.81), channel_id=1, source_target_pairs={{0,20},{4,16},{24,12},{28,8},{8,24},{12,28},{16,0},{20,4},{1,21},{... | collective-permute-start | bytes 1597448 | tf_op jit(solution)/shard_map/ppermute | solution.py:599
  63.8 37.4 %copy-start.20 = (bf16[2,65,16,128]{3,2,1,0:T(8,128)(2,1)}, bf16[2,65,16,128]{3,2,1,0:T(8,128)(2,1)S(1)}, u32[]{:S(2)}) copy-start(bf16[2,65,16,128]{3,2,1,0:T(8,128)(2,1)S(1)} %collective-permute-done.12.refs_12_.refs_13_) | copy-start | bytes 1597444
  63.8 53.4 %collective-permute-start.7 = (bf16[2,65,16,128]{3,2,1,0:T(8,128)(2,1)S(1)}, bf16[2,65,16,128]{3,2,1,0:T(8,128)(2,1)S(1)}, u32[]{:S(2)}, u32[]{:S(2)}) collective-permute-start(bf16[2,65,16,128]{3,2,1,0:T(8,128)(2,1)S(1)} %copy-done.16), channel_id=1, source_target_pairs={{0,8},{4,12},{24,16},{28,20},{1,9},{5,13},{25,17},{29,21},{2,10},{... | collective-permute-start | bytes 1597448 | tf_op jit(solution)/shard_map/ppermute | solution.py:599
  66.7 34.4 %copy-start.21 = (bf16[2,65,16,128]{3,2,1,0:T(8,128)(2,1)}, bf16[2,65,16,128]{3,2,1,0:T(8,128)(2,1)S(1)}, u32[]{:S(2)}) copy-start(bf16[2,65,16,128]{3,2,1,0:T(8,128)(2,1)S(1)} %collective-permute-done.13.refs_14_.refs_15_) | copy-start | bytes 1597444
  66.7 50.5 %collective-permute-start.9 = (bf16[2,65,16,128]{3,2,1,0:T(8,128)(2,1)S(1)}, bf16[2,65,16,128]{3,2,1,0:T(8,128)(2,1)S(1)}, u32[]{:S(2)}, u32[]{:S(2)}) collective-permute-start(bf16[2,65,16,128]{3,2,1,0:T(8,128)(2,1)S(1)} %copy-done.15), channel_id=1, source_target_pairs={{0,12},{4,8},{24,20},{28,16},{1,13},{5,9},{25,21},{29,17},{2,14},{... | collective-permute-start | bytes 1597448 | tf_op jit(solution)/shard_map/ppermute | solution.py:599
  101.2 16.0 %copy-start.22 = (bf16[2,65,16,128]{3,2,1,0:T(8,128)(2,1)}, bf16[2,65,16,128]{3,2,1,0:T(8,128)(2,1)S(1)}, u32[]{:S(2)}) copy-start(bf16[2,65,16,128]{3,2,1,0:T(8,128)(2,1)S(1)} %collective-permute-done.refs_2_.refs_3_) | copy-start | bytes 1597444
  105.9 11.3 %copy-start.23 = (bf16[2,65,16,128]{3,2,1,0:T(8,128)(2,1)}, bf16[2,65,16,128]{3,2,1,0:T(8,128)(2,1)S(1)}, u32[]{:S(2)}) copy-start(bf16[2,65,16,128]{3,2,1,0:T(8,128)(2,1)S(1)} %collective-permute-done.4.refs_4_.refs_5_) | copy-start | bytes 1597444
  117.2 1.2 copy-start.26
  124.8 9.8 %copy-start.14 = (bf16[2,65,16,128]{3,2,1,0:T(8,128)(2,1)S(1)}, bf16[2,65,16,128]{3,2,1,0:T(8,128)(2,1)}, u32[]{:S(2)}) copy-start(bf16[2,65,16,128]{3,2,1,0:T(8,128)(2,1)} %get-tuple-element.114) | copy-start | bytes 1597444
  124.8 11.9 %copy-start.13 = (bf16[2,65,16,128]{3,2,1,0:T(8,128)(2,1)S(1)}, bf16[2,65,16,128]{3,2,1,0:T(8,128)(2,1)}, u32[]{:S(2)}) copy-start(bf16[2,65,16,128]{3,2,1,0:T(8,128)(2,1)} %get-tuple-element.117) | copy-start | bytes 1597444
  124.8 29.0 %all-to-all-start = ((bf16[4,2,2,2,128,256]{5,4,3,2,1,0:T(8,128)(2,1)}), bf16[4,2,2,2,128,256]{5,4,3,2,1,0:T(8,128)(2,1)S(1)}, u32[]{:S(2)}, u32[]{:S(2)}) async-start(bf16[4,2,2,2,128,256]{5,4,3,2,1,0:T(8,128)(2,1)} %bitcast.17), calls=%async_computation | async-start | bytes 4194304 | tf_op jit(solution)/shard_map/all_to_all | solution.py:698
  128.7 37.9 %collective-permute-start.16 = (bf16[2,65,16,128]{3,2,1,0:T(8,128)(2,1)}, bf16[2,65,16,128]{3,2,1,0:T(8,128)(2,1)}, u32[]{:S(2)}, u32[]{:S(2)}) collective-permute-start(bf16[2,65,16,128]{3,2,1,0:T(8,128)(2,1)} %get-tuple-element.112), channel_id=1, source_target_pairs={{0,20},{4,16},{24,12},{28,8},{8,24},{12,28},{16,0},{20,4},{1,21},{... | collective-permute-start | bytes 1597448 | tf_op jit(solution)/shard_map/ppermute | solution.py:599
  128.7 49.2 %collective-permute-start.15 = (bf16[2,65,16,128]{3,2,1,0:T(8,128)(2,1)}, bf16[2,65,16,128]{3,2,1,0:T(8,128)(2,1)}, u32[]{:S(2)}, u32[]{:S(2)}) collective-permute-start(bf16[2,65,16,128]{3,2,1,0:T(8,128)(2,1)} %get-tuple-element.111), channel_id=1, source_target_pairs={{0,16},{4,20},{8,24},{12,28},{16,0},{20,4},{24,8},{28,12},{1,17},{... | collective-permute-start | bytes 1597448 | tf_op jit(solution)/shard_map/ppermute | solution.py:599
  131.6 46.3 %collective-permute-start.17 = (bf16[2,65,16,128]{3,2,1,0:T(8,128)(2,1)}, bf16[2,65,16,128]{3,2,1,0:T(8,128)(2,1)}, u32[]{:S(2)}, u32[]{:S(2)}) collective-permute-start(bf16[2,65,16,128]{3,2,1,0:T(8,128)(2,1)} %get-tuple-element.113), channel_id=1, source_target_pairs={{0,8},{4,12},{24,16},{28,20},{1,9},{5,13},{25,17},{29,21},{2,10},{... | collective-permute-start | bytes 1597448 | tf_op jit(solution)/shard_map/ppermute | solution.py:599
  134.7 43.3 %collective-permute-start.18 = (bf16[2,65,16,128]{3,2,1,0:T(8,128)(2,1)S(1)}, bf16[2,65,16,128]{3,2,1,0:T(8,128)(2,1)}, u32[]{:S(2)}, u32[]{:S(2)}) collective-permute-start(bf16[2,65,16,128]{3,2,1,0:T(8,128)(2,1)S(1)} %copy-done.14), channel_id=1, source_target_pairs={{0,12},{4,8},{24,20},{28,16},{1,13},{5,9},{25,21},{29,17},{2,14},{... | collective-permute-start | bytes 1597448 | tf_op jit(solution)/shard_map/ppermute | solution.py:599
  136.8 41.2 %collective-permute-start.19 = (bf16[2,65,16,128]{3,2,1,0:T(8,128)(2,1)S(1)}, bf16[2,65,16,128]{3,2,1,0:T(8,128)(2,1)}, u32[]{:S(2)}, u32[]{:S(2)}) collective-permute-start(bf16[2,65,16,128]{3,2,1,0:T(8,128)(2,1)S(1)} %copy-done.13), channel_id=1, source_target_pairs={{0,4},{4,0},{8,12},{12,8},{16,20},{20,16},{24,28},{28,24},{1,5},{5... | collective-permute-start | bytes 1597448 | tf_op jit(solution)/shard_map/ppermute | solution.py:599
  153.8 1.3 copy-start
  177.9 45.8 %all-to-all-start.1 = ((bf16[8,6,2,2,32,128]{5,4,3,2,1,0:T(8,128)(2,1)}), bf16[8,6,2,2,32,128]{5,4,3,2,1,0:T(8,128)(2,1)S(1)}, u32[]{:S(2)}, u32[]{:S(2)}) async-start(bf16[8,6,2,2,32,128]{5,4,3,2,1,0:T(8,128)(2,1)} %bitcast.15), calls=%async_computation.1 | async-start | bytes 3145728 | tf_op jit(solution)/shard_map/all_to_all | solution.py:711
  188.0 15.0 %collective-permute-start.20 = (bf16[2,2,2,128,256]{4,3,2,1,0:T(8,128)(2,1)}, bf16[2,2,2,128,256]{4,3,2,1,0:T(8,128)(2,1)S(1)}, u32[]{:S(2)}, u32[]{:S(2)}) collective-permute-start(bf16[2,2,2,128,256]{4,3,2,1,0:T(8,128)(2,1)} %bitcast.21), channel_id=1, source_target_pairs={{0,1},{1,0},{2,3},{3,2},{4,5},{5,4},{6,7},{7,6},{8,9},{9,8},{10,11... | collective-permute-start | bytes 1572872 | tf_op jit(solution)/shard_map/ppermute | solution.py:606
  189.9 25.4 %collective-permute-start.21 = (bf16[2,2,2,128,256]{4,3,2,1,0:T(8,128)(2,1)}, bf16[2,2,2,128,256]{4,3,2,1,0:T(8,128)(2,1)S(1)}, u32[]{:S(2)}, u32[]{:S(2)}) collective-permute-start(bf16[2,2,2,128,256]{4,3,2,1,0:T(8,128)(2,1)} %bitcast.20), channel_id=1, source_target_pairs={{0,2},{1,3},{2,0},{3,1},{4,6},{5,7},{6,4},{7,5},{8,10},{9,11},{10,... | collective-permute-start | bytes 1572872 | tf_op jit(solution)/shard_map/ppermute | solution.py:606
  191.4 23.9 %collective-permute-start.22 = (bf16[2,2,2,128,256]{4,3,2,1,0:T(8,128)(2,1)}, bf16[2,2,2,128,256]{4,3,2,1,0:T(8,128)(2,1)S(1)}, u32[]{:S(2)}, u32[]{:S(2)}) collective-permute-start(bf16[2,2,2,128,256]{4,3,2,1,0:T(8,128)(2,1)} %bitcast.19), channel_id=1, source_target_pairs={{0,3},{1,2},{2,1},{3,0},{4,7},{5,6},{6,5},{7,4},{8,11},{9,10},{10,... | collective-permute-start | bytes 1572872 | tf_op jit(solution)/shard_map/ppermute | solution.py:606
  203.1 12.2 %copy-start.8 = (bf16[2,2,2,128,256]{4,3,2,1,0:T(8,128)(2,1)}, bf16[2,2,2,128,256]{4,3,2,1,0:T(8,128)(2,1)S(1)}, u32[]{:S(2)}) copy-start(bf16[2,2,2,128,256]{4,3,2,1,0:T(8,128)(2,1)S(1)} %collective-permute-done.20.refs_1_) | copy-start | bytes 1572868
  223.7 42.7 %copy-start.1 = (bf16[8,6,2,2,32,128]{5,4,3,2,1,0:T(8,128)(2,1)}, bf16[8,6,2,2,32,128]{5,4,3,2,1,0:T(8,128)(2,1)S(1)}, u32[]{:S(2)}) copy-start(bf16[8,6,2,2,32,128]{5,4,3,2,1,0:T(8,128)(2,1)S(1)} %all-to-all-done.1.refs_0_) | copy-start | bytes 4718596
  (4 other events, 3.6 us)

commit v4 on v3

--- a/solution.py
+++ b/solution.py
@@ -1,4 +1,5 @@
 import functools
+import itertools
 import math
 
 import jax
@@ -11,6 +12,8 @@
 
 CHUNKS = 2
 MID_COST = 40
+HOLD_COST = 100_000_000_000
+ROWS_PER_STEP = 3
 VMEM_LIMIT = 56 * 1024 * 1024
 
 
@@ -202,13 +205,11 @@
     return jnp.asarray(np.stack([plain, turned]), jnp.bfloat16)
 
 
-def long_tables(long_len, block_len, pencils):
-    cos, sin = host_tables(long_len)
+def long_tables(long_len, block_len):
+    tables = host_tables(long_len)
     order = np.arange(long_len).reshape(long_len // block_len, block_len // 2, 2).transpose(2, 0, 1).reshape(-1)
-    real = np.stack([cos, -sin]).reshape(2, long_len, pencils, -1).transpose(1, 2, 0, 3).reshape(long_len, -1)
-    imag = np.stack([sin, cos]).reshape(2, long_len, pencils, -1).transpose(1, 2, 0, 3).reshape(long_len, -1)
-    first = np.concatenate([real[order], imag[order]], axis=0)
-    second = np.concatenate([real, imag], axis=0).T
+    first = np.concatenate([table[order] for table in tables], axis=0)
+    second = np.concatenate(tables, axis=1)
     return jnp.asarray(first, jnp.bfloat16), jnp.asarray(second, jnp.bfloat16)
 
 
@@ -251,7 +252,7 @@
 def transform_z(samples, levels, coefficients, failed, table):
     local_long, mid_len, z_len = samples.shape
     chunks, units, columns, _ = table.shape
-    rows = 8
+    rows = 32
     lines = local_long // chunks
     steps = lines // rows
     tiles = 2
@@ -344,7 +345,12 @@
     )(*[ref for source in sources for ref in (source, source)], *passing)
 
 
-def mid_kernel(first_chunk, apart, table_ref, *refs):
+def turning(outer, inner):
+    rows = np.arange(outer * inner)
+    return jnp.asarray(rows[:, None] % outer * inner + rows[:, None] // outer == rows[None, :], jnp.bfloat16)
+
+
+def mid_kernel(first_chunk, apart, turn_ref, table_ref, *refs):
     out_refs = []
     if apart:
         refs, out_refs = refs[: -apart - 1] + refs[-1:], refs[-apart - 1 : -1]
@@ -356,8 +362,6 @@
     groups = pencils // 2
     lead = lax.axis_index("grid") == 0
     outer = is_outer()
-    row_ids = lax.broadcasted_iota(jnp.int32, (rows, half, mid_len), 1)
-    special = lead & (row_ids % (groups * slots) == 0)
     sources = [ref[...] for ref in refs[0::2]]
     weights = [ref[...] for ref in refs[1::2]]
     for kept in (sources, weights):
@@ -369,28 +373,28 @@
     for kind in range(classes):
         total = weighted_sum(sources, weights, kind).astype(jnp.bfloat16)
         lines = jnp.concatenate([total[tile].reshape(rows * columns, lanes) for tile in range(tiles)], axis=1)
+        lines = jnp.dot(turn_ref[...], lines, preferred_element_type=jnp.float32).astype(jnp.bfloat16)
         product = jnp.dot(lines, table_ref[kind], preferred_element_type=jnp.float32)
-        product = product.reshape(rows, columns, 2 * mid_len)
-        re_cos, re_sin = product[:, :half, :mid_len], product[:, :half, mid_len:]
-        im_cos, im_sin = product[:, half:, :mid_len], product[:, half:, mid_len:]
-        plus = [re_cos - im_sin, re_sin + im_cos]
-        minus = [re_cos + im_sin, re_sin - im_cos]
-        if first_chunk:
-            plus = [jnp.where(special, re_cos, plus[0]), jnp.where(special, re_sin, plus[1])]
-            minus = [jnp.where(special, im_cos, minus[0]), jnp.where(special, im_sin, minus[1])]
+        product = product.reshape(columns, rows, 2 * mid_len)
+        re_cos, re_sin = product[:half, :, :mid_len], product[:half, :, mid_len:]
+        im_cos, im_sin = product[half:, :, :mid_len], product[half:, :, mid_len:]
         for part in range(2):
-            up = jnp.transpose(plus[part], (1, 0, 2))
-            down = jnp.transpose(minus[part], (1, 0, 2))
+            alone, other = (re_cos, im_cos) if part == 0 else (re_sin, im_sin)
+            up = re_cos - im_sin if part == 0 else re_sin + im_cos
+            down = re_cos + im_sin if part == 0 else re_sin - im_cos
             for piece in range(halves):
                 for group in range(groups):
                     for slot in range(slots):
                         at = (piece * groups + group) * slots + slot
-                        out_ref[group, kind, slot, part, piece] = up[at].astype(jnp.bfloat16)
-                        value = down[at]
+                        value, mirrored = up[at], down[at]
                         if first_chunk and slot == 0:
-                            other = (piece * groups + (group + 1) % groups) * slots
-                            value = jnp.where(lead, down[other], value)
-                        out_ref[pencils - 1 - group, kind, slot, part, piece] = value.astype(jnp.bfloat16)
+                            follower = (piece * groups + (group + 1) % groups) * slots
+                            if group == 0:
+                                value = jnp.where(lead, alone[at], value)
+                            turn = down[follower] if group + 1 < groups else other[follower]
+                            mirrored = jnp.where(lead, turn, mirrored)
+                        out_ref[group, kind, slot, part, piece] = value.astype(jnp.bfloat16)
+                        out_ref[pencils - 1 - group, kind, slot, part, piece] = mirrored.astype(jnp.bfloat16)
     for step, apart_ref in enumerate(out_refs):
         apart_ref[...] = out_ref[lax.axis_index("pencil") ^ step]
 
@@ -399,7 +403,7 @@
     tiles, lines, columns, lanes = sources[0].shape
     lines -= 1
     classes, mid_len, _ = table.shape
-    rows = 16
+    rows = 32
     shape = (pencils, classes, slots, 2, chunks, lines, mid_len)
     block = shape[:5] + (rows, mid_len)
     if apart:
@@ -417,7 +421,10 @@
     return pl.pallas_call(
         functools.partial(mid_kernel, first_chunk, pencils if apart else 0),
         grid=(lines // rows,),
-        in_specs=[pl.BlockSpec(table.shape, lambda i: (0, 0, 0))]
+        in_specs=[
+            pl.BlockSpec((rows * columns, rows * columns), lambda i: (0, 0)),
+            pl.BlockSpec(table.shape, lambda i: (0, 0, 0)),
+        ]
         + unit_specs(sources[0].shape, rows) * len(sources),
         compiler_params=pltpu.CompilerParams(vmem_limit_bytes=VMEM_LIMIT),
         cost_estimate=pl.CostEstimate(
@@ -427,10 +434,10 @@
         ),
         name="transform_mid",
         **layout,
-    )(table, *[ref for source in sources for ref in (source, source)])
-
-
-def long_kernel(rows_ref, z_ref, first_ref, second_ref, plane_ref, *refs):
+    )(turning(rows, columns), table, *[ref for source in sources for ref in (source, source)])
+
+
+def long_kernel(rows_ref, z_ref, x_ref, y_ref, first_ref, second_ref, *refs):
     if len(refs) == 2:
         source_ref, out_ref = refs
     else:
@@ -438,20 +445,21 @@
         for step, source in enumerate(sources):
             source_ref[lax.axis_index("pencil") ^ step] = source[...]
     pencils, classes, _, _, local_long, mid_len = source_ref.shape
-    depth = 2 * pencils * local_long
     long_len = pencils * local_long
     pairs = out_ref.shape[3]
     per_long = long_len // (2 * pairs)
     per_mid = mid_len // (2 * pairs)
     edge = per_mid // 2
     slot = pl.program_id(0)
-    lines = [source_ref[:, kind, 0].reshape(depth, mid_len) for kind in range(classes)]
+    lines = [
+        jnp.concatenate(
+            [source_ref[:, kind, 0, part].reshape(long_len, mid_len) for part in range(2)], axis=1
+        )
+        for kind in range(classes)
+    ]
     first = jnp.dot(first_ref[...], lines[0], preferred_element_type=jnp.float32)
     second = lax.dot_general(
-        lines[1],
-        second_ref[...],
-        (((0,), (0,)), ((), ())),
-        preferred_element_type=jnp.float32,
+        lines[1], second_ref[...], (((0,), (0,)), ((), ())), preferred_element_type=jnp.float32
     )
     z_re, z_im = z_ref[0, slot], z_ref[1, slot]
     low = lax.broadcasted_iota(jnp.int32, (pairs, 4 * pairs), 1) < 2 * pairs
@@ -459,30 +467,40 @@
     for across in range(per_long):
         held = across < edge or across >= per_long - edge
         narrow = across if across < edge else across - (per_long - per_mid)
+        columns = []
+        for parity in range(2):
+            x_re, x_im = (x_ref[part, parity, across * pairs : (across + 1) * pairs] for part in range(2))
+            column = (x_re * z_re - x_im * z_im, x_re * z_im + x_im * z_re)
+            columns.append([jnp.broadcast_to(value, (pairs, span)) for value in column])
         for couple in range(per_long // 2):
             near = couple < edge // 2 or couple >= (per_long - edge) // 2
             thin = couple if couple < edge // 2 else couple - (per_long - per_mid) // 2
             if not held and not near:
                 continue
+            y_re, y_im = (y_ref[part : part + 1, couple * span : (couple + 1) * span] for part in range(2))
             tiles = []
             for parity in range(2):
-                parts = []
-                for part in range(2):
-                    value = None
-                    if near:
-                        top = ((part * 2 + parity) * per_long + across) * pairs
-                        value = first[top : top + pairs, thin * span : (thin + 1) * span]
-                    if held:
-                        top = (parity * per_mid + narrow) * pairs
-                        left = part * long_len + couple * span
-                        term = second[top : top + pairs, left : left + span]
-                        value = term if value is None else value + term
-                    parts.append(value)
-                top = across * pairs
-                plane_re = plane_ref[0, parity, top : top + pairs, couple * span : (couple + 1) * span]
-                plane_im = plane_ref[1, parity, top : top + pairs, couple * span : (couple + 1) * span]
-                factor_re = plane_re * z_re - plane_im * z_im
-                factor_im = plane_re * z_im + plane_im * z_re
+                parts = [None, None]
+                if near:
+                    top = (parity * per_long + across) * pairs
+
+                    def taken(table, part):
+                        left = part * mid_len + thin * span
+                        return first[table * long_len + top : table * long_len + top + pairs, left : left + span]
+
+                    parts = [taken(0, 0) - taken(1, 1), taken(1, 0) + taken(0, 1)]
+                if held:
+                    top = (parity * per_mid + narrow) * pairs
+
+                    def turned(table, part):
+                        left = table * long_len + couple * span
+                        return second[part * mid_len + top : part * mid_len + top + pairs, left : left + span]
+
+                    terms = [turned(0, 0) - turned(1, 1), turned(1, 0) + turned(0, 1)]
+                    parts = [a + b for a, b in zip(parts, terms)] if near else terms
+                x_re, x_im = columns[parity]
+                factor_re = x_re * y_re - x_im * y_im
+                factor_im = x_re * y_im + x_im * y_re
                 tiles.append(
                     [
                         parts[0] * factor_re - parts[1] * factor_im,
@@ -498,7 +516,7 @@
                 out_ref[rows_ref[block + 1], 0, part] = right.astype(jnp.bfloat16)
 
 
-def transform_long(sources, row_ids, z_factor, first, second, plane, row_count, pairs):
+def transform_long(sources, row_ids, z_factor, x_factor, y_factor, first, second, row_count, pairs):
     if len(sources) == 1:
         pencils, classes, slots, _, local_long, mid_len = sources[0].shape
     else:
@@ -519,9 +537,10 @@
         in_specs=[
             pl.BlockSpec(memory_space=pltpu.SMEM),
             pl.BlockSpec(memory_space=pltpu.SMEM),
+            pl.BlockSpec(x_factor.shape, lambda i: (0, 0, 0, 0)),
+            pl.BlockSpec(y_factor.shape, lambda i: (0, 0)),
             pl.BlockSpec(first.shape, lambda i: (0, 0)),
             pl.BlockSpec(second.shape, lambda i: (0, 0)),
-            pl.BlockSpec(plane.shape, lambda i: (0, 0, 0, 0)),
         ]
         + specs,
         scratch_shapes=scratch,
@@ -534,25 +553,33 @@
             transcendentals=0,
         ),
         name="transform_long",
-    )(row_ids, z_factor, first, second, plane, *sources)
-
-
-def rows_kernel(*refs):
+    )(row_ids, z_factor, x_factor, y_factor, first, second, *sources)
+
+
+def rows_kernel(turn_ref, *refs):
     sources, out_ref = refs[:-1], refs[-1]
     back = lax.axis_index("pencil") >= 2
-    _, _, slots, _, pairs, span = sources[0].shape
+    _, _, slots, parts, pairs, span = sources[0].shape
     z_local = out_ref.shape[2]
 
     def write(order):
-        for top in range(0, z_local, 8):
-            taken = []
-            for z in range(top, top + 8):
-                chunk, slot = divmod(order(z) % (len(sources) * slots), slots)
-                device = order(z) // (len(sources) * slots)
-                taken.append(sources[chunk][device, 0, slot, 0].astype(jnp.float32))
-            turned = jnp.transpose(jnp.stack(taken), (1, 0, 2))
-            for pair in range(pairs):
-                out_ref[0, 0, top : top + 8, pair * span : (pair + 1) * span] = turned[pair]
+        for row, top in itertools.product(range(out_ref.shape[0]), range(0, z_local, 8)):
+            sides = []
+            for part in range(parts):
+                taken = []
+                for z in range(top, top + 8):
+                    device, place = divmod(order(z), len(sources) * slots)
+                    chunk, slot = divmod(place, slots)
+                    taken.append(sources[chunk][device, row, slot, part])
+                sides.append(jnp.concatenate(taken, axis=0))
+            turned = jnp.dot(
+                turn_ref[...], jnp.concatenate(sides, axis=1), preferred_element_type=jnp.float32
+            )
+            for part in range(parts):
+                for pair in range(pairs):
+                    out_ref[row, part, top : top + 8, pair * span : (pair + 1) * span] = turned[
+                        pair * 8 : (pair + 1) * 8, part * span : (part + 1) * span
+                    ]
 
     @pl.when(jnp.logical_not(back))
     def _():
@@ -564,19 +591,21 @@
 
 
 def lay_rows(sources, z_local):
-    grid_count, rows, slots, _, pairs, span = sources[0].shape
+    grid_count, rows, slots, parts, pairs, span = sources[0].shape
     return pl.pallas_call(
         rows_kernel,
-        grid=(rows, 2),
-        in_specs=[pl.BlockSpec((grid_count, 1, slots, 1, pairs, span), lambda i, j: (0, i, 0, j, 0, 0))] * len(sources),
-        out_specs=pl.BlockSpec((1, 1, z_local, pairs * span), lambda i, j: (i, j, 0, 0)),
-        out_shape=jax.ShapeDtypeStruct((rows, 2, z_local, pairs * span), jnp.float32),
+        grid=(rows // ROWS_PER_STEP,),
+        in_specs=[pl.BlockSpec((8 * pairs, 8 * pairs), lambda i: (0, 0))]
+        + [pl.BlockSpec((grid_count, ROWS_PER_STEP, slots, parts, pairs, span), lambda i: (0, i, 0, 0, 0, 0))]
+        * len(sources),
+        out_specs=pl.BlockSpec((ROWS_PER_STEP, parts, z_local, pairs * span), lambda i: (i, 0, 0, 0)),
+        out_shape=jax.ShapeDtypeStruct((rows, parts, z_local, pairs * span), jnp.float32),
         compiler_params=pltpu.CompilerParams(vmem_limit_bytes=VMEM_LIMIT),
         cost_estimate=pl.CostEstimate(
             flops=0, bytes_accessed=6 * len(sources) * sources[0].size, transcendentals=0
         ),
         name="lay_rows",
-    )(*sources)
+    )(turning(8, pairs), *sources)
 
 
 PAIR_SAME = [(d, d ^ 2) for d in range(8)]
@@ -599,6 +628,25 @@
     return lax.ppermute(value, "grid", pairs)
 
 
+def hold_kernel(value_ref, *refs):
+    out_ref = refs[-1]
+    for row in range(value_ref.shape[0]):
+        for column in range(value_ref.shape[1]):
+            out_ref[row, column] = value_ref[row, column]
+
+
+def hold(value, earlier):
+    return pl.pallas_call(
+        hold_kernel,
+        in_specs=[pl.BlockSpec(memory_space=pltpu.SMEM)]
+        + [pl.BlockSpec(memory_space=pl.ANY)] * len(earlier),
+        out_specs=pl.BlockSpec(memory_space=pltpu.SMEM),
+        out_shape=jax.ShapeDtypeStruct(value.shape, value.dtype),
+        cost_estimate=pl.CostEstimate(flops=HOLD_COST, bytes_accessed=0, transcendentals=0),
+        name="hold",
+    )(value, *earlier)
+
+
 def exchange(parts, axis):
     count = len(parts)
     got = {0: parts[0]}
@@ -607,31 +655,26 @@
     return [got[step] for step in range(count)]
 
 
-def gather_grids(chunks):
-    early = []
-    for units in chunks:
-        first = [units[0], units[1], units[5], units[2], units[3]]
-        if early:
-            first = [after([value], [twin])[0] for value, twin in zip(first, early[-1])]
-        plans = (PAIR_SAME, PAIR_CROSS, INNER_CORES, INNER_SAME, INNER_CROSS)
-        early.append([send(value, pairs) for value, pairs in zip(first, plans)])
-    sums = []
-    for units, got in zip(chunks, early):
-        third = after(units[4:6], got[3:] if sums else [])
-        sums.append(relay([third[0], got[2], got[0], got[1]], third))
-    late = []
-    for units, passed in zip(chunks, sums):
-        second = [passed[0], passed[1], units[2], units[3]]
-        twins = late[-1] if late else [None, None] + early[-1][:2]
-        second = [value if twin is None else after([value], [twin])[0] for value, twin in zip(second, twins)]
-        plans = (JUMP_SAME, JUMP_MIXED, ENTER_SAME, ENTER_CROSS)
-        late.append([send(value, pairs) for value, pairs in zip(second, plans)])
-    cores = [send(units[7], CORES) for units in chunks]
-    found = [
-        [units[6], core] + second + first[3:5] + first[0:2]
-        for units, core, second, first in zip(chunks, cores, late, early)
-    ]
-    return found, sums, late
+def tied(values, twins):
+    return [after([value], [twin])[0] for value, twin in zip(values, twins)]
+
+
+def send_early(units, twins):
+    values = [units[0], units[1], units[5], units[2], units[3]]
+    plans = (PAIR_SAME, PAIR_CROSS, INNER_CORES, INNER_SAME, INNER_CROSS)
+    if twins:
+        values = tied(values, twins)
+    return [send(value, pairs) for value, pairs in zip(values, plans)]
+
+
+def send_jump(sums, twins):
+    if twins:
+        sums = tied(sums, twins)
+    return [send(value, pairs) for value, pairs in zip(sums, (JUMP_SAME, JUMP_MIXED))]
+
+
+def send_enter(units, twins):
+    return [send(value, pairs) for value, pairs in zip(tied(units[2:4], twins), (ENTER_SAME, ENTER_CROSS))]
 
 
 def mode_factor(modes, diffusion, speed, long_len, mid_len):
@@ -660,10 +703,8 @@
     modes = signed_modes(positions, long_len)
     x_re, x_im = mode_factor(modes, diffusivity[0], velocity[0], long_len, mid_len)
     y_re, y_im = mode_factor(modes, diffusivity[1], velocity[1], long_len, mid_len)
-    by_parity = [v.reshape(long_len // 2, 2).T[:, :, None] for v in (x_re, x_im)]
-    plane = jnp.stack(
-        [by_parity[0] * y_re - by_parity[1] * y_im, by_parity[0] * y_im + by_parity[1] * y_re]
-    )
+    x_factor = jnp.stack([x_re, x_im]).reshape(2, long_len // 2, 2).transpose(0, 2, 1)[..., None]
+    y_factor = jnp.stack([y_re, y_im])
     place_in = me * per_device + jnp.arange(per_device, dtype=jnp.int32)
     back = pencil >= pencils // 2
     z_index = pencil * z_local + jnp.where(back, (z_local - place_in) % z_local, place_in)
@@ -673,41 +714,59 @@
     z_factor = jnp.stack([z_re, z_im]) * (1.0 / math.sqrt(long_len * mid_len * z_len))
 
     mid = mid_table(mid_len, block_len)
-    first, second = long_tables(long_len, block_len, pencils)
+    first, second = long_tables(long_len, block_len)
     tables = [z_table(chunk, CHUNKS, grid_count, pencils, z_len) for chunk in range(CHUNKS)]
     tables = jnp.stack([v.reshape(grid_count, -1, v.shape[1]) for v in tables])
     units = transform_z(samples, levels, coefficients, failed, tables)
     units = [list(units[chunk * grid_count : (chunk + 1) * grid_count]) for chunk in range(CHUNKS)]
 
-    units[0][4], plane, z_factor = lax.optimization_barrier((units[0][4], plane, z_factor))
-    found, sums, late = gather_grids(units)
+    units[0][4], x_factor, y_factor, z_factor = lax.optimization_barrier(
+        (units[0][4], x_factor, y_factor, z_factor)
+    )
+    early, sums = [], []
+    for chunk in range(CHUNKS):
+        early.append(send_early(units[chunk], early[-1] if early else None))
+    for chunk in range(CHUNKS):
+        got = early[chunk]
+        third = after(units[chunk][4:6], got[3:] if chunk else [])
+        sums.append(relay([third[0], got[2], got[0], got[1]], third))
+    cores = [send(units[chunk][7], CORES) for chunk in range(CHUNKS)]
+    jumps = [send_jump(sums[0], None)]
+    enters = [send_enter(units[0], early[-1][:2])]
     arrived = []
     rows = None
-    for chunk, sources in enumerate(found):
-        if chunk + 1 < CHUNKS:
+    for chunk in range(CHUNKS):
+        got = early[chunk]
+        sources = [units[chunk][6], cores[chunk]] + enters[chunk] + jumps[chunk] + got[3:5] + got[0:2]
+        last = chunk == CHUNKS - 1
+        if not last:
             sources = after(sources, sums[chunk + 1])
-        if rows is not None:
+            jumps.append(send_jump(sums[chunk + 1], jumps[chunk]))
+        else:
             sources = after(sources, [rows])
-        apart = chunk == CHUNKS - 1
-        along_mid = transform_mid(sources, mid, chunk == 0, apart, CHUNKS, pencils, slots)
-        if apart:
+        along_mid = transform_mid(sources, mid, chunk == 0, last, CHUNKS, pencils, slots)
+        factor = z_factor[:, chunk * slots : (chunk + 1) * slots]
+        if not last:
+            enters.append(send_enter(units[chunk + 1], enters[chunk]))
+            factor = hold(factor, [cores[chunk + 1]])
+            along_mid = along_mid.reshape(along_mid.shape[:4] + (local_long, mid_len))
+            lines = [lax.all_to_all(along_mid, "pencil", split_axis=0, concat_axis=0, tiled=True)]
+        else:
             along_mid = [v.reshape(v.shape[:3] + (local_long, mid_len)) for v in along_mid]
             lines = exchange(along_mid, "pencil")
-        else:
-            along_mid = along_mid.reshape(along_mid.shape[:4] + (local_long, mid_len))
-            lines = [lax.all_to_all(along_mid, "pencil", split_axis=0, concat_axis=0, tiled=True)]
         rows = transform_long(
             lines,
             owner_map,
-            z_factor[:, chunk * slots : (chunk + 1) * slots],
+            factor,
+            x_factor,
+            y_factor,
             first,
             second,
-            plane,
             row_count,
             block_len // 2,
         )
         rows = rows.reshape((grid_count, -1) + rows.shape[1:])
-        sent = after([rows], late[-1])[0]
+        sent = after([rows], jumps[-1] + enters[-1])[0]
         arrived.append(lax.all_to_all(sent, "grid", split_axis=0, concat_axis=0, tiled=True))
     return lay_rows(arrived, z_local)
 

time: 277 us -> 251 us (0.906)
  starting transfers between devices: 66.6 us -> 55.3 us
  Pallas kernels: 55.9 us -> 46.4 us
  waiting for transfers between devices: 97.6 us -> 93.8 us
    ppermute x20, starting transfers between devices: 55.6 us -> 44 us  [send(): return lax.ppermute(value, 'grid', pairs)]
    ppermute x20, waiting for transfers between devices: 57.5 us -> 53.2 us  [send(): return lax.ppermute(value, 'grid', pairs)]
    pallas_call x1 -> x2, Pallas kernels: 9.15 us -> 5.92 us  [the longest x1 4.66 us: lay_rows(): pl.pallas_call(rows_kernel, grid=(rows // ROWS_PER_STEP,), in_specs=[pl.B...]
    pallas_call x1, Pallas kernels: 10.3 us -> 7.12 us  [transform_z(): pl.pallas_call(z_kernel, grid=(steps + 1,), in_specs=[pl.BlockSpec(memory...]
  transfers between devices with their start and end apart: 25 -> 25, of which waited for: 11 -> 11; matrix products, arithmetic and copies ran while one was open for 3% -> 3% of each run, Pallas kernels for 11% -> 14%
where the time goes in v4:
time: 251 us; the launch traced here: 250 us
  waiting for transfers between devices  93.8 us (37%)
  starting transfers between devices  55.3 us (22%)
  Pallas kernels  46.4 us (18%)
  blocking collectives  42.7 us (17%)
  local copies, waits for them, and re-layouts  5.33 us (2%)
  other arithmetic  4.55 us (2%)
    ppermute x20, waiting for transfers between devices, send(): return lax.ppermute(value, 'grid', pairs)  53.2 us
    ppermute x20, starting transfers between devices, send(): return lax.ppermute(value, 'grid', pairs)  44 us
    all_to_all x1, blocking collectives, body(): lax.all_to_all(sent, 'grid', split_axis=0, concat_axis=0, tiled=True)  42.7 us
    ppermute x3, waiting for transfers between devices, exchange(): lax.ppermute(parts[step], axis, [(d, d ^ step) for d in range(count)])  23.5 us
    all_to_all x1, waiting for transfers between devices, body(): lax.all_to_all(along_mid, 'pencil', split_axis=0, concat_axis=0, tiled=True)  17 us
    pallas_call x2, Pallas kernels, transform_long(): pl.pallas_call(long_kernel, grid=(slots,), in_specs=[pl.BlockSpec(memory_...  12.5 us
    pallas_call x2, Pallas kernels, transform_mid(): pl.pallas_call(functools.partial(mid_kernel, first_chunk, pencils if apar...  12 us
    pallas_call x2, Pallas kernels, relay(): pl.pallas_call(relay_kernel, grid=(shape[1] // rows,), in_specs=specs * l...  8.8 us
  transfers between devices with their start and end apart: 25, of which 11 were waited for; matrix products, arithmetic and copies ran while one was open for 3% of the time, Pallas kernels for 14%

profile of v4, /device:TPU:0, one launch (start us, length us, event | category | flops | bytes accessed | tf_op | source)
XLA Modules:
  0.0 249.6 jit_solution(18278085722382641289)
XLA Ops:
  1.3 7.1 %transform_z.1 = (bf16[2,65,16,128]{3,2,1,0:T(8,128)(2,1)}, bf16[2,65,16,128]{3,2,1,0:T(8,128)(2,1)}, bf16[2,65,16,128]{3,2,1,0:T(8,128)(2,1)}, bf16[2,65,16,128...) custom-call(s32[1,3]{1,0:T(1,128)} %levels_ref.1, ...), custom_call_target="tpu_custom_call" | custom-call | flops 2147483648 | bytes 16777216 | tf_op jit(solution)/shard_map/transform_z/pallas_call | solution.py:262
  8.4 0.7 collective-permute-start.12
  9.1 0.7 collective-permute-start.11
  9.8 7.0 %collective-permute-start.5 = (bf16[2,65,16,128]{3,2,1,0:T(8,128)(2,1)}, bf16[2,65,16,128]{3,2,1,0:T(8,128)(2,1)S(1)}, u32[]{:S(2)}, u32[]{:S(2)}) collective-permute-start(bf16[2,65,16,128]{3,2,1,0:T(8,128)(2,1)} %get-tuple-element.84), channel_id=1, source_target_pairs={{0,12},{4,8},{8,4},{12,0},{16,28},{20,24},{24,20},{28,16},{1,13},{... | collective-permute-start | bytes 1597448 | tf_op jit(solution)/shard_map/ppermute | solution.py:628
  17.0 0.7 collective-permute-start.8
  18.4 0.7 fusion.12
  19.0 1.4 sine_multiply_fusion.2
  20.4 0.7 collective-permute-start.14
  21.1 0.7 collective-permute-start.13
  21.8 7.7 %collective-permute-done.5.refs_6_.refs_7_.refs_18_.refs_19_ = bf16[2,65,16,128]{3,2,1,0:T(8,128)(2,1)S(1)} collective-permute-done((bf16[2,65,16,128]{3,2,1,0:T(8,128)(2,1)}, bf16[2,65,16,128]{3,2,1,0:T(8,128)(2,1)S(1)}, u32[]{:S(2)}, u32[]{:S(2)}) %collective-permute-start.5) | collective-permute-done | bytes 532512 | tf_op jit(solution)/shard_map/ppermute | solution.py:628
  29.6 12.8 %collective-permute-start.6 = (bf16[2,65,16,128]{3,2,1,0:T(8,128)(2,1)}, bf16[2,65,16,128]{3,2,1,0:T(8,128)(2,1)S(1)}, u32[]{:S(2)}, u32[]{:S(2)}) collective-permute-start(bf16[2,65,16,128]{3,2,1,0:T(8,128)(2,1)} %get-tuple-element.85), channel_id=1, source_target_pairs={{0,12},{4,8},{8,4},{12,0},{16,28},{20,24},{24,20},{28,16},{1,13},{... | collective-permute-start | bytes 1597448 | tf_op jit(solution)/shard_map/ppermute | solution.py:628
  42.4 0.7 collective-permute-start.3
  43.1 1.5 collective-permute-start.15
  44.5 1.2 sine_multiply_fusion.1
  45.8 1.3 sine_multiply_fusion
  47.7 4.5 %relay.2 = (bf16[2,65,16,128]{3,2,1,0:T(8,128)(2,1)}, bf16[2,65,16,128]{3,2,1,0:T(8,128)(2,1)}) custom-call(bf16[2,65,16,128]{3,2,1,0:T(8,128)(2,1)} %get-tuple-element.89.refs_0_.refs_1_.refs_8_, bf16[2,65,16,128]{3,2,1,0:T(8,128)(2,1)} %get-tuple-element.89.refs_0_.refs_1_.refs_8_, bf16[2,65,16,128]{3,2,1,0:T(8,128)(2,1)} %copy-done.5, ...), custom_call_target="tpu_custom_call" | custom-call | bytes 4259840 | tf_op jit(solution)/shard_map/relay/pallas_call | solution.py:334
  52.2 2.9 %collective-permute-done.6.refs_6_.refs_7_.refs_18_.refs_19_ = bf16[2,65,16,128]{3,2,1,0:T(8,128)(2,1)S(1)} collective-permute-done((bf16[2,65,16,128]{3,2,1,0:T(8,128)(2,1)}, bf16[2,65,16,128]{3,2,1,0:T(8,128)(2,1)S(1)}, u32[]{:S(2)}, u32[]{:S(2)}) %collective-permute-start.6) | collective-permute-done | bytes 532512 | tf_op jit(solution)/shard_map/ppermute | solution.py:628
  55.2 1.6 collective-permute-start.10
  56.8 16.5 %collective-permute-done.3.refs_4_.refs_5_.refs_16_.refs_17_ = bf16[2,65,16,128]{3,2,1,0:T(8,128)(2,1)S(1)} collective-permute-done((bf16[2,65,16,128]{3,2,1,0:T(8,128)(2,1)}, bf16[2,65,16,128]{3,2,1,0:T(8,128)(2,1)S(1)}, u32[]{:S(2)}, u32[]{:S(2)}) %collective-permute-start.3) | collective-permute-done | bytes 532512 | tf_op jit(solution)/shard_map/ppermute | solution.py:628
  73.4 4.6 %collective-permute-start.7 = (bf16[2,65,16,128]{3,2,1,0:T(8,128)(2,1)}, bf16[2,65,16,128]{3,2,1,0:T(8,128)(2,1)}, u32[]{:S(2)}, u32[]{:S(2)}) collective-permute-start(bf16[2,65,16,128]{3,2,1,0:T(8,128)(2,1)} %get-tuple-element.86), channel_id=1, source_target_pairs={{0,12},{4,8},{24,20},{28,16},{1,13},{5,9},{25,21},{29,17},{2,14},{... | collective-permute-start | bytes 1597448 | tf_op jit(solution)/shard_map/ppermute | solution.py:628
  78.0 2.1 collective-permute-start.4
  80.1 1.0 copy.16.x_ref
  81.2 0.7 fusion.10
  81.8 4.3 %relay.3 = (bf16[2,65,16,128]{3,2,1,0:T(8,128)(2,1)}, bf16[2,65,16,128]{3,2,1,0:T(8,128)(2,1)}) custom-call(bf16[2,65,16,128]{3,2,1,0:T(8,128)(2,1)} %get-tuple-element.99.refs_0_.refs_1_.refs_8_, bf16[2,65,16,128]{3,2,1,0:T(8,128)(2,1)} %get-tuple-element.99.refs_0_.refs_1_.refs_8_, bf16[2,65,16,128]{3,2,1,0:T(8,128)(2,1)} %collective-permute-done.15.refs_2_.refs_3_, ...), custom_call_target="tpu_custom_call" | custom-call | bytes 4259840 | tf_op jit(solution)/shard_map/relay/pallas_call | solution.py:334
  86.2 9.9 %collective-permute-done.10.refs_10_.refs_11_ = bf16[2,65,16,128]{3,2,1,0:T(8,128)(2,1)S(1)} collective-permute-done((bf16[2,65,16,128]{3,2,1,0:T(8,128)(2,1)}, bf16[2,65,16,128]{3,2,1,0:T(8,128)(2,1)S(1)}, u32[]{:S(2)}, u32[]{:S(2)}) %collective-permute-start.10) | collective-permute-done | bytes 532512 | tf_op jit(solution)/shard_map/ppermute | solution.py:628
  96.1 11.3 %collective-permute-done.9.refs_8_.refs_9_ = bf16[2,65,16,128]{3,2,1,0:T(8,128)(2,1)S(1)} collective-permute-done((bf16[2,65,16,128]{3,2,1,0:T(8,128)(2,1)}, bf16[2,65,16,128]{3,2,1,0:T(8,128)(2,1)S(1)}, u32[]{:S(2)}, u32[]{:S(2)}) %collective-permute-start.9) | collective-permute-done | bytes 532512 | tf_op jit(solution)/shard_map/ppermute | solution.py:628
  107.3 2.9 %collective-permute-start.16 = (bf16[2,65,16,128]{3,2,1,0:T(8,128)(2,1)}, bf16[2,65,16,128]{3,2,1,0:T(8,128)(2,1)}, u32[]{:S(2)}, u32[]{:S(2)}) collective-permute-start(bf16[2,65,16,128]{3,2,1,0:T(8,128)(2,1)} %get-tuple-element.114), channel_id=1, source_target_pairs={{0,16},{4,20},{8,24},{12,28},{16,0},{20,4},{24,8},{28,12},{1,17},{... | collective-permute-start | bytes 1597448 | tf_op jit(solution)/shard_map/ppermute | solution.py:628
  110.3 1.9 collective-permute-done.4.refs_4_.refs_5_
  112.2 5.9 %transform_mid.2 = bf16[4,2,2,2,2,64,256]{6,5,4,3,2,1,0:T(8,128)(2,1)} custom-call(bf16[512,512]{1,0:T(8,128)(2,1)} %constant.68.clone.turn_ref, bf16[2,256,512]{2,1,0:T(8,128)(2,1)} %constant.63.clone.table_ref, bf16[2,65,16,128]{3,2,1,0:T(8,128)(2,1)} %get-tuple-element.104.refs_0_.refs_1_, bf16[2,65,16,128]{3,2,1,0:T(8,128)(2,1)} %get-tuple-element.104.refs_0_.refs_1_, ...), custom_call_target="tpu_custom_call" | custom-call | flops 21810380800 | bytes 7421952 | tf_op jit(solution)/shard_map/transform_mid/pallas_call | solution.py:421
  118.1 3.9 %all-to-all-start = ((bf16[4,2,2,2,128,256]{5,4,3,2,1,0:T(8,128)(2,1)}), bf16[4,2,2,2,128,256]{5,4,3,2,1,0:T(8,128)(2,1)S(1)}, u32[]{:S(2)}, u32[]{:S(2)}) async-start(bf16[4,2,2,2,128,256]{5,4,3,2,1,0:T(8,128)(2,1)} %bitcast.19), calls=%async_computation | async-start | bytes 4194304 | tf_op jit(solution)/shard_map/all_to_all | solution.py:753
  122.0 5.0 %collective-permute-start.19 = (bf16[2,65,16,128]{3,2,1,0:T(8,128)(2,1)S(1)}, bf16[2,65,16,128]{3,2,1,0:T(8,128)(2,1)}, u32[]{:S(2)}, u32[]{:S(2)}) collective-permute-start(bf16[2,65,16,128]{3,2,1,0:T(8,128)(2,1)S(1)} %copy-done.10), channel_id=1, source_target_pairs={{0,12},{4,8},{24,20},{28,16},{1,13},{5,9},{25,21},{29,17},{2,14},{... | collective-permute-start | bytes 1597448 | tf_op jit(solution)/shard_map/ppermute | solution.py:628
  126.9 2.1 collective-permute-start.18
  129.0 1.3 hold.1.z_ref
  130.3 17.0 %all-to-all-done.refs_0_ = bf16[4,2,2,2,128,256]{5,4,3,2,1,0:T(8,128)(2,1)S(1)} async-done(((bf16[4,2,2,2,128,256]{5,4,3,2,1,0:T(8,128)(2,1)}), bf16[4,2,2,2,128,256]{5,4,3,2,1,0:T(8,128)(2,1)S(1)}, u32[]{:S(2)}, u32[]{:S(2)}) %all-to-all-start) | async-done | bytes 2097184 | tf_op jit(solution)/shard_map/all_to_all | solution.py:753
  147.3 1.3 copy-done.6
  148.6 6.2 %transform_long.2 = bf16[48,2,2,32,128]{4,3,2,1,0:T(8,128)(2,1)} custom-call(s32[64]{0:T(128)} %rows_ref.3, f32[2,2]{1,0:T(2,128)} %hold.1.z_ref, f32[2,2,256,1]{3,2,1,0:T(8,128)} %copy.16.x_ref, f32[2,512]{1,0:T(2,128)} %pad_maximum_fusion.y_ref, bf16[1024,512]{1,0:T(8,128)(2,1)} %constant.64.clone.first_ref, bf16[512,1024]{1,0:T(8,128)(2,1)} %constant.65.clone.second_ref, ...), custom_call_target="tpu_custom_call" | custom-call | flops 2147483648 | bytes 9961472 | tf_op jit(solution)/shard_map/transform_long/pallas_call | solution.py:534
  154.8 1.9 collective-permute-done.16.refs_8_.refs_9_
  156.8 1.1 collective-permute-done.18.refs_4_.refs_5_
  157.8 3.9 %all-to-all-start.1 = ((bf16[8,6,2,2,32,128]{5,4,3,2,1,0:T(8,128)(2,1)}), bf16[8,6,2,2,32,128]{5,4,3,2,1,0:T(8,128)(2,1)S(1)}, u32[]{:S(2)}, u32[]{:S(2)}) async-start(bf16[8,6,2,2,32,128]{5,4,3,2,1,0:T(8,128)(2,1)} %bitcast.20), calls=%async_computation.1 | async-start | bytes 3145728 | tf_op jit(solution)/shard_map/all_to_all | solution.py:770
  161.7 6.1 %transform_mid.3 = (bf16[2,2,2,2,64,256]{5,4,3,2,1,0:T(8,128)(2,1)}, bf16[2,2,2,2,64,256]{5,4,3,2,1,0:T(8,128)(2,1)}, bf16[2,2,2,2,64,256]{5,4,3,2,1,0:T(8,128)(2,1)}, bf16[2,2,2,2,64,256]{5,4,3,2,1,0:T(8,128)(2,1)}) custom-call(bf16[512,512]{1,0:T(8,128)(2,1)} %constant.68.clone.turn_ref, bf16[2,256,512]{2,1,0:T(8,128)(2,1)} %constant.63.clone.table_ref, ...), custom_call_target="tpu_custom_call" | custom-call | flops 21810380800 | bytes 7421952 | tf_op jit(solution)/shard_map/transform_mid/pallas_call | solution.py:421
  167.8 1.6 collective-permute-start.20
  169.4 1.5 collective-permute-start.21
  171.4 11.4 %collective-permute-done.20.refs_1_ = bf16[2,2,2,128,256]{4,3,2,1,0:T(8,128)(2,1)S(1)} collective-permute-done((bf16[2,2,2,128,256]{4,3,2,1,0:T(8,128)(2,1)}, bf16[2,2,2,128,256]{4,3,2,1,0:T(8,128)(2,1)S(1)}, u32[]{:S(2)}, u32[]{:S(2)}) %collective-permute-start.20) | collective-permute-done | bytes 524320 | tf_op jit(solution)/shard_map/ppermute | solution.py:654
  182.8 12.1 %collective-permute-done.21.refs_2_ = bf16[2,2,2,128,256]{4,3,2,1,0:T(8,128)(2,1)S(1)} collective-permute-done((bf16[2,2,2,128,256]{4,3,2,1,0:T(8,128)(2,1)}, bf16[2,2,2,128,256]{4,3,2,1,0:T(8,128)(2,1)S(1)}, u32[]{:S(2)}, u32[]{:S(2)}) %collective-permute-start.21) | collective-permute-done | bytes 524320 | tf_op jit(solution)/shard_map/ppermute | solution.py:654
  194.9 0.8 copy-done.20
  195.9 6.3 %transform_long.3 = bf16[48,2,2,32,128]{4,3,2,1,0:T(8,128)(2,1)} custom-call(s32[64]{0:T(128)} %rows_ref.3, f32[2,2]{1,0:T(2,128)} %get-tuple-element.135.z_ref, f32[2,2,256,1]{3,2,1,0:T(8,128)} %copy.16.x_ref, f32[2,512]{1,0:T(2,128)} %pad_maximum_fusion.y_ref, bf16[1024,512]{1,0:T(8,128)(2,1)} %constant.64.clone.first_ref, ...), custom_call_target="tpu_custom_call" | custom-call | flops 2147483648 | bytes 9961472 | tf_op jit(solution)/shard_map/transform_long/pallas_call | solution.py:534
  202.3 42.7 %all_to_all.15.refs_1_ = bf16[8,6,2,2,32,128]{5,4,3,2,1,0:T(8,128)(2,1)} all-to-all(bf16[8,6,2,2,32,128]{5,4,3,2,1,0:T(8,128)(2,1)} %bitcast.21), channel_id=1, replica_groups=mesh['grid'=8,'pencil'=4] {'grid'}, dimensions={0} | all-to-all | bytes 3145728 | tf_op jit(solution)/shard_map/all_to_all | solution.py:770
  244.9 4.7 %lay_rows.1 = f32[6,2,32,4096]{3,2,1,0:T(8,128)} custom-call(bf16[256,256]{1,0:T(8,128)(2,1)} %constant.69.clone.turn_ref, bf16[8,6,2,2,32,128]{5,4,3,2,1,0:T(8,128)(2,1)} %copy-done, bf16[8,6,2,2,32,128]{5,4,3,2,1,0:T(8,128)(2,1)} %all_to_all.15.refs_1_), custom_call_target="tpu_custom_call" | custom-call | bytes 9437184 | tf_op jit(solution)/shard_map/lay_rows/pallas_call | solution.py:595
  (66 shorter events, 2.3 us)
Async XLA Ops:
  1.3 16.4 %copy-start.7 = (f32[3]{0:T(128)S(1)}, f32[3]{0:T(128)}, u32[]{:S(2)}) copy-start(f32[3]{0:T(128)} %param.21) | copy-start | bytes 40
  1.3 17.1 %copy-start.8 = (f32[3]{0:T(128)S(1)}, f32[3]{0:T(128)}, u32[]{:S(2)}) copy-start(f32[3]{0:T(128)} %param.20) | copy-start | bytes 40
  8.4 12.0 %collective-permute-start.12 = (bf16[2,65,16,128]{3,2,1,0:T(8,128)(2,1)}, bf16[2,65,16,128]{3,2,1,0:T(8,128)(2,1)S(1)}, u32[]{:S(2)}, u32[]{:S(2)}) collective-permute-start(bf16[2,65,16,128]{3,2,1,0:T(8,128)(2,1)} %get-tuple-element.86), channel_id=1, source_target_pairs={{8,20},{20,8},{12,16},{16,12},{9,21},{21,9},{13,17},{17,13},{10,22... | collective-permute-start | bytes 1597448 | tf_op jit(solution)/shard_map/ppermute | solution.py:628
  9.1 12.0 %collective-permute-start.11 = (bf16[2,65,16,128]{3,2,1,0:T(8,128)(2,1)}, bf16[2,65,16,128]{3,2,1,0:T(8,128)(2,1)S(1)}, u32[]{:S(2)}, u32[]{:S(2)}) collective-permute-start(bf16[2,65,16,128]{3,2,1,0:T(8,128)(2,1)} %get-tuple-element.81), channel_id=1, source_target_pairs={{8,16},{16,8},{12,20},{20,12},{9,17},{17,9},{13,21},{21,13},{10,18... | collective-permute-start | bytes 1597448 | tf_op jit(solution)/shard_map/ppermute | solution.py:628
  9.8 19.7 %collective-permute-start.5 = (bf16[2,65,16,128]{3,2,1,0:T(8,128)(2,1)}, bf16[2,65,16,128]{3,2,1,0:T(8,128)(2,1)S(1)}, u32[]{:S(2)}, u32[]{:S(2)}) collective-permute-start(bf16[2,65,16,128]{3,2,1,0:T(8,128)(2,1)} %get-tuple-element.84), channel_id=1, source_target_pairs={{0,12},{4,8},{8,4},{12,0},{16,28},{20,24},{24,20},{28,16},{1,13},{... | collective-permute-start | bytes 1597448 | tf_op jit(solution)/shard_map/ppermute | solution.py:628
  16.8 25.6 %collective-permute-start.2 = (bf16[2,65,16,128]{3,2,1,0:T(8,128)(2,1)}, bf16[2,65,16,128]{3,2,1,0:T(8,128)(2,1)S(1)}, u32[]{:S(2)}, u32[]{:S(2)}) collective-permute-start(bf16[2,65,16,128]{3,2,1,0:T(8,128)(2,1)} %get-tuple-element.79), channel_id=1, source_target_pairs={{0,8},{4,12},{8,0},{12,4},{16,24},{20,28},{24,16},{28,20},{1,9},{5... | collective-permute-start | bytes 1597448 | tf_op jit(solution)/shard_map/ppermute | solution.py:628
  17.0 26.0 %collective-permute-start.8 = (bf16[2,65,16,128]{3,2,1,0:T(8,128)(2,1)}, bf16[2,65,16,128]{3,2,1,0:T(8,128)(2,1)S(1)}, u32[]{:S(2)}, u32[]{:S(2)}) collective-permute-start(bf16[2,65,16,128]{3,2,1,0:T(8,128)(2,1)} %get-tuple-element.90.refs_9_), channel_id=1, source_target_pairs={{8,12},{12,8},{16,20},{20,16},{9,13},{13,9},{17,21},{21,17},{10,14... | collective-permute-start | bytes 1597448 | tf_op jit(solution)/shard_map/ppermute | solution.py:628
  20.4 9.2 %copy-start.13 = (bf16[2,65,16,128]{3,2,1,0:T(8,128)(2,1)}, bf16[2,65,16,128]{3,2,1,0:T(8,128)(2,1)S(1)}, u32[]{:S(2)}) copy-start(bf16[2,65,16,128]{3,2,1,0:T(8,128)(2,1)S(1)} %collective-permute-done.12.refs_14_.refs_15_) | copy-start | bytes 1597444
  20.4 52.8 %collective-permute-start.14 = (bf16[2,65,16,128]{3,2,1,0:T(8,128)(2,1)}, bf16[2,65,16,128]{3,2,1,0:T(8,128)(2,1)S(1)}, u32[]{:S(2)}, u32[]{:S(2)}) collective-permute-start(bf16[2,65,16,128]{3,2,1,0:T(8,128)(2,1)} %get-tuple-element.117), channel_id=1, source_target_pairs={{8,20},{20,8},{12,16},{16,12},{9,21},{21,9},{13,17},{17,13},{10,22... | collective-permute-start | bytes 1597448 | tf_op jit(solution)/shard_map/ppermute | solution.py:628
  21.1 23.4 %copy-start.15 = (bf16[2,65,16,128]{3,2,1,0:T(8,128)(2,1)}, bf16[2,65,16,128]{3,2,1,0:T(8,128)(2,1)S(1)}, u32[]{:S(2)}) copy-start(bf16[2,65,16,128]{3,2,1,0:T(8,128)(2,1)S(1)} %collective-permute-done.11.refs_12_.refs_13_) | copy-start | bytes 1597444
  21.1 52.2 %collective-permute-start.13 = (bf16[2,65,16,128]{3,2,1,0:T(8,128)(2,1)}, bf16[2,65,16,128]{3,2,1,0:T(8,128)(2,1)S(1)}, u32[]{:S(2)}, u32[]{:S(2)}) collective-permute-start(bf16[2,65,16,128]{3,2,1,0:T(8,128)(2,1)} %get-tuple-element.116), channel_id=1, source_target_pairs={{8,16},{16,8},{12,20},{20,12},{9,17},{17,9},{13,21},{21,13},{10,18... | collective-permute-start | bytes 1597448 | tf_op jit(solution)/shard_map/ppermute | solution.py:628
  29.6 18.2 %copy-start.1 = (bf16[2,65,16,128]{3,2,1,0:T(8,128)(2,1)}, bf16[2,65,16,128]{3,2,1,0:T(8,128)(2,1)S(1)}, u32[]{:S(2)}) copy-start(bf16[2,65,16,128]{3,2,1,0:T(8,128)(2,1)S(1)} %collective-permute-done.5.refs_6_.refs_7_.refs_18_.refs_19_) | copy-start | bytes 1597444
  29.6 25.6 %collective-permute-start.6 = (bf16[2,65,16,128]{3,2,1,0:T(8,128)(2,1)}, bf16[2,65,16,128]{3,2,1,0:T(8,128)(2,1)S(1)}, u32[]{:S(2)}, u32[]{:S(2)}) collective-permute-start(bf16[2,65,16,128]{3,2,1,0:T(8,128)(2,1)} %get-tuple-element.85), channel_id=1, source_target_pairs={{0,12},{4,8},{8,4},{12,0},{16,28},{20,24},{24,20},{28,16},{1,13},{... | collective-permute-start | bytes 1597448 | tf_op jit(solution)/shard_map/ppermute | solution.py:628
  42.4 5.4 %copy-start.3 = (bf16[2,65,16,128]{3,2,1,0:T(8,128)(2,1)}, bf16[2,65,16,128]{3,2,1,0:T(8,128)(2,1)S(1)}, u32[]{:S(2)}) copy-start(bf16[2,65,16,128]{3,2,1,0:T(8,128)(2,1)S(1)} %collective-permute-done.2.refs_4_.refs_5_.refs_16_.refs_17_) | copy-start | bytes 1597444
  42.4 30.9 %collective-permute-start.3 = (bf16[2,65,16,128]{3,2,1,0:T(8,128)(2,1)}, bf16[2,65,16,128]{3,2,1,0:T(8,128)(2,1)S(1)}, u32[]{:S(2)}, u32[]{:S(2)}) collective-permute-start(bf16[2,65,16,128]{3,2,1,0:T(8,128)(2,1)} %get-tuple-element.80), channel_id=1, source_target_pairs={{0,8},{4,12},{8,0},{12,4},{16,24},{20,28},{24,16},{28,20},{1,9},{5... | collective-permute-start | bytes 1597448 | tf_op jit(solution)/shard_map/ppermute | solution.py:628
  43.1 4.7 %copy-start.5 = (bf16[2,65,16,128]{3,2,1,0:T(8,128)(2,1)}, bf16[2,65,16,128]{3,2,1,0:T(8,128)(2,1)S(1)}, u32[]{:S(2)}) copy-start(bf16[2,65,16,128]{3,2,1,0:T(8,128)(2,1)S(1)} %collective-permute-done.8.refs_2_.refs_3_) | copy-start | bytes 1597444
  43.1 34.9 %collective-permute-start.15 = (bf16[2,65,16,128]{3,2,1,0:T(8,128)(2,1)}, bf16[2,65,16,128]{3,2,1,0:T(8,128)(2,1)}, u32[]{:S(2)}, u32[]{:S(2)}) collective-permute-start(bf16[2,65,16,128]{3,2,1,0:T(8,128)(2,1)} %get-tuple-element.101.refs_9_), channel_id=1, source_target_pairs={{8,12},{12,8},{16,20},{20,16},{9,13},{13,9},{17,21},{21,17},{10,14... | collective-permute-start | bytes 1597448 | tf_op jit(solution)/shard_map/ppermute | solution.py:628
  47.7 30.3 %copy-start.11 = (bf16[2,65,16,128]{3,2,1,0:T(8,128)(2,1)S(1)}, bf16[2,65,16,128]{3,2,1,0:T(8,128)(2,1)}, u32[]{:S(2)}) copy-start(bf16[2,65,16,128]{3,2,1,0:T(8,128)(2,1)} %get-tuple-element.81) | copy-start | bytes 1597444
  55.2 26.7 %copy-start.2 = (bf16[2,65,16,128]{3,2,1,0:T(8,128)(2,1)}, bf16[2,65,16,128]{3,2,1,0:T(8,128)(2,1)S(1)}, u32[]{:S(2)}) copy-start(bf16[2,65,16,128]{3,2,1,0:T(8,128)(2,1)S(1)} %collective-permute-done.6.refs_6_.refs_7_.refs_18_.refs_19_) | copy-start | bytes 1597444
  55.2 40.9 %collective-permute-start.10 = (bf16[2,65,16,128]{3,2,1,0:T(8,128)(2,1)}, bf16[2,65,16,128]{3,2,1,0:T(8,128)(2,1)S(1)}, u32[]{:S(2)}, u32[]{:S(2)}) collective-permute-start(bf16[2,65,16,128]{3,2,1,0:T(8,128)(2,1)} %get-tuple-element.92), channel_id=1, source_target_pairs={{0,20},{4,16},{24,12},{28,8},{8,24},{12,28},{16,0},{20,4},{1,21},{... | collective-permute-start | bytes 1597448 | tf_op jit(solution)/shard_map/ppermute | solution.py:628
  73.2 8.6 %copy-start.4 = (bf16[2,65,16,128]{3,2,1,0:T(8,128)(2,1)}, bf16[2,65,16,128]{3,2,1,0:T(8,128)(2,1)S(1)}, u32[]{:S(2)}) copy-start(bf16[2,65,16,128]{3,2,1,0:T(8,128)(2,1)S(1)} %collective-permute-done.3.refs_4_.refs_5_.refs_16_.refs_17_) | copy-start | bytes 1597444
  73.2 34.1 %collective-permute-start.9 = (bf16[2,65,16,128]{3,2,1,0:T(8,128)(2,1)}, bf16[2,65,16,128]{3,2,1,0:T(8,128)(2,1)S(1)}, u32[]{:S(2)}, u32[]{:S(2)}) collective-permute-start(bf16[2,65,16,128]{3,2,1,0:T(8,128)(2,1)} %get-tuple-element.91), channel_id=1, source_target_pairs={{0,16},{4,20},{8,24},{12,28},{16,0},{20,4},{24,8},{28,12},{1,17},{... | collective-permute-start | bytes 1597448 | tf_op jit(solution)/shard_map/ppermute | solution.py:628
  73.3 4.7 %copy-start.12 = (bf16[2,65,16,128]{3,2,1,0:T(8,128)(2,1)}, bf16[2,65,16,128]{3,2,1,0:T(8,128)(2,1)S(1)}, u32[]{:S(2)}) copy-start(bf16[2,65,16,128]{3,2,1,0:T(8,128)(2,1)S(1)} %collective-permute-done.14.refs_14_.refs_15_) | copy-start | bytes 1597444
  73.3 34.1 %collective-permute-start.1 = (bf16[2,65,16,128]{3,2,1,0:T(8,128)(2,1)}, bf16[2,65,16,128]{3,2,1,0:T(8,128)(2,1)S(1)}, u32[]{:S(2)}, u32[]{:S(2)}) collective-permute-start(bf16[2,65,16,128]{3,2,1,0:T(8,128)(2,1)} %get-tuple-element.76), channel_id=1, source_target_pairs={{0,4},{4,0},{8,12},{12,8},{16,20},{20,16},{24,28},{28,24},{1,5},{5... | collective-permute-start | bytes 1597448 | tf_op jit(solution)/shard_map/ppermute | solution.py:628
  73.4 4.7 %copy-start.14 = (bf16[2,65,16,128]{3,2,1,0:T(8,128)(2,1)}, bf16[2,65,16,128]{3,2,1,0:T(8,128)(2,1)S(1)}, u32[]{:S(2)}) copy-start(bf16[2,65,16,128]{3,2,1,0:T(8,128)(2,1)S(1)} %collective-permute-done.13.refs_12_.refs_13_) | copy-start | bytes 1597444
  73.4 36.9 %collective-permute-start.7 = (bf16[2,65,16,128]{3,2,1,0:T(8,128)(2,1)}, bf16[2,65,16,128]{3,2,1,0:T(8,128)(2,1)}, u32[]{:S(2)}, u32[]{:S(2)}) collective-permute-start(bf16[2,65,16,128]{3,2,1,0:T(8,128)(2,1)} %get-tuple-element.86), channel_id=1, source_target_pairs={{0,12},{4,8},{24,20},{28,16},{1,13},{5,9},{25,21},{29,17},{2,14},{... | collective-permute-start | bytes 1597448 | tf_op jit(solution)/shard_map/ppermute | solution.py:628
  78.0 34.1 %collective-permute-start.4 = (bf16[2,65,16,128]{3,2,1,0:T(8,128)(2,1)S(1)}, bf16[2,65,16,128]{3,2,1,0:T(8,128)(2,1)}, u32[]{:S(2)}, u32[]{:S(2)}) collective-permute-start(bf16[2,65,16,128]{3,2,1,0:T(8,128)(2,1)S(1)} %copy-done.11), channel_id=1, source_target_pairs={{0,8},{4,12},{24,16},{28,20},{1,9},{5,13},{25,17},{29,21},{2,10},{... | collective-permute-start | bytes 1597448 | tf_op jit(solution)/shard_map/ppermute | solution.py:628
  96.1 16.1 %copy-start.16 = (bf16[2,65,16,128]{3,2,1,0:T(8,128)(2,1)}, bf16[2,65,16,128]{3,2,1,0:T(8,128)(2,1)S(1)}, u32[]{:S(2)}) copy-start(bf16[2,65,16,128]{3,2,1,0:T(8,128)(2,1)S(1)} %collective-permute-done.10.refs_10_.refs_11_) | copy-start | bytes 1597444
  96.1 32.9 %collective-permute-start = (bf16[2,65,16,128]{3,2,1,0:T(8,128)(2,1)}, bf16[2,65,16,128]{3,2,1,0:T(8,128)(2,1)}, u32[]{:S(2)}, u32[]{:S(2)}) collective-permute-start(bf16[2,65,16,128]{3,2,1,0:T(8,128)(2,1)} %get-tuple-element.72), channel_id=1, source_target_pairs={{0,4},{4,0},{8,12},{12,8},{16,20},{20,16},{24,28},{28,24},{1,5},{5... | collective-permute-start | bytes 1597448 | tf_op jit(solution)/shard_map/ppermute | solution.py:628
  107.3 4.8 %copy-start.17 = (bf16[2,65,16,128]{3,2,1,0:T(8,128)(2,1)}, bf16[2,65,16,128]{3,2,1,0:T(8,128)(2,1)S(1)}, u32[]{:S(2)}) copy-start(bf16[2,65,16,128]{3,2,1,0:T(8,128)(2,1)S(1)} %collective-permute-done.9.refs_8_.refs_9_) | copy-start | bytes 1597444
  107.3 47.5 %collective-permute-start.17 = (bf16[2,65,16,128]{3,2,1,0:T(8,128)(2,1)}, bf16[2,65,16,128]{3,2,1,0:T(8,128)(2,1)}, u32[]{:S(2)}, u32[]{:S(2)}) collective-permute-start(bf16[2,65,16,128]{3,2,1,0:T(8,128)(2,1)} %get-tuple-element.115), channel_id=1, source_target_pairs={{0,20},{4,16},{24,12},{28,8},{8,24},{12,28},{16,0},{20,4},{1,21},{... | collective-permute-start | bytes 1597448 | tf_op jit(solution)/shard_map/ppermute | solution.py:628
  107.3 4.8 %copy-start.18 = (bf16[2,65,16,128]{3,2,1,0:T(8,128)(2,1)}, bf16[2,65,16,128]{3,2,1,0:T(8,128)(2,1)S(1)}, u32[]{:S(2)}) copy-start(bf16[2,65,16,128]{3,2,1,0:T(8,128)(2,1)S(1)} %collective-permute-done.1.refs_2_.refs_3_) | copy-start | bytes 1597444
  107.3 49.4 %collective-permute-start.16 = (bf16[2,65,16,128]{3,2,1,0:T(8,128)(2,1)}, bf16[2,65,16,128]{3,2,1,0:T(8,128)(2,1)}, u32[]{:S(2)}, u32[]{:S(2)}) collective-permute-start(bf16[2,65,16,128]{3,2,1,0:T(8,128)(2,1)} %get-tuple-element.114), channel_id=1, source_target_pairs={{0,16},{4,20},{8,24},{12,28},{16,0},{20,4},{24,8},{28,12},{1,17},{... | collective-permute-start | bytes 1597448 | tf_op jit(solution)/shard_map/ppermute | solution.py:628
  118.1 3.9 %copy-start.10 = (bf16[2,65,16,128]{3,2,1,0:T(8,128)(2,1)S(1)}, bf16[2,65,16,128]{3,2,1,0:T(8,128)(2,1)}, u32[]{:S(2)}) copy-start(bf16[2,65,16,128]{3,2,1,0:T(8,128)(2,1)} %get-tuple-element.117) | copy-start | bytes 1597444
  118.1 8.8 %copy-start.9 = (bf16[2,65,16,128]{3,2,1,0:T(8,128)(2,1)S(1)}, bf16[2,65,16,128]{3,2,1,0:T(8,128)(2,1)}, u32[]{:S(2)}) copy-start(bf16[2,65,16,128]{3,2,1,0:T(8,128)(2,1)} %get-tuple-element.116) | copy-start | bytes 1597444
  118.1 29.2 %all-to-all-start = ((bf16[4,2,2,2,128,256]{5,4,3,2,1,0:T(8,128)(2,1)}), bf16[4,2,2,2,128,256]{5,4,3,2,1,0:T(8,128)(2,1)S(1)}, u32[]{:S(2)}, u32[]{:S(2)}) async-start(bf16[4,2,2,2,128,256]{5,4,3,2,1,0:T(8,128)(2,1)} %bitcast.19), calls=%async_computation | async-start | bytes 4194304 | tf_op jit(solution)/shard_map/all_to_all | solution.py:753
  122.0 34.8 %collective-permute-start.19 = (bf16[2,65,16,128]{3,2,1,0:T(8,128)(2,1)S(1)}, bf16[2,65,16,128]{3,2,1,0:T(8,128)(2,1)}, u32[]{:S(2)}, u32[]{:S(2)}) collective-permute-start(bf16[2,65,16,128]{3,2,1,0:T(8,128)(2,1)S(1)} %copy-done.10), channel_id=1, source_target_pairs={{0,12},{4,8},{24,20},{28,16},{1,13},{5,9},{25,21},{29,17},{2,14},{... | collective-permute-start | bytes 1597448 | tf_op jit(solution)/shard_map/ppermute | solution.py:628
  126.9 30.9 %collective-permute-start.18 = (bf16[2,65,16,128]{3,2,1,0:T(8,128)(2,1)S(1)}, bf16[2,65,16,128]{3,2,1,0:T(8,128)(2,1)}, u32[]{:S(2)}, u32[]{:S(2)}) collective-permute-start(bf16[2,65,16,128]{3,2,1,0:T(8,128)(2,1)S(1)} %copy-done.9), channel_id=1, source_target_pairs={{0,8},{4,12},{24,16},{28,20},{1,9},{5,13},{25,17},{29,21},{2,10},{... | collective-permute-start | bytes 1597448 | tf_op jit(solution)/shard_map/ppermute | solution.py:628
  147.3 1.3 copy-start.6
  157.8 44.4 %all-to-all-start.1 = ((bf16[8,6,2,2,32,128]{5,4,3,2,1,0:T(8,128)(2,1)}), bf16[8,6,2,2,32,128]{5,4,3,2,1,0:T(8,128)(2,1)S(1)}, u32[]{:S(2)}, u32[]{:S(2)}) async-start(bf16[8,6,2,2,32,128]{5,4,3,2,1,0:T(8,128)(2,1)} %bitcast.20), calls=%async_computation.1 | async-start | bytes 3145728 | tf_op jit(solution)/shard_map/all_to_all | solution.py:770
  167.8 15.0 %collective-permute-start.20 = (bf16[2,2,2,128,256]{4,3,2,1,0:T(8,128)(2,1)}, bf16[2,2,2,128,256]{4,3,2,1,0:T(8,128)(2,1)S(1)}, u32[]{:S(2)}, u32[]{:S(2)}) collective-permute-start(bf16[2,2,2,128,256]{4,3,2,1,0:T(8,128)(2,1)} %bitcast.24), channel_id=1, source_target_pairs={{0,1},{1,0},{2,3},{3,2},{4,5},{5,4},{6,7},{7,6},{8,9},{9,8},{10,11... | collective-permute-start | bytes 1572872 | tf_op jit(solution)/shard_map/ppermute | solution.py:654
  169.4 25.5 %collective-permute-start.21 = (bf16[2,2,2,128,256]{4,3,2,1,0:T(8,128)(2,1)}, bf16[2,2,2,128,256]{4,3,2,1,0:T(8,128)(2,1)S(1)}, u32[]{:S(2)}, u32[]{:S(2)}) collective-permute-start(bf16[2,2,2,128,256]{4,3,2,1,0:T(8,128)(2,1)} %bitcast.23), channel_id=1, source_target_pairs={{0,2},{1,3},{2,0},{3,1},{4,6},{5,7},{6,4},{7,5},{8,10},{9,11},{10,... | collective-permute-start | bytes 1572872 | tf_op jit(solution)/shard_map/ppermute | solution.py:654
  170.9 24.0 %collective-permute-start.22 = (bf16[2,2,2,128,256]{4,3,2,1,0:T(8,128)(2,1)}, bf16[2,2,2,128,256]{4,3,2,1,0:T(8,128)(2,1)S(1)}, u32[]{:S(2)}, u32[]{:S(2)}) collective-permute-start(bf16[2,2,2,128,256]{4,3,2,1,0:T(8,128)(2,1)} %bitcast.22), channel_id=1, source_target_pairs={{0,3},{1,2},{2,1},{3,0},{4,7},{5,6},{6,5},{7,4},{8,11},{9,10},{10,... | collective-permute-start | bytes 1572872 | tf_op jit(solution)/shard_map/ppermute | solution.py:654
  182.8 12.1 %copy-start.19 = (bf16[2,2,2,128,256]{4,3,2,1,0:T(8,128)(2,1)}, bf16[2,2,2,128,256]{4,3,2,1,0:T(8,128)(2,1)S(1)}, u32[]{:S(2)}) copy-start(bf16[2,2,2,128,256]{4,3,2,1,0:T(8,128)(2,1)S(1)} %collective-permute-done.20.refs_1_) | copy-start | bytes 1572868
  194.9 0.8 copy-start.20
  194.9 1.0 copy-start.21
  202.2 42.7 %copy-start = (bf16[8,6,2,2,32,128]{5,4,3,2,1,0:T(8,128)(2,1)}, bf16[8,6,2,2,32,128]{5,4,3,2,1,0:T(8,128)(2,1)S(1)}, u32[]{:S(2)}) copy-start(bf16[8,6,2,2,32,128]{5,4,3,2,1,0:T(8,128)(2,1)S(1)} %all-to-all-done.1.refs_0_) | copy-start | bytes 4718596

commit v5 on v4

--- a/solution.py
+++ b/solution.py
@@ -766,7 +766,7 @@
             block_len // 2,
         )
         rows = rows.reshape((grid_count, -1) + rows.shape[1:])
-        sent = after([rows], jumps[-1] + enters[-1])[0]
+        sent = rows
         arrived.append(lax.all_to_all(sent, "grid", split_axis=0, concat_axis=0, tiled=True))
     return lay_rows(arrived, z_local)
 

time: 251 us -> 247 us (0.984)
  waiting for transfers between devices: 93.8 us -> 90.7 us
    ppermute x20, waiting for transfers between devices: 53.2 us -> 50.2 us  [send(): return lax.ppermute(value, 'grid', pairs)]
  transfers between devices with their start and end apart: 25 -> 25, of which waited for: 11 -> 9; matrix products, arithmetic and copies ran while one was open for 3% -> 3% of each run, Pallas kernels for 14% -> 14%
where the time goes in v5:
time: 247 us
  waiting for transfers between devices  90.7 us (37%)
  starting transfers between devices  55.3 us (22%)
  Pallas kernels  46.4 us (19%)
  blocking collectives  42.7 us (17%)
  local copies, waits for them, and re-layouts  5.33 us (2%)
  other arithmetic  4.55 us (2%)
    ppermute x20, waiting for transfers between devices, send(): return lax.ppermute(value, 'grid', pairs)  50.2 us
    ppermute x20, starting transfers between devices, send(): return lax.ppermute(value, 'grid', pairs)  44 us
    all_to_all x1, blocking collectives, body(): lax.all_to_all(sent, 'grid', split_axis=0, concat_axis=0, tiled=True)  42.7 us
    ppermute x3, waiting for transfers between devices, exchange(): lax.ppermute(parts[step], axis, [(d, d ^ step) for d in range(count)])  23.5 us
    all_to_all x1, waiting for transfers between devices, body(): lax.all_to_all(along_mid, 'pencil', split_axis=0, concat_axis=0, tiled=True)  17 us
    pallas_call x2, Pallas kernels, transform_long(): pl.pallas_call(long_kernel, grid=(slots,), in_specs=[pl.BlockSpec(memory_...  12.5 us
    pallas_call x2, Pallas kernels, transform_mid(): pl.pallas_call(functools.partial(mid_kernel, first_chunk, pencils if apar...  12.1 us
    pallas_call x2, Pallas kernels, relay(): pl.pallas_call(relay_kernel, grid=(shape[1] // rows,), in_specs=specs * l...  8.8 us
  transfers between devices with their start and end apart: 25, of which 9 were waited for; matrix products, arithmetic and copies ran while one was open for 3% of the time, Pallas kernels for 14%

profile of v5, /device:TPU:0, one launch (start us, length us, event | category | flops | bytes accessed | tf_op | source)
XLA Modules:
  0.0 246.5 jit_solution(13721456533968602604)
XLA Ops:
  1.3 7.1 %transform_z.1 = (bf16[2,65,16,128]{3,2,1,0:T(8,128)(2,1)}, bf16[2,65,16,128]{3,2,1,0:T(8,128)(2,1)}, bf16[2,65,16,128]{3,2,1,0:T(8,128)(2,1)}, bf16[2,65,16,128...) custom-call(s32[1,3]{1,0:T(1,128)} %levels_ref.1, ...), custom_call_target="tpu_custom_call" | custom-call | flops 2147483648 | bytes 16777216 | tf_op jit(solution)/shard_map/transform_z/pallas_call | solution.py:262
  8.4 0.7 collective-permute-start.12
  9.1 0.7 collective-permute-start.11
  9.8 7.0 %collective-permute-start.5 = (bf16[2,65,16,128]{3,2,1,0:T(8,128)(2,1)}, bf16[2,65,16,128]{3,2,1,0:T(8,128)(2,1)S(1)}, u32[]{:S(2)}, u32[]{:S(2)}) collective-permute-start(bf16[2,65,16,128]{3,2,1,0:T(8,128)(2,1)} %get-tuple-element.82), channel_id=1, source_target_pairs={{0,12},{4,8},{8,4},{12,0},{16,28},{20,24},{24,20},{28,16},{1,13},{... | collective-permute-start | bytes 1597448 | tf_op jit(solution)/shard_map/ppermute | solution.py:628
  17.0 0.7 collective-permute-start.8
  17.7 0.6 fusion.11
  18.4 0.7 fusion.12
  19.0 1.4 sine_multiply_fusion.2
  20.4 0.7 collective-permute-start.14
  21.1 0.7 collective-permute-start.13
  21.8 7.7 %collective-permute-done.5.refs_6_.refs_7_.refs_18_.refs_19_ = bf16[2,65,16,128]{3,2,1,0:T(8,128)(2,1)S(1)} collective-permute-done((bf16[2,65,16,128]{3,2,1,0:T(8,128)(2,1)}, bf16[2,65,16,128]{3,2,1,0:T(8,128)(2,1)S(1)}, u32[]{:S(2)}, u32[]{:S(2)}) %collective-permute-start.5) | collective-permute-done | bytes 532512 | tf_op jit(solution)/shard_map/ppermute | solution.py:628
  29.6 12.8 %collective-permute-start.6 = (bf16[2,65,16,128]{3,2,1,0:T(8,128)(2,1)}, bf16[2,65,16,128]{3,2,1,0:T(8,128)(2,1)S(1)}, u32[]{:S(2)}, u32[]{:S(2)}) collective-permute-start(bf16[2,65,16,128]{3,2,1,0:T(8,128)(2,1)} %get-tuple-element.83), channel_id=1, source_target_pairs={{0,12},{4,8},{8,4},{12,0},{16,28},{20,24},{24,20},{28,16},{1,13},{... | collective-permute-start | bytes 1597448 | tf_op jit(solution)/shard_map/ppermute | solution.py:628
  42.4 0.7 collective-permute-start.3
  43.1 1.5 collective-permute-start.15
  44.5 1.2 sine_multiply_fusion.1
  45.8 1.3 sine_multiply_fusion
  47.7 4.5 %relay.2 = (bf16[2,65,16,128]{3,2,1,0:T(8,128)(2,1)}, bf16[2,65,16,128]{3,2,1,0:T(8,128)(2,1)}) custom-call(bf16[2,65,16,128]{3,2,1,0:T(8,128)(2,1)} %get-tuple-element.87.refs_0_.refs_1_.refs_8_, bf16[2,65,16,128]{3,2,1,0:T(8,128)(2,1)} %get-tuple-element.87.refs_0_.refs_1_.refs_8_, bf16[2,65,16,128]{3,2,1,0:T(8,128)(2,1)} %copy-done.5, ...), custom_call_target="tpu_custom_call" | custom-call | bytes 4259840 | tf_op jit(solution)/shard_map/relay/pallas_call | solution.py:334
  52.2 2.9 %collective-permute-done.6.refs_6_.refs_7_.refs_18_.refs_19_ = bf16[2,65,16,128]{3,2,1,0:T(8,128)(2,1)S(1)} collective-permute-done((bf16[2,65,16,128]{3,2,1,0:T(8,128)(2,1)}, bf16[2,65,16,128]{3,2,1,0:T(8,128)(2,1)S(1)}, u32[]{:S(2)}, u32[]{:S(2)}) %collective-permute-start.6) | collective-permute-done | bytes 532512 | tf_op jit(solution)/shard_map/ppermute | solution.py:628
  55.2 1.6 collective-permute-start.10
  56.8 16.5 %collective-permute-done.3.refs_4_.refs_5_.refs_16_.refs_17_ = bf16[2,65,16,128]{3,2,1,0:T(8,128)(2,1)S(1)} collective-permute-done((bf16[2,65,16,128]{3,2,1,0:T(8,128)(2,1)}, bf16[2,65,16,128]{3,2,1,0:T(8,128)(2,1)S(1)}, u32[]{:S(2)}, u32[]{:S(2)}) %collective-permute-start.3) | collective-permute-done | bytes 532512 | tf_op jit(solution)/shard_map/ppermute | solution.py:628
  73.4 4.6 %collective-permute-start.7 = (bf16[2,65,16,128]{3,2,1,0:T(8,128)(2,1)}, bf16[2,65,16,128]{3,2,1,0:T(8,128)(2,1)}, u32[]{:S(2)}, u32[]{:S(2)}) collective-permute-start(bf16[2,65,16,128]{3,2,1,0:T(8,128)(2,1)} %get-tuple-element.84), channel_id=1, source_target_pairs={{0,12},{4,8},{24,20},{28,16},{1,13},{5,9},{25,21},{29,17},{2,14},{... | collective-permute-start | bytes 1597448 | tf_op jit(solution)/shard_map/ppermute | solution.py:628
  78.0 2.1 collective-permute-start.4
  80.1 1.0 copy.16.x_ref
  81.2 0.7 fusion.10
  81.8 4.3 %relay.3 = (bf16[2,65,16,128]{3,2,1,0:T(8,128)(2,1)}, bf16[2,65,16,128]{3,2,1,0:T(8,128)(2,1)}) custom-call(bf16[2,65,16,128]{3,2,1,0:T(8,128)(2,1)} %get-tuple-element.97.refs_0_.refs_1_.refs_8_, bf16[2,65,16,128]{3,2,1,0:T(8,128)(2,1)} %get-tuple-element.97.refs_0_.refs_1_.refs_8_, bf16[2,65,16,128]{3,2,1,0:T(8,128)(2,1)} %collective-permute-done.15.refs_2_.refs_3_, ...), custom_call_target="tpu_custom_call" | custom-call | bytes 4259840 | tf_op jit(solution)/shard_map/relay/pallas_call | solution.py:334
  86.2 9.9 %collective-permute-done.10.refs_10_.refs_11_ = bf16[2,65,16,128]{3,2,1,0:T(8,128)(2,1)S(1)} collective-permute-done((bf16[2,65,16,128]{3,2,1,0:T(8,128)(2,1)}, bf16[2,65,16,128]{3,2,1,0:T(8,128)(2,1)S(1)}, u32[]{:S(2)}, u32[]{:S(2)}) %collective-permute-start.10) | collective-permute-done | bytes 532512 | tf_op jit(solution)/shard_map/ppermute | solution.py:628
  96.1 11.3 %collective-permute-done.9.refs_8_.refs_9_ = bf16[2,65,16,128]{3,2,1,0:T(8,128)(2,1)S(1)} collective-permute-done((bf16[2,65,16,128]{3,2,1,0:T(8,128)(2,1)}, bf16[2,65,16,128]{3,2,1,0:T(8,128)(2,1)S(1)}, u32[]{:S(2)}, u32[]{:S(2)}) %collective-permute-start.9) | collective-permute-done | bytes 532512 | tf_op jit(solution)/shard_map/ppermute | solution.py:628
  107.3 2.9 %collective-permute-start.18 = (bf16[2,65,16,128]{3,2,1,0:T(8,128)(2,1)}, bf16[2,65,16,128]{3,2,1,0:T(8,128)(2,1)}, u32[]{:S(2)}, u32[]{:S(2)}) collective-permute-start(bf16[2,65,16,128]{3,2,1,0:T(8,128)(2,1)} %get-tuple-element.115), channel_id=1, source_target_pairs={{0,16},{4,20},{8,24},{12,28},{16,0},{20,4},{24,8},{28,12},{1,17},{... | collective-permute-start | bytes 1597448 | tf_op jit(solution)/shard_map/ppermute | solution.py:628
  110.3 1.9 collective-permute-done.4.refs_4_.refs_5_
  112.2 5.9 %transform_mid.2 = bf16[4,2,2,2,2,64,256]{6,5,4,3,2,1,0:T(8,128)(2,1)} custom-call(bf16[512,512]{1,0:T(8,128)(2,1)} %constant.68.clone.turn_ref, bf16[2,256,512]{2,1,0:T(8,128)(2,1)} %constant.63.clone.table_ref, bf16[2,65,16,128]{3,2,1,0:T(8,128)(2,1)} %get-tuple-element.102.refs_0_.refs_1_, bf16[2,65,16,128]{3,2,1,0:T(8,128)(2,1)} %get-tuple-element.102.refs_0_.refs_1_, ...), custom_call_target="tpu_custom_call" | custom-call | flops 21810380800 | bytes 7421952 | tf_op jit(solution)/shard_map/transform_mid/pallas_call | solution.py:421
  118.1 3.9 %all-to-all-start = ((bf16[4,2,2,2,128,256]{5,4,3,2,1,0:T(8,128)(2,1)}), bf16[4,2,2,2,128,256]{5,4,3,2,1,0:T(8,128)(2,1)S(1)}, u32[]{:S(2)}, u32[]{:S(2)}) async-start(bf16[4,2,2,2,128,256]{5,4,3,2,1,0:T(8,128)(2,1)} %bitcast.19), calls=%async_computation | async-start | bytes 4194304 | tf_op jit(solution)/shard_map/all_to_all | solution.py:753
  122.0 5.0 %collective-permute-start.17 = (bf16[2,65,16,128]{3,2,1,0:T(8,128)(2,1)S(1)}, bf16[2,65,16,128]{3,2,1,0:T(8,128)(2,1)}, u32[]{:S(2)}, u32[]{:S(2)}) collective-permute-start(bf16[2,65,16,128]{3,2,1,0:T(8,128)(2,1)S(1)} %copy-done.10), channel_id=1, source_target_pairs={{0,12},{4,8},{24,20},{28,16},{1,13},{5,9},{25,21},{29,17},{2,14},{... | collective-permute-start | bytes 1597448 | tf_op jit(solution)/shard_map/ppermute | solution.py:628
  126.9 2.1 collective-permute-start.16
  129.0 1.3 hold.1.z_ref
  130.3 17.0 %all-to-all-done.refs_0_ = bf16[4,2,2,2,128,256]{5,4,3,2,1,0:T(8,128)(2,1)S(1)} async-done(((bf16[4,2,2,2,128,256]{5,4,3,2,1,0:T(8,128)(2,1)}), bf16[4,2,2,2,128,256]{5,4,3,2,1,0:T(8,128)(2,1)S(1)}, u32[]{:S(2)}, u32[]{:S(2)}) %all-to-all-start) | async-done | bytes 2097184 | tf_op jit(solution)/shard_map/all_to_all | solution.py:753
  147.3 1.3 copy-done.6
  148.6 6.2 %transform_long.2 = bf16[48,2,2,32,128]{4,3,2,1,0:T(8,128)(2,1)} custom-call(s32[64]{0:T(128)} %rows_ref.3, f32[2,2]{1,0:T(2,128)} %hold.1.z_ref, f32[2,2,256,1]{3,2,1,0:T(8,128)} %copy.16.x_ref, f32[2,512]{1,0:T(2,128)} %pad_maximum_fusion.y_ref, bf16[1024,512]{1,0:T(8,128)(2,1)} %constant.64.clone.first_ref, bf16[512,1024]{1,0:T(8,128)(2,1)} %constant.65.clone.second_ref, ...), custom_call_target="tpu_custom_call" | custom-call | flops 2147483648 | bytes 9961472 | tf_op jit(solution)/shard_map/transform_long/pallas_call | solution.py:534
  154.8 3.8 %all-to-all-start.1 = ((bf16[8,6,2,2,32,128]{5,4,3,2,1,0:T(8,128)(2,1)}), bf16[8,6,2,2,32,128]{5,4,3,2,1,0:T(8,128)(2,1)S(1)}, u32[]{:S(2)}, u32[]{:S(2)}) async-start(bf16[8,6,2,2,32,128]{5,4,3,2,1,0:T(8,128)(2,1)} %bitcast.20), calls=%async_computation.1 | async-start | bytes 3145728 | tf_op jit(solution)/shard_map/all_to_all | solution.py:770
  158.7 6.1 %transform_mid.3 = (bf16[2,2,2,2,64,256]{5,4,3,2,1,0:T(8,128)(2,1)}, bf16[2,2,2,2,64,256]{5,4,3,2,1,0:T(8,128)(2,1)}, bf16[2,2,2,2,64,256]{5,4,3,2,1,0:T(8,128)(2,1)}, bf16[2,2,2,2,64,256]{5,4,3,2,1,0:T(8,128)(2,1)}) custom-call(bf16[512,512]{1,0:T(8,128)(2,1)} %constant.68.clone.turn_ref, bf16[2,256,512]{2,1,0:T(8,128)(2,1)} %constant.63.clone.table_ref, ...), custom_call_target="tpu_custom_call" | custom-call | flops 21810380800 | bytes 7421952 | tf_op jit(solution)/shard_map/transform_mid/pallas_call | solution.py:421
  164.8 1.5 collective-permute-start.20
  166.3 0.7 collective-permute-start.21
  167.0 1.3 collective-permute-start.22
  168.4 11.4 %collective-permute-done.20.refs_1_ = bf16[2,2,2,128,256]{4,3,2,1,0:T(8,128)(2,1)S(1)} collective-permute-done((bf16[2,2,2,128,256]{4,3,2,1,0:T(8,128)(2,1)}, bf16[2,2,2,128,256]{4,3,2,1,0:T(8,128)(2,1)S(1)}, u32[]{:S(2)}, u32[]{:S(2)}) %collective-permute-start.20) | collective-permute-done | bytes 524320 | tf_op jit(solution)/shard_map/ppermute | solution.py:654
  179.8 12.0 %collective-permute-done.21.refs_2_ = bf16[2,2,2,128,256]{4,3,2,1,0:T(8,128)(2,1)S(1)} collective-permute-done((bf16[2,2,2,128,256]{4,3,2,1,0:T(8,128)(2,1)}, bf16[2,2,2,128,256]{4,3,2,1,0:T(8,128)(2,1)S(1)}, u32[]{:S(2)}, u32[]{:S(2)}) %collective-permute-start.21) | collective-permute-done | bytes 524320 | tf_op jit(solution)/shard_map/ppermute | solution.py:654
  191.9 0.8 copy-done.20
  192.8 6.4 %transform_long.3 = bf16[48,2,2,32,128]{4,3,2,1,0:T(8,128)(2,1)} custom-call(s32[64]{0:T(128)} %rows_ref.3, f32[2,2]{1,0:T(2,128)} %get-tuple-element.131.z_ref, f32[2,2,256,1]{3,2,1,0:T(8,128)} %copy.16.x_ref, f32[2,512]{1,0:T(2,128)} %pad_maximum_fusion.y_ref, bf16[1024,512]{1,0:T(8,128)(2,1)} %constant.64.clone.first_ref, ...), custom_call_target="tpu_custom_call" | custom-call | flops 2147483648 | bytes 9961472 | tf_op jit(solution)/shard_map/transform_long/pallas_call | solution.py:534
  199.2 42.7 %all_to_all.15.refs_1_ = bf16[8,6,2,2,32,128]{5,4,3,2,1,0:T(8,128)(2,1)} all-to-all(bf16[8,6,2,2,32,128]{5,4,3,2,1,0:T(8,128)(2,1)} %bitcast.21), channel_id=1, replica_groups=mesh['grid'=8,'pencil'=4] {'grid'}, dimensions={0} | all-to-all | bytes 3145728 | tf_op jit(solution)/shard_map/all_to_all | solution.py:770
  241.9 4.7 %lay_rows.1 = f32[6,2,32,4096]{3,2,1,0:T(8,128)} custom-call(bf16[256,256]{1,0:T(8,128)(2,1)} %constant.69.clone.turn_ref, bf16[8,6,2,2,32,128]{5,4,3,2,1,0:T(8,128)(2,1)} %copy-done, bf16[8,6,2,2,32,128]{5,4,3,2,1,0:T(8,128)(2,1)} %all_to_all.15.refs_1_), custom_call_target="tpu_custom_call" | custom-call | bytes 9437184 | tf_op jit(solution)/shard_map/lay_rows/pallas_call | solution.py:595
  (66 shorter events, 1.2 us)
Async XLA Ops:
  1.3 16.4 %copy-start.7 = (f32[3]{0:T(128)S(1)}, f32[3]{0:T(128)}, u32[]{:S(2)}) copy-start(f32[3]{0:T(128)} %param.21) | copy-start | bytes 40
  1.3 17.1 %copy-start.8 = (f32[3]{0:T(128)S(1)}, f32[3]{0:T(128)}, u32[]{:S(2)}) copy-start(f32[3]{0:T(128)} %param.20) | copy-start | bytes 40
  8.4 12.0 %collective-permute-start.12 = (bf16[2,65,16,128]{3,2,1,0:T(8,128)(2,1)}, bf16[2,65,16,128]{3,2,1,0:T(8,128)(2,1)S(1)}, u32[]{:S(2)}, u32[]{:S(2)}) collective-permute-start(bf16[2,65,16,128]{3,2,1,0:T(8,128)(2,1)} %get-tuple-element.84), channel_id=1, source_target_pairs={{8,20},{20,8},{12,16},{16,12},{9,21},{21,9},{13,17},{17,13},{10,22... | collective-permute-start | bytes 1597448 | tf_op jit(solution)/shard_map/ppermute | solution.py:628
  9.1 12.0 %collective-permute-start.11 = (bf16[2,65,16,128]{3,2,1,0:T(8,128)(2,1)}, bf16[2,65,16,128]{3,2,1,0:T(8,128)(2,1)S(1)}, u32[]{:S(2)}, u32[]{:S(2)}) collective-permute-start(bf16[2,65,16,128]{3,2,1,0:T(8,128)(2,1)} %get-tuple-element.79), channel_id=1, source_target_pairs={{8,16},{16,8},{12,20},{20,12},{9,17},{17,9},{13,21},{21,13},{10,18... | collective-permute-start | bytes 1597448 | tf_op jit(solution)/shard_map/ppermute | solution.py:628
  9.8 19.7 %collective-permute-start.5 = (bf16[2,65,16,128]{3,2,1,0:T(8,128)(2,1)}, bf16[2,65,16,128]{3,2,1,0:T(8,128)(2,1)S(1)}, u32[]{:S(2)}, u32[]{:S(2)}) collective-permute-start(bf16[2,65,16,128]{3,2,1,0:T(8,128)(2,1)} %get-tuple-element.82), channel_id=1, source_target_pairs={{0,12},{4,8},{8,4},{12,0},{16,28},{20,24},{24,20},{28,16},{1,13},{... | collective-permute-start | bytes 1597448 | tf_op jit(solution)/shard_map/ppermute | solution.py:628
  16.8 25.6 %collective-permute-start.2 = (bf16[2,65,16,128]{3,2,1,0:T(8,128)(2,1)}, bf16[2,65,16,128]{3,2,1,0:T(8,128)(2,1)S(1)}, u32[]{:S(2)}, u32[]{:S(2)}) collective-permute-start(bf16[2,65,16,128]{3,2,1,0:T(8,128)(2,1)} %get-tuple-element.77), channel_id=1, source_target_pairs={{0,8},{4,12},{8,0},{12,4},{16,24},{20,28},{24,16},{28,20},{1,9},{5... | collective-permute-start | bytes 1597448 | tf_op jit(solution)/shard_map/ppermute | solution.py:628
  17.0 26.0 %collective-permute-start.8 = (bf16[2,65,16,128]{3,2,1,0:T(8,128)(2,1)}, bf16[2,65,16,128]{3,2,1,0:T(8,128)(2,1)S(1)}, u32[]{:S(2)}, u32[]{:S(2)}) collective-permute-start(bf16[2,65,16,128]{3,2,1,0:T(8,128)(2,1)} %get-tuple-element.88.refs_9_), channel_id=1, source_target_pairs={{8,12},{12,8},{16,20},{20,16},{9,13},{13,9},{17,21},{21,17},{10,14... | collective-permute-start | bytes 1597448 | tf_op jit(solution)/shard_map/ppermute | solution.py:628
  20.4 9.2 %copy-start.13 = (bf16[2,65,16,128]{3,2,1,0:T(8,128)(2,1)}, bf16[2,65,16,128]{3,2,1,0:T(8,128)(2,1)S(1)}, u32[]{:S(2)}) copy-start(bf16[2,65,16,128]{3,2,1,0:T(8,128)(2,1)S(1)} %collective-permute-done.12.refs_14_.refs_15_) | copy-start | bytes 1597444
  20.4 52.8 %collective-permute-start.14 = (bf16[2,65,16,128]{3,2,1,0:T(8,128)(2,1)}, bf16[2,65,16,128]{3,2,1,0:T(8,128)(2,1)S(1)}, u32[]{:S(2)}, u32[]{:S(2)}) collective-permute-start(bf16[2,65,16,128]{3,2,1,0:T(8,128)(2,1)} %get-tuple-element.114), channel_id=1, source_target_pairs={{8,20},{20,8},{12,16},{16,12},{9,21},{21,9},{13,17},{17,13},{10,22... | collective-permute-start | bytes 1597448 | tf_op jit(solution)/shard_map/ppermute | solution.py:628
  21.1 23.4 %copy-start.15 = (bf16[2,65,16,128]{3,2,1,0:T(8,128)(2,1)}, bf16[2,65,16,128]{3,2,1,0:T(8,128)(2,1)S(1)}, u32[]{:S(2)}) copy-start(bf16[2,65,16,128]{3,2,1,0:T(8,128)(2,1)S(1)} %collective-permute-done.11.refs_12_.refs_13_) | copy-start | bytes 1597444
  21.1 52.2 %collective-permute-start.13 = (bf16[2,65,16,128]{3,2,1,0:T(8,128)(2,1)}, bf16[2,65,16,128]{3,2,1,0:T(8,128)(2,1)S(1)}, u32[]{:S(2)}, u32[]{:S(2)}) collective-permute-start(bf16[2,65,16,128]{3,2,1,0:T(8,128)(2,1)} %get-tuple-element.113), channel_id=1, source_target_pairs={{8,16},{16,8},{12,20},{20,12},{9,17},{17,9},{13,21},{21,13},{10,18... | collective-permute-start | bytes 1597448 | tf_op jit(solution)/shard_map/ppermute | solution.py:628
  29.6 18.2 %copy-start.1 = (bf16[2,65,16,128]{3,2,1,0:T(8,128)(2,1)}, bf16[2,65,16,128]{3,2,1,0:T(8,128)(2,1)S(1)}, u32[]{:S(2)}) copy-start(bf16[2,65,16,128]{3,2,1,0:T(8,128)(2,1)S(1)} %collective-permute-done.5.refs_6_.refs_7_.refs_18_.refs_19_) | copy-start | bytes 1597444
  29.6 25.6 %collective-permute-start.6 = (bf16[2,65,16,128]{3,2,1,0:T(8,128)(2,1)}, bf16[2,65,16,128]{3,2,1,0:T(8,128)(2,1)S(1)}, u32[]{:S(2)}, u32[]{:S(2)}) collective-permute-start(bf16[2,65,16,128]{3,2,1,0:T(8,128)(2,1)} %get-tuple-element.83), channel_id=1, source_target_pairs={{0,12},{4,8},{8,4},{12,0},{16,28},{20,24},{24,20},{28,16},{1,13},{... | collective-permute-start | bytes 1597448 | tf_op jit(solution)/shard_map/ppermute | solution.py:628
  42.4 5.4 %copy-start.3 = (bf16[2,65,16,128]{3,2,1,0:T(8,128)(2,1)}, bf16[2,65,16,128]{3,2,1,0:T(8,128)(2,1)S(1)}, u32[]{:S(2)}) copy-start(bf16[2,65,16,128]{3,2,1,0:T(8,128)(2,1)S(1)} %collective-permute-done.2.refs_4_.refs_5_.refs_16_.refs_17_) | copy-start | bytes 1597444
  42.4 30.9 %collective-permute-start.3 = (bf16[2,65,16,128]{3,2,1,0:T(8,128)(2,1)}, bf16[2,65,16,128]{3,2,1,0:T(8,128)(2,1)S(1)}, u32[]{:S(2)}, u32[]{:S(2)}) collective-permute-start(bf16[2,65,16,128]{3,2,1,0:T(8,128)(2,1)} %get-tuple-element.78), channel_id=1, source_target_pairs={{0,8},{4,12},{8,0},{12,4},{16,24},{20,28},{24,16},{28,20},{1,9},{5... | collective-permute-start | bytes 1597448 | tf_op jit(solution)/shard_map/ppermute | solution.py:628
  43.1 4.7 %copy-start.5 = (bf16[2,65,16,128]{3,2,1,0:T(8,128)(2,1)}, bf16[2,65,16,128]{3,2,1,0:T(8,128)(2,1)S(1)}, u32[]{:S(2)}) copy-start(bf16[2,65,16,128]{3,2,1,0:T(8,128)(2,1)S(1)} %collective-permute-done.8.refs_2_.refs_3_) | copy-start | bytes 1597444
  43.1 34.9 %collective-permute-start.15 = (bf16[2,65,16,128]{3,2,1,0:T(8,128)(2,1)}, bf16[2,65,16,128]{3,2,1,0:T(8,128)(2,1)}, u32[]{:S(2)}, u32[]{:S(2)}) collective-permute-start(bf16[2,65,16,128]{3,2,1,0:T(8,128)(2,1)} %get-tuple-element.99.refs_9_), channel_id=1, source_target_pairs={{8,12},{12,8},{16,20},{20,16},{9,13},{13,9},{17,21},{21,17},{10,14... | collective-permute-start | bytes 1597448 | tf_op jit(solution)/shard_map/ppermute | solution.py:628
  47.7 30.3 %copy-start.11 = (bf16[2,65,16,128]{3,2,1,0:T(8,128)(2,1)S(1)}, bf16[2,65,16,128]{3,2,1,0:T(8,128)(2,1)}, u32[]{:S(2)}) copy-start(bf16[2,65,16,128]{3,2,1,0:T(8,128)(2,1)} %get-tuple-element.79) | copy-start | bytes 1597444
  55.2 26.7 %copy-start.2 = (bf16[2,65,16,128]{3,2,1,0:T(8,128)(2,1)}, bf16[2,65,16,128]{3,2,1,0:T(8,128)(2,1)S(1)}, u32[]{:S(2)}) copy-start(bf16[2,65,16,128]{3,2,1,0:T(8,128)(2,1)S(1)} %collective-permute-done.6.refs_6_.refs_7_.refs_18_.refs_19_) | copy-start | bytes 1597444
  55.2 40.9 %collective-permute-start.10 = (bf16[2,65,16,128]{3,2,1,0:T(8,128)(2,1)}, bf16[2,65,16,128]{3,2,1,0:T(8,128)(2,1)S(1)}, u32[]{:S(2)}, u32[]{:S(2)}) collective-permute-start(bf16[2,65,16,128]{3,2,1,0:T(8,128)(2,1)} %get-tuple-element.90), channel_id=1, source_target_pairs={{0,20},{4,16},{24,12},{28,8},{8,24},{12,28},{16,0},{20,4},{1,21},{... | collective-permute-start | bytes 1597448 | tf_op jit(solution)/shard_map/ppermute | solution.py:628
  73.2 8.6 %copy-start.4 = (bf16[2,65,16,128]{3,2,1,0:T(8,128)(2,1)}, bf16[2,65,16,128]{3,2,1,0:T(8,128)(2,1)S(1)}, u32[]{:S(2)}) copy-start(bf16[2,65,16,128]{3,2,1,0:T(8,128)(2,1)S(1)} %collective-permute-done.3.refs_4_.refs_5_.refs_16_.refs_17_) | copy-start | bytes 1597444
  73.2 34.1 %collective-permute-start.9 = (bf16[2,65,16,128]{3,2,1,0:T(8,128)(2,1)}, bf16[2,65,16,128]{3,2,1,0:T(8,128)(2,1)S(1)}, u32[]{:S(2)}, u32[]{:S(2)}) collective-permute-start(bf16[2,65,16,128]{3,2,1,0:T(8,128)(2,1)} %get-tuple-element.89), channel_id=1, source_target_pairs={{0,16},{4,20},{8,24},{12,28},{16,0},{20,4},{24,8},{28,12},{1,17},{... | collective-permute-start | bytes 1597448 | tf_op jit(solution)/shard_map/ppermute | solution.py:628
  73.3 4.7 %copy-start.12 = (bf16[2,65,16,128]{3,2,1,0:T(8,128)(2,1)}, bf16[2,65,16,128]{3,2,1,0:T(8,128)(2,1)S(1)}, u32[]{:S(2)}) copy-start(bf16[2,65,16,128]{3,2,1,0:T(8,128)(2,1)S(1)} %collective-permute-done.14.refs_14_.refs_15_) | copy-start | bytes 1597444
  73.3 34.1 %collective-permute-start.1 = (bf16[2,65,16,128]{3,2,1,0:T(8,128)(2,1)}, bf16[2,65,16,128]{3,2,1,0:T(8,128)(2,1)S(1)}, u32[]{:S(2)}, u32[]{:S(2)}) collective-permute-start(bf16[2,65,16,128]{3,2,1,0:T(8,128)(2,1)} %get-tuple-element.74), channel_id=1, source_target_pairs={{0,4},{4,0},{8,12},{12,8},{16,20},{20,16},{24,28},{28,24},{1,5},{5... | collective-permute-start | bytes 1597448 | tf_op jit(solution)/shard_map/ppermute | solution.py:628
  73.4 4.7 %copy-start.14 = (bf16[2,65,16,128]{3,2,1,0:T(8,128)(2,1)}, bf16[2,65,16,128]{3,2,1,0:T(8,128)(2,1)S(1)}, u32[]{:S(2)}) copy-start(bf16[2,65,16,128]{3,2,1,0:T(8,128)(2,1)S(1)} %collective-permute-done.13.refs_12_.refs_13_) | copy-start | bytes 1597444
  73.4 36.9 %collective-permute-start.7 = (bf16[2,65,16,128]{3,2,1,0:T(8,128)(2,1)}, bf16[2,65,16,128]{3,2,1,0:T(8,128)(2,1)}, u32[]{:S(2)}, u32[]{:S(2)}) collective-permute-start(bf16[2,65,16,128]{3,2,1,0:T(8,128)(2,1)} %get-tuple-element.84), channel_id=1, source_target_pairs={{0,12},{4,8},{24,20},{28,16},{1,13},{5,9},{25,21},{29,17},{2,14},{... | collective-permute-start | bytes 1597448 | tf_op jit(solution)/shard_map/ppermute | solution.py:628
  78.0 34.1 %collective-permute-start.4 = (bf16[2,65,16,128]{3,2,1,0:T(8,128)(2,1)S(1)}, bf16[2,65,16,128]{3,2,1,0:T(8,128)(2,1)}, u32[]{:S(2)}, u32[]{:S(2)}) collective-permute-start(bf16[2,65,16,128]{3,2,1,0:T(8,128)(2,1)S(1)} %copy-done.11), channel_id=1, source_target_pairs={{0,8},{4,12},{24,16},{28,20},{1,9},{5,13},{25,17},{29,21},{2,10},{... | collective-permute-start | bytes 1597448 | tf_op jit(solution)/shard_map/ppermute | solution.py:628
  96.1 16.1 %copy-start.16 = (bf16[2,65,16,128]{3,2,1,0:T(8,128)(2,1)}, bf16[2,65,16,128]{3,2,1,0:T(8,128)(2,1)S(1)}, u32[]{:S(2)}) copy-start(bf16[2,65,16,128]{3,2,1,0:T(8,128)(2,1)S(1)} %collective-permute-done.10.refs_10_.refs_11_) | copy-start | bytes 1597444
  96.1 32.9 %collective-permute-start = (bf16[2,65,16,128]{3,2,1,0:T(8,128)(2,1)}, bf16[2,65,16,128]{3,2,1,0:T(8,128)(2,1)}, u32[]{:S(2)}, u32[]{:S(2)}) collective-permute-start(bf16[2,65,16,128]{3,2,1,0:T(8,128)(2,1)} %get-tuple-element.70), channel_id=1, source_target_pairs={{0,4},{4,0},{8,12},{12,8},{16,20},{20,16},{24,28},{28,24},{1,5},{5... | collective-permute-start | bytes 1597448 | tf_op jit(solution)/shard_map/ppermute | solution.py:628
  107.3 4.8 %copy-start.17 = (bf16[2,65,16,128]{3,2,1,0:T(8,128)(2,1)}, bf16[2,65,16,128]{3,2,1,0:T(8,128)(2,1)S(1)}, u32[]{:S(2)}) copy-start(bf16[2,65,16,128]{3,2,1,0:T(8,128)(2,1)S(1)} %collective-permute-done.9.refs_8_.refs_9_) | copy-start | bytes 1597444
  107.3 51.3 %collective-permute-start.19 = (bf16[2,65,16,128]{3,2,1,0:T(8,128)(2,1)}, bf16[2,65,16,128]{3,2,1,0:T(8,128)(2,1)}, u32[]{:S(2)}, u32[]{:S(2)}) collective-permute-start(bf16[2,65,16,128]{3,2,1,0:T(8,128)(2,1)} %get-tuple-element.116), channel_id=1, source_target_pairs={{0,20},{4,16},{24,12},{28,8},{8,24},{12,28},{16,0},{20,4},{1,21},{... | collective-permute-start | bytes 1597448 | tf_op jit(solution)/shard_map/ppermute | solution.py:628
  107.3 4.8 %copy-start.18 = (bf16[2,65,16,128]{3,2,1,0:T(8,128)(2,1)}, bf16[2,65,16,128]{3,2,1,0:T(8,128)(2,1)S(1)}, u32[]{:S(2)}) copy-start(bf16[2,65,16,128]{3,2,1,0:T(8,128)(2,1)S(1)} %collective-permute-done.1.refs_2_.refs_3_) | copy-start | bytes 1597444
  107.3 51.3 %collective-permute-start.18 = (bf16[2,65,16,128]{3,2,1,0:T(8,128)(2,1)}, bf16[2,65,16,128]{3,2,1,0:T(8,128)(2,1)}, u32[]{:S(2)}, u32[]{:S(2)}) collective-permute-start(bf16[2,65,16,128]{3,2,1,0:T(8,128)(2,1)} %get-tuple-element.115), channel_id=1, source_target_pairs={{0,16},{4,20},{8,24},{12,28},{16,0},{20,4},{24,8},{28,12},{1,17},{... | collective-permute-start | bytes 1597448 | tf_op jit(solution)/shard_map/ppermute | solution.py:628
  118.1 3.9 %copy-start.10 = (bf16[2,65,16,128]{3,2,1,0:T(8,128)(2,1)S(1)}, bf16[2,65,16,128]{3,2,1,0:T(8,128)(2,1)}, u32[]{:S(2)}) copy-start(bf16[2,65,16,128]{3,2,1,0:T(8,128)(2,1)} %get-tuple-element.114) | copy-start | bytes 1597444
  118.1 8.8 %copy-start.9 = (bf16[2,65,16,128]{3,2,1,0:T(8,128)(2,1)S(1)}, bf16[2,65,16,128]{3,2,1,0:T(8,128)(2,1)}, u32[]{:S(2)}) copy-start(bf16[2,65,16,128]{3,2,1,0:T(8,128)(2,1)} %get-tuple-element.113) | copy-start | bytes 1597444
  118.1 29.2 %all-to-all-start = ((bf16[4,2,2,2,128,256]{5,4,3,2,1,0:T(8,128)(2,1)}), bf16[4,2,2,2,128,256]{5,4,3,2,1,0:T(8,128)(2,1)S(1)}, u32[]{:S(2)}, u32[]{:S(2)}) async-start(bf16[4,2,2,2,128,256]{5,4,3,2,1,0:T(8,128)(2,1)} %bitcast.19), calls=%async_computation | async-start | bytes 4194304 | tf_op jit(solution)/shard_map/all_to_all | solution.py:753
  122.0 36.7 %collective-permute-start.17 = (bf16[2,65,16,128]{3,2,1,0:T(8,128)(2,1)S(1)}, bf16[2,65,16,128]{3,2,1,0:T(8,128)(2,1)}, u32[]{:S(2)}, u32[]{:S(2)}) collective-permute-start(bf16[2,65,16,128]{3,2,1,0:T(8,128)(2,1)S(1)} %copy-done.10), channel_id=1, source_target_pairs={{0,12},{4,8},{24,20},{28,16},{1,13},{5,9},{25,21},{29,17},{2,14},{... | collective-permute-start | bytes 1597448 | tf_op jit(solution)/shard_map/ppermute | solution.py:628
  126.9 31.8 %collective-permute-start.16 = (bf16[2,65,16,128]{3,2,1,0:T(8,128)(2,1)S(1)}, bf16[2,65,16,128]{3,2,1,0:T(8,128)(2,1)}, u32[]{:S(2)}, u32[]{:S(2)}) collective-permute-start(bf16[2,65,16,128]{3,2,1,0:T(8,128)(2,1)S(1)} %copy-done.9), channel_id=1, source_target_pairs={{0,8},{4,12},{24,16},{28,20},{1,9},{5,13},{25,17},{29,21},{2,10},{... | collective-permute-start | bytes 1597448 | tf_op jit(solution)/shard_map/ppermute | solution.py:628
  147.3 1.3 copy-start.6
  154.8 44.4 %all-to-all-start.1 = ((bf16[8,6,2,2,32,128]{5,4,3,2,1,0:T(8,128)(2,1)}), bf16[8,6,2,2,32,128]{5,4,3,2,1,0:T(8,128)(2,1)S(1)}, u32[]{:S(2)}, u32[]{:S(2)}) async-start(bf16[8,6,2,2,32,128]{5,4,3,2,1,0:T(8,128)(2,1)} %bitcast.20), calls=%async_computation.1 | async-start | bytes 3145728 | tf_op jit(solution)/shard_map/all_to_all | solution.py:770
  164.8 15.0 %collective-permute-start.20 = (bf16[2,2,2,128,256]{4,3,2,1,0:T(8,128)(2,1)}, bf16[2,2,2,128,256]{4,3,2,1,0:T(8,128)(2,1)S(1)}, u32[]{:S(2)}, u32[]{:S(2)}) collective-permute-start(bf16[2,2,2,128,256]{4,3,2,1,0:T(8,128)(2,1)} %bitcast.24), channel_id=1, source_target_pairs={{0,1},{1,0},{2,3},{3,2},{4,5},{5,4},{6,7},{7,6},{8,9},{9,8},{10,11... | collective-permute-start | bytes 1572872 | tf_op jit(solution)/shard_map/ppermute | solution.py:654
  166.3 25.5 %collective-permute-start.21 = (bf16[2,2,2,128,256]{4,3,2,1,0:T(8,128)(2,1)}, bf16[2,2,2,128,256]{4,3,2,1,0:T(8,128)(2,1)S(1)}, u32[]{:S(2)}, u32[]{:S(2)}) collective-permute-start(bf16[2,2,2,128,256]{4,3,2,1,0:T(8,128)(2,1)} %bitcast.23), channel_id=1, source_target_pairs={{0,2},{1,3},{2,0},{3,1},{4,6},{5,7},{6,4},{7,5},{8,10},{9,11},{10,... | collective-permute-start | bytes 1572872 | tf_op jit(solution)/shard_map/ppermute | solution.py:654
  167.0 24.8 %collective-permute-start.22 = (bf16[2,2,2,128,256]{4,3,2,1,0:T(8,128)(2,1)}, bf16[2,2,2,128,256]{4,3,2,1,0:T(8,128)(2,1)S(1)}, u32[]{:S(2)}, u32[]{:S(2)}) collective-permute-start(bf16[2,2,2,128,256]{4,3,2,1,0:T(8,128)(2,1)} %bitcast.22), channel_id=1, source_target_pairs={{0,3},{1,2},{2,1},{3,0},{4,7},{5,6},{6,5},{7,4},{8,11},{9,10},{10,... | collective-permute-start | bytes 1572872 | tf_op jit(solution)/shard_map/ppermute | solution.py:654
  179.8 12.0 %copy-start.19 = (bf16[2,2,2,128,256]{4,3,2,1,0:T(8,128)(2,1)}, bf16[2,2,2,128,256]{4,3,2,1,0:T(8,128)(2,1)S(1)}, u32[]{:S(2)}) copy-start(bf16[2,2,2,128,256]{4,3,2,1,0:T(8,128)(2,1)S(1)} %collective-permute-done.20.refs_1_) | copy-start | bytes 1572868
  191.8 0.8 copy-start.20
  191.8 1.0 copy-start.21
  199.2 42.7 %copy-start = (bf16[8,6,2,2,32,128]{5,4,3,2,1,0:T(8,128)(2,1)}, bf16[8,6,2,2,32,128]{5,4,3,2,1,0:T(8,128)(2,1)S(1)}, u32[]{:S(2)}) copy-start(bf16[8,6,2,2,32,128]{5,4,3,2,1,0:T(8,128)(2,1)S(1)} %all-to-all-done.1.refs_0_) | copy-start | bytes 4718596

commit v6 on v5

--- a/solution.py
+++ b/solution.py
@@ -12,7 +12,7 @@
 
 CHUNKS = 2
 MID_COST = 40
-HOLD_COST = 100_000_000_000
+HOLD_COST = 1000_000_000_000
 ROWS_PER_STEP = 3
 VMEM_LIMIT = 56 * 1024 * 1024
 
@@ -546,7 +546,7 @@
         scratch_shapes=scratch,
         out_specs=pl.BlockSpec((row_count, 1, 2, pairs, 4 * pairs), lambda i: (0, i, 0, 0, 0)),
         out_shape=jax.ShapeDtypeStruct(shape, jnp.bfloat16),
-        compiler_params=pltpu.CompilerParams(vmem_limit_bytes=VMEM_LIMIT),
+        compiler_params=pltpu.CompilerParams(vmem_limit_bytes=20 * 1024 * 1024),
         cost_estimate=pl.CostEstimate(
             flops=2 * classes * slots * depth * depth * mid_len,
             bytes_accessed=4 * slots * math.prod(block) + 2 * math.prod(shape) + 4 * depth * depth,
@@ -600,7 +600,7 @@
         * len(sources),
         out_specs=pl.BlockSpec((ROWS_PER_STEP, parts, z_local, pairs * span), lambda i: (i, 0, 0, 0)),
         out_shape=jax.ShapeDtypeStruct((rows, parts, z_local, pairs * span), jnp.float32),
-        compiler_params=pltpu.CompilerParams(vmem_limit_bytes=VMEM_LIMIT),
+        compiler_params=pltpu.CompilerParams(vmem_limit_bytes=20 * 1024 * 1024),
         cost_estimate=pl.CostEstimate(
             flops=0, bytes_accessed=6 * len(sources) * sources[0].size, transcendentals=0
         ),
@@ -732,7 +732,7 @@
         sums.append(relay([third[0], got[2], got[0], got[1]], third))
     cores = [send(units[chunk][7], CORES) for chunk in range(CHUNKS)]
     jumps = [send_jump(sums[0], None)]
-    enters = [send_enter(units[0], early[-1][:2])]
+    enters = [send_enter(units[0], early[0][3:])]
     arrived = []
     rows = None
     for chunk in range(CHUNKS):

time: 247 us -> 242 us (0.980)
  waiting for transfers between devices: 90.7 us -> 81.6 us
  starting transfers between devices: 55.3 us -> 62.8 us
  Pallas kernels: 46.4 us -> 42.8 us
    ppermute x20, starting transfers between devices: 44 us -> 50.4 us  [send(): return lax.ppermute(value, 'grid', pairs)]
    ppermute x20, waiting for transfers between devices: 50.2 us -> 45.4 us  [send(): return lax.ppermute(value, 'grid', pairs)]
    pallas_call x2, Pallas kernels: 12.5 us -> 9.58 us  [transform_long(): pl.pallas_call(long_kernel, grid=(slots,), in_specs=[pl.BlockSpec(memory_...]
    all_to_all x1, waiting for transfers between devices: 17 us -> 14.2 us  [body(): lax.all_to_all(along_mid, 'pencil', split_axis=0, concat_axis=0, tiled=True)]
  transfers between devices with their start and end apart: 25 -> 25, of which waited for: 9 -> 10; matrix products, arithmetic and copies ran while one was open for 3% -> 3% of each run, Pallas kernels for 14% -> 13%
where the time goes in v6:
time: 242 us; the launch traced here: 241 us
  waiting for transfers between devices  81.6 us (34%)
  starting transfers between devices  62.8 us (26%)
  Pallas kernels  42.8 us (18%)
  blocking collectives  42.5 us (18%)
  local copies, waits for them, and re-layouts  5.47 us (2%)
  other arithmetic  4.15 us (2%)
    ppermute x20, starting transfers between devices, send(): return lax.ppermute(value, 'grid', pairs)  50.4 us
    ppermute x20, waiting for transfers between devices, send(): return lax.ppermute(value, 'grid', pairs)  45.4 us
    all_to_all x1, blocking collectives, body(): lax.all_to_all(sent, 'grid', split_axis=0, concat_axis=0, tiled=True)  42.5 us
    ppermute x3, waiting for transfers between devices, exchange(): lax.ppermute(parts[step], axis, [(d, d ^ step) for d in range(count)])  22 us
    all_to_all x1, waiting for transfers between devices, body(): lax.all_to_all(along_mid, 'pencil', split_axis=0, concat_axis=0, tiled=True)  14.2 us
    pallas_call x2, Pallas kernels, transform_mid(): pl.pallas_call(functools.partial(mid_kernel, first_chunk, pencils if apar...  12.2 us
    pallas_call x2, Pallas kernels, transform_long(): pl.pallas_call(long_kernel, grid=(slots,), in_specs=[pl.BlockSpec(memory_...  9.58 us
    pallas_call x2, Pallas kernels, relay(): pl.pallas_call(relay_kernel, grid=(shape[1] // rows,), in_specs=specs * l...  8.98 us
  transfers between devices with their start and end apart: 25, of which 10 were waited for; matrix products, arithmetic and copies ran while one was open for 3% of the time, Pallas kernels for 13%

profile of v6, /device:TPU:0, one launch (start us, length us, event | category | flops | bytes accessed | tf_op | source)
XLA Modules:
  0.0 240.9 jit_solution(9898857570549838940)
XLA Ops:
  1.3 7.1 %transform_z.1 = (bf16[2,65,16,128]{3,2,1,0:T(8,128)(2,1)}, bf16[2,65,16,128]{3,2,1,0:T(8,128)(2,1)}, bf16[2,65,16,128]{3,2,1,0:T(8,128)(2,1)}, bf16[2,65,16,128...) custom-call(s32[1,3]{1,0:T(1,128)} %levels_ref.1, ...), custom_call_target="tpu_custom_call" | custom-call | flops 2147483648 | bytes 16777216 | tf_op jit(solution)/shard_map/transform_z/pallas_call | solution.py:262
  8.4 0.7 collective-permute-start.4
  9.1 0.7 collective-permute-start.2
  9.8 7.1 %collective-permute-start.7 = (bf16[2,65,16,128]{3,2,1,0:T(8,128)(2,1)}, bf16[2,65,16,128]{3,2,1,0:T(8,128)(2,1)S(1)}, u32[]{:S(2)}, u32[]{:S(2)}) collective-permute-start(bf16[2,65,16,128]{3,2,1,0:T(8,128)(2,1)} %get-tuple-element.82), channel_id=1, source_target_pairs={{0,8},{4,12},{8,0},{12,4},{16,24},{20,28},{24,16},{28,20},{1,9},{5... | collective-permute-start | bytes 1597448 | tf_op jit(solution)/shard_map/ppermute | solution.py:628
  17.0 0.7 collective-permute-start.6
  17.7 0.6 fusion.11
  18.3 0.7 fusion.12
  19.0 1.4 sine_multiply_fusion.2
  20.4 0.7 collective-permute-start.12
  21.1 0.7 collective-permute-start.11
  21.8 8.2 %collective-permute-done.7.refs_4_.refs_5_.refs_16_.refs_17_ = bf16[2,65,16,128]{3,2,1,0:T(8,128)(2,1)S(1)} collective-permute-done((bf16[2,65,16,128]{3,2,1,0:T(8,128)(2,1)}, bf16[2,65,16,128]{3,2,1,0:T(8,128)(2,1)S(1)}, u32[]{:S(2)}, u32[]{:S(2)}) %collective-permute-start.7) | collective-permute-done | bytes 532512 | tf_op jit(solution)/shard_map/ppermute | solution.py:628
  30.0 12.9 %collective-permute-start.14 = (bf16[2,65,16,128]{3,2,1,0:T(8,128)(2,1)}, bf16[2,65,16,128]{3,2,1,0:T(8,128)(2,1)S(1)}, u32[]{:S(2)}, u32[]{:S(2)}) collective-permute-start(bf16[2,65,16,128]{3,2,1,0:T(8,128)(2,1)} %get-tuple-element.96), channel_id=1, source_target_pairs={{0,8},{4,12},{8,0},{12,4},{16,24},{20,28},{24,16},{28,20},{1,9},{5... | collective-permute-start | bytes 1597448 | tf_op jit(solution)/shard_map/ppermute | solution.py:628
  43.0 0.7 collective-permute-start.13
  43.7 1.4 sine_multiply_fusion.1
  45.2 1.3 sine_multiply_fusion
  46.6 4.5 %relay.2 = (bf16[2,65,16,128]{3,2,1,0:T(8,128)(2,1)}, bf16[2,65,16,128]{3,2,1,0:T(8,128)(2,1)}) custom-call(bf16[2,65,16,128]{3,2,1,0:T(8,128)(2,1)} %get-tuple-element.81.refs_0_.refs_1_.refs_8_, bf16[2,65,16,128]{3,2,1,0:T(8,128)(2,1)} %get-tuple-element.81.refs_0_.refs_1_.refs_8_, bf16[2,65,16,128]{3,2,1,0:T(8,128)(2,1)} %copy-done.14, ...), custom_call_target="tpu_custom_call" | custom-call | bytes 4259840 | tf_op jit(solution)/shard_map/relay/pallas_call | solution.py:334
  51.1 3.5 %collective-permute-start.10 = (bf16[2,65,16,128]{3,2,1,0:T(8,128)(2,1)}, bf16[2,65,16,128]{3,2,1,0:T(8,128)(2,1)}, u32[]{:S(2)}, u32[]{:S(2)}) collective-permute-start(bf16[2,65,16,128]{3,2,1,0:T(8,128)(2,1)} %get-tuple-element.86), channel_id=1, source_target_pairs={{0,20},{4,16},{24,12},{28,8},{8,24},{12,28},{16,0},{20,4},{1,21},{... | collective-permute-start | bytes 1597448 | tf_op jit(solution)/shard_map/ppermute | solution.py:628
  54.7 8.6 %collective-permute-start.9 = (bf16[2,65,16,128]{3,2,1,0:T(8,128)(2,1)}, bf16[2,65,16,128]{3,2,1,0:T(8,128)(2,1)}, u32[]{:S(2)}, u32[]{:S(2)}) collective-permute-start(bf16[2,65,16,128]{3,2,1,0:T(8,128)(2,1)} %get-tuple-element.85), channel_id=1, source_target_pairs={{0,16},{4,20},{8,24},{12,28},{16,0},{20,4},{24,8},{28,12},{1,17},{... | collective-permute-start | bytes 1597448 | tf_op jit(solution)/shard_map/ppermute | solution.py:628
  63.2 8.6 %collective-permute-done.15.refs_6_.refs_7_.refs_18_.refs_19_ = bf16[2,65,16,128]{3,2,1,0:T(8,128)(2,1)S(1)} collective-permute-done((bf16[2,65,16,128]{3,2,1,0:T(8,128)(2,1)}, bf16[2,65,16,128]{3,2,1,0:T(8,128)(2,1)S(1)}, u32[]{:S(2)}, u32[]{:S(2)}) %collective-permute-start.15) | collective-permute-done | bytes 532512 | tf_op jit(solution)/shard_map/ppermute | solution.py:628
  71.8 2.1 collective-permute-start.5
  73.9 0.8 copy-done.15
  74.7 2.5 %collective-permute-start.3 = (bf16[2,65,16,128]{3,2,1,0:T(8,128)(2,1)S(1)}, bf16[2,65,16,128]{3,2,1,0:T(8,128)(2,1)}, u32[]{:S(2)}, u32[]{:S(2)}) collective-permute-start(bf16[2,65,16,128]{3,2,1,0:T(8,128)(2,1)S(1)} %copy-done.19), channel_id=1, source_target_pairs={{0,8},{4,12},{24,16},{28,20},{1,9},{5,13},{25,17},{29,21},{2,10},{... | collective-permute-start | bytes 1597448 | tf_op jit(solution)/shard_map/ppermute | solution.py:628
  77.4 0.6 fusion.10
  78.0 4.5 %relay.3 = (bf16[2,65,16,128]{3,2,1,0:T(8,128)(2,1)}, bf16[2,65,16,128]{3,2,1,0:T(8,128)(2,1)}) custom-call(bf16[2,65,16,128]{3,2,1,0:T(8,128)(2,1)} %get-tuple-element.93.refs_0_.refs_1_.refs_8_, bf16[2,65,16,128]{3,2,1,0:T(8,128)(2,1)} %get-tuple-element.93.refs_0_.refs_1_.refs_8_, bf16[2,65,16,128]{3,2,1,0:T(8,128)(2,1)} %copy-done.15, ...), custom_call_target="tpu_custom_call" | custom-call | bytes 4259840 | tf_op jit(solution)/shard_map/relay/pallas_call | solution.py:334
  82.4 13.7 %collective-permute-done.10.refs_10_.refs_11_ = bf16[2,65,16,128]{3,2,1,0:T(8,128)(2,1)} collective-permute-done((bf16[2,65,16,128]{3,2,1,0:T(8,128)(2,1)}, bf16[2,65,16,128]{3,2,1,0:T(8,128)(2,1)}, u32[]{:S(2)}, u32[]{:S(2)}) %collective-permute-start.10) | collective-permute-done | bytes 532512 | tf_op jit(solution)/shard_map/ppermute | solution.py:628
  96.2 11.3 %collective-permute-done.9.refs_8_.refs_9_ = bf16[2,65,16,128]{3,2,1,0:T(8,128)(2,1)} collective-permute-done((bf16[2,65,16,128]{3,2,1,0:T(8,128)(2,1)}, bf16[2,65,16,128]{3,2,1,0:T(8,128)(2,1)}, u32[]{:S(2)}, u32[]{:S(2)}) %collective-permute-start.9) | collective-permute-done | bytes 532512 | tf_op jit(solution)/shard_map/ppermute | solution.py:628
  107.4 2.9 %collective-permute-start.18 = (bf16[2,65,16,128]{3,2,1,0:T(8,128)(2,1)}, bf16[2,65,16,128]{3,2,1,0:T(8,128)(2,1)}, u32[]{:S(2)}, u32[]{:S(2)}) collective-permute-start(bf16[2,65,16,128]{3,2,1,0:T(8,128)(2,1)} %get-tuple-element.115), channel_id=1, source_target_pairs={{0,16},{4,20},{8,24},{12,28},{16,0},{20,4},{24,8},{28,12},{1,17},{... | collective-permute-start | bytes 1597448 | tf_op jit(solution)/shard_map/ppermute | solution.py:628
  110.4 2.4 %collective-permute-done.3.refs_4_.refs_5_ = bf16[2,65,16,128]{3,2,1,0:T(8,128)(2,1)} collective-permute-done((bf16[2,65,16,128]{3,2,1,0:T(8,128)(2,1)S(1)}, bf16[2,65,16,128]{3,2,1,0:T(8,128)(2,1)}, u32[]{:S(2)}, u32[]{:S(2)}) %collective-permute-start.3) | collective-permute-done | bytes 532512 | tf_op jit(solution)/shard_map/ppermute | solution.py:628
  112.8 5.9 %transform_mid.2 = bf16[4,2,2,2,2,64,256]{6,5,4,3,2,1,0:T(8,128)(2,1)} custom-call(bf16[512,512]{1,0:T(8,128)(2,1)} %constant.68.clone.turn_ref, bf16[2,256,512]{2,1,0:T(8,128)(2,1)} %constant.63.clone.table_ref, bf16[2,65,16,128]{3,2,1,0:T(8,128)(2,1)} %get-tuple-element.102.refs_0_.refs_1_, bf16[2,65,16,128]{3,2,1,0:T(8,128)(2,1)} %get-tuple-element.102.refs_0_.refs_1_, ...), custom_call_target="tpu_custom_call" | custom-call | flops 21810380800 | bytes 7421952 | tf_op jit(solution)/shard_map/transform_mid/pallas_call | solution.py:421
  118.7 4.5 %all-to-all-start = ((bf16[4,2,2,2,128,256]{5,4,3,2,1,0:T(8,128)(2,1)}), bf16[4,2,2,2,128,256]{5,4,3,2,1,0:T(8,128)(2,1)}, u32[]{:S(2)}, u32[]{:S(2)}) async-start(bf16[4,2,2,2,128,256]{5,4,3,2,1,0:T(8,128)(2,1)} %bitcast.21), calls=%async_computation | async-start | bytes 4194304 | tf_op jit(solution)/shard_map/all_to_all | solution.py:753
  123.2 2.6 %collective-permute-start.17 = (bf16[2,65,16,128]{3,2,1,0:T(8,128)(2,1)}, bf16[2,65,16,128]{3,2,1,0:T(8,128)(2,1)}, u32[]{:S(2)}, u32[]{:S(2)}) collective-permute-start(bf16[2,65,16,128]{3,2,1,0:T(8,128)(2,1)} %get-tuple-element.114), channel_id=1, source_target_pairs={{0,12},{4,8},{24,20},{28,16},{1,13},{5,9},{25,21},{29,17},{2,14},{... | collective-permute-start | bytes 1597448 | tf_op jit(solution)/shard_map/ppermute | solution.py:628
  125.8 4.0 %collective-permute-start.16 = (bf16[2,65,16,128]{3,2,1,0:T(8,128)(2,1)}, bf16[2,65,16,128]{3,2,1,0:T(8,128)(2,1)}, u32[]{:S(2)}, u32[]{:S(2)}) collective-permute-start(bf16[2,65,16,128]{3,2,1,0:T(8,128)(2,1)} %get-tuple-element.113), channel_id=1, source_target_pairs={{0,8},{4,12},{24,16},{28,20},{1,9},{5,13},{25,17},{29,21},{2,10},{... | collective-permute-start | bytes 1597448 | tf_op jit(solution)/shard_map/ppermute | solution.py:628
  129.8 0.8 copy-done.25
  130.7 1.4 hold.1.z_ref
  132.1 14.2 %all-to-all-done.refs_0_ = bf16[4,2,2,2,128,256]{5,4,3,2,1,0:T(8,128)(2,1)} async-done(((bf16[4,2,2,2,128,256]{5,4,3,2,1,0:T(8,128)(2,1)}), bf16[4,2,2,2,128,256]{5,4,3,2,1,0:T(8,128)(2,1)}, u32[]{:S(2)}, u32[]{:S(2)}) %all-to-all-start) | async-done | bytes 2097184 | tf_op jit(solution)/shard_map/all_to_all | solution.py:753
  146.3 0.6 copy-done.9
  146.9 5.5 %transform_long.2 = bf16[48,2,2,32,128]{4,3,2,1,0:T(8,128)(2,1)} custom-call(s32[64]{0:T(128)S(1)} %copy-done.3, f32[2,2]{1,0:T(2,128)S(1)} %copy-done.9, f32[2,2,256,1]{3,2,1,0:T(8,128)S(1)} %copy.16.x_ref, f32[2,512]{1,0:T(2,128)S(1)} %pad_maximum_fusion.y_ref, bf16[1024,512]{1,0:T(8,128)(2,1)S(1)} %copy-done.4, bf16[512,1024]{1,0:T(8,128)(2,1)S(1)} %copy-done.6, ...), custom_call_target="tpu_custom_call" | custom-call | flops 2147483648 | bytes 9961472 | tf_op jit(solution)/shard_map/transform_long/pallas_call | solution.py:534
  152.4 3.9 %all-to-all-start.1 = ((bf16[8,6,2,2,32,128]{5,4,3,2,1,0:T(8,128)(2,1)}), bf16[8,6,2,2,32,128]{5,4,3,2,1,0:T(8,128)(2,1)S(1)}, u32[]{:S(2)}, u32[]{:S(2)}) async-start(bf16[8,6,2,2,32,128]{5,4,3,2,1,0:T(8,128)(2,1)} %bitcast.10), calls=%async_computation.1 | async-start | bytes 3145728 | tf_op jit(solution)/shard_map/all_to_all | solution.py:770
  156.3 0.6 collective-permute-done.18.refs_8_.refs_9_
  157.4 6.3 %transform_mid.3 = (bf16[2,2,2,2,64,256]{5,4,3,2,1,0:T(8,128)(2,1)}, bf16[2,2,2,2,64,256]{5,4,3,2,1,0:T(8,128)(2,1)}, bf16[2,2,2,2,64,256]{5,4,3,2,1,0:T(8,128)(2,1)}, bf16[2,2,2,2,64,256]{5,4,3,2,1,0:T(8,128)(2,1)}) custom-call(bf16[512,512]{1,0:T(8,128)(2,1)} %constant.68.clone.turn_ref, bf16[2,256,512]{2,1,0:T(8,128)(2,1)} %constant.63.clone.table_ref, ...), custom_call_target="tpu_custom_call" | custom-call | flops 21810380800 | bytes 7421952 | tf_op jit(solution)/shard_map/transform_mid/pallas_call | solution.py:421
  163.7 1.6 collective-permute-start.20
  165.3 2.4 collective-permute-start.21
  167.7 11.1 %collective-permute-done.20.refs_1_ = bf16[2,2,2,128,256]{4,3,2,1,0:T(8,128)(2,1)S(1)} collective-permute-done((bf16[2,2,2,128,256]{4,3,2,1,0:T(8,128)(2,1)}, bf16[2,2,2,128,256]{4,3,2,1,0:T(8,128)(2,1)S(1)}, u32[]{:S(2)}, u32[]{:S(2)}) %collective-permute-start.20) | collective-permute-done | bytes 524320 | tf_op jit(solution)/shard_map/ppermute | solution.py:654
  178.9 10.8 %collective-permute-done.21.refs_2_ = bf16[2,2,2,128,256]{4,3,2,1,0:T(8,128)(2,1)S(1)} collective-permute-done((bf16[2,2,2,128,256]{4,3,2,1,0:T(8,128)(2,1)}, bf16[2,2,2,128,256]{4,3,2,1,0:T(8,128)(2,1)S(1)}, u32[]{:S(2)}, u32[]{:S(2)}) %collective-permute-start.21) | collective-permute-done | bytes 524320 | tf_op jit(solution)/shard_map/ppermute | solution.py:654
  189.7 1.0 copy-done.8
  190.7 4.1 %transform_long.3 = bf16[48,2,2,32,128]{4,3,2,1,0:T(8,128)(2,1)S(1)} custom-call(s32[64]{0:T(128)S(1)} %copy-done.3, f32[2,2]{1,0:T(2,128)S(1)} %get-tuple-element.131.z_ref, f32[2,2,256,1]{3,2,1,0:T(8,128)S(1)} %copy-done.1, f32[2,512]{1,0:T(2,128)S(1)} %pad_maximum_fusion.y_ref, bf16[1024,512]{1,0:T(8,128)(2,1)S(1)} %copy-done.5, ...), custom_call_target="tpu_custom_call" | custom-call | flops 2147483648 | bytes 9961472 | tf_op jit(solution)/shard_map/transform_long/pallas_call | solution.py:534
  194.9 42.5 %all_to_all.15.refs_1_ = bf16[8,6,2,2,32,128]{5,4,3,2,1,0:T(8,128)(2,1)S(1)} all-to-all(bf16[8,6,2,2,32,128]{5,4,3,2,1,0:T(8,128)(2,1)S(1)} %bitcast.18), channel_id=1, replica_groups=mesh['grid'=8,'pencil'=4] {'grid'}, dimensions={0} | all-to-all | bytes 3145728 | tf_op jit(solution)/shard_map/all_to_all | solution.py:770
  237.4 3.5 %lay_rows.1 = f32[6,2,32,4096]{3,2,1,0:T(8,128)} custom-call(bf16[256,256]{1,0:T(8,128)(2,1)S(1)} %copy-done.2, bf16[8,6,2,2,32,128]{5,4,3,2,1,0:T(8,128)(2,1)S(1)} %all-to-all-done.1.refs_0_, bf16[8,6,2,2,32,128]{5,4,3,2,1,0:T(8,128)(2,1)S(1)} %all_to_all.15.refs_1_), custom_call_target="tpu_custom_call" | custom-call | bytes 9437184 | tf_op jit(solution)/shard_map/lay_rows/pallas_call | solution.py:595
  (74 shorter events, 0.9 us)
Async XLA Ops:
  1.3 16.4 %copy-start.16 = (f32[3]{0:T(128)S(1)}, f32[3]{0:T(128)}, u32[]{:S(2)}) copy-start(f32[3]{0:T(128)} %param.21) | copy-start | bytes 40
  1.3 17.0 %copy-start.17 = (f32[3]{0:T(128)S(1)}, f32[3]{0:T(128)}, u32[]{:S(2)}) copy-start(f32[3]{0:T(128)} %param.20) | copy-start | bytes 40
  8.4 11.9 %collective-permute-start.4 = (bf16[2,65,16,128]{3,2,1,0:T(8,128)(2,1)}, bf16[2,65,16,128]{3,2,1,0:T(8,128)(2,1)S(1)}, u32[]{:S(2)}, u32[]{:S(2)}) collective-permute-start(bf16[2,65,16,128]{3,2,1,0:T(8,128)(2,1)} %get-tuple-element.78), channel_id=1, source_target_pairs={{8,20},{20,8},{12,16},{16,12},{9,21},{21,9},{13,17},{17,13},{10,22... | collective-permute-start | bytes 1597448 | tf_op jit(solution)/shard_map/ppermute | solution.py:628
  9.1 11.9 %collective-permute-start.2 = (bf16[2,65,16,128]{3,2,1,0:T(8,128)(2,1)}, bf16[2,65,16,128]{3,2,1,0:T(8,128)(2,1)S(1)}, u32[]{:S(2)}, u32[]{:S(2)}) collective-permute-start(bf16[2,65,16,128]{3,2,1,0:T(8,128)(2,1)} %get-tuple-element.76), channel_id=1, source_target_pairs={{8,16},{16,8},{12,20},{20,12},{9,17},{17,9},{13,21},{21,13},{10,18... | collective-permute-start | bytes 1597448 | tf_op jit(solution)/shard_map/ppermute | solution.py:628
  9.8 20.2 %collective-permute-start.7 = (bf16[2,65,16,128]{3,2,1,0:T(8,128)(2,1)}, bf16[2,65,16,128]{3,2,1,0:T(8,128)(2,1)S(1)}, u32[]{:S(2)}, u32[]{:S(2)}) collective-permute-start(bf16[2,65,16,128]{3,2,1,0:T(8,128)(2,1)} %get-tuple-element.82), channel_id=1, source_target_pairs={{0,8},{4,12},{8,0},{12,4},{16,24},{20,28},{24,16},{28,20},{1,9},{5... | collective-permute-start | bytes 1597448 | tf_op jit(solution)/shard_map/ppermute | solution.py:628
  16.9 26.0 %collective-permute-start.8 = (bf16[2,65,16,128]{3,2,1,0:T(8,128)(2,1)}, bf16[2,65,16,128]{3,2,1,0:T(8,128)(2,1)S(1)}, u32[]{:S(2)}, u32[]{:S(2)}) collective-permute-start(bf16[2,65,16,128]{3,2,1,0:T(8,128)(2,1)} %get-tuple-element.83), channel_id=1, source_target_pairs={{0,12},{4,8},{8,4},{12,0},{16,28},{20,24},{24,20},{28,16},{1,13},{... | collective-permute-start | bytes 1597448 | tf_op jit(solution)/shard_map/ppermute | solution.py:628
  17.0 26.0 %collective-permute-start.6 = (bf16[2,65,16,128]{3,2,1,0:T(8,128)(2,1)}, bf16[2,65,16,128]{3,2,1,0:T(8,128)(2,1)S(1)}, u32[]{:S(2)}, u32[]{:S(2)}) collective-permute-start(bf16[2,65,16,128]{3,2,1,0:T(8,128)(2,1)} %get-tuple-element.84.refs_9_), channel_id=1, source_target_pairs={{8,12},{12,8},{16,20},{20,16},{9,13},{13,9},{17,21},{21,17},{10,14... | collective-permute-start | bytes 1597448 | tf_op jit(solution)/shard_map/ppermute | solution.py:628
  20.4 9.7 %copy-start.22 = (bf16[2,65,16,128]{3,2,1,0:T(8,128)(2,1)}, bf16[2,65,16,128]{3,2,1,0:T(8,128)(2,1)S(1)}, u32[]{:S(2)}) copy-start(bf16[2,65,16,128]{3,2,1,0:T(8,128)(2,1)S(1)} %collective-permute-done.4.refs_14_.refs_15_) | copy-start | bytes 1597444
  20.4 30.7 %collective-permute-start.12 = (bf16[2,65,16,128]{3,2,1,0:T(8,128)(2,1)}, bf16[2,65,16,128]{3,2,1,0:T(8,128)(2,1)S(1)}, u32[]{:S(2)}, u32[]{:S(2)}) collective-permute-start(bf16[2,65,16,128]{3,2,1,0:T(8,128)(2,1)} %get-tuple-element.114), channel_id=1, source_target_pairs={{8,20},{20,8},{12,16},{16,12},{9,21},{21,9},{13,17},{17,13},{10,22... | collective-permute-start | bytes 1597448 | tf_op jit(solution)/shard_map/ppermute | solution.py:628
  21.1 22.6 %copy-start.24 = (bf16[2,65,16,128]{3,2,1,0:T(8,128)(2,1)}, bf16[2,65,16,128]{3,2,1,0:T(8,128)(2,1)S(1)}, u32[]{:S(2)}) copy-start(bf16[2,65,16,128]{3,2,1,0:T(8,128)(2,1)S(1)} %collective-permute-done.2.refs_12_.refs_13_) | copy-start | bytes 1597444
  21.1 33.6 %collective-permute-start.11 = (bf16[2,65,16,128]{3,2,1,0:T(8,128)(2,1)}, bf16[2,65,16,128]{3,2,1,0:T(8,128)(2,1)S(1)}, u32[]{:S(2)}, u32[]{:S(2)}) collective-permute-start(bf16[2,65,16,128]{3,2,1,0:T(8,128)(2,1)} %get-tuple-element.113), channel_id=1, source_target_pairs={{8,16},{16,8},{12,20},{20,12},{9,17},{17,9},{13,21},{21,13},{10,18... | collective-permute-start | bytes 1597448 | tf_op jit(solution)/shard_map/ppermute | solution.py:628
  30.0 16.5 %copy-start.10 = (bf16[2,65,16,128]{3,2,1,0:T(8,128)(2,1)}, bf16[2,65,16,128]{3,2,1,0:T(8,128)(2,1)S(1)}, u32[]{:S(2)}) copy-start(bf16[2,65,16,128]{3,2,1,0:T(8,128)(2,1)S(1)} %collective-permute-done.7.refs_4_.refs_5_.refs_16_.refs_17_) | copy-start | bytes 1597444
  30.0 33.2 %collective-permute-start.14 = (bf16[2,65,16,128]{3,2,1,0:T(8,128)(2,1)}, bf16[2,65,16,128]{3,2,1,0:T(8,128)(2,1)S(1)}, u32[]{:S(2)}, u32[]{:S(2)}) collective-permute-start(bf16[2,65,16,128]{3,2,1,0:T(8,128)(2,1)} %get-tuple-element.96), channel_id=1, source_target_pairs={{0,8},{4,12},{8,0},{12,4},{16,24},{20,28},{24,16},{28,20},{1,9},{5... | collective-permute-start | bytes 1597448 | tf_op jit(solution)/shard_map/ppermute | solution.py:628
  43.0 3.6 %copy-start.12 = (bf16[2,65,16,128]{3,2,1,0:T(8,128)(2,1)}, bf16[2,65,16,128]{3,2,1,0:T(8,128)(2,1)S(1)}, u32[]{:S(2)}) copy-start(bf16[2,65,16,128]{3,2,1,0:T(8,128)(2,1)S(1)} %collective-permute-done.8.refs_6_.refs_7_.refs_18_.refs_19_) | copy-start | bytes 1597444
  43.0 28.8 %collective-permute-start.15 = (bf16[2,65,16,128]{3,2,1,0:T(8,128)(2,1)}, bf16[2,65,16,128]{3,2,1,0:T(8,128)(2,1)S(1)}, u32[]{:S(2)}, u32[]{:S(2)}) collective-permute-start(bf16[2,65,16,128]{3,2,1,0:T(8,128)(2,1)} %get-tuple-element.98), channel_id=1, source_target_pairs={{0,12},{4,8},{8,4},{12,0},{16,28},{20,24},{24,20},{28,16},{1,13},{... | collective-permute-start | bytes 1597448 | tf_op jit(solution)/shard_map/ppermute | solution.py:628
  43.0 3.5 %copy-start.14 = (bf16[2,65,16,128]{3,2,1,0:T(8,128)(2,1)}, bf16[2,65,16,128]{3,2,1,0:T(8,128)(2,1)S(1)}, u32[]{:S(2)}) copy-start(bf16[2,65,16,128]{3,2,1,0:T(8,128)(2,1)S(1)} %collective-permute-done.6.refs_2_.refs_3_) | copy-start | bytes 1597444
  43.0 30.9 %collective-permute-start.13 = (bf16[2,65,16,128]{3,2,1,0:T(8,128)(2,1)}, bf16[2,65,16,128]{3,2,1,0:T(8,128)(2,1)S(1)}, u32[]{:S(2)}, u32[]{:S(2)}) collective-permute-start(bf16[2,65,16,128]{3,2,1,0:T(8,128)(2,1)} %get-tuple-element.99.refs_9_), channel_id=1, source_target_pairs={{8,12},{12,8},{16,20},{20,16},{9,13},{13,9},{17,21},{21,17},{10,14... | collective-permute-start | bytes 1597448 | tf_op jit(solution)/shard_map/ppermute | solution.py:628
  46.5 25.3 %copy-start.21 = (bf16[2,65,16,128]{3,2,1,0:T(8,128)(2,1)S(1)}, bf16[2,65,16,128]{3,2,1,0:T(8,128)(2,1)}, u32[]{:S(2)}) copy-start(bf16[2,65,16,128]{3,2,1,0:T(8,128)(2,1)} %get-tuple-element.78) | copy-start | bytes 1597444
  46.6 28.1 %copy-start.19 = (bf16[2,65,16,128]{3,2,1,0:T(8,128)(2,1)S(1)}, bf16[2,65,16,128]{3,2,1,0:T(8,128)(2,1)}, u32[]{:S(2)}) copy-start(bf16[2,65,16,128]{3,2,1,0:T(8,128)(2,1)} %get-tuple-element.76) | copy-start | bytes 1597444
  51.1 22.8 %copy-start.20 = (bf16[2,65,16,128]{3,2,1,0:T(8,128)(2,1)}, bf16[2,65,16,128]{3,2,1,0:T(8,128)(2,1)S(1)}, u32[]{:S(2)}) copy-start(bf16[2,65,16,128]{3,2,1,0:T(8,128)(2,1)S(1)} %collective-permute-done.12.refs_14_.refs_15_) | copy-start | bytes 1597444
  51.1 45.1 %collective-permute-start.10 = (bf16[2,65,16,128]{3,2,1,0:T(8,128)(2,1)}, bf16[2,65,16,128]{3,2,1,0:T(8,128)(2,1)}, u32[]{:S(2)}, u32[]{:S(2)}) collective-permute-start(bf16[2,65,16,128]{3,2,1,0:T(8,128)(2,1)} %get-tuple-element.86), channel_id=1, source_target_pairs={{0,20},{4,16},{24,12},{28,8},{8,24},{12,28},{16,0},{20,4},{1,21},{... | collective-permute-start | bytes 1597448 | tf_op jit(solution)/shard_map/ppermute | solution.py:628
  54.7 19.3 %copy-start.23 = (bf16[2,65,16,128]{3,2,1,0:T(8,128)(2,1)}, bf16[2,65,16,128]{3,2,1,0:T(8,128)(2,1)S(1)}, u32[]{:S(2)}) copy-start(bf16[2,65,16,128]{3,2,1,0:T(8,128)(2,1)S(1)} %collective-permute-done.11.refs_12_.refs_13_) | copy-start | bytes 1597444
  54.7 52.8 %collective-permute-start.9 = (bf16[2,65,16,128]{3,2,1,0:T(8,128)(2,1)}, bf16[2,65,16,128]{3,2,1,0:T(8,128)(2,1)}, u32[]{:S(2)}, u32[]{:S(2)}) collective-permute-start(bf16[2,65,16,128]{3,2,1,0:T(8,128)(2,1)} %get-tuple-element.85), channel_id=1, source_target_pairs={{0,16},{4,20},{8,24},{12,28},{16,0},{20,4},{24,8},{28,12},{1,17},{... | collective-permute-start | bytes 1597448 | tf_op jit(solution)/shard_map/ppermute | solution.py:628
  63.2 14.7 %copy-start.11 = (bf16[2,65,16,128]{3,2,1,0:T(8,128)(2,1)}, bf16[2,65,16,128]{3,2,1,0:T(8,128)(2,1)S(1)}, u32[]{:S(2)}) copy-start(bf16[2,65,16,128]{3,2,1,0:T(8,128)(2,1)S(1)} %collective-permute-done.14.refs_4_.refs_5_.refs_16_.refs_17_) | copy-start | bytes 1597444
  63.2 44.2 %collective-permute-start.1 = (bf16[2,65,16,128]{3,2,1,0:T(8,128)(2,1)}, bf16[2,65,16,128]{3,2,1,0:T(8,128)(2,1)}, u32[]{:S(2)}, u32[]{:S(2)}) collective-permute-start(bf16[2,65,16,128]{3,2,1,0:T(8,128)(2,1)} %get-tuple-element.74), channel_id=1, source_target_pairs={{0,4},{4,0},{8,12},{12,8},{16,20},{20,16},{24,28},{28,24},{1,5},{5... | collective-permute-start | bytes 1597448 | tf_op jit(solution)/shard_map/ppermute | solution.py:628
  71.8 6.2 %copy-start.13 = (bf16[2,65,16,128]{3,2,1,0:T(8,128)(2,1)}, bf16[2,65,16,128]{3,2,1,0:T(8,128)(2,1)S(1)}, u32[]{:S(2)}) copy-start(bf16[2,65,16,128]{3,2,1,0:T(8,128)(2,1)S(1)} %collective-permute-done.15.refs_6_.refs_7_.refs_18_.refs_19_) | copy-start | bytes 1597444
  71.8 38.6 %collective-permute-start.5 = (bf16[2,65,16,128]{3,2,1,0:T(8,128)(2,1)S(1)}, bf16[2,65,16,128]{3,2,1,0:T(8,128)(2,1)}, u32[]{:S(2)}, u32[]{:S(2)}) collective-permute-start(bf16[2,65,16,128]{3,2,1,0:T(8,128)(2,1)S(1)} %copy-done.21), channel_id=1, source_target_pairs={{0,12},{4,8},{24,20},{28,16},{1,13},{5,9},{25,21},{29,17},{2,14},{... | collective-permute-start | bytes 1597448 | tf_op jit(solution)/shard_map/ppermute | solution.py:628
  74.7 38.1 %collective-permute-start.3 = (bf16[2,65,16,128]{3,2,1,0:T(8,128)(2,1)S(1)}, bf16[2,65,16,128]{3,2,1,0:T(8,128)(2,1)}, u32[]{:S(2)}, u32[]{:S(2)}) collective-permute-start(bf16[2,65,16,128]{3,2,1,0:T(8,128)(2,1)S(1)} %copy-done.19), channel_id=1, source_target_pairs={{0,8},{4,12},{24,16},{28,20},{1,9},{5,13},{25,17},{29,21},{2,10},{... | collective-permute-start | bytes 1597448 | tf_op jit(solution)/shard_map/ppermute | solution.py:628
  77.4 68.9 %copy-start = (f32[2,2,256,1]{3,2,1,0:T(8,128)}, f32[2,2,256,1]{3,2,1,0:T(8,128)S(1)}, u32[]{:S(2)}) copy-start(f32[2,2,256,1]{3,2,1,0:T(8,128)S(1)} %copy.16.x_ref) | copy-start | bytes 12292
  78.0 18.2 %copy-start.18 = (bf16[2,65,16,128]{3,2,1,0:T(8,128)(2,1)S(1)}, bf16[2,65,16,128]{3,2,1,0:T(8,128)(2,1)}, u32[]{:S(2)}) copy-start(bf16[2,65,16,128]{3,2,1,0:T(8,128)(2,1)} %get-tuple-element.70) | copy-start | bytes 1597444
  96.2 33.6 %collective-permute-start = (bf16[2,65,16,128]{3,2,1,0:T(8,128)(2,1)S(1)}, bf16[2,65,16,128]{3,2,1,0:T(8,128)(2,1)S(1)}, u32[]{:S(2)}, u32[]{:S(2)}) collective-permute-start(bf16[2,65,16,128]{3,2,1,0:T(8,128)(2,1)S(1)} %copy-done.18), channel_id=1, source_target_pairs={{0,4},{4,0},{8,12},{12,8},{16,20},{20,16},{24,28},{28,24},{1,5},{5... | collective-permute-start | bytes 1597448 | tf_op jit(solution)/shard_map/ppermute | solution.py:628
  107.4 48.8 %collective-permute-start.19 = (bf16[2,65,16,128]{3,2,1,0:T(8,128)(2,1)}, bf16[2,65,16,128]{3,2,1,0:T(8,128)(2,1)}, u32[]{:S(2)}, u32[]{:S(2)}) collective-permute-start(bf16[2,65,16,128]{3,2,1,0:T(8,128)(2,1)} %get-tuple-element.116), channel_id=1, source_target_pairs={{0,20},{4,16},{24,12},{28,8},{8,24},{12,28},{16,0},{20,4},{1,21},{... | collective-permute-start | bytes 1597448 | tf_op jit(solution)/shard_map/ppermute | solution.py:628
  107.4 49.4 %collective-permute-start.18 = (bf16[2,65,16,128]{3,2,1,0:T(8,128)(2,1)}, bf16[2,65,16,128]{3,2,1,0:T(8,128)(2,1)}, u32[]{:S(2)}, u32[]{:S(2)}) collective-permute-start(bf16[2,65,16,128]{3,2,1,0:T(8,128)(2,1)} %get-tuple-element.115), channel_id=1, source_target_pairs={{0,16},{4,20},{8,24},{12,28},{16,0},{20,4},{24,8},{28,12},{1,17},{... | collective-permute-start | bytes 1597448 | tf_op jit(solution)/shard_map/ppermute | solution.py:628
  118.7 27.6 %all-to-all-start = ((bf16[4,2,2,2,128,256]{5,4,3,2,1,0:T(8,128)(2,1)}), bf16[4,2,2,2,128,256]{5,4,3,2,1,0:T(8,128)(2,1)}, u32[]{:S(2)}, u32[]{:S(2)}) async-start(bf16[4,2,2,2,128,256]{5,4,3,2,1,0:T(8,128)(2,1)} %bitcast.21), calls=%async_computation | async-start | bytes 4194304 | tf_op jit(solution)/shard_map/all_to_all | solution.py:753
  123.2 33.7 %collective-permute-start.17 = (bf16[2,65,16,128]{3,2,1,0:T(8,128)(2,1)}, bf16[2,65,16,128]{3,2,1,0:T(8,128)(2,1)}, u32[]{:S(2)}, u32[]{:S(2)}) collective-permute-start(bf16[2,65,16,128]{3,2,1,0:T(8,128)(2,1)} %get-tuple-element.114), channel_id=1, source_target_pairs={{0,12},{4,8},{24,20},{28,16},{1,13},{5,9},{25,21},{29,17},{2,14},{... | collective-permute-start | bytes 1597448 | tf_op jit(solution)/shard_map/ppermute | solution.py:628
  125.8 31.6 %collective-permute-start.16 = (bf16[2,65,16,128]{3,2,1,0:T(8,128)(2,1)}, bf16[2,65,16,128]{3,2,1,0:T(8,128)(2,1)}, u32[]{:S(2)}, u32[]{:S(2)}) collective-permute-start(bf16[2,65,16,128]{3,2,1,0:T(8,128)(2,1)} %get-tuple-element.113), channel_id=1, source_target_pairs={{0,8},{4,12},{24,16},{28,20},{1,9},{5,13},{25,17},{29,21},{2,10},{... | collective-permute-start | bytes 1597448 | tf_op jit(solution)/shard_map/ppermute | solution.py:628
  130.7 15.6 %copy-start.3 = (s32[64]{0:T(128)S(1)}, s32[64]{0:T(128)}, u32[]{:S(2)}) copy-start(s32[64]{0:T(128)} %rows_ref.3) | copy-start | bytes 772
  130.7 15.6 %copy-start.4 = (bf16[1024,512]{1,0:T(8,128)(2,1)S(1)}, bf16[1024,512]{1,0:T(8,128)(2,1)}, u32[]{:S(2)}) copy-start(bf16[1024,512]{1,0:T(8,128)(2,1)} %constant.64.clone.first_ref) | copy-start | bytes 3145732
  130.7 15.6 %copy-start.6 = (bf16[512,1024]{1,0:T(8,128)(2,1)S(1)}, bf16[512,1024]{1,0:T(8,128)(2,1)}, u32[]{:S(2)}) copy-start(bf16[512,1024]{1,0:T(8,128)(2,1)} %constant.65.clone.second_ref) | copy-start | bytes 3145732
  152.4 42.5 %all-to-all-start.1 = ((bf16[8,6,2,2,32,128]{5,4,3,2,1,0:T(8,128)(2,1)}), bf16[8,6,2,2,32,128]{5,4,3,2,1,0:T(8,128)(2,1)S(1)}, u32[]{:S(2)}, u32[]{:S(2)}) async-start(bf16[8,6,2,2,32,128]{5,4,3,2,1,0:T(8,128)(2,1)} %bitcast.10), calls=%async_computation.1 | async-start | bytes 3145728 | tf_op jit(solution)/shard_map/all_to_all | solution.py:770
  157.4 32.3 %copy-start.1 = (f32[2,2,256,1]{3,2,1,0:T(8,128)S(1)}, f32[2,2,256,1]{3,2,1,0:T(8,128)}, u32[]{:S(2)}) copy-start(f32[2,2,256,1]{3,2,1,0:T(8,128)} %copy-done) | copy-start | bytes 12292
  157.4 32.3 %copy-start.5 = (bf16[1024,512]{1,0:T(8,128)(2,1)S(1)}, bf16[1024,512]{1,0:T(8,128)(2,1)}, u32[]{:S(2)}) copy-start(bf16[1024,512]{1,0:T(8,128)(2,1)} %constant.64.clone.first_ref) | copy-start | bytes 3145732
  157.4 32.3 %copy-start.7 = (bf16[512,1024]{1,0:T(8,128)(2,1)S(1)}, bf16[512,1024]{1,0:T(8,128)(2,1)}, u32[]{:S(2)}) copy-start(bf16[512,1024]{1,0:T(8,128)(2,1)} %constant.65.clone.second_ref) | copy-start | bytes 3145732
  163.7 15.1 %collective-permute-start.20 = (bf16[2,2,2,128,256]{4,3,2,1,0:T(8,128)(2,1)}, bf16[2,2,2,128,256]{4,3,2,1,0:T(8,128)(2,1)S(1)}, u32[]{:S(2)}, u32[]{:S(2)}) collective-permute-start(bf16[2,2,2,128,256]{4,3,2,1,0:T(8,128)(2,1)} %bitcast.24), channel_id=1, source_target_pairs={{0,1},{1,0},{2,3},{3,2},{4,5},{5,4},{6,7},{7,6},{8,9},{9,8},{10,11... | collective-permute-start | bytes 1572872 | tf_op jit(solution)/shard_map/ppermute | solution.py:654
  165.3 24.4 %collective-permute-start.21 = (bf16[2,2,2,128,256]{4,3,2,1,0:T(8,128)(2,1)}, bf16[2,2,2,128,256]{4,3,2,1,0:T(8,128)(2,1)S(1)}, u32[]{:S(2)}, u32[]{:S(2)}) collective-permute-start(bf16[2,2,2,128,256]{4,3,2,1,0:T(8,128)(2,1)} %bitcast.23), channel_id=1, source_target_pairs={{0,2},{1,3},{2,0},{3,1},{4,6},{5,7},{6,4},{7,5},{8,10},{9,11},{10,... | collective-permute-start | bytes 1572872 | tf_op jit(solution)/shard_map/ppermute | solution.py:654
  167.7 22.0 %collective-permute-start.22 = (bf16[2,2,2,128,256]{4,3,2,1,0:T(8,128)(2,1)}, bf16[2,2,2,128,256]{4,3,2,1,0:T(8,128)(2,1)S(1)}, u32[]{:S(2)}, u32[]{:S(2)}) collective-permute-start(bf16[2,2,2,128,256]{4,3,2,1,0:T(8,128)(2,1)} %bitcast.22), channel_id=1, source_target_pairs={{0,3},{1,2},{2,1},{3,0},{4,7},{5,6},{6,5},{7,4},{8,11},{9,10},{10,... | collective-permute-start | bytes 1572872 | tf_op jit(solution)/shard_map/ppermute | solution.py:654
  189.7 1.0 copy-start.8
  194.9 42.5 %copy-start.2 = (bf16[256,256]{1,0:T(8,128)(2,1)S(1)}, bf16[256,256]{1,0:T(8,128)(2,1)}, u32[]{:S(2)}) copy-start(bf16[256,256]{1,0:T(8,128)(2,1)} %constant.69.clone.turn_ref) | copy-start | bytes 393220
  (3 other events, 2.3 us)

commit v7 on v6

--- a/solution.py
+++ b/solution.py
@@ -13,7 +13,7 @@
 CHUNKS = 2
 MID_COST = 40
 HOLD_COST = 1000_000_000_000
-ROWS_PER_STEP = 3
+ROWS_PER_STEP = 2
 VMEM_LIMIT = 56 * 1024 * 1024
 
 
@@ -329,7 +329,7 @@
 
 def relay(sources, passing):
     shape = sources[0].shape
-    rows = 13 if shape[1] % 13 == 0 else 1
+    rows = shape[1]
     specs = unit_specs(shape, rows)
     return pl.pallas_call(
         relay_kernel,
@@ -747,7 +747,7 @@
         along_mid = transform_mid(sources, mid, chunk == 0, last, CHUNKS, pencils, slots)
         factor = z_factor[:, chunk * slots : (chunk + 1) * slots]
         if not last:
-            enters.append(send_enter(units[chunk + 1], enters[chunk]))
+            enters.append(send_enter(units[chunk + 1], jumps[chunk]))
             factor = hold(factor, [cores[chunk + 1]])
             along_mid = along_mid.reshape(along_mid.shape[:4] + (local_long, mid_len))
             lines = [lax.all_to_all(along_mid, "pencil", split_axis=0, concat_axis=0, tiled=True)]

time: 242 us -> 242 us (level)
  Pallas kernels: 42.8 us -> 40.2 us
    pallas_call x2, Pallas kernels: 8.98 us -> 6.19 us  [relay(): pl.pallas_call(relay_kernel, grid=(shape[1] // rows,), in_specs=specs * l...]
  transfers between devices with their start and end apart: 25 -> 25, of which waited for: 10 -> 10; matrix products, arithmetic and copies ran while one was open for 3% -> 3% of each run, Pallas kernels for 13% -> 12%
where the time goes in v7:
time: 242 us; the launch traced here: 241 us
  waiting for transfers between devices  82.9 us (34%)
  starting transfers between devices  64.2 us (27%)
  blocking collectives  42.5 us (18%)
  Pallas kernels  40.2 us (17%)
  local copies, waits for them, and re-layouts  5.47 us (2%)
  other arithmetic  4.15 us (2%)
    ppermute x20, starting transfers between devices, send(): return lax.ppermute(value, 'grid', pairs)  51.9 us
    ppermute x20, waiting for transfers between devices, send(): return lax.ppermute(value, 'grid', pairs)  46.7 us
    all_to_all x1, blocking collectives, body(): lax.all_to_all(sent, 'grid', split_axis=0, concat_axis=0, tiled=True)  42.5 us
    ppermute x3, waiting for transfers between devices, exchange(): lax.ppermute(parts[step], axis, [(d, d ^ step) for d in range(count)])  22 us
    all_to_all x1, waiting for transfers between devices, body(): lax.all_to_all(along_mid, 'pencil', split_axis=0, concat_axis=0, tiled=True)  14.2 us
    pallas_call x2, Pallas kernels, transform_mid(): pl.pallas_call(functools.partial(mid_kernel, first_chunk, pencils if apar...  12.2 us
    pallas_call x2, Pallas kernels, transform_long(): pl.pallas_call(long_kernel, grid=(slots,), in_specs=[pl.BlockSpec(memory_...  9.58 us
    pallas_call x1, Pallas kernels, transform_z(): pl.pallas_call(z_kernel, grid=(steps + 1,), in_specs=[pl.BlockSpec(memory...  7.12 us
  transfers between devices with their start and end apart: 25, of which 10 were waited for; matrix products, arithmetic and copies ran while one was open for 3% of the time, Pallas kernels for 12%

profile of v7, /device:TPU:0, one launch (start us, length us, event | category | flops | bytes accessed | tf_op | source)
XLA Modules:
  0.0 241.1 jit_solution(2377116780982563918)
XLA Ops:
  1.3 7.1 %transform_z.1 = (bf16[2,65,16,128]{3,2,1,0:T(8,128)(2,1)}, bf16[2,65,16,128]{3,2,1,0:T(8,128)(2,1)}, bf16[2,65,16,128]{3,2,1,0:T(8,128)(2,1)}, bf16[2,65,16,128...) custom-call(s32[1,3]{1,0:T(1,128)} %levels_ref.1, ...), custom_call_target="tpu_custom_call" | custom-call | flops 2147483648 | bytes 16777216 | tf_op jit(solution)/shard_map/transform_z/pallas_call | solution.py:262
  8.4 0.7 collective-permute-start.4
  9.1 0.7 collective-permute-start.2
  9.8 7.1 %collective-permute-start.7 = (bf16[2,65,16,128]{3,2,1,0:T(8,128)(2,1)}, bf16[2,65,16,128]{3,2,1,0:T(8,128)(2,1)S(1)}, u32[]{:S(2)}, u32[]{:S(2)}) collective-permute-start(bf16[2,65,16,128]{3,2,1,0:T(8,128)(2,1)} %get-tuple-element.82), channel_id=1, source_target_pairs={{0,8},{4,12},{8,0},{12,4},{16,24},{20,28},{24,16},{28,20},{1,9},{5... | collective-permute-start | bytes 1597448 | tf_op jit(solution)/shard_map/ppermute | solution.py:628
  17.0 0.7 collective-permute-start.6
  17.7 0.6 fusion.11
  18.3 0.7 fusion.12
  19.0 1.4 sine_multiply_fusion.2
  20.4 0.7 collective-permute-start.12
  21.1 0.7 collective-permute-start.11
  21.8 8.2 %collective-permute-done.7.refs_4_.refs_5_.refs_16_.refs_17_ = bf16[2,65,16,128]{3,2,1,0:T(8,128)(2,1)S(1)} collective-permute-done((bf16[2,65,16,128]{3,2,1,0:T(8,128)(2,1)}, bf16[2,65,16,128]{3,2,1,0:T(8,128)(2,1)S(1)}, u32[]{:S(2)}, u32[]{:S(2)}) %collective-permute-start.7) | collective-permute-done | bytes 532512 | tf_op jit(solution)/shard_map/ppermute | solution.py:628
  30.0 12.9 %collective-permute-start.14 = (bf16[2,65,16,128]{3,2,1,0:T(8,128)(2,1)}, bf16[2,65,16,128]{3,2,1,0:T(8,128)(2,1)S(1)}, u32[]{:S(2)}, u32[]{:S(2)}) collective-permute-start(bf16[2,65,16,128]{3,2,1,0:T(8,128)(2,1)} %get-tuple-element.96), channel_id=1, source_target_pairs={{0,8},{4,12},{8,0},{12,4},{16,24},{20,28},{24,16},{28,20},{1,9},{5... | collective-permute-start | bytes 1597448 | tf_op jit(solution)/shard_map/ppermute | solution.py:628
  43.0 0.7 collective-permute-start.13
  43.7 1.4 sine_multiply_fusion.1
  45.2 1.3 sine_multiply_fusion
  46.6 3.1 %relay.2 = (bf16[2,65,16,128]{3,2,1,0:T(8,128)(2,1)}, bf16[2,65,16,128]{3,2,1,0:T(8,128)(2,1)}) custom-call(bf16[2,65,16,128]{3,2,1,0:T(8,128)(2,1)} %get-tuple-element.81.refs_0_.refs_1_.refs_8_, bf16[2,65,16,128]{3,2,1,0:T(8,128)(2,1)} %get-tuple-element.81.refs_0_.refs_1_.refs_8_, bf16[2,65,16,128]{3,2,1,0:T(8,128)(2,1)} %copy-done.14, ...), custom_call_target="tpu_custom_call" | custom-call | bytes 4259840 | tf_op jit(solution)/shard_map/relay/pallas_call | solution.py:334
  49.6 4.5 %collective-permute-start.10 = (bf16[2,65,16,128]{3,2,1,0:T(8,128)(2,1)}, bf16[2,65,16,128]{3,2,1,0:T(8,128)(2,1)}, u32[]{:S(2)}, u32[]{:S(2)}) collective-permute-start(bf16[2,65,16,128]{3,2,1,0:T(8,128)(2,1)} %get-tuple-element.86), channel_id=1, source_target_pairs={{0,20},{4,16},{24,12},{28,8},{8,24},{12,28},{16,0},{20,4},{1,21},{... | collective-permute-start | bytes 1597448 | tf_op jit(solution)/shard_map/ppermute | solution.py:628
  54.2 9.1 %collective-permute-start.9 = (bf16[2,65,16,128]{3,2,1,0:T(8,128)(2,1)}, bf16[2,65,16,128]{3,2,1,0:T(8,128)(2,1)}, u32[]{:S(2)}, u32[]{:S(2)}) collective-permute-start(bf16[2,65,16,128]{3,2,1,0:T(8,128)(2,1)} %get-tuple-element.85), channel_id=1, source_target_pairs={{0,16},{4,20},{8,24},{12,28},{16,0},{20,4},{24,8},{28,12},{1,17},{... | collective-permute-start | bytes 1597448 | tf_op jit(solution)/shard_map/ppermute | solution.py:628
  63.2 8.6 %collective-permute-done.15.refs_6_.refs_7_.refs_18_.refs_19_ = bf16[2,65,16,128]{3,2,1,0:T(8,128)(2,1)S(1)} collective-permute-done((bf16[2,65,16,128]{3,2,1,0:T(8,128)(2,1)}, bf16[2,65,16,128]{3,2,1,0:T(8,128)(2,1)S(1)}, u32[]{:S(2)}, u32[]{:S(2)}) %collective-permute-start.15) | collective-permute-done | bytes 532512 | tf_op jit(solution)/shard_map/ppermute | solution.py:628
  71.8 2.1 collective-permute-start.5
  73.9 0.8 copy-done.15
  74.7 2.5 %collective-permute-start.3 = (bf16[2,65,16,128]{3,2,1,0:T(8,128)(2,1)S(1)}, bf16[2,65,16,128]{3,2,1,0:T(8,128)(2,1)}, u32[]{:S(2)}, u32[]{:S(2)}) collective-permute-start(bf16[2,65,16,128]{3,2,1,0:T(8,128)(2,1)S(1)} %copy-done.19), channel_id=1, source_target_pairs={{0,8},{4,12},{24,16},{28,20},{1,9},{5,13},{25,17},{29,21},{2,10},{... | collective-permute-start | bytes 1597448 | tf_op jit(solution)/shard_map/ppermute | solution.py:628
  77.4 0.6 fusion.10
  78.0 3.1 %relay.3 = (bf16[2,65,16,128]{3,2,1,0:T(8,128)(2,1)}, bf16[2,65,16,128]{3,2,1,0:T(8,128)(2,1)}) custom-call(bf16[2,65,16,128]{3,2,1,0:T(8,128)(2,1)} %get-tuple-element.93.refs_0_.refs_1_.refs_8_, bf16[2,65,16,128]{3,2,1,0:T(8,128)(2,1)} %get-tuple-element.93.refs_0_.refs_1_.refs_8_, bf16[2,65,16,128]{3,2,1,0:T(8,128)(2,1)} %copy-done.15, ...), custom_call_target="tpu_custom_call" | custom-call | bytes 4259840 | tf_op jit(solution)/shard_map/relay/pallas_call | solution.py:334
  81.1 15.1 %collective-permute-done.10.refs_10_.refs_11_ = bf16[2,65,16,128]{3,2,1,0:T(8,128)(2,1)} collective-permute-done((bf16[2,65,16,128]{3,2,1,0:T(8,128)(2,1)}, bf16[2,65,16,128]{3,2,1,0:T(8,128)(2,1)}, u32[]{:S(2)}, u32[]{:S(2)}) %collective-permute-start.10) | collective-permute-done | bytes 532512 | tf_op jit(solution)/shard_map/ppermute | solution.py:628
  96.2 11.3 %collective-permute-done.9.refs_8_.refs_9_ = bf16[2,65,16,128]{3,2,1,0:T(8,128)(2,1)} collective-permute-done((bf16[2,65,16,128]{3,2,1,0:T(8,128)(2,1)}, bf16[2,65,16,128]{3,2,1,0:T(8,128)(2,1)}, u32[]{:S(2)}, u32[]{:S(2)}) %collective-permute-start.9) | collective-permute-done | bytes 532512 | tf_op jit(solution)/shard_map/ppermute | solution.py:628
  107.4 2.9 %collective-permute-start.18 = (bf16[2,65,16,128]{3,2,1,0:T(8,128)(2,1)}, bf16[2,65,16,128]{3,2,1,0:T(8,128)(2,1)}, u32[]{:S(2)}, u32[]{:S(2)}) collective-permute-start(bf16[2,65,16,128]{3,2,1,0:T(8,128)(2,1)} %get-tuple-element.115), channel_id=1, source_target_pairs={{0,16},{4,20},{8,24},{12,28},{16,0},{20,4},{24,8},{28,12},{1,17},{... | collective-permute-start | bytes 1597448 | tf_op jit(solution)/shard_map/ppermute | solution.py:628
  110.4 2.4 %collective-permute-done.3.refs_4_.refs_5_ = bf16[2,65,16,128]{3,2,1,0:T(8,128)(2,1)} collective-permute-done((bf16[2,65,16,128]{3,2,1,0:T(8,128)(2,1)S(1)}, bf16[2,65,16,128]{3,2,1,0:T(8,128)(2,1)}, u32[]{:S(2)}, u32[]{:S(2)}) %collective-permute-start.3) | collective-permute-done | bytes 532512 | tf_op jit(solution)/shard_map/ppermute | solution.py:628
  112.8 5.9 %transform_mid.2 = bf16[4,2,2,2,2,64,256]{6,5,4,3,2,1,0:T(8,128)(2,1)} custom-call(bf16[512,512]{1,0:T(8,128)(2,1)} %constant.68.clone.turn_ref, bf16[2,256,512]{2,1,0:T(8,128)(2,1)} %constant.63.clone.table_ref, bf16[2,65,16,128]{3,2,1,0:T(8,128)(2,1)} %get-tuple-element.102.refs_0_.refs_1_, bf16[2,65,16,128]{3,2,1,0:T(8,128)(2,1)} %get-tuple-element.102.refs_0_.refs_1_, ...), custom_call_target="tpu_custom_call" | custom-call | flops 21810380800 | bytes 7421952 | tf_op jit(solution)/shard_map/transform_mid/pallas_call | solution.py:421
  118.7 4.5 %all-to-all-start = ((bf16[4,2,2,2,128,256]{5,4,3,2,1,0:T(8,128)(2,1)}), bf16[4,2,2,2,128,256]{5,4,3,2,1,0:T(8,128)(2,1)}, u32[]{:S(2)}, u32[]{:S(2)}) async-start(bf16[4,2,2,2,128,256]{5,4,3,2,1,0:T(8,128)(2,1)} %bitcast.21), calls=%async_computation | async-start | bytes 4194304 | tf_op jit(solution)/shard_map/all_to_all | solution.py:753
  123.2 2.6 %collective-permute-start.17 = (bf16[2,65,16,128]{3,2,1,0:T(8,128)(2,1)}, bf16[2,65,16,128]{3,2,1,0:T(8,128)(2,1)}, u32[]{:S(2)}, u32[]{:S(2)}) collective-permute-start(bf16[2,65,16,128]{3,2,1,0:T(8,128)(2,1)} %get-tuple-element.114), channel_id=1, source_target_pairs={{0,12},{4,8},{24,20},{28,16},{1,13},{5,9},{25,21},{29,17},{2,14},{... | collective-permute-start | bytes 1597448 | tf_op jit(solution)/shard_map/ppermute | solution.py:628
  125.8 4.0 %collective-permute-start.16 = (bf16[2,65,16,128]{3,2,1,0:T(8,128)(2,1)}, bf16[2,65,16,128]{3,2,1,0:T(8,128)(2,1)}, u32[]{:S(2)}, u32[]{:S(2)}) collective-permute-start(bf16[2,65,16,128]{3,2,1,0:T(8,128)(2,1)} %get-tuple-element.113), channel_id=1, source_target_pairs={{0,8},{4,12},{24,16},{28,20},{1,9},{5,13},{25,17},{29,21},{2,10},{... | collective-permute-start | bytes 1597448 | tf_op jit(solution)/shard_map/ppermute | solution.py:628
  129.8 0.8 copy-done.25
  130.7 1.4 hold.1.z_ref
  132.1 14.2 %all-to-all-done.refs_0_ = bf16[4,2,2,2,128,256]{5,4,3,2,1,0:T(8,128)(2,1)} async-done(((bf16[4,2,2,2,128,256]{5,4,3,2,1,0:T(8,128)(2,1)}), bf16[4,2,2,2,128,256]{5,4,3,2,1,0:T(8,128)(2,1)}, u32[]{:S(2)}, u32[]{:S(2)}) %all-to-all-start) | async-done | bytes 2097184 | tf_op jit(solution)/shard_map/all_to_all | solution.py:753
  146.3 0.6 copy-done.9
  146.9 5.5 %transform_long.2 = bf16[48,2,2,32,128]{4,3,2,1,0:T(8,128)(2,1)} custom-call(s32[64]{0:T(128)S(1)} %copy-done.3, f32[2,2]{1,0:T(2,128)S(1)} %copy-done.9, f32[2,2,256,1]{3,2,1,0:T(8,128)S(1)} %copy.16.x_ref, f32[2,512]{1,0:T(2,128)S(1)} %pad_maximum_fusion.y_ref, bf16[1024,512]{1,0:T(8,128)(2,1)S(1)} %copy-done.4, bf16[512,1024]{1,0:T(8,128)(2,1)S(1)} %copy-done.6, ...), custom_call_target="tpu_custom_call" | custom-call | flops 2147483648 | bytes 9961472 | tf_op jit(solution)/shard_map/transform_long/pallas_call | solution.py:534
  152.4 3.9 %all-to-all-start.1 = ((bf16[8,6,2,2,32,128]{5,4,3,2,1,0:T(8,128)(2,1)}), bf16[8,6,2,2,32,128]{5,4,3,2,1,0:T(8,128)(2,1)S(1)}, u32[]{:S(2)}, u32[]{:S(2)}) async-start(bf16[8,6,2,2,32,128]{5,4,3,2,1,0:T(8,128)(2,1)} %bitcast.10), calls=%async_computation.1 | async-start | bytes 3145728 | tf_op jit(solution)/shard_map/all_to_all | solution.py:770
  156.3 0.6 collective-permute-done.18.refs_8_.refs_9_
  157.4 6.3 %transform_mid.3 = (bf16[2,2,2,2,64,256]{5,4,3,2,1,0:T(8,128)(2,1)}, bf16[2,2,2,2,64,256]{5,4,3,2,1,0:T(8,128)(2,1)}, bf16[2,2,2,2,64,256]{5,4,3,2,1,0:T(8,128)(2,1)}, bf16[2,2,2,2,64,256]{5,4,3,2,1,0:T(8,128)(2,1)}) custom-call(bf16[512,512]{1,0:T(8,128)(2,1)} %constant.68.clone.turn_ref, bf16[2,256,512]{2,1,0:T(8,128)(2,1)} %constant.63.clone.table_ref, ...), custom_call_target="tpu_custom_call" | custom-call | flops 21810380800 | bytes 7421952 | tf_op jit(solution)/shard_map/transform_mid/pallas_call | solution.py:421
  163.7 1.6 collective-permute-start.20
  165.3 2.4 collective-permute-start.21
  167.7 11.1 %collective-permute-done.20.refs_1_ = bf16[2,2,2,128,256]{4,3,2,1,0:T(8,128)(2,1)S(1)} collective-permute-done((bf16[2,2,2,128,256]{4,3,2,1,0:T(8,128)(2,1)}, bf16[2,2,2,128,256]{4,3,2,1,0:T(8,128)(2,1)S(1)}, u32[]{:S(2)}, u32[]{:S(2)}) %collective-permute-start.20) | collective-permute-done | bytes 524320 | tf_op jit(solution)/shard_map/ppermute | solution.py:654
  178.9 10.8 %collective-permute-done.21.refs_2_ = bf16[2,2,2,128,256]{4,3,2,1,0:T(8,128)(2,1)S(1)} collective-permute-done((bf16[2,2,2,128,256]{4,3,2,1,0:T(8,128)(2,1)}, bf16[2,2,2,128,256]{4,3,2,1,0:T(8,128)(2,1)S(1)}, u32[]{:S(2)}, u32[]{:S(2)}) %collective-permute-start.21) | collective-permute-done | bytes 524320 | tf_op jit(solution)/shard_map/ppermute | solution.py:654
  189.7 1.0 copy-done.8
  190.7 4.1 %transform_long.3 = bf16[48,2,2,32,128]{4,3,2,1,0:T(8,128)(2,1)S(1)} custom-call(s32[64]{0:T(128)S(1)} %copy-done.3, f32[2,2]{1,0:T(2,128)S(1)} %get-tuple-element.131.z_ref, f32[2,2,256,1]{3,2,1,0:T(8,128)S(1)} %copy-done.1, f32[2,512]{1,0:T(2,128)S(1)} %pad_maximum_fusion.y_ref, bf16[1024,512]{1,0:T(8,128)(2,1)S(1)} %copy-done.5, ...), custom_call_target="tpu_custom_call" | custom-call | flops 2147483648 | bytes 9961472 | tf_op jit(solution)/shard_map/transform_long/pallas_call | solution.py:534
  194.9 42.5 %all_to_all.15.refs_1_ = bf16[8,6,2,2,32,128]{5,4,3,2,1,0:T(8,128)(2,1)S(1)} all-to-all(bf16[8,6,2,2,32,128]{5,4,3,2,1,0:T(8,128)(2,1)S(1)} %bitcast.18), channel_id=1, replica_groups=mesh['grid'=8,'pencil'=4] {'grid'}, dimensions={0} | all-to-all | bytes 3145728 | tf_op jit(solution)/shard_map/all_to_all | solution.py:770
  237.4 3.7 %lay_rows.1 = f32[6,2,32,4096]{3,2,1,0:T(8,128)} custom-call(bf16[256,256]{1,0:T(8,128)(2,1)S(1)} %copy-done.2, bf16[8,6,2,2,32,128]{5,4,3,2,1,0:T(8,128)(2,1)S(1)} %all-to-all-done.1.refs_0_, bf16[8,6,2,2,32,128]{5,4,3,2,1,0:T(8,128)(2,1)S(1)} %all_to_all.15.refs_1_), custom_call_target="tpu_custom_call" | custom-call | bytes 9437184 | tf_op jit(solution)/shard_map/lay_rows/pallas_call | solution.py:595
  (74 shorter events, 0.9 us)
Async XLA Ops:
  1.3 16.4 %copy-start.16 = (f32[3]{0:T(128)S(1)}, f32[3]{0:T(128)}, u32[]{:S(2)}) copy-start(f32[3]{0:T(128)} %param.21) | copy-start | bytes 40
  1.3 17.0 %copy-start.17 = (f32[3]{0:T(128)S(1)}, f32[3]{0:T(128)}, u32[]{:S(2)}) copy-start(f32[3]{0:T(128)} %param.20) | copy-start | bytes 40
  8.4 11.9 %collective-permute-start.4 = (bf16[2,65,16,128]{3,2,1,0:T(8,128)(2,1)}, bf16[2,65,16,128]{3,2,1,0:T(8,128)(2,1)S(1)}, u32[]{:S(2)}, u32[]{:S(2)}) collective-permute-start(bf16[2,65,16,128]{3,2,1,0:T(8,128)(2,1)} %get-tuple-element.78), channel_id=1, source_target_pairs={{8,20},{20,8},{12,16},{16,12},{9,21},{21,9},{13,17},{17,13},{10,22... | collective-permute-start | bytes 1597448 | tf_op jit(solution)/shard_map/ppermute | solution.py:628
  9.1 11.9 %collective-permute-start.2 = (bf16[2,65,16,128]{3,2,1,0:T(8,128)(2,1)}, bf16[2,65,16,128]{3,2,1,0:T(8,128)(2,1)S(1)}, u32[]{:S(2)}, u32[]{:S(2)}) collective-permute-start(bf16[2,65,16,128]{3,2,1,0:T(8,128)(2,1)} %get-tuple-element.76), channel_id=1, source_target_pairs={{8,16},{16,8},{12,20},{20,12},{9,17},{17,9},{13,21},{21,13},{10,18... | collective-permute-start | bytes 1597448 | tf_op jit(solution)/shard_map/ppermute | solution.py:628
  9.8 20.2 %collective-permute-start.7 = (bf16[2,65,16,128]{3,2,1,0:T(8,128)(2,1)}, bf16[2,65,16,128]{3,2,1,0:T(8,128)(2,1)S(1)}, u32[]{:S(2)}, u32[]{:S(2)}) collective-permute-start(bf16[2,65,16,128]{3,2,1,0:T(8,128)(2,1)} %get-tuple-element.82), channel_id=1, source_target_pairs={{0,8},{4,12},{8,0},{12,4},{16,24},{20,28},{24,16},{28,20},{1,9},{5... | collective-permute-start | bytes 1597448 | tf_op jit(solution)/shard_map/ppermute | solution.py:628
  16.9 26.0 %collective-permute-start.8 = (bf16[2,65,16,128]{3,2,1,0:T(8,128)(2,1)}, bf16[2,65,16,128]{3,2,1,0:T(8,128)(2,1)S(1)}, u32[]{:S(2)}, u32[]{:S(2)}) collective-permute-start(bf16[2,65,16,128]{3,2,1,0:T(8,128)(2,1)} %get-tuple-element.83), channel_id=1, source_target_pairs={{0,12},{4,8},{8,4},{12,0},{16,28},{20,24},{24,20},{28,16},{1,13},{... | collective-permute-start | bytes 1597448 | tf_op jit(solution)/shard_map/ppermute | solution.py:628
  17.0 26.0 %collective-permute-start.6 = (bf16[2,65,16,128]{3,2,1,0:T(8,128)(2,1)}, bf16[2,65,16,128]{3,2,1,0:T(8,128)(2,1)S(1)}, u32[]{:S(2)}, u32[]{:S(2)}) collective-permute-start(bf16[2,65,16,128]{3,2,1,0:T(8,128)(2,1)} %get-tuple-element.84.refs_9_), channel_id=1, source_target_pairs={{8,12},{12,8},{16,20},{20,16},{9,13},{13,9},{17,21},{21,17},{10,14... | collective-permute-start | bytes 1597448 | tf_op jit(solution)/shard_map/ppermute | solution.py:628
  20.4 9.7 %copy-start.22 = (bf16[2,65,16,128]{3,2,1,0:T(8,128)(2,1)}, bf16[2,65,16,128]{3,2,1,0:T(8,128)(2,1)S(1)}, u32[]{:S(2)}) copy-start(bf16[2,65,16,128]{3,2,1,0:T(8,128)(2,1)S(1)} %collective-permute-done.4.refs_14_.refs_15_) | copy-start | bytes 1597444
  20.4 29.3 %collective-permute-start.12 = (bf16[2,65,16,128]{3,2,1,0:T(8,128)(2,1)}, bf16[2,65,16,128]{3,2,1,0:T(8,128)(2,1)S(1)}, u32[]{:S(2)}, u32[]{:S(2)}) collective-permute-start(bf16[2,65,16,128]{3,2,1,0:T(8,128)(2,1)} %get-tuple-element.114), channel_id=1, source_target_pairs={{8,20},{20,8},{12,16},{16,12},{9,21},{21,9},{13,17},{17,13},{10,22... | collective-permute-start | bytes 1597448 | tf_op jit(solution)/shard_map/ppermute | solution.py:628
  21.1 22.6 %copy-start.24 = (bf16[2,65,16,128]{3,2,1,0:T(8,128)(2,1)}, bf16[2,65,16,128]{3,2,1,0:T(8,128)(2,1)S(1)}, u32[]{:S(2)}) copy-start(bf16[2,65,16,128]{3,2,1,0:T(8,128)(2,1)S(1)} %collective-permute-done.2.refs_12_.refs_13_) | copy-start | bytes 1597444
  21.1 33.1 %collective-permute-start.11 = (bf16[2,65,16,128]{3,2,1,0:T(8,128)(2,1)}, bf16[2,65,16,128]{3,2,1,0:T(8,128)(2,1)S(1)}, u32[]{:S(2)}, u32[]{:S(2)}) collective-permute-start(bf16[2,65,16,128]{3,2,1,0:T(8,128)(2,1)} %get-tuple-element.113), channel_id=1, source_target_pairs={{8,16},{16,8},{12,20},{20,12},{9,17},{17,9},{13,21},{21,13},{10,18... | collective-permute-start | bytes 1597448 | tf_op jit(solution)/shard_map/ppermute | solution.py:628
  30.0 16.5 %copy-start.10 = (bf16[2,65,16,128]{3,2,1,0:T(8,128)(2,1)}, bf16[2,65,16,128]{3,2,1,0:T(8,128)(2,1)S(1)}, u32[]{:S(2)}) copy-start(bf16[2,65,16,128]{3,2,1,0:T(8,128)(2,1)S(1)} %collective-permute-done.7.refs_4_.refs_5_.refs_16_.refs_17_) | copy-start | bytes 1597444
  30.0 33.2 %collective-permute-start.14 = (bf16[2,65,16,128]{3,2,1,0:T(8,128)(2,1)}, bf16[2,65,16,128]{3,2,1,0:T(8,128)(2,1)S(1)}, u32[]{:S(2)}, u32[]{:S(2)}) collective-permute-start(bf16[2,65,16,128]{3,2,1,0:T(8,128)(2,1)} %get-tuple-element.96), channel_id=1, source_target_pairs={{0,8},{4,12},{8,0},{12,4},{16,24},{20,28},{24,16},{28,20},{1,9},{5... | collective-permute-start | bytes 1597448 | tf_op jit(solution)/shard_map/ppermute | solution.py:628
  43.0 3.6 %copy-start.12 = (bf16[2,65,16,128]{3,2,1,0:T(8,128)(2,1)}, bf16[2,65,16,128]{3,2,1,0:T(8,128)(2,1)S(1)}, u32[]{:S(2)}) copy-start(bf16[2,65,16,128]{3,2,1,0:T(8,128)(2,1)S(1)} %collective-permute-done.8.refs_6_.refs_7_.refs_18_.refs_19_) | copy-start | bytes 1597444
  43.0 28.8 %collective-permute-start.15 = (bf16[2,65,16,128]{3,2,1,0:T(8,128)(2,1)}, bf16[2,65,16,128]{3,2,1,0:T(8,128)(2,1)S(1)}, u32[]{:S(2)}, u32[]{:S(2)}) collective-permute-start(bf16[2,65,16,128]{3,2,1,0:T(8,128)(2,1)} %get-tuple-element.98), channel_id=1, source_target_pairs={{0,12},{4,8},{8,4},{12,0},{16,28},{20,24},{24,20},{28,16},{1,13},{... | collective-permute-start | bytes 1597448 | tf_op jit(solution)/shard_map/ppermute | solution.py:628
  43.0 3.5 %copy-start.14 = (bf16[2,65,16,128]{3,2,1,0:T(8,128)(2,1)}, bf16[2,65,16,128]{3,2,1,0:T(8,128)(2,1)S(1)}, u32[]{:S(2)}) copy-start(bf16[2,65,16,128]{3,2,1,0:T(8,128)(2,1)S(1)} %collective-permute-done.6.refs_2_.refs_3_) | copy-start | bytes 1597444
  43.0 30.9 %collective-permute-start.13 = (bf16[2,65,16,128]{3,2,1,0:T(8,128)(2,1)}, bf16[2,65,16,128]{3,2,1,0:T(8,128)(2,1)S(1)}, u32[]{:S(2)}, u32[]{:S(2)}) collective-permute-start(bf16[2,65,16,128]{3,2,1,0:T(8,128)(2,1)} %get-tuple-element.99.refs_9_), channel_id=1, source_target_pairs={{8,12},{12,8},{16,20},{20,16},{9,13},{13,9},{17,21},{21,17},{10,14... | collective-permute-start | bytes 1597448 | tf_op jit(solution)/shard_map/ppermute | solution.py:628
  46.5 25.3 %copy-start.21 = (bf16[2,65,16,128]{3,2,1,0:T(8,128)(2,1)S(1)}, bf16[2,65,16,128]{3,2,1,0:T(8,128)(2,1)}, u32[]{:S(2)}) copy-start(bf16[2,65,16,128]{3,2,1,0:T(8,128)(2,1)} %get-tuple-element.78) | copy-start | bytes 1597444
  46.6 28.1 %copy-start.19 = (bf16[2,65,16,128]{3,2,1,0:T(8,128)(2,1)S(1)}, bf16[2,65,16,128]{3,2,1,0:T(8,128)(2,1)}, u32[]{:S(2)}) copy-start(bf16[2,65,16,128]{3,2,1,0:T(8,128)(2,1)} %get-tuple-element.76) | copy-start | bytes 1597444
  49.6 24.3 %copy-start.20 = (bf16[2,65,16,128]{3,2,1,0:T(8,128)(2,1)}, bf16[2,65,16,128]{3,2,1,0:T(8,128)(2,1)S(1)}, u32[]{:S(2)}) copy-start(bf16[2,65,16,128]{3,2,1,0:T(8,128)(2,1)S(1)} %collective-permute-done.12.refs_14_.refs_15_) | copy-start | bytes 1597444
  49.6 46.5 %collective-permute-start.10 = (bf16[2,65,16,128]{3,2,1,0:T(8,128)(2,1)}, bf16[2,65,16,128]{3,2,1,0:T(8,128)(2,1)}, u32[]{:S(2)}, u32[]{:S(2)}) collective-permute-start(bf16[2,65,16,128]{3,2,1,0:T(8,128)(2,1)} %get-tuple-element.86), channel_id=1, source_target_pairs={{0,20},{4,16},{24,12},{28,8},{8,24},{12,28},{16,0},{20,4},{1,21},{... | collective-permute-start | bytes 1597448 | tf_op jit(solution)/shard_map/ppermute | solution.py:628
  54.2 19.7 %copy-start.23 = (bf16[2,65,16,128]{3,2,1,0:T(8,128)(2,1)}, bf16[2,65,16,128]{3,2,1,0:T(8,128)(2,1)S(1)}, u32[]{:S(2)}) copy-start(bf16[2,65,16,128]{3,2,1,0:T(8,128)(2,1)S(1)} %collective-permute-done.11.refs_12_.refs_13_) | copy-start | bytes 1597444
  54.2 53.3 %collective-permute-start.9 = (bf16[2,65,16,128]{3,2,1,0:T(8,128)(2,1)}, bf16[2,65,16,128]{3,2,1,0:T(8,128)(2,1)}, u32[]{:S(2)}, u32[]{:S(2)}) collective-permute-start(bf16[2,65,16,128]{3,2,1,0:T(8,128)(2,1)} %get-tuple-element.85), channel_id=1, source_target_pairs={{0,16},{4,20},{8,24},{12,28},{16,0},{20,4},{24,8},{28,12},{1,17},{... | collective-permute-start | bytes 1597448 | tf_op jit(solution)/shard_map/ppermute | solution.py:628
  63.2 14.7 %copy-start.11 = (bf16[2,65,16,128]{3,2,1,0:T(8,128)(2,1)}, bf16[2,65,16,128]{3,2,1,0:T(8,128)(2,1)S(1)}, u32[]{:S(2)}) copy-start(bf16[2,65,16,128]{3,2,1,0:T(8,128)(2,1)S(1)} %collective-permute-done.14.refs_4_.refs_5_.refs_16_.refs_17_) | copy-start | bytes 1597444
  63.2 44.2 %collective-permute-start.1 = (bf16[2,65,16,128]{3,2,1,0:T(8,128)(2,1)}, bf16[2,65,16,128]{3,2,1,0:T(8,128)(2,1)}, u32[]{:S(2)}, u32[]{:S(2)}) collective-permute-start(bf16[2,65,16,128]{3,2,1,0:T(8,128)(2,1)} %get-tuple-element.74), channel_id=1, source_target_pairs={{0,4},{4,0},{8,12},{12,8},{16,20},{20,16},{24,28},{28,24},{1,5},{5... | collective-permute-start | bytes 1597448 | tf_op jit(solution)/shard_map/ppermute | solution.py:628
  71.8 6.2 %copy-start.13 = (bf16[2,65,16,128]{3,2,1,0:T(8,128)(2,1)}, bf16[2,65,16,128]{3,2,1,0:T(8,128)(2,1)S(1)}, u32[]{:S(2)}) copy-start(bf16[2,65,16,128]{3,2,1,0:T(8,128)(2,1)S(1)} %collective-permute-done.15.refs_6_.refs_7_.refs_18_.refs_19_) | copy-start | bytes 1597444
  71.8 38.6 %collective-permute-start.5 = (bf16[2,65,16,128]{3,2,1,0:T(8,128)(2,1)S(1)}, bf16[2,65,16,128]{3,2,1,0:T(8,128)(2,1)}, u32[]{:S(2)}, u32[]{:S(2)}) collective-permute-start(bf16[2,65,16,128]{3,2,1,0:T(8,128)(2,1)S(1)} %copy-done.21), channel_id=1, source_target_pairs={{0,12},{4,8},{24,20},{28,16},{1,13},{5,9},{25,21},{29,17},{2,14},{... | collective-permute-start | bytes 1597448 | tf_op jit(solution)/shard_map/ppermute | solution.py:628
  74.7 38.1 %collective-permute-start.3 = (bf16[2,65,16,128]{3,2,1,0:T(8,128)(2,1)S(1)}, bf16[2,65,16,128]{3,2,1,0:T(8,128)(2,1)}, u32[]{:S(2)}, u32[]{:S(2)}) collective-permute-start(bf16[2,65,16,128]{3,2,1,0:T(8,128)(2,1)S(1)} %copy-done.19), channel_id=1, source_target_pairs={{0,8},{4,12},{24,16},{28,20},{1,9},{5,13},{25,17},{29,21},{2,10},{... | collective-permute-start | bytes 1597448 | tf_op jit(solution)/shard_map/ppermute | solution.py:628
  77.4 68.9 %copy-start = (f32[2,2,256,1]{3,2,1,0:T(8,128)}, f32[2,2,256,1]{3,2,1,0:T(8,128)S(1)}, u32[]{:S(2)}) copy-start(f32[2,2,256,1]{3,2,1,0:T(8,128)S(1)} %copy.16.x_ref) | copy-start | bytes 12292
  78.0 18.2 %copy-start.18 = (bf16[2,65,16,128]{3,2,1,0:T(8,128)(2,1)S(1)}, bf16[2,65,16,128]{3,2,1,0:T(8,128)(2,1)}, u32[]{:S(2)}) copy-start(bf16[2,65,16,128]{3,2,1,0:T(8,128)(2,1)} %get-tuple-element.70) | copy-start | bytes 1597444
  96.2 33.6 %collective-permute-start = (bf16[2,65,16,128]{3,2,1,0:T(8,128)(2,1)S(1)}, bf16[2,65,16,128]{3,2,1,0:T(8,128)(2,1)S(1)}, u32[]{:S(2)}, u32[]{:S(2)}) collective-permute-start(bf16[2,65,16,128]{3,2,1,0:T(8,128)(2,1)S(1)} %copy-done.18), channel_id=1, source_target_pairs={{0,4},{4,0},{8,12},{12,8},{16,20},{20,16},{24,28},{28,24},{1,5},{5... | collective-permute-start | bytes 1597448 | tf_op jit(solution)/shard_map/ppermute | solution.py:628
  107.4 48.8 %collective-permute-start.19 = (bf16[2,65,16,128]{3,2,1,0:T(8,128)(2,1)}, bf16[2,65,16,128]{3,2,1,0:T(8,128)(2,1)}, u32[]{:S(2)}, u32[]{:S(2)}) collective-permute-start(bf16[2,65,16,128]{3,2,1,0:T(8,128)(2,1)} %get-tuple-element.116), channel_id=1, source_target_pairs={{0,20},{4,16},{24,12},{28,8},{8,24},{12,28},{16,0},{20,4},{1,21},{... | collective-permute-start | bytes 1597448 | tf_op jit(solution)/shard_map/ppermute | solution.py:628
  107.4 49.4 %collective-permute-start.18 = (bf16[2,65,16,128]{3,2,1,0:T(8,128)(2,1)}, bf16[2,65,16,128]{3,2,1,0:T(8,128)(2,1)}, u32[]{:S(2)}, u32[]{:S(2)}) collective-permute-start(bf16[2,65,16,128]{3,2,1,0:T(8,128)(2,1)} %get-tuple-element.115), channel_id=1, source_target_pairs={{0,16},{4,20},{8,24},{12,28},{16,0},{20,4},{24,8},{28,12},{1,17},{... | collective-permute-start | bytes 1597448 | tf_op jit(solution)/shard_map/ppermute | solution.py:628
  118.7 27.6 %all-to-all-start = ((bf16[4,2,2,2,128,256]{5,4,3,2,1,0:T(8,128)(2,1)}), bf16[4,2,2,2,128,256]{5,4,3,2,1,0:T(8,128)(2,1)}, u32[]{:S(2)}, u32[]{:S(2)}) async-start(bf16[4,2,2,2,128,256]{5,4,3,2,1,0:T(8,128)(2,1)} %bitcast.21), calls=%async_computation | async-start | bytes 4194304 | tf_op jit(solution)/shard_map/all_to_all | solution.py:753
  123.2 33.7 %collective-permute-start.17 = (bf16[2,65,16,128]{3,2,1,0:T(8,128)(2,1)}, bf16[2,65,16,128]{3,2,1,0:T(8,128)(2,1)}, u32[]{:S(2)}, u32[]{:S(2)}) collective-permute-start(bf16[2,65,16,128]{3,2,1,0:T(8,128)(2,1)} %get-tuple-element.114), channel_id=1, source_target_pairs={{0,12},{4,8},{24,20},{28,16},{1,13},{5,9},{25,21},{29,17},{2,14},{... | collective-permute-start | bytes 1597448 | tf_op jit(solution)/shard_map/ppermute | solution.py:628
  125.8 31.6 %collective-permute-start.16 = (bf16[2,65,16,128]{3,2,1,0:T(8,128)(2,1)}, bf16[2,65,16,128]{3,2,1,0:T(8,128)(2,1)}, u32[]{:S(2)}, u32[]{:S(2)}) collective-permute-start(bf16[2,65,16,128]{3,2,1,0:T(8,128)(2,1)} %get-tuple-element.113), channel_id=1, source_target_pairs={{0,8},{4,12},{24,16},{28,20},{1,9},{5,13},{25,17},{29,21},{2,10},{... | collective-permute-start | bytes 1597448 | tf_op jit(solution)/shard_map/ppermute | solution.py:628
  130.7 15.6 %copy-start.3 = (s32[64]{0:T(128)S(1)}, s32[64]{0:T(128)}, u32[]{:S(2)}) copy-start(s32[64]{0:T(128)} %rows_ref.3) | copy-start | bytes 772
  130.7 15.6 %copy-start.4 = (bf16[1024,512]{1,0:T(8,128)(2,1)S(1)}, bf16[1024,512]{1,0:T(8,128)(2,1)}, u32[]{:S(2)}) copy-start(bf16[1024,512]{1,0:T(8,128)(2,1)} %constant.64.clone.first_ref) | copy-start | bytes 3145732
  130.7 15.6 %copy-start.6 = (bf16[512,1024]{1,0:T(8,128)(2,1)S(1)}, bf16[512,1024]{1,0:T(8,128)(2,1)}, u32[]{:S(2)}) copy-start(bf16[512,1024]{1,0:T(8,128)(2,1)} %constant.65.clone.second_ref) | copy-start | bytes 3145732
  152.4 42.5 %all-to-all-start.1 = ((bf16[8,6,2,2,32,128]{5,4,3,2,1,0:T(8,128)(2,1)}), bf16[8,6,2,2,32,128]{5,4,3,2,1,0:T(8,128)(2,1)S(1)}, u32[]{:S(2)}, u32[]{:S(2)}) async-start(bf16[8,6,2,2,32,128]{5,4,3,2,1,0:T(8,128)(2,1)} %bitcast.10), calls=%async_computation.1 | async-start | bytes 3145728 | tf_op jit(solution)/shard_map/all_to_all | solution.py:770
  157.4 32.3 %copy-start.1 = (f32[2,2,256,1]{3,2,1,0:T(8,128)S(1)}, f32[2,2,256,1]{3,2,1,0:T(8,128)}, u32[]{:S(2)}) copy-start(f32[2,2,256,1]{3,2,1,0:T(8,128)} %copy-done) | copy-start | bytes 12292
  157.4 32.3 %copy-start.5 = (bf16[1024,512]{1,0:T(8,128)(2,1)S(1)}, bf16[1024,512]{1,0:T(8,128)(2,1)}, u32[]{:S(2)}) copy-start(bf16[1024,512]{1,0:T(8,128)(2,1)} %constant.64.clone.first_ref) | copy-start | bytes 3145732
  157.4 32.3 %copy-start.7 = (bf16[512,1024]{1,0:T(8,128)(2,1)S(1)}, bf16[512,1024]{1,0:T(8,128)(2,1)}, u32[]{:S(2)}) copy-start(bf16[512,1024]{1,0:T(8,128)(2,1)} %constant.65.clone.second_ref) | copy-start | bytes 3145732
  163.7 15.1 %collective-permute-start.20 = (bf16[2,2,2,128,256]{4,3,2,1,0:T(8,128)(2,1)}, bf16[2,2,2,128,256]{4,3,2,1,0:T(8,128)(2,1)S(1)}, u32[]{:S(2)}, u32[]{:S(2)}) collective-permute-start(bf16[2,2,2,128,256]{4,3,2,1,0:T(8,128)(2,1)} %bitcast.24), channel_id=1, source_target_pairs={{0,1},{1,0},{2,3},{3,2},{4,5},{5,4},{6,7},{7,6},{8,9},{9,8},{10,11... | collective-permute-start | bytes 1572872 | tf_op jit(solution)/shard_map/ppermute | solution.py:654
  165.3 24.4 %collective-permute-start.21 = (bf16[2,2,2,128,256]{4,3,2,1,0:T(8,128)(2,1)}, bf16[2,2,2,128,256]{4,3,2,1,0:T(8,128)(2,1)S(1)}, u32[]{:S(2)}, u32[]{:S(2)}) collective-permute-start(bf16[2,2,2,128,256]{4,3,2,1,0:T(8,128)(2,1)} %bitcast.23), channel_id=1, source_target_pairs={{0,2},{1,3},{2,0},{3,1},{4,6},{5,7},{6,4},{7,5},{8,10},{9,11},{10,... | collective-permute-start | bytes 1572872 | tf_op jit(solution)/shard_map/ppermute | solution.py:654
  167.7 22.0 %collective-permute-start.22 = (bf16[2,2,2,128,256]{4,3,2,1,0:T(8,128)(2,1)}, bf16[2,2,2,128,256]{4,3,2,1,0:T(8,128)(2,1)S(1)}, u32[]{:S(2)}, u32[]{:S(2)}) collective-permute-start(bf16[2,2,2,128,256]{4,3,2,1,0:T(8,128)(2,1)} %bitcast.22), channel_id=1, source_target_pairs={{0,3},{1,2},{2,1},{3,0},{4,7},{5,6},{6,5},{7,4},{8,11},{9,10},{10,... | collective-permute-start | bytes 1572872 | tf_op jit(solution)/shard_map/ppermute | solution.py:654
  189.7 1.0 copy-start.8
  194.9 42.5 %copy-start.2 = (bf16[256,256]{1,0:T(8,128)(2,1)S(1)}, bf16[256,256]{1,0:T(8,128)(2,1)}, u32[]{:S(2)}) copy-start(bf16[256,256]{1,0:T(8,128)(2,1)} %constant.69.clone.turn_ref) | copy-start | bytes 393220
  (3 other events, 2.3 us)
